TPU v7x, 32 devices: a whole 2x2x4 slice. The times are simulated.
32 devices in a mesh: groups: 2 (over y), space: 8 (over z, x), node: 2 (over core).
Axes of the slice: x: 2, y: 2, z: 4, core: 2. Of those that a mesh axis runs over, the one named last changes fastest.
Arguments:
- concentration: float32 [2, 64, 64, 512], P('node', ('groups', 'space')), parts along dimension 1, may hold values from -6 to 6
- adjoint_next: bfloat16 [2, 64, 64, 512], P('node', ('groups', 'space')), parts along dimension 1, may hold values from -6 to 6
- speed: bfloat16 [3, 64, 64, 512], P(None, ('groups', 'space')), parts along dimension 1, may hold values from 0.099609375 to 0.29882812
- direction_mask: int32 [3, 64, 64, 64], P(None, ('groups', 'space')), parts along dimension 1, may hold values 0 or 1
- decay_rate: bfloat16 [64, 64, 512], P(('groups', 'space')), parts along dimension 0, may hold values from 0.019897461 to 0.29882812
- control: float32 [64, 64, 512], P(('groups', 'space')), parts along dimension 0, may hold values from -6 to 6
- goal_weight: bfloat16 [64, 64, 512], P(('groups', 'space')), parts along dimension 0, may hold values from 0.25 to 5.25, as said below
- node_index: int32 [2, 8], P('node'), may hold values from 0 to 8
- weight_num: int32 [2], P('node'), may hold values from -8 to 24
- step_index: int32 [2], P('groups'), parts along dimension 0, may hold values from 0 to 63
Outputs:
- adjoint: float32 [2, 64, 64, 512], P('node', ('groups', 'space')), parts along dimension 1
- gradient: float32 [64, 64, 512], P(('groups', 'space'), None, 'node'), parts along dimension 0
- objective: float32 [2], P('groups'), parts along dimension 0
There are 2 independent parts, one for each index of `groups`. A program takes and returns all parts, laid end to end along the dimension named above; an argument that names none is the same for every part. Nothing has to cross between parts.
Inputs may be any that keep to these rules, and one draw needn't show every extreme that they name: `node_index`: level indices of the nested rule. `weight_num`: signed weight numerators. `goal_weight`: positive weights.
All inputs are finite; a program needn't handle non-finite values. No bound on the sum of `direction_mask` on one device may be relied on, other than what follows from the above.
Results may differ from a plain program's by a relative error of at most 0.0003.
Values sent between devices are 32-bit elements; how exact they have to be, the bound alone decides.
No kernel may reach another device: no remote copies, remote signals or barrier semaphores. Data moves between devices by JAX's collectives and lax.ppermute only.
A program may use at most 64 MiB of HBM per device.

v0:
```python
import math

import jax
import jax.numpy as jnp
from jax import lax
from jax.sharding import PartitionSpec as P

time_step = 0.6
variance_gain = 0.5
penalty = 0.1
weight_denominator = 16.0


def shifted(value, axis, steps):
    count = lax.axis_size(axis)
    first, last = (max(0, -steps), min(count, count - steps))
    return lax.ppermute(value, axis, [(source, source + steps) for source in range(first, last)])


def with_halo(block, sides, width):
    for axis, dim in sides:
        count = lax.axis_size(axis)
        forward = [(i, i + 1) for i in range(count - 1)]
        backward = [(target, source) for source, target in forward]
        low = lax.ppermute(
            lax.slice_in_dim(block, block.shape[dim] - width, None, axis=dim), axis, forward
        )
        high = lax.ppermute(lax.slice_in_dim(block, 0, width, axis=dim), axis, backward)
        block = jnp.concatenate([low, block, high], axis=dim)
    return block


def node_scales(node_index, step_index):
    points = -jnp.cos(math.pi * node_index.astype(jnp.float32) / 8.0)
    source_phase = 1.0 + 0.5 * jnp.sin(2.0 * math.pi * step_index.astype(jnp.float32)[0] / 64.0)
    first_axis = 1.0 + 0.3 * points[:, 0]
    second_axis = 1.0 + 0.3 * points[:, 1]
    third_axis = (1.0 + 0.3 * points[:, 2]) * (1.0 + 0.2 * points[:, 7])
    kappa = jnp.exp(0.5 * (points[:, 3] + 0.5 * points[:, 5]))
    source = (1.0 + 0.3 * points[:, 4] + 0.2 * points[:, 6]) * source_phase
    return jnp.stack([first_axis, second_axis, third_axis, kappa, source], axis=1)


def expand_sign(direction_mask):
    signs = direction_mask.astype(jnp.float32) * 2.0 - 1.0
    extent = signs.shape
    return jnp.broadcast_to(signs[..., None], extent + (8,)).reshape(
        extent[:-1] + (extent[-1] * 8,)
    )


def tendency(extended, fields, scales):
    center = extended[:, 1:-1]
    padded = jnp.pad(center, ((0, 0), (0, 0), (1, 1), (1, 1)))
    lower = (extended[:, :-2], padded[:, :, :-2, 1:-1], padded[:, :, 1:-1, :-2])
    higher = (extended[:, 2:], padded[:, :, 2:, 1:-1], padded[:, :, 1:-1, 2:])
    advection = jnp.zeros_like(center)
    for component in range(3):
        velocity = fields[component][None] * scales[:, component, None, None, None]
        upwind = jnp.where(
            fields[3 + component][None] > 0, center - lower[component], center - higher[component]
        )
        advection = advection + velocity * upwind
    reaction = fields[6][None] * scales[:, 3, None, None, None] * center
    return -advection - reaction + fields[7][None] * scales[:, 4, None, None, None]


def transpose_step(cotangent, fields, scales):
    zero_rim = jnp.zeros(
        cotangent.shape[:1] + (cotangent.shape[1] + 2,) + cotangent.shape[2:], jnp.float32
    )
    _, pullback = jax.vjp(lambda extended: tendency(extended, fields, scales), zero_rim)
    spread_terms = pullback(time_step * cotangent)[0]
    interior = spread_terms[:, 1:-1]
    from_lower = shifted(spread_terms[:, -1:], "space", 1)
    from_upper = shifted(spread_terms[:, :1], "space", -1)
    interior = interior.at[:, :1].add(from_lower)
    interior = interior.at[:, -1:].add(from_upper)
    return cotangent + interior


def shards(
    concentration,
    adjoint_next,
    speed,
    direction_mask,
    decay_rate,
    control,
    goal_weight,
    node_index,
    weight_num,
    step_index,
):
    fields = jnp.concatenate(
        [
            speed.astype(jnp.float32),
            expand_sign(direction_mask),
            decay_rate.astype(jnp.float32)[None],
            control[None],
        ],
        0,
    )
    scales = node_scales(node_index, step_index)
    weights = weight_num.astype(jnp.float32) / weight_denominator
    goal = goal_weight.astype(jnp.float32)

    def advance(state):
        extended = with_halo(state, (("space", 1),), 1)
        return state + time_step * tendency(extended, fields, scales)

    first_section = advance(concentration)
    second_section = 0.75 * concentration + 0.25 * advance(first_section)
    final_state = concentration / 3.0 + 2.0 / 3.0 * advance(second_section)
    weighted = weights[:, None, None, None] * final_state
    first_part = jnp.sum(weighted, 0)
    second_part = jnp.sum(weighted * final_state, 0)
    cells = (
        final_state.shape[1] * lax.axis_size("space") * final_state.shape[2] * final_state.shape[3]
    )
    half_width = final_state.shape[3] // lax.axis_size("node")
    node_rank = lax.axis_index("node")
    first_moment, second_moment = lax.psum((first_part, second_part), "node")
    local_cost = jnp.sum(
        goal * (first_moment + variance_gain * (second_moment - first_moment * first_moment))
    )
    summed_cost = lax.psum(local_cost, "space")
    objective = jnp.reshape(summed_cost / cells, (1,))
    terminal = adjoint_next.astype(jnp.float32) + goal[None] * weights[:, None, None, None] * (
        1.0 + 2.0 * variance_gain * (final_state - first_moment[None])
    )
    third_cot = 2.0 / 3.0 * terminal
    second_adjoint = transpose_step(third_cot, fields, scales)
    second_cot = 0.25 * second_adjoint
    first_adjoint = transpose_step(second_cot, fields, scales)
    adjoint = terminal / 3.0 + 0.75 * second_adjoint + transpose_step(first_adjoint, fields, scales)
    source_total = time_step * jnp.sum(
        scales[:, 4, None, None, None] * (third_cot + second_cot + first_adjoint), 0
    )
    summed_terms = lax.psum(source_total, "node")
    share = lax.dynamic_slice_in_dim(summed_terms, node_rank * half_width, half_width, 2)
    gradient = share + penalty * lax.dynamic_slice_in_dim(
        control, node_rank * half_width, half_width, 2
    )
    return (adjoint, gradient, objective)


def solution(mesh):
    return jax.shard_map(
        shards,
        mesh=mesh,
        in_specs=(
            P("node", ("groups", "space"), None, None),
            P("node", ("groups", "space"), None, None),
            P(None, ("groups", "space"), None, None),
            P(None, ("groups", "space"), None, None),
            P(("groups", "space"), None, None),
            P(("groups", "space"), None, None),
            P(("groups", "space"), None, None),
            P("node", None),
            P("node"),
            P("groups"),
        ),
        out_specs=(
            P("node", ("groups", "space"), None, None),
            P(("groups", "space"), None, "node"),
            P("groups"),
        ),
        check_vma=False,
    )
```

profile of v0, /device:TPU:0, one launch (start us, length us, event | category | flops | bytes accessed | tf_op | source)
XLA Modules:
  0.0 216.8 jit_solution(17288027434937989722)
XLA Ops:
  7.2 1.4 copy.15
  9.6 5.5 %collective-permute-start = (f32[1,1,64,512]{2,3,1,0:T(8,128)}, f32[1,1,64,512]{2,3,1,0:T(8,128)}, u32[]{:S(2)}, u32[]{:S(2)}) collective-permute-start(f32[1,1,64,512]{2,3,1,0:T(8,128)} %get-tuple-element.124), channel_id=1, source_target_pairs={{0,2},{2,4},{4,6},{6,8},{8,10},{10,12},{12,14},{1,3},{3,5},{5,7},{... | collective-permute-start | bytes 393224 | tf_op jit(solution)/shard_map/ppermute | solution.py:25
  23.0 1.6 copy.17
  24.5 1.7 convert_element_type.31
  28.2 2.4 %copy.34 = f32[4,64,512]{1,2,0:T(8,128)} copy(f32[4,64,512]{2,1,0:T(8,128)} %param.27) | data formatting | bytes 1048576 | tf_op args[5]
  30.6 5.1 %fusion.12 = f32[1,4,64,512]{2,3,1,0:T(8,128)S(1)} fusion(f32[1,4,64,512]{2,3,1,0:T(8,128)} %copy-done.4, f32[1,1,64,512]{2,3,1,0:T(8,128)} %collective-permute-done.1, f32[1,1,64,512]{2,3,1,0:T(8,128)} %collective-permute-done, bf16[4,64,512]{1,2,0:T(8,128)(2,1)} %copy.32, f32[4,64,512]{1,2,0:T(8,128)} %copy.34, f32[]{:T(128)} %bitcast.14, f32[]{:T(128)} %bitcast.11, ...), kind=kLoop, calls=%fused_computation.46 | loop fusion | flops 3670016 | bytes 3719188 | tf_op jit(solution)/shard_map/add | solution.py:109
  35.7 4.7 %collective-permute-start.2 = (f32[1,1,64,512]{2,3,1,0:T(8,128)S(1)}, f32[1,1,64,512]{2,3,1,0:T(8,128)S(1)}, u32[]{:S(2)}, u32[]{:S(2)}) collective-permute-start(f32[1,1,64,512]{2,3,1,0:T(8,128)S(1)} %get-tuple-element.122), channel_id=1, source_target_pairs={{0,2},{2,4},{4,6},{6,8},{8,10},{10,12},{12,14},{1,3},{3,5},{5,7},{... | collective-permute-start | bytes 393224 | tf_op jit(solution)/shard_map/ppermute | solution.py:25
  41.7 9.3 %collective-permute-done.2 = f32[1,1,64,512]{2,3,1,0:T(8,128)S(1)} collective-permute-done((f32[1,1,64,512]{2,3,1,0:T(8,128)S(1)}, f32[1,1,64,512]{2,3,1,0:T(8,128)S(1)}, u32[]{:S(2)}, u32[]{:S(2)}) %collective-permute-start.2) | collective-permute-done | bytes 131104 | tf_op jit(solution)/shard_map/ppermute | solution.py:25
  51.0 1.8 fusion.22
  52.9 4.4 %collective-permute-start.4 = (f32[1,1,64,512]{2,3,1,0:T(8,128)S(1)}, f32[1,1,64,512]{2,3,1,0:T(8,128)S(1)}, u32[]{:S(2)}, u32[]{:S(2)}) collective-permute-start(f32[1,1,64,512]{2,3,1,0:T(8,128)S(1)} %get-tuple-element.120), channel_id=1, source_target_pairs={{0,2},{2,4},{4,6},{6,8},{8,10},{10,12},{12,14},{1,3},{3,5},{5,7},{... | collective-permute-start | bytes 393224 | tf_op jit(solution)/shard_map/ppermute | solution.py:25
  59.2 1.9 collective-permute-done.4
  61.1 6.9 %collective-permute-done.5 = f32[1,1,64,512]{2,3,1,0:T(8,128)S(1)} collective-permute-done((f32[1,1,64,512]{2,3,1,0:T(8,128)S(1)}, f32[1,1,64,512]{2,3,1,0:T(8,128)S(1)}, u32[]{:S(2)}, u32[]{:S(2)}) %collective-permute-start.5) | collective-permute-done | bytes 131104 | tf_op jit(solution)/shard_map/ppermute | solution.py:28
  68.0 2.6 %fusion.4 = (f32[4,64,512]{1,2,0:T(8,128)}, f32[1,4,64,512]{2,3,1,0:T(8,128)S(1)}) fusion(f32[]{:T(128)} %bitcast, f32[1,4,64,512]{2,3,1,0:T(8,128)S(1)} %fusion.22, f32[4,64,512]{1,2,0:T(8,128)S(1)} %copy-done.2, f32[]{:T(128)} %bitcast.14, f32[]{:T(128)} %bitcast.11, bf16[4,64,512]{1,2,0:T(8,128)(2,1)S(1)} %copy-done, pred[4,64,64]{1,2,0:T(8,128)(4,1)S(1)} %copy.29, ...), kind=kLoop, calls=%fused_computation.38 | loop fusion | flops 4325376 | bytes 4767768 | tf_op jit(solution)/shard_map/reduce_sum | solution.py:116
  73.8 1.9 copy.13
  75.8 20.6 %all-reduce.28.cloned.1.call-done = f32[4,64,512]{1,2,0:T(8,128)} async-done(((f32[4,64,512]{1,2,0:T(8,128)}), f32[4,64,512]{1,2,0:T(8,128)}) %all-reduce.28.cloned.1.call-update) | async-done | bytes 524304 | tf_op jit(solution)/shard_map/psum | solution.py:122
  96.4 2.3 %fusion.73 = (f32[1,4,64,512]{2,3,1,0:T(8,128)S(1)}, f32[1,4,64,512]{2,3,1,0:T(8,128)S(1)}) fusion(pred[4,64,64]{1,2,0:T(8,128)(4,1)S(1)} %copy.18, f32[]{:T(128)} %bitcast.2, f32[3,4,64,512]{2,3,1,0:T(8,128)S(1)} %convert_element_type.31, f32[1,4,64,512]{2,3,1,0:T(8,128)} %copy-done.6, f32[4,64,512]{1,2,0:T(8,128)} %all-reduce.28.cloned.1.call-done, ...), kind=kLoop, calls=%fused_computation.144 | loop fusion | flops 1703936 | bytes 3162120 | tf_op jit(solution)/shard_map/transpose(jvp())/neg | solution.py:61
  99.8 1.6 fusion.74
  101.4 3.7 %collective-permute-start.6 = (f32[1,1,64,512]{2,3,1,0:T(8,128)S(1)}, f32[1,1,64,512]{2,3,1,0:T(8,128)S(1)}, u32[]{:S(2)}, u32[]{:S(2)}) collective-permute-start(f32[1,1,64,512]{2,3,1,0:T(8,128)S(1)} %get-tuple-element.119), channel_id=1, source_target_pairs={{0,2},{2,4},{4,6},{6,8},{8,10},{10,12},{12,14},{1,3},{3,5},{5,7},{... | collective-permute-start | bytes 393224 | tf_op jit(solution)/shard_map/ppermute | solution.py:17
  106.6 10.0 %collective-permute-done.6 = f32[1,1,64,512]{2,3,1,0:T(8,128)S(1)} collective-permute-done((f32[1,1,64,512]{2,3,1,0:T(8,128)S(1)}, f32[1,1,64,512]{2,3,1,0:T(8,128)S(1)}, u32[]{:S(2)}, u32[]{:S(2)}) %collective-permute-start.6) | collective-permute-done | bytes 131104 | tf_op jit(solution)/shard_map/ppermute | solution.py:17
  117.9 1.6 fusion.76
  119.5 4.6 %collective-permute-start.8 = (f32[1,1,64,512]{2,3,1,0:T(8,128)S(1)}, f32[1,1,64,512]{2,3,1,0:T(8,128)S(1)}, u32[]{:S(2)}, u32[]{:S(2)}) collective-permute-start(f32[1,1,64,512]{2,3,1,0:T(8,128)S(1)} %get-tuple-element.117), channel_id=1, source_target_pairs={{0,2},{2,4},{4,6},{6,8},{8,10},{10,12},{12,14},{1,3},{3,5},{5,7},{... | collective-permute-start | bytes 393224 | tf_op jit(solution)/shard_map/ppermute | solution.py:17
  125.6 3.4 %collective-permute-done.8 = f32[1,1,64,512]{2,3,1,0:T(8,128)S(1)} collective-permute-done((f32[1,1,64,512]{2,3,1,0:T(8,128)S(1)}, f32[1,1,64,512]{2,3,1,0:T(8,128)S(1)}, u32[]{:S(2)}, u32[]{:S(2)}) %collective-permute-start.8) | collective-permute-done | bytes 131104 | tf_op jit(solution)/shard_map/ppermute | solution.py:17
  129.1 5.6 %collective-permute-done.9 = f32[1,1,64,512]{2,3,1,0:T(8,128)S(1)} collective-permute-done((f32[1,1,64,512]{2,3,1,0:T(8,128)S(1)}, f32[1,1,64,512]{2,3,1,0:T(8,128)S(1)}, u32[]{:S(2)}, u32[]{:S(2)}) %collective-permute-start.9) | collective-permute-done | bytes 131104 | tf_op jit(solution)/shard_map/ppermute | solution.py:17
  135.9 1.6 fusion.78
  137.5 4.6 %collective-permute-start.10 = (f32[1,1,64,512]{2,3,1,0:T(8,128)S(1)}, f32[1,1,64,512]{2,3,1,0:T(8,128)S(1)}, u32[]{:S(2)}, u32[]{:S(2)}) collective-permute-start(f32[1,1,64,512]{2,3,1,0:T(8,128)S(1)} %get-tuple-element.115), channel_id=1, source_target_pairs={{0,2},{2,4},{4,6},{6,8},{8,10},{10,12},{12,14},{1,3},{3,5},{5,7},{... | collective-permute-start | bytes 393224 | tf_op jit(solution)/shard_map/ppermute | solution.py:17
  142.3 1.3 collective-permute-start.11
  143.6 3.0 %collective-permute-done.10 = f32[1,1,64,512]{2,3,1,0:T(8,128)S(1)} collective-permute-done((f32[1,1,64,512]{2,3,1,0:T(8,128)S(1)}, f32[1,1,64,512]{2,3,1,0:T(8,128)S(1)}, u32[]{:S(2)}, u32[]{:S(2)}) %collective-permute-start.10) | collective-permute-done | bytes 131104 | tf_op jit(solution)/shard_map/ppermute | solution.py:17
  146.6 7.3 %collective-permute-done.11 = f32[1,1,64,512]{2,3,1,0:T(8,128)S(1)} collective-permute-done((f32[1,1,64,512]{2,3,1,0:T(8,128)S(1)}, f32[1,1,64,512]{2,3,1,0:T(8,128)S(1)}, u32[]{:S(2)}, u32[]{:S(2)}) %collective-permute-start.11) | collective-permute-done | bytes 131104 | tf_op jit(solution)/shard_map/ppermute | solution.py:17
  154.0 1.4 multiply_bitcast_fusion.1
  155.4 24.8 %all-reduce.30.cloned.1.call-done = (f32[4,64,512]{1,2,0:T(8,128)}, f32[4,64,512]{1,2,0:T(8,128)}) async-done(((f32[4,64,512]{1,2,0:T(8,128)}, f32[4,64,512]{1,2,0:T(8,128)}), (f32[4,64,512]{1,2,0:T(8,128)}, f32[4,64,512]{1,2,0:T(8,128)})) %all-reduce.30.cloned.1.call-update) | async-done | bytes 1048592 | tf_op jit(solution)/shard_map/psum | solution.py:139
  180.3 2.5 %fusion.3 = f32[]{:T(128)} fusion(bf16[4,64,512]{1,2,0:T(8,128)(2,1)S(1)} %copy-done.7, f32[4,64,512]{1,2,0:T(8,128)} %all-reduce.28.cloned.1.call-done, f32[4,64,512]{1,2,0:T(8,128)} %get-tuple-element.79), kind=kLoop, calls=%fused_computation.37 | loop fusion | flops 917503 | bytes 1310724 | tf_op jit(solution)/shard_map/reduce_sum | solution.py:123
  183.9 22.2 %psum.31 = f32[]{:T(128)} all-reduce(f32[]{:T(128)} %fusion.3), channel_id=1, replica_groups=mesh['groups'=2,'space'=8,'node'=2] {'space'}, use_global_device_ids=true, to_apply=%region_4.5 | all-reduce | flops 1 | bytes 8 | tf_op jit(solution)/shard_map/psum | solution.py:126
  (75 shorter events, 20.7 us)
Async XLA Ops:
  7.2 9.2 %copy-start.12 = (s32[1,8]{1,0:T(1,128)S(1)}, s32[1,8]{1,0:T(1,128)}, u32[]{:S(2)}) copy-start(s32[1,8]{1,0:T(1,128)} %param.29) | copy-start | bytes 100
  7.2 15.8 %copy-start.8 = (bf16[3,4,64,512]{3,2,1,0:T(8,128)(2,1)S(1)}, bf16[3,4,64,512]{3,2,1,0:T(8,128)(2,1)}, u32[]{:S(2)}) copy-start(bf16[3,4,64,512]{3,2,1,0:T(8,128)(2,1)} %param.24) | copy-start | bytes 2359300
  7.2 89.2 %all-reduce.28.cloned.1.call-start = ((), (), s32[]{:S(2)}) async-start(), calls=%async_computation | async-start | bytes 2097152 | tf_op jit(solution)/shard_map/psum | solution.py:122
  8.7 14.3 %copy-start.4 = (f32[1,4,64,512]{2,3,1,0:T(8,128)}, f32[1,4,64,512]{2,3,1,0:T(8,128)S(1)}, u32[]{:S(2)}) copy-start(f32[1,4,64,512]{2,3,1,0:T(8,128)S(1)} %copy.15) | copy-start | bytes 1572868
  9.6 21.0 %collective-permute-start = (f32[1,1,64,512]{2,3,1,0:T(8,128)}, f32[1,1,64,512]{2,3,1,0:T(8,128)}, u32[]{:S(2)}, u32[]{:S(2)}) collective-permute-start(f32[1,1,64,512]{2,3,1,0:T(8,128)} %get-tuple-element.124), channel_id=1, source_target_pairs={{0,2},{2,4},{4,6},{6,8},{8,10},{10,12},{12,14},{1,3},{3,5},{5,7},{... | collective-permute-start | bytes 393224 | tf_op jit(solution)/shard_map/ppermute | solution.py:25
  15.1 15.5 %collective-permute-start.1 = (f32[1,1,64,512]{2,3,1,0:T(8,128)}, f32[1,1,64,512]{2,3,1,0:T(8,128)}, u32[]{:S(2)}, u32[]{:S(2)}) collective-permute-start(f32[1,1,64,512]{2,3,1,0:T(8,128)} %get-tuple-element.125), channel_id=1, source_target_pairs={{2,0},{4,2},{6,4},{8,6},{10,8},{12,10},{14,12},{3,1},{5,3},{7,5},{... | collective-permute-start | bytes 393224 | tf_op jit(solution)/shard_map/ppermute | solution.py:28
  24.5 1.7 copy-start.9
  26.3 1.0 copy-start.10
  30.6 20.4 %copy-start = (bf16[4,64,512]{1,2,0:T(8,128)(2,1)S(1)}, bf16[4,64,512]{1,2,0:T(8,128)(2,1)}, u32[]{:S(2)}) copy-start(bf16[4,64,512]{1,2,0:T(8,128)(2,1)} %copy.32) | copy-start | bytes 786436
  30.6 20.4 %copy-start.5 = (f32[1,4,64,512]{2,3,1,0:T(8,128)S(1)}, f32[1,4,64,512]{2,3,1,0:T(8,128)}, u32[]{:S(2)}) copy-start(f32[1,4,64,512]{2,3,1,0:T(8,128)} %copy-done.4) | copy-start | bytes 1572868
  35.7 15.4 %copy-start.2 = (f32[4,64,512]{1,2,0:T(8,128)S(1)}, f32[4,64,512]{1,2,0:T(8,128)}, u32[]{:S(2)}) copy-start(f32[4,64,512]{1,2,0:T(8,128)} %copy.34) | copy-start | bytes 1572868
  35.7 15.3 %collective-permute-start.2 = (f32[1,1,64,512]{2,3,1,0:T(8,128)S(1)}, f32[1,1,64,512]{2,3,1,0:T(8,128)S(1)}, u32[]{:S(2)}, u32[]{:S(2)}) collective-permute-start(f32[1,1,64,512]{2,3,1,0:T(8,128)S(1)} %get-tuple-element.122), channel_id=1, source_target_pairs={{0,2},{2,4},{4,6},{6,8},{8,10},{10,12},{12,14},{1,3},{3,5},{5,7},{... | collective-permute-start | bytes 393224 | tf_op jit(solution)/shard_map/ppermute | solution.py:25
  40.4 10.6 %collective-permute-start.3 = (f32[1,1,64,512]{2,3,1,0:T(8,128)S(1)}, f32[1,1,64,512]{2,3,1,0:T(8,128)S(1)}, u32[]{:S(2)}, u32[]{:S(2)}) collective-permute-start(f32[1,1,64,512]{2,3,1,0:T(8,128)S(1)} %get-tuple-element.123), channel_id=1, source_target_pairs={{2,0},{4,2},{6,4},{8,6},{10,8},{12,10},{14,12},{3,1},{5,3},{7,5},{... | collective-permute-start | bytes 393224 | tf_op jit(solution)/shard_map/ppermute | solution.py:28
  52.9 8.3 %collective-permute-start.4 = (f32[1,1,64,512]{2,3,1,0:T(8,128)S(1)}, f32[1,1,64,512]{2,3,1,0:T(8,128)S(1)}, u32[]{:S(2)}, u32[]{:S(2)}) collective-permute-start(f32[1,1,64,512]{2,3,1,0:T(8,128)S(1)} %get-tuple-element.120), channel_id=1, source_target_pairs={{0,2},{2,4},{4,6},{6,8},{8,10},{10,12},{12,14},{1,3},{3,5},{5,7},{... | collective-permute-start | bytes 393224 | tf_op jit(solution)/shard_map/ppermute | solution.py:25
  57.3 10.8 %collective-permute-start.5 = (f32[1,1,64,512]{2,3,1,0:T(8,128)S(1)}, f32[1,1,64,512]{2,3,1,0:T(8,128)S(1)}, u32[]{:S(2)}, u32[]{:S(2)}) collective-permute-start(f32[1,1,64,512]{2,3,1,0:T(8,128)S(1)} %get-tuple-element.121), channel_id=1, source_target_pairs={{2,0},{4,2},{6,4},{8,6},{10,8},{12,10},{14,12},{3,1},{5,3},{7,5},{... | collective-permute-start | bytes 393224 | tf_op jit(solution)/shard_map/ppermute | solution.py:28
  70.6 1.0 copy-start.6
  71.7 1.2 copy-start.11
  72.8 107.5 %all-reduce.30.cloned.1.call-start = ((), (), s32[]{:S(2)}) async-start(), calls=%async_computation.1 | async-start | bytes 4194304 | tf_op jit(solution)/shard_map/psum | solution.py:139
  98.7 1.0 copy-start.1
  101.4 15.3 %collective-permute-start.6 = (f32[1,1,64,512]{2,3,1,0:T(8,128)S(1)}, f32[1,1,64,512]{2,3,1,0:T(8,128)S(1)}, u32[]{:S(2)}, u32[]{:S(2)}) collective-permute-start(f32[1,1,64,512]{2,3,1,0:T(8,128)S(1)} %get-tuple-element.119), channel_id=1, source_target_pairs={{0,2},{2,4},{4,6},{6,8},{8,10},{10,12},{12,14},{1,3},{3,5},{5,7},{... | collective-permute-start | bytes 393224 | tf_op jit(solution)/shard_map/ppermute | solution.py:17
  105.3 11.4 %collective-permute-start.7 = (f32[1,1,64,512]{2,3,1,0:T(8,128)S(1)}, f32[1,1,64,512]{2,3,1,0:T(8,128)S(1)}, u32[]{:S(2)}, u32[]{:S(2)}) collective-permute-start(f32[1,1,64,512]{2,3,1,0:T(8,128)S(1)} %get-tuple-element.118), channel_id=1, source_target_pairs={{2,0},{4,2},{6,4},{8,6},{10,8},{12,10},{14,12},{3,1},{5,3},{7,5},{... | collective-permute-start | bytes 393224 | tf_op jit(solution)/shard_map/ppermute | solution.py:17
  119.5 9.6 %collective-permute-start.8 = (f32[1,1,64,512]{2,3,1,0:T(8,128)S(1)}, f32[1,1,64,512]{2,3,1,0:T(8,128)S(1)}, u32[]{:S(2)}, u32[]{:S(2)}) collective-permute-start(f32[1,1,64,512]{2,3,1,0:T(8,128)S(1)} %get-tuple-element.117), channel_id=1, source_target_pairs={{0,2},{2,4},{4,6},{6,8},{8,10},{10,12},{12,14},{1,3},{3,5},{5,7},{... | collective-permute-start | bytes 393224 | tf_op jit(solution)/shard_map/ppermute | solution.py:17
  124.3 10.4 %collective-permute-start.9 = (f32[1,1,64,512]{2,3,1,0:T(8,128)S(1)}, f32[1,1,64,512]{2,3,1,0:T(8,128)S(1)}, u32[]{:S(2)}, u32[]{:S(2)}) collective-permute-start(f32[1,1,64,512]{2,3,1,0:T(8,128)S(1)} %get-tuple-element.116), channel_id=1, source_target_pairs={{2,0},{4,2},{6,4},{8,6},{10,8},{12,10},{14,12},{3,1},{5,3},{7,5},{... | collective-permute-start | bytes 393224 | tf_op jit(solution)/shard_map/ppermute | solution.py:17
  137.5 9.1 %collective-permute-start.10 = (f32[1,1,64,512]{2,3,1,0:T(8,128)S(1)}, f32[1,1,64,512]{2,3,1,0:T(8,128)S(1)}, u32[]{:S(2)}, u32[]{:S(2)}) collective-permute-start(f32[1,1,64,512]{2,3,1,0:T(8,128)S(1)} %get-tuple-element.115), channel_id=1, source_target_pairs={{0,2},{2,4},{4,6},{6,8},{8,10},{10,12},{12,14},{1,3},{3,5},{5,7},{... | collective-permute-start | bytes 393224 | tf_op jit(solution)/shard_map/ppermute | solution.py:17
  142.3 11.6 %collective-permute-start.11 = (f32[1,1,64,512]{2,3,1,0:T(8,128)S(1)}, f32[1,1,64,512]{2,3,1,0:T(8,128)S(1)}, u32[]{:S(2)}, u32[]{:S(2)}) collective-permute-start(f32[1,1,64,512]{2,3,1,0:T(8,128)S(1)} %get-tuple-element.114), channel_id=1, source_target_pairs={{2,0},{4,2},{6,4},{8,6},{10,8},{12,10},{14,12},{3,1},{5,3},{7,5},{... | collective-permute-start | bytes 393224 | tf_op jit(solution)/shard_map/ppermute | solution.py:17
  155.4 24.9 %copy-start.7 = (bf16[4,64,512]{1,2,0:T(8,128)(2,1)S(1)}, bf16[4,64,512]{1,2,0:T(8,128)(2,1)}, u32[]{:S(2)}) copy-start(bf16[4,64,512]{1,2,0:T(8,128)(2,1)} %copy.14) | copy-start | bytes 786436
  180.3 25.9 %copy-start.3 = (f32[4,64,512]{1,2,0:T(8,128)S(1)}, f32[4,64,512]{1,2,0:T(8,128)}, u32[]{:S(2)}) copy-start(f32[4,64,512]{1,2,0:T(8,128)} %copy.34) | copy-start | bytes 1572868
Sparse Core Ops, SparseCore 0:
  72.9 23.4 all-reduce.27
  155.6 24.6 all-reduce.29
where the time goes:
time: 218 us; the launch traced here: 217 us
  waiting for transfers between devices  93 us (43%)
  starting transfers between devices  35.2 us (16%)
  other arithmetic  28.2 us (13%)
  between operations  22.7 us (10%)
  blocking collectives  22.2 us (10%)
  local copies, waits for them, and re-layouts  15.4 us (7%)
    ppermute x6, waiting for transfers between devices, shifted(): lax.ppermute(value, axis, [(source, source + steps) for source in range(f...  29.4 us
    psum x1, waiting for transfers between devices, shards(): summed_terms = lax.psum(source_total, 'node')  24.8 us
    psum x1, blocking collectives, shards(): summed_cost = lax.psum(local_cost, 'space')  22.2 us
    psum x1, waiting for transfers between devices, shards(): first_moment, second_moment = lax.psum((first_part, second_part), 'node')  20.6 us
    ppermute x6, starting transfers between devices, shifted(): lax.ppermute(value, axis, [(source, source + steps) for source in range(f...  16.7 us
    ppermute x3, starting transfers between devices, with_halo(): lax.ppermute(lax.slice_in_dim(block, block.shape[dim] - width, None, axis...  14.6 us
    unnamed x34, local copies, waits for them, and re-layouts  13.2 us
    ppermute x3, waiting for transfers between devices, with_halo(): lax.ppermute(lax.slice_in_dim(block, block.shape[dim] - width, None, axis...  11.2 us
  transfers between devices with their start and end apart: 14, of which 10 were waited for; matrix products, arithmetic and copies ran while one was open for 5% of the time, Pallas kernels for 0%

commit v1 on v0

v1 whole, which is shorter than its diff:
```python
import functools
import math

import jax
import jax.numpy as jnp
from jax import lax
from jax.experimental import pallas as pl
from jax.experimental.pallas import tpu as pltpu
from jax.sharding import PartitionSpec as P

time_step = 0.6
variance_gain = 0.5
penalty = 0.1
weight_denominator = 16.0

VMEM_LIMIT = 24 * 1024 * 1024
AXES = ("space", "node")


def node_scales(node_index, step_index):
    points = -jnp.cos(math.pi * node_index.astype(jnp.float32) / 8.0)
    source_phase = 1.0 + 0.5 * jnp.sin(2.0 * math.pi * step_index.astype(jnp.float32)[0] / 64.0)
    first_axis = 1.0 + 0.3 * points[:, 0]
    second_axis = 1.0 + 0.3 * points[:, 1]
    third_axis = (1.0 + 0.3 * points[:, 2]) * (1.0 + 0.2 * points[:, 7])
    kappa = jnp.exp(0.5 * (points[:, 3] + 0.5 * points[:, 5]))
    source = (1.0 + 0.3 * points[:, 4] + 0.2 * points[:, 6]) * source_phase
    return jnp.stack([first_axis, second_axis, third_axis, kappa, source], axis=1)


def roll(value, steps, axis):
    return pltpu.roll(value, steps % value.shape[axis], axis)


def in_plane(value, a, cy, cz, k):
    return a[1] * (cy[0, k] * roll(value, 1, 0) + cy[1, k] * roll(value, -1, 0)) + a[2] * (
        cz[0, k] * roll(value, 1, 1) + cz[1, k] * roll(value, -1, 1)
    )


def in_plane_back(value, a, cy, cz, k):
    return a[1] * (roll(cy[0, k] * value, -1, 0) + roll(cy[1, k] * value, 1, 0)) + a[2] * (
        roll(cz[0, k] * value, -1, 1) + roll(cz[1, k] * value, 1, 1)
    )


def rows_of(scal, j):
    return [scal[j, k] for k in range(6)]


def prepare(core, scal, speed, mask, decay, control, goal, own_adj, far_adj, cx, cy, cz, dg, edge, ctl, goals, adj, adj_out):
    me = core[0]
    rows, columns = speed.shape[2:]
    blocks = mask.shape[3]
    spread = (
        lax.broadcasted_iota(jnp.int32, (blocks, columns), 1) // (columns // blocks)
        == lax.broadcasted_iota(jnp.int32, (blocks, columns), 0)
    ).astype(jnp.bfloat16)
    row = lax.broadcasted_iota(jnp.int32, (rows, columns), 0)
    column = lax.broadcasted_iota(jnp.int32, (rows, columns), 1)
    flip = (me == 1).astype(jnp.float32)
    for k in range(2):
        at = me if k == 0 else 1 - me
        s, up = [], []
        for d in range(3):
            bits = mask[d, at].astype(jnp.float32).astype(jnp.bfloat16)
            up.append(jnp.dot(bits, spread, preferred_element_type=jnp.float32))
            s.append(speed[d, at].astype(jnp.float32))
        toward_outer = up[0] + flip - 2.0 * flip * up[0]
        outer = s[0] * toward_outer
        cx[0, k] = outer
        cx[1, k] = s[0] - outer
        if k == 0:
            edge[...] = outer
        lower = s[1] * up[1]
        cy[0, k] = jnp.where(row == 0, 0.0, lower)
        cy[1, k] = jnp.where(row == rows - 1, 0.0, s[1] - lower)
        lower = s[2] * up[2]
        cz[0, k] = jnp.where(column == 0, 0.0, lower)
        cz[1, k] = jnp.where(column == columns - 1, 0.0, s[2] - lower)
        rate = decay[at].astype(jnp.float32)
        for j in range(2):
            a = rows_of(scal, j)
            dg[j, k] = a[0] * s[0] + a[1] * s[1] + a[2] * s[2] + a[3] * rate
        ctl[k] = control[at]
        goals[k] = goal[at].astype(jnp.float32)
        adj[k] = own_adj[0, at].astype(jnp.float32)
        adj_out[k] = far_adj[0, 1 - at].astype(jnp.float32)


def first_stage(core, scal, own, far, own_halo, far_halo, cx, cy, cz, dg, ctl, msg, s1_in):
    me = core[0]
    outer, inner, beyond = 3 * me, 1 + me, 2 - me
    for j, (c, halo) in enumerate(((own, own_halo), (far, far_halo))):
        a = rows_of(scal, j)
        c_o, c_i = c[0, outer], c[0, inner]
        push_o, push_i = a[4] * ctl[0], a[4] * ctl[1]
        l_o = a[0] * (cx[0, 0] * halo[0] + cx[1, 0] * c_i) + in_plane(c_o, a, cy, cz, 0) - dg[j, 0] * c_o
        l_i = a[0] * (cx[0, 1] * c_o + cx[1, 1] * c[0, beyond]) + in_plane(c_i, a, cy, cz, 1) - dg[j, 1] * c_i
        s1_o = c_o + time_step * (l_o + push_o)
        s1_i = c_i + time_step * (l_i + push_i)
        s1_in[j] = s1_i
        msg[j, 0] = s1_o
        l_o = a[0] * (cx[1, 0] * s1_i) + in_plane(s1_o, a, cy, cz, 0) - dg[j, 0] * s1_o
        msg[j, 1] = 0.75 * c_o + 0.25 * (s1_o + time_step * (l_o + push_o))


def second_stage_inner(core, scal, own, far, msg, s1_in, s1_far, cx, cy, cz, dg, ctl, s2_in):
    inner = 1 + core[0]
    for j, c in enumerate((own, far)):
        a = rows_of(scal, j)
        s1_i = s1_in[j]
        l_i = a[0] * (cx[0, 1] * msg[j, 0] + cx[1, 1] * s1_far[1 - j]) + in_plane(s1_i, a, cy, cz, 1) - dg[j, 1] * s1_i
        s2_in[j] = 0.75 * c[0, inner] + 0.25 * (s1_i + time_step * (l_i + a[4] * ctl[1]))


def middle(core, scal, own, far, msg, halo, s2_in, s2_far, near_edge, cx, cy, cz, dg, ctl, goals, adj, adj_far, cost, term, msg3, pin):
    me = core[0]
    place = (3 * me, 1 + me)
    ahead, first, second = [], [0.0, 0.0], [0.0, 0.0]
    for j, c in enumerate((own, far)):
        a = rows_of(scal, j)
        s1_o = msg[j, 0]
        s2_o = msg[j, 1] + (0.25 * time_step * a[0]) * (cx[0, 0] * halo[1 - j, 0])
        s2_h = halo[1 - j, 1] + (0.25 * time_step * a[0]) * (near_edge[...] * s1_o)
        s2_i = s2_in[j]
        l_o = a[0] * (cx[0, 0] * s2_h + cx[1, 0] * s2_i) + in_plane(s2_o, a, cy, cz, 0) - dg[j, 0] * s2_o
        l_i = a[0] * (cx[0, 1] * s2_o + cx[1, 1] * s2_far[1 - j]) + in_plane(s2_i, a, cy, cz, 1) - dg[j, 1] * s2_i
        final = []
        for k, (s2, l) in enumerate(((s2_o, l_o), (s2_i, l_i))):
            f = c[0, place[k]] / 3.0 + 2.0 / 3.0 * (s2 + time_step * (l + a[4] * ctl[k]))
            final.append(f)
            weighted = a[5] * f
            first[k] = first[k] + weighted
            second[k] = second[k] + weighted * f
        ahead.append(final)
    total = sum(
        goals[k] * (first[k] + variance_gain * (second[k] - first[k] * first[k])) for k in range(2)
    )
    rows, columns = total.shape
    total = sum(total[8 * r : 8 * r + 8] for r in range(rows // 8))
    cost[...] = sum(total[:, 128 * k : 128 * k + 128] for k in range(columns // 128))
    for j in range(2):
        a = rows_of(scal, j)
        u = []
        for k in range(2):
            after = adj[k] if j == 0 else adj_far[k]
            t = after + goals[k] * a[5] * (1.0 + 2.0 * variance_gain * (ahead[j][k] - first[k]))
            term[j, k] = t
            u.append(2.0 / 3.0 * t)
        pin[j] = a[0] * (cx[1, 1] * u[1])
        msg3[j, 0] = a[0] * (cx[0, 0] * u[0])
        spread = a[0] * (cx[0, 1] * u[1]) + in_plane_back(u[0], a, cy, cz, 0) - dg[j, 0] * u[0]
        msg3[j, 1] = a[0] * cx[0, 0] * (u[0] + time_step * spread)


def back_inner(scal, term, pin_far, cx, cy, cz, dg, a2, a2_part, pin2):
    for j in range(2):
        a = rows_of(scal, j)
        u = [2.0 / 3.0 * term[j, k] for k in range(2)]
        spread = a[0] * (cx[0, 1] * u[1]) + in_plane_back(u[0], a, cy, cz, 0) - dg[j, 0] * u[0]
        a2_part[j] = u[0] + time_step * spread
        spread = a[0] * (cx[1, 0] * u[0]) + in_plane_back(u[1], a, cy, cz, 1) - dg[j, 1] * u[1] + pin_far[1 - j]
        a2_i = u[1] + time_step * spread
        a2[j] = a2_i
        pin2[j] = (0.25 * a[0]) * (cx[1, 1] * a2_i)


def back_outer(core, scal, term, msg3, halo, near_edge, a2, a2_part, pin_far, cx, cy, cz, dg, ctl, a2_o, a1, msg4, pin3, keep, give):
    sources = [0.0, 0.0]
    for j in range(2):
        a = rows_of(scal, j)
        second = [a2_part[j] + time_step * halo[1 - j, 0], a2[j]]
        a2_o[j] = second[0]
        u2 = [0.25 * second[k] for k in range(2)]
        arrived = 0.25 * (halo[1 - j, 1] + (time_step * a[0]) * (near_edge[...] * msg3[j, 0]))
        spread = a[0] * (cx[0, 1] * u2[1]) + in_plane_back(u2[0], a, cy, cz, 0) - dg[j, 0] * u2[0] + arrived
        a1_o = u2[0] + time_step * spread
        spread = a[0] * (cx[1, 0] * u2[0]) + in_plane_back(u2[1], a, cy, cz, 1) - dg[j, 1] * u2[1] + pin_far[1 - j]
        a1_i = u2[1] + time_step * spread
        a1[j, 0] = a1_o
        a1[j, 1] = a1_i
        msg4[j] = a[0] * (cx[0, 0] * a1_o)
        pin3[j] = a[0] * (cx[1, 1] * a1_i)
        for k, last in enumerate((a1_o, a1_i)):
            sources[k] = sources[k] + a[4] * (2.0 / 3.0 * term[j, k] + u2[k] + last)
    half = ctl.shape[2] // 2
    zero = core[0] == 0
    for k in range(2):
        gradient = time_step * sources[k] + penalty * ctl[k]
        low, high = gradient[:, :half], gradient[:, half:]
        keep[k] = jnp.where(zero, low, high)
        give[k] = jnp.where(zero, high, low)


def last_inner(core, scal, term, a2, a2_o, a1, pin_far, keep, taken, cx, cy, cz, dg, part, adj_in, adj_out, gradient):
    me = core[0]
    for j in range(2):
        a = rows_of(scal, j)
        x = [a1[j, 0], a1[j, 1]]
        spread = a[0] * (cx[0, 1] * x[1]) + in_plane_back(x[0], a, cy, cz, 0) - dg[j, 0] * x[0]
        part[j] = term[j, 0] / 3.0 + 0.75 * a2_o[j] + (x[0] + time_step * spread)
        spread = a[0] * (cx[1, 0] * x[0]) + in_plane_back(x[1], a, cy, cz, 1) - dg[j, 1] * x[1] + pin_far[1 - j]
        inner = term[j, 1] / 3.0 + 0.75 * a2[j] + (x[1] + time_step * spread)
        if j == 0:
            adj_in[...] = inner
        else:
            adj_out[...] = inner
    gradient[3 * me] = keep[0]
    gradient[1 + me] = keep[1]
    gradient[3 - 3 * me] = taken[0]
    gradient[2 - me] = taken[1]


def last_outer(part, halo, mine, give):
    mine[...] = part[0] + time_step * halo[1]
    give[...] = part[1] + time_step * halo[0]


def assemble(core, mine, taken, adj_in, adj_taken, out):
    me = core[0]
    out[0, 3 * me] = mine[...]
    out[0, 1 + me] = adj_in[...]
    out[0, 3 - 3 * me] = taken[...]
    out[0, 2 - me] = adj_taken[...]


def on_core(body, outs, scalars, arrays, hbm_out=(), name=None):
    out_shape = [
        jax.ShapeDtypeStruct(s, jnp.float32) if i in hbm_out else pltpu.VMEM(s, jnp.float32)
        for i, s in enumerate(outs)
    ]
    held = [pltpu.with_memory_space_constraint(x, pltpu.VMEM) for x in arrays]
    return pl.pallas_call(
        body,
        out_shape=out_shape,
        in_specs=[pl.BlockSpec(memory_space=pltpu.SMEM)] * len(scalars)
        + [pl.BlockSpec(memory_space=pltpu.VMEM)] * len(arrays),
        out_specs=[pl.BlockSpec(memory_space=pltpu.VMEM)] * len(outs),
        compiler_params=pltpu.CompilerParams(vmem_limit_bytes=VMEM_LIMIT),
        name=name or body.__name__,
    )(*scalars, *held)


def sum_everywhere(value, ranks):
    if ranks & (ranks - 1):
        return lax.psum(value, AXES)
    step = 1
    while step < ranks:
        value = value + lax.ppermute(value, AXES, [(i, i ^ step) for i in range(ranks)])
        step *= 2
    return value


def shards(
    concentration,
    adjoint_next,
    speed,
    direction_mask,
    decay_rate,
    control,
    goal_weight,
    node_index,
    weight_num,
    step_index,
):
    sections = lax.axis_size("space")
    ranks = sections * lax.axis_size("node")
    within = [(i, i ^ 1) for i in range(ranks)]
    across = [p for i in range(1, ranks - 1, 2) for p in ((i, i + 1), (i + 1, i))]
    swap = lambda x: lax.ppermute(x, AXES, within)
    pass_on = lambda x: lax.ppermute(x, AXES, across)

    _, layers, rows, columns = concentration.shape
    me = lax.axis_index("node").astype(jnp.int32)
    core = jnp.reshape(me, (1,))
    scales = node_scales(node_index, step_index)
    weights = weight_num.astype(jnp.float32)[:, None] / weight_denominator
    scal = jnp.concatenate([scales, weights, jnp.zeros((1, 2), jnp.float32)], 1)
    scal = jnp.concatenate([scal, swap(scal)], 0)

    far = swap(concentration)
    take = lambda x: lax.dynamic_slice_in_dim(x, 3 * me, 1, axis=1)[0]
    far_halo = pass_on(take(concentration))
    own_halo = pass_on(take(far))

    plane = (rows, columns)
    pair = (2,) + plane
    four = (2,) + pair
    specs = [
        pl.BlockSpec((3, 2, rows, columns), lambda g, c: (0, c[0], 0, 0)),
        pl.BlockSpec((3, 2, rows, direction_mask.shape[3]), lambda g, c: (0, c[0], 0, 0)),
        pl.BlockSpec((2, rows, columns), lambda g, c: (c[0], 0, 0)),
        pl.BlockSpec((2, rows, columns), lambda g, c: (c[0], 0, 0)),
        pl.BlockSpec((2, rows, columns), lambda g, c: (c[0], 0, 0)),
        pl.BlockSpec((1, 2, rows, columns), lambda g, c: (0, c[0], 0, 0)),
        pl.BlockSpec((1, 2, rows, columns), lambda g, c: (0, 1 - c[0], 0, 0)),
    ]
    shapes = [four, four, four, four, plane, pair, pair, pair, pair]
    cx, cy, cz, dg, edge, ctl, goals, adj, adj_out = pl.pallas_call(
        prepare,
        out_shape=[pltpu.VMEM(s, jnp.float32) for s in shapes],
        grid_spec=pltpu.PrefetchScalarGridSpec(
            num_scalar_prefetch=1,
            grid=(1,),
            in_specs=[pl.BlockSpec(memory_space=pltpu.SMEM)] + specs,
            out_specs=[pl.BlockSpec(memory_space=pltpu.VMEM)] * len(shapes),
        ),
        compiler_params=pltpu.CompilerParams(vmem_limit_bytes=VMEM_LIMIT),
        name="prepare",
    )(core, scal, speed, direction_mask, decay_rate, control, goal_weight, adjoint_next, adjoint_next)
    adj_far = swap(adj_out)
    near_edge = pass_on(edge)

    fields = [cx, cy, cz, dg]
    msg, s1_in = on_core(
        first_stage, [four, pair], [core, scal], [concentration, far, own_halo, far_halo] + fields + [ctl]
    )
    halo2 = pass_on(msg)
    s1_far = swap(s1_in)
    (s2_in,) = on_core(
        second_stage_inner, [pair], [core, scal], [concentration, far, msg, s1_in, s1_far] + fields + [ctl]
    )
    s2_far = swap(s2_in)
    cost, term, msg3, pin = on_core(
        middle,
        [(8, 128), four, four, pair],
        [core, scal],
        [concentration, far, msg, halo2, s2_in, s2_far, near_edge] + fields + [ctl, goals, adj, adj_far],
    )
    halo3 = pass_on(msg3)
    pin_far = swap(pin)
    a2, a2_part, pin2 = on_core(back_inner, [pair, pair, pair], [scal], [term, pin_far] + fields)
    pin2_far = swap(pin2)
    half = (2, rows, columns // 2)
    a2_o, a1, msg4, pin3, keep, give = on_core(
        back_outer,
        [pair, four, pair, pair, half, half],
        [core, scal],
        [term, msg3, halo3, near_edge, a2, a2_part, pin2_far] + fields + [ctl],
    )
    halo4 = pass_on(msg4)
    pin3_far = swap(pin3)
    taken = swap(give)
    part, adj_in, adj_give, gradient = on_core(
        last_inner,
        [pair, plane, plane, (layers, rows, columns // 2)],
        [core, scal],
        [term, a2, a2_o, a1, pin3_far, keep, taken] + fields,
        hbm_out=(3,),
    )
    adj_taken = swap(adj_give)
    mine, edge_give = on_core(last_outer, [plane, plane], [], [part, halo4])
    edge_taken = swap(edge_give)
    (adjoint,) = on_core(
        assemble, [(1, layers, rows, columns)], [core], [mine, edge_taken, adj_in, adj_taken], hbm_out=(0,)
    )
    cells = sections * layers * rows * columns
    objective = jnp.reshape(jnp.sum(sum_everywhere(cost, ranks)) / cells, (1,))
    return (adjoint, gradient, objective)


def solution(mesh):
    return jax.shard_map(
        shards,
        mesh=mesh,
        in_specs=(
            P("node", ("groups", "space"), None, None),
            P("node", ("groups", "space"), None, None),
            P(None, ("groups", "space"), None, None),
            P(None, ("groups", "space"), None, None),
            P(("groups", "space"), None, None),
            P(("groups", "space"), None, None),
            P(("groups", "space"), None, None),
            P("node", None),
            P("node"),
            P("groups"),
        ),
        out_specs=(
            P("node", ("groups", "space"), None, None),
            P(("groups", "space"), None, "node"),
            P("groups"),
        ),
        check_vma=False,
    )
```

time: 218 us -> 91.2 us (0.42)
  waiting for transfers between devices: 93 us -> 10.2 us
  other arithmetic: 28.2 us -> 0.66 us
  blocking collectives: 22.2 us -> 0 us
  starting transfers between devices: 35.2 us -> 53.7 us
  between operations: 22.7 us -> 9.08 us
  Pallas kernels: 0 us -> 11 us
  local copies, waits for them, and re-layouts: 15.4 us -> 5.96 us
    psum x2 -> x0, waiting for transfers between devices: 45.5 us -> none  [the longest x1 24.8 us: shards(): summed_terms = lax.psum(source_total, 'node')]
    ppermute x12 -> x21, waiting for transfers between devices: 47.5 us -> 10.2 us  [the longest x4 5.9 us: sum_everywhere(): lax.ppermute(value, AXES, [(i, i ^ step) for i in range(ranks)])]
    psum x1 -> x0, blocking collectives: 22.2 us -> none  [shards(): summed_cost = lax.psum(local_cost, 'space')]
    ppermute x12 -> x21, starting transfers between devices: 35.2 us -> 53.7 us  [the longest x11 42.1 us: shards(): swap = lambda x: lax.ppermute(x, AXES, within)]
    pallas_call x0 -> x9, Pallas kernels: none -> 11 us  [the longest x8 10.1 us: on_core(): pl.pallas_call(body, out_shape=out_shape, in_specs=[pl.BlockSpec(memory_s...]
    neg x9 -> x0, other arithmetic: 9.79 us -> none  [the longest x6 5.09 us: tendency(): center - higher[component]]
    unnamed x34 -> x16, local copies, waits for them, and re-layouts: 13.2 us -> 4.2 us
    add x3, other arithmetic: 7.95 us -> 0.01 us  [sum_everywhere(): value + lax.ppermute(value, AXES, [(i, i ^ step) for i in range(ranks)])]
  transfers between devices with their start and end apart: 14 -> 21, of which waited for: 10 -> 9; matrix products, arithmetic and copies ran while one was open for 5% -> 3% of each run, Pallas kernels for 0% -> 6%
where the time goes in v1:
time: 91.2 us; the launch traced here: 90.6 us
  starting transfers between devices  53.7 us (59%)
  Pallas kernels  11 us (12%)
  waiting for transfers between devices  10.2 us (11%)
  between operations  9.08 us (10%)
  local copies, waits for them, and re-layouts  5.96 us (7%)
    ppermute x11, starting transfers between devices, shards(): swap = lambda x: lax.ppermute(x, AXES, within)  42.1 us
    pallas_call x8, Pallas kernels, on_core(): pl.pallas_call(body, out_shape=out_shape, in_specs=[pl.BlockSpec(memory_s...  10.1 us
    ppermute x4, starting transfers between devices, sum_everywhere(): lax.ppermute(value, AXES, [(i, i ^ step) for i in range(ranks)])  7.57 us
    ppermute x4, waiting for transfers between devices, sum_everywhere(): lax.ppermute(value, AXES, [(i, i ^ step) for i in range(ranks)])  5.9 us
    ppermute x11, waiting for transfers between devices, shards(): swap = lambda x: lax.ppermute(x, AXES, within)  4.3 us
    unnamed x16, local copies, waits for them, and re-layouts  4.2 us
    ppermute x6, starting transfers between devices, shards(): pass_on = lambda x: lax.ppermute(x, AXES, across)  4.03 us
  transfers between devices with their start and end apart: 21, of which 9 were waited for; matrix products, arithmetic and copies ran while one was open for 3% of the time, Pallas kernels for 6%

profile of v1, /device:TPU:0, one launch (start us, length us, event | category | flops | bytes accessed | tf_op | source)
XLA Modules:
  0.0 90.6 jit_solution(8746123954545101504)
XLA Ops:
  1.2 1.0 %dynamic-slice_bitcast_fusion = f32[1,64,512]{2,1,0:T(8,128)S(1)} fusion(f32[1,4,64,512]{3,2,1,0:T(8,128)} %own.5, s32[]{:T(128)S(6)} %select_n.4), kind=kLoop, calls=%fused_computation | loop fusion | bytes 262148 | tf_op jit(solution)/shard_map/squeeze | solution.py:283
  10.8 5.1 %collective-permute-start = (f32[1,8]{1,0:T(1,128)S(1)}, f32[1,8]{1,0:T(1,128)S(1)}, u32[]{:S(2)}, u32[]{:S(2)}) collective-permute-start(f32[1,8]{1,0:T(1,128)S(1)} %concatenate.6), channel_id=1, source_target_pairs={{0,1},{1,0},{2,3},{3,2},{4,5},{5,4},{6,7},{7,6},{8,9},{9,8},{10,11... | collective-permute-start | bytes 104 | tf_op jit(solution)/shard_map/ppermute | solution.py:271
  16.0 0.8 collective-permute-done
  16.8 1.1 %copy-done.2 = bf16[3,4,64,512]{3,2,1,0:T(8,128)(2,1)S(1)} copy-done((bf16[3,4,64,512]{3,2,1,0:T(8,128)(2,1)S(1)}, bf16[3,4,64,512]{3,2,1,0:T(8,128)(2,1)}, u32[]{:S(2)}) %copy-start.2) | copy-done | bytes 786456
  18.0 1.0 %copy-done.3 = f32[4,64,512]{2,1,0:T(8,128)S(1)} copy-done((f32[4,64,512]{2,1,0:T(8,128)S(1)}, f32[4,64,512]{2,1,0:T(8,128)}, u32[]{:S(2)}) %copy-start.3) | copy-done | bytes 524312
  19.0 1.0 %copy-done.4 = s32[3,4,64,64]{3,2,1,0:T(8,128)S(1)} copy-done((s32[3,4,64,64]{3,2,1,0:T(8,128)S(1)}, s32[3,4,64,64]{3,2,1,0:T(8,128)}, u32[]{:S(2)}) %copy-start.4) | copy-done | bytes 196632
  20.0 0.9 %copy-done.6 = bf16[4,64,512]{2,1,0:T(8,128)(2,1)S(1)} copy-done((bf16[4,64,512]{2,1,0:T(8,128)(2,1)S(1)}, bf16[4,64,512]{2,1,0:T(8,128)(2,1)}, u32[]{:S(2)}) %copy-start.6) | copy-done | bytes 262168
  20.9 0.9 %prepare.1 = (f32[2,2,64,512]{3,2,1,0:T(8,128)S(1)}, f32[2,2,64,512]{3,2,1,0:T(8,128)S(1)}, f32[2,2,64,512]{3,2,1,0:T(8,128)S(1)}, f32[2,2,64,512]{3,2,1,0:T(8,1...) custom-call(s32[1]{0:T(128)} %bitcast.core, ...), custom_call_target="tpu_custom_call" | custom-call | tf_op jit(solution)/shard_map/prepare/pallas_call | solution.py:300
  22.0 1.6 %first_stage.1 = (f32[2,2,64,512]{3,2,1,0:T(8,128)S(1)}, f32[2,64,512]{2,1,0:T(8,128)S(1)}) custom-call(s32[1]{0:T(128)} %bitcast.core, f32[2,8]{1,0:T(2,128)S(1)} %pad_maximum_fusion.scal, f32[1,4,64,512]{3,2,1,0:T(8,128)S(1)} %copy-done, f32[1,4,64,512]{3,2,1,0:T(8,128)S(1)} %collective-permute-done.1.far, ...), custom_call_target="tpu_custom_call" | custom-call | tf_op jit(solution)/shard_map/first_stage/pallas_call | solution.py:234
  24.6 4.4 %collective-permute-start.8 = (f32[2,64,512]{2,1,0:T(8,128)S(1)}, f32[2,64,512]{2,1,0:T(8,128)S(1)}, u32[]{:S(2)}, u32[]{:S(2)}) collective-permute-start(f32[2,64,512]{2,1,0:T(8,128)S(1)} %get-tuple-element.43), channel_id=1, source_target_pairs={{0,1},{1,0},{2,3},{3,2},{4,5},{5,4},{6,7},{7,6},{8,9},{9,8},{10,11... | collective-permute-start | bytes 786440 | tf_op jit(solution)/shard_map/ppermute | solution.py:271
  29.0 1.0 %second_stage_inner.1.s2_in = f32[2,64,512]{2,1,0:T(8,128)S(1)} custom-call(s32[1]{0:T(128)} %bitcast.core, f32[2,8]{1,0:T(2,128)S(1)} %pad_maximum_fusion.scal, f32[1,4,64,512]{3,2,1,0:T(8,128)S(1)} %copy-done, f32[1,4,64,512]{3,2,1,0:T(8,128)S(1)} %collective-permute-done.1.far, f32[2,2,64,512]{3,2,1,0:T(8,128)S(1)} %get-tuple-element.38.msg, ...), custom_call_target="tpu_custom_call" | custom-call | tf_op jit(solution)/shard_map/second_stage_inner/pallas_call | solution.py:234
  30.8 0.8 collective-permute-done.6.s2_far
  31.6 2.0 %middle.1 = (f32[8,128]{1,0:T(8,128)S(1)}, f32[2,2,64,512]{3,2,1,0:T(8,128)S(1)}, f32[2,2,64,512]{3,2,1,0:T(8,128)S(1)}, f32[2,64,512]{2,1,0:T(8,128)S(1)}) custom-call(s32[1]{0:T(128)} %bitcast.core, f32[2,8]{1,0:T(2,128)S(1)} %pad_maximum_fusion.scal, f32[1,4,64,512]{3,2,1,0:T(8,128)S(1)} %copy-done, f32[1,4,64,512]{3,2,1,0:T(8,128)S(1)} %collective-permute-done.1.far, ...), custom_call_target="tpu_custom_call" | custom-call | tf_op jit(solution)/shard_map/middle/pallas_call | solution.py:234
  33.6 12.0 %collective-permute-start.9 = (f32[2,64,512]{2,1,0:T(8,128)S(1)}, f32[2,64,512]{2,1,0:T(8,128)S(1)}, u32[]{:S(2)}, u32[]{:S(2)}) collective-permute-start(f32[2,64,512]{2,1,0:T(8,128)S(1)} %get-tuple-element.45), channel_id=1, source_target_pairs={{0,1},{1,0},{2,3},{3,2},{4,5},{5,4},{6,7},{7,6},{8,9},{9,8},{10,11... | collective-permute-start | bytes 786440 | tf_op jit(solution)/shard_map/ppermute | solution.py:271
  45.6 0.7 collective-permute-start.10
  46.7 1.3 %back_inner.1 = (f32[2,64,512]{2,1,0:T(8,128)S(1)}, f32[2,64,512]{2,1,0:T(8,128)S(1)}, f32[2,64,512]{2,1,0:T(8,128)S(1)}) custom-call(f32[2,8]{1,0:T(2,128)S(1)} %pad_maximum_fusion.scal, f32[2,2,64,512]{3,2,1,0:T(8,128)S(1)} %get-tuple-element.44.term, f32[2,64,512]{2,1,0:T(8,128)S(1)} %collective-permute-done.9.pin_far, ...), custom_call_target="tpu_custom_call" | custom-call | tf_op jit(solution)/shard_map/back_inner/pallas_call | solution.py:234
  48.0 3.3 %collective-permute-start.11 = (f32[2,64,512]{2,1,0:T(8,128)S(1)}, f32[2,64,512]{2,1,0:T(8,128)S(1)}, u32[]{:S(2)}, u32[]{:S(2)}) collective-permute-start(f32[2,64,512]{2,1,0:T(8,128)S(1)} %get-tuple-element.49), channel_id=1, source_target_pairs={{0,1},{1,0},{2,3},{3,2},{4,5},{5,4},{6,7},{7,6},{8,9},{9,8},{10,11... | collective-permute-start | bytes 786440 | tf_op jit(solution)/shard_map/ppermute | solution.py:271
  51.3 1.2 %collective-permute-done.11.pin_far = f32[2,64,512]{2,1,0:T(8,128)S(1)} collective-permute-done((f32[2,64,512]{2,1,0:T(8,128)S(1)}, f32[2,64,512]{2,1,0:T(8,128)S(1)}, u32[]{:S(2)}, u32[]{:S(2)}) %collective-permute-start.11) | collective-permute-done | bytes 262176 | tf_op jit(solution)/shard_map/ppermute | solution.py:271
  52.5 1.5 %back_outer.1 = (f32[2,64,512]{2,1,0:T(8,128)S(1)}, f32[2,2,64,512]{3,2,1,0:T(8,128)S(1)}, f32[2,64,512]{2,1,0:T(8,128)S(1)}, f32[2,64,512]{2,1,0:T(8,128)S(1)},...) custom-call(s32[1]{0:T(128)} %bitcast.core, f32[2,8]{1,0:T(2,128)S(1)} %pad_maximum_fusion.scal, ...), custom_call_target="tpu_custom_call" | custom-call | tf_op jit(solution)/shard_map/back_outer/pallas_call | solution.py:234
  54.0 9.3 %collective-permute-start.12 = (f32[2,64,512]{2,1,0:T(8,128)S(1)}, f32[2,64,512]{2,1,0:T(8,128)S(1)}, u32[]{:S(2)}, u32[]{:S(2)}) collective-permute-start(f32[2,64,512]{2,1,0:T(8,128)S(1)} %get-tuple-element.52), channel_id=1, source_target_pairs={{0,1},{1,0},{2,3},{3,2},{4,5},{5,4},{6,7},{7,6},{8,9},{9,8},{10,11... | collective-permute-start | bytes 786440 | tf_op jit(solution)/shard_map/ppermute | solution.py:271
  63.9 3.8 %collective-permute-start.13 = (f32[2,64,256]{2,1,0:T(8,128)S(1)}, f32[2,64,256]{2,1,0:T(8,128)S(1)}, u32[]{:S(2)}, u32[]{:S(2)}) collective-permute-start(f32[2,64,256]{2,1,0:T(8,128)S(1)} %get-tuple-element.54), channel_id=1, source_target_pairs={{0,1},{1,0},{2,3},{3,2},{4,5},{5,4},{6,7},{7,6},{8,9},{9,8},{10,11... | collective-permute-start | bytes 393224 | tf_op jit(solution)/shard_map/ppermute | solution.py:271
  67.7 1.0 %collective-permute-done.13.taken = f32[2,64,256]{2,1,0:T(8,128)S(1)} collective-permute-done((f32[2,64,256]{2,1,0:T(8,128)S(1)}, f32[2,64,256]{2,1,0:T(8,128)S(1)}, u32[]{:S(2)}, u32[]{:S(2)}) %collective-permute-start.13) | collective-permute-done | bytes 131104 | tf_op jit(solution)/shard_map/ppermute | solution.py:271
  68.7 1.9 %last_inner.1 = (f32[2,64,512]{2,1,0:T(8,128)S(1)}, f32[64,512]{1,0:T(8,128)S(1)}, f32[64,512]{1,0:T(8,128)S(1)}, f32[4,64,256]{2,1,0:T(8,128)}) custom-call(s32[1]{0:T(128)} %bitcast.core, f32[2,8]{1,0:T(2,128)S(1)} %pad_maximum_fusion.scal, f32[2,2,64,512]{3,2,1,0:T(8,128)S(1)} %get-tuple-element.44.term, f32[2,64,512]{2,1,0:T(8,128)S(1)} %get-tuple-element.46.a2, ...), custom_call_target="tpu_custom_call" | custom-call | tf_op jit(solution)/shard_map/last_inner/pallas_call | solution.py:234
  71.1 2.8 %collective-permute-start.15 = (f32[64,512]{1,0:T(8,128)S(1)}, f32[64,512]{1,0:T(8,128)S(1)}, u32[]{:S(2)}, u32[]{:S(2)}) collective-permute-start(f32[64,512]{1,0:T(8,128)S(1)} %get-tuple-element.58), channel_id=1, source_target_pairs={{0,1},{1,0},{2,3},{3,2},{4,5},{5,4},{6,7},{7,6},{8,9},{9,8},{10,11... | collective-permute-start | bytes 393224 | tf_op jit(solution)/shard_map/ppermute | solution.py:271
  74.0 1.1 %collective-permute-done.17 = f32[8,128]{1,0:T(8,128)S(1)} collective-permute-done((f32[8,128]{1,0:T(8,128)S(1)}, f32[8,128]{1,0:T(8,128)S(1)}, u32[]{:S(2)}, u32[]{:S(2)}) %collective-permute-start.17) | collective-permute-done | bytes 4128 | tf_op jit(solution)/shard_map/ppermute | solution.py:250
  75.1 2.6 %collective-permute-start.18 = (f32[8,128]{1,0:T(8,128)S(1)}, f32[8,128]{1,0:T(8,128)S(1)}, u32[]{:S(2)}, u32[]{:S(2)}) collective-permute-start(f32[8,128]{1,0:T(8,128)S(1)} %add.60), channel_id=1, source_target_pairs={{0,2},{1,3},{2,0},{3,1},{4,6},{5,7},{6,4},{7,5},{8,10},{9,11},{10,... | collective-permute-start | bytes 12296 | tf_op jit(solution)/shard_map/ppermute | solution.py:250
  77.6 1.6 %collective-permute-done.18 = f32[8,128]{1,0:T(8,128)S(1)} collective-permute-done((f32[8,128]{1,0:T(8,128)S(1)}, f32[8,128]{1,0:T(8,128)S(1)}, u32[]{:S(2)}, u32[]{:S(2)}) %collective-permute-start.18) | collective-permute-done | bytes 4128 | tf_op jit(solution)/shard_map/ppermute | solution.py:250
  79.2 2.0 %collective-permute-start.19 = (f32[8,128]{1,0:T(8,128)S(1)}, f32[8,128]{1,0:T(8,128)S(1)}, u32[]{:S(2)}, u32[]{:S(2)}) collective-permute-start(f32[8,128]{1,0:T(8,128)S(1)} %add.61), channel_id=1, source_target_pairs={{0,4},{1,5},{2,6},{3,7},{4,0},{5,1},{6,2},{7,3},{8,12},{9,13},{10,... | collective-permute-start | bytes 12296 | tf_op jit(solution)/shard_map/ppermute | solution.py:250
  81.2 1.6 %collective-permute-done.19 = f32[8,128]{1,0:T(8,128)S(1)} collective-permute-done((f32[8,128]{1,0:T(8,128)S(1)}, f32[8,128]{1,0:T(8,128)S(1)}, u32[]{:S(2)}, u32[]{:S(2)}) %collective-permute-start.19) | collective-permute-done | bytes 4128 | tf_op jit(solution)/shard_map/ppermute | solution.py:250
  82.8 3.0 %collective-permute-start.20 = (f32[8,128]{1,0:T(8,128)S(1)}, f32[8,128]{1,0:T(8,128)S(1)}, u32[]{:S(2)}, u32[]{:S(2)}) collective-permute-start(f32[8,128]{1,0:T(8,128)S(1)} %add.62), channel_id=1, source_target_pairs={{0,8},{1,9},{2,10},{3,11},{4,12},{5,13},{6,14},{7,15},{8,0},{9,1},... | collective-permute-start | bytes 12296 | tf_op jit(solution)/shard_map/ppermute | solution.py:250
  85.8 1.6 %collective-permute-done.20 = f32[8,128]{1,0:T(8,128)S(1)} collective-permute-done((f32[8,128]{1,0:T(8,128)S(1)}, f32[8,128]{1,0:T(8,128)S(1)}, u32[]{:S(2)}, u32[]{:S(2)}) %collective-permute-start.20) | collective-permute-done | bytes 4128 | tf_op jit(solution)/shard_map/ppermute | solution.py:250
  88.6 0.8 assemble.1
  (46 shorter events, 6.9 us)
Async XLA Ops:
  0.6 2.3 %collective-permute-start.1 = (f32[1,4,64,512]{3,2,1,0:T(8,128)}, f32[1,4,64,512]{3,2,1,0:T(8,128)S(1)}, u32[]{:S(2)}, u32[]{:S(2)}) collective-permute-start(f32[1,4,64,512]{3,2,1,0:T(8,128)} %own.5), channel_id=1, source_target_pairs={{0,1},{1,0},{2,3},{3,2},{4,5},{5,4},{6,7},{7,6},{8,9},{9,8},{10,11... | collective-permute-start | bytes 1572872 | tf_op jit(solution)/shard_map/ppermute | solution.py:271
  1.1 1.7 %copy-start.7 = (s32[1,8]{1,0:T(1,128)S(1)}, s32[1,8]{1,0:T(1,128)}, u32[]{:S(2)}) copy-start(s32[1,8]{1,0:T(1,128)} %param.17) | copy-start | bytes 100
  1.2 15.7 %copy-start.1 = (bf16[1,4,64,512]{3,2,1,0:T(8,128)(2,1)S(1)}, bf16[1,4,64,512]{3,2,1,0:T(8,128)(2,1)}, u32[]{:S(2)}) copy-start(bf16[1,4,64,512]{3,2,1,0:T(8,128)(2,1)} %far_adj.1) | copy-start | bytes 786436
  1.2 15.7 %copy-start.5 = (bf16[4,64,512]{2,1,0:T(8,128)(2,1)S(1)}, bf16[4,64,512]{2,1,0:T(8,128)(2,1)}, u32[]{:S(2)}) copy-start(bf16[4,64,512]{2,1,0:T(8,128)(2,1)} %decay.1) | copy-start | bytes 786436
  2.1 19.8 %collective-permute-start.3 = (f32[1,64,512]{2,1,0:T(8,128)S(1)}, f32[1,64,512]{2,1,0:T(8,128)S(1)}, u32[]{:S(2)}, u32[]{:S(2)}) collective-permute-start(f32[1,64,512]{2,1,0:T(8,128)S(1)} %dynamic-slice_bitcast_fusion), channel_id=1, source_target_pairs={{1,2},{2,1},{3,4},{4,3},{5,6},{6,5},{7,8},{8,7},{9,10},{10,9},{11,... | collective-permute-start | bytes 393224 | tf_op jit(solution)/shard_map/ppermute | solution.py:272
  2.9 19.0 %collective-permute-start.2 = (f32[1,64,512]{2,1,0:T(8,128)S(1)}, f32[1,64,512]{2,1,0:T(8,128)S(1)}, u32[]{:S(2)}, u32[]{:S(2)}) collective-permute-start(f32[1,64,512]{2,1,0:T(8,128)S(1)} %dynamic-slice_bitcast_fusion.1), channel_id=1, source_target_pairs={{1,2},{2,1},{3,4},{4,3},{5,6},{6,5},{7,8},{8,7},{9,10},{10,9},{11,... | collective-permute-start | bytes 393224 | tf_op jit(solution)/shard_map/ppermute | solution.py:272
  10.8 5.9 %collective-permute-start = (f32[1,8]{1,0:T(1,128)S(1)}, f32[1,8]{1,0:T(1,128)S(1)}, u32[]{:S(2)}, u32[]{:S(2)}) collective-permute-start(f32[1,8]{1,0:T(1,128)S(1)} %concatenate.6), channel_id=1, source_target_pairs={{0,1},{1,0},{2,3},{3,2},{4,5},{5,4},{6,7},{7,6},{8,9},{9,8},{10,11... | collective-permute-start | bytes 104 | tf_op jit(solution)/shard_map/ppermute | solution.py:271
  16.8 1.1 %copy-start.2 = (bf16[3,4,64,512]{3,2,1,0:T(8,128)(2,1)S(1)}, bf16[3,4,64,512]{3,2,1,0:T(8,128)(2,1)}, u32[]{:S(2)}) copy-start(bf16[3,4,64,512]{3,2,1,0:T(8,128)(2,1)} %speed.1) | copy-start | bytes 2359300
  18.0 1.0 %copy-start.3 = (f32[4,64,512]{2,1,0:T(8,128)S(1)}, f32[4,64,512]{2,1,0:T(8,128)}, u32[]{:S(2)}) copy-start(f32[4,64,512]{2,1,0:T(8,128)} %control.1) | copy-start | bytes 1572868
  19.0 1.0 %copy-start.4 = (s32[3,4,64,64]{3,2,1,0:T(8,128)S(1)}, s32[3,4,64,64]{3,2,1,0:T(8,128)}, u32[]{:S(2)}) copy-start(s32[3,4,64,64]{3,2,1,0:T(8,128)} %mask.1) | copy-start | bytes 589828
  20.0 0.9 %copy-start.6 = (bf16[4,64,512]{2,1,0:T(8,128)(2,1)S(1)}, bf16[4,64,512]{2,1,0:T(8,128)(2,1)}, u32[]{:S(2)}) copy-start(bf16[4,64,512]{2,1,0:T(8,128)(2,1)} %goal.1) | copy-start | bytes 786436
  20.9 1.0 %copy-start = (f32[1,4,64,512]{3,2,1,0:T(8,128)S(1)}, f32[1,4,64,512]{3,2,1,0:T(8,128)}, u32[]{:S(2)}) copy-start(f32[1,4,64,512]{3,2,1,0:T(8,128)} %own.5) | copy-start | bytes 1572868
  23.6 5.4 %collective-permute-start.5 = (f32[2,64,512]{2,1,0:T(8,128)S(1)}, f32[2,64,512]{2,1,0:T(8,128)S(1)}, u32[]{:S(2)}, u32[]{:S(2)}) collective-permute-start(f32[2,64,512]{2,1,0:T(8,128)S(1)} %get-tuple-element.39.s1_in), channel_id=1, source_target_pairs={{0,1},{1,0},{2,3},{3,2},{4,5},{5,4},{6,7},{7,6},{8,9},{9,8},{10,11... | collective-permute-start | bytes 786440 | tf_op jit(solution)/shard_map/ppermute | solution.py:271
  23.9 6.8 %collective-permute-start.4 = (f32[2,2,64,512]{3,2,1,0:T(8,128)S(1)}, f32[2,2,64,512]{3,2,1,0:T(8,128)S(1)}, u32[]{:S(2)}, u32[]{:S(2)}) collective-permute-start(f32[2,2,64,512]{3,2,1,0:T(8,128)S(1)} %get-tuple-element.38.msg), channel_id=1, source_target_pairs={{1,2},{2,1},{3,4},{4,3},{5,6},{6,5},{7,8},{8,7},{9,10},{10,9},{11,... | collective-permute-start | bytes 1572872 | tf_op jit(solution)/shard_map/ppermute | solution.py:272
  24.6 6.1 %collective-permute-start.8 = (f32[2,64,512]{2,1,0:T(8,128)S(1)}, f32[2,64,512]{2,1,0:T(8,128)S(1)}, u32[]{:S(2)}, u32[]{:S(2)}) collective-permute-start(f32[2,64,512]{2,1,0:T(8,128)S(1)} %get-tuple-element.43), channel_id=1, source_target_pairs={{0,1},{1,0},{2,3},{3,2},{4,5},{5,4},{6,7},{7,6},{8,9},{9,8},{10,11... | collective-permute-start | bytes 786440 | tf_op jit(solution)/shard_map/ppermute | solution.py:271
  30.0 1.6 %collective-permute-start.6 = (f32[2,64,512]{2,1,0:T(8,128)S(1)}, f32[2,64,512]{2,1,0:T(8,128)S(1)}, u32[]{:S(2)}, u32[]{:S(2)}) collective-permute-start(f32[2,64,512]{2,1,0:T(8,128)S(1)} %second_stage_inner.1.s2_in), channel_id=1, source_target_pairs={{0,1},{1,0},{2,3},{3,2},{4,5},{5,4},{6,7},{7,6},{8,9},{9,8},{10,11... | collective-permute-start | bytes 786440 | tf_op jit(solution)/shard_map/ppermute | solution.py:271
  30.1 0.7 collective-permute-start.7
  33.6 13.2 %collective-permute-start.9 = (f32[2,64,512]{2,1,0:T(8,128)S(1)}, f32[2,64,512]{2,1,0:T(8,128)S(1)}, u32[]{:S(2)}, u32[]{:S(2)}) collective-permute-start(f32[2,64,512]{2,1,0:T(8,128)S(1)} %get-tuple-element.45), channel_id=1, source_target_pairs={{0,1},{1,0},{2,3},{3,2},{4,5},{5,4},{6,7},{7,6},{8,9},{9,8},{10,11... | collective-permute-start | bytes 786440 | tf_op jit(solution)/shard_map/ppermute | solution.py:271
  45.6 6.9 %collective-permute-start.10 = (f32[2,2,64,512]{3,2,1,0:T(8,128)S(1)}, f32[2,2,64,512]{3,2,1,0:T(8,128)S(1)}, u32[]{:S(2)}, u32[]{:S(2)}) collective-permute-start(f32[2,2,64,512]{3,2,1,0:T(8,128)S(1)} %get-tuple-element.47.msg3), channel_id=1, source_target_pairs={{1,2},{2,1},{3,4},{4,3},{5,6},{6,5},{7,8},{8,7},{9,10},{10,9},{11,... | collective-permute-start | bytes 1572872 | tf_op jit(solution)/shard_map/ppermute | solution.py:272
  48.0 4.5 %collective-permute-start.11 = (f32[2,64,512]{2,1,0:T(8,128)S(1)}, f32[2,64,512]{2,1,0:T(8,128)S(1)}, u32[]{:S(2)}, u32[]{:S(2)}) collective-permute-start(f32[2,64,512]{2,1,0:T(8,128)S(1)} %get-tuple-element.49), channel_id=1, source_target_pairs={{0,1},{1,0},{2,3},{3,2},{4,5},{5,4},{6,7},{7,6},{8,9},{9,8},{10,11... | collective-permute-start | bytes 786440 | tf_op jit(solution)/shard_map/ppermute | solution.py:271
  54.0 14.7 %collective-permute-start.12 = (f32[2,64,512]{2,1,0:T(8,128)S(1)}, f32[2,64,512]{2,1,0:T(8,128)S(1)}, u32[]{:S(2)}, u32[]{:S(2)}) collective-permute-start(f32[2,64,512]{2,1,0:T(8,128)S(1)} %get-tuple-element.52), channel_id=1, source_target_pairs={{0,1},{1,0},{2,3},{3,2},{4,5},{5,4},{6,7},{7,6},{8,9},{9,8},{10,11... | collective-permute-start | bytes 786440 | tf_op jit(solution)/shard_map/ppermute | solution.py:271
  63.3 7.7 %collective-permute-start.14 = (f32[2,64,512]{2,1,0:T(8,128)S(1)}, f32[2,64,512]{2,1,0:T(8,128)S(1)}, u32[]{:S(2)}, u32[]{:S(2)}) collective-permute-start(f32[2,64,512]{2,1,0:T(8,128)S(1)} %get-tuple-element.56), channel_id=1, source_target_pairs={{1,2},{2,1},{3,4},{4,3},{5,6},{6,5},{7,8},{8,7},{9,10},{10,9},{11,... | collective-permute-start | bytes 786440 | tf_op jit(solution)/shard_map/ppermute | solution.py:272
  63.9 4.8 %collective-permute-start.13 = (f32[2,64,256]{2,1,0:T(8,128)S(1)}, f32[2,64,256]{2,1,0:T(8,128)S(1)}, u32[]{:S(2)}, u32[]{:S(2)}) collective-permute-start(f32[2,64,256]{2,1,0:T(8,128)S(1)} %get-tuple-element.54), channel_id=1, source_target_pairs={{0,1},{1,0},{2,3},{3,2},{4,5},{5,4},{6,7},{7,6},{8,9},{9,8},{10,11... | collective-permute-start | bytes 393224 | tf_op jit(solution)/shard_map/ppermute | solution.py:271
  70.7 18.0 %collective-permute-start.16 = (f32[64,512]{1,0:T(8,128)S(1)}, f32[64,512]{1,0:T(8,128)S(1)}, u32[]{:S(2)}, u32[]{:S(2)}) collective-permute-start(f32[64,512]{1,0:T(8,128)S(1)} %get-tuple-element.60), channel_id=1, source_target_pairs={{0,1},{1,0},{2,3},{3,2},{4,5},{5,4},{6,7},{7,6},{8,9},{9,8},{10,11... | collective-permute-start | bytes 393224 | tf_op jit(solution)/shard_map/ppermute | solution.py:271
  71.1 17.6 %collective-permute-start.15 = (f32[64,512]{1,0:T(8,128)S(1)}, f32[64,512]{1,0:T(8,128)S(1)}, u32[]{:S(2)}, u32[]{:S(2)}) collective-permute-start(f32[64,512]{1,0:T(8,128)S(1)} %get-tuple-element.58), channel_id=1, source_target_pairs={{0,1},{1,0},{2,3},{3,2},{4,5},{5,4},{6,7},{7,6},{8,9},{9,8},{10,11... | collective-permute-start | bytes 393224 | tf_op jit(solution)/shard_map/ppermute | solution.py:271
  73.9 1.2 %collective-permute-start.17 = (f32[8,128]{1,0:T(8,128)S(1)}, f32[8,128]{1,0:T(8,128)S(1)}, u32[]{:S(2)}, u32[]{:S(2)}) collective-permute-start(f32[8,128]{1,0:T(8,128)S(1)} %get-tuple-element.62), channel_id=1, source_target_pairs={{0,1},{1,0},{2,3},{3,2},{4,5},{5,4},{6,7},{7,6},{8,9},{9,8},{10,11... | collective-permute-start | bytes 12296 | tf_op jit(solution)/shard_map/ppermute | solution.py:250
  75.1 4.1 %collective-permute-start.18 = (f32[8,128]{1,0:T(8,128)S(1)}, f32[8,128]{1,0:T(8,128)S(1)}, u32[]{:S(2)}, u32[]{:S(2)}) collective-permute-start(f32[8,128]{1,0:T(8,128)S(1)} %add.60), channel_id=1, source_target_pairs={{0,2},{1,3},{2,0},{3,1},{4,6},{5,7},{6,4},{7,5},{8,10},{9,11},{10,... | collective-permute-start | bytes 12296 | tf_op jit(solution)/shard_map/ppermute | solution.py:250
  79.2 3.6 %collective-permute-start.19 = (f32[8,128]{1,0:T(8,128)S(1)}, f32[8,128]{1,0:T(8,128)S(1)}, u32[]{:S(2)}, u32[]{:S(2)}) collective-permute-start(f32[8,128]{1,0:T(8,128)S(1)} %add.61), channel_id=1, source_target_pairs={{0,4},{1,5},{2,6},{3,7},{4,0},{5,1},{6,2},{7,3},{8,12},{9,13},{10,... | collective-permute-start | bytes 12296 | tf_op jit(solution)/shard_map/ppermute | solution.py:250
  82.8 4.6 %collective-permute-start.20 = (f32[8,128]{1,0:T(8,128)S(1)}, f32[8,128]{1,0:T(8,128)S(1)}, u32[]{:S(2)}, u32[]{:S(2)}) collective-permute-start(f32[8,128]{1,0:T(8,128)S(1)} %add.62), channel_id=1, source_target_pairs={{0,8},{1,9},{2,10},{3,11},{4,12},{5,13},{6,14},{7,15},{8,0},{9,1},... | collective-permute-start | bytes 12296 | tf_op jit(solution)/shard_map/ppermute | solution.py:250

commit v2 on v1

v2 whole, which is shorter than its diff:
```python
import functools
import math

import jax
import jax.numpy as jnp
from jax import lax
from jax.experimental import pallas as pl
from jax.experimental.pallas import tpu as pltpu
from jax.sharding import PartitionSpec as P

time_step = 0.6
variance_gain = 0.5
penalty = 0.1
weight_denominator = 16.0

VMEM_LIMIT = 24 * 1024 * 1024
AXES = ("space", "node")


def roll(value, steps, axis):
    return pltpu.roll(value, steps % value.shape[axis], axis)


def in_plane(value, a, cy, cz, k):
    return a[1] * (cy[0, k] * roll(value, 1, 0) + cy[1, k] * roll(value, -1, 0)) + a[2] * (
        cz[0, k] * roll(value, 1, 1) + cz[1, k] * roll(value, -1, 1)
    )


def in_plane_back(value, a, cy, cz, k):
    return a[1] * (roll(cy[0, k] * value, -1, 0) + roll(cy[1, k] * value, 1, 0)) + a[2] * (
        roll(cz[0, k] * value, -1, 1) + roll(cz[1, k] * value, 1, 1)
    )


def rows_of(scal, j):
    return [scal[j, k] for k in range(6)]


def node_scales(own_raw, far_raw, scal):
    lanes = own_raw.shape[1]
    lane = lax.broadcasted_iota(jnp.int32, (8, lanes), 1)
    row = lax.broadcasted_iota(jnp.int32, (8, lanes), 0)
    raw = jnp.where(row == 0, own_raw[...], far_raw[...])
    points = -jnp.cos(math.pi * raw / 8.0)
    phase = 1.0 + 0.5 * jnp.sin(2.0 * math.pi * raw / 64.0)
    factor = 1.0 + 0.3 * points
    third = factor * (1.0 + 0.2 * roll(points, -5, 1))
    kappa = jnp.exp(0.5 * (points + 0.5 * roll(points, -2, 1)))
    source = (factor + 0.2 * roll(points, -2, 1)) * roll(phase, -5, 1)
    weight = roll(raw, -3, 1) / weight_denominator
    for j in range(2):
        for k, value in enumerate((factor, factor, third, kappa, source, weight)):
            scal[j, k] = jnp.sum(jnp.where((lane == k) & (row == j), value, 0.0))


def prepare(core, own_raw, far_raw, speed, mask, decay, control, goal, own_adj, far_adj, scal, cx, cy, cz, dg, edge, ctl, goals, adj, adj_out):
    me = core[0]
    node_scales(own_raw, far_raw, scal)
    rows, columns = speed.shape[2:]
    blocks = mask.shape[3]
    spread = (
        lax.broadcasted_iota(jnp.int32, (blocks, columns), 1) // (columns // blocks)
        == lax.broadcasted_iota(jnp.int32, (blocks, columns), 0)
    ).astype(jnp.bfloat16)
    row = lax.broadcasted_iota(jnp.int32, (rows, columns), 0)
    column = lax.broadcasted_iota(jnp.int32, (rows, columns), 1)
    flip = (me == 1).astype(jnp.float32)
    for k in range(2):
        at = me if k == 0 else 1 - me
        s, up = [], []
        for d in range(3):
            bits = mask[d, at].astype(jnp.float32).astype(jnp.bfloat16)
            up.append(jnp.dot(bits, spread, preferred_element_type=jnp.float32))
            s.append(speed[d, at].astype(jnp.float32))
        toward_outer = up[0] + flip - 2.0 * flip * up[0]
        outer = s[0] * toward_outer
        cx[0, k] = outer
        cx[1, k] = s[0] - outer
        if k == 0:
            edge[...] = outer
        lower = s[1] * up[1]
        cy[0, k] = jnp.where(row == 0, 0.0, lower)
        cy[1, k] = jnp.where(row == rows - 1, 0.0, s[1] - lower)
        lower = s[2] * up[2]
        cz[0, k] = jnp.where(column == 0, 0.0, lower)
        cz[1, k] = jnp.where(column == columns - 1, 0.0, s[2] - lower)
        rate = decay[at].astype(jnp.float32)
        for j in range(2):
            a = rows_of(scal, j)
            dg[j, k] = a[0] * s[0] + a[1] * s[1] + a[2] * s[2] + a[3] * rate
        ctl[k] = control[at]
        goals[k] = goal[at].astype(jnp.float32)
        adj[k] = own_adj[0, at].astype(jnp.float32)
        adj_out[k] = far_adj[0, 1 - at].astype(jnp.float32)


def first_stage(core, scal, own, far, cx, cy, cz, dg, ctl, base, base_q, s1_in):
    me = core[0]
    for j, c in enumerate((own, far)):
        a = rows_of(scal, j)
        c_o, c_i = c[0, 3 * me], c[0, 1 + me]
        push_o, push_i = a[4] * ctl[0], a[4] * ctl[1]
        l_i = a[0] * (cx[0, 1] * c_o + cx[1, 1] * c[0, 2 - me]) + in_plane(c_i, a, cy, cz, 1) - dg[j, 1] * c_i
        s1_i = c_i + time_step * (l_i + push_i)
        s1_in[j] = s1_i
        l_o = a[0] * (cx[1, 0] * c_i) + in_plane(c_o, a, cy, cz, 0) - dg[j, 0] * c_o
        base[j] = c_o + time_step * (l_o + push_o)
        base_q[j] = 0.75 * c_o + (0.25 * time_step) * (a[0] * (cx[1, 0] * s1_i) + push_o)


def first_edge(j, scal, halo, base, base_q, cx, cy, cz, dg, msg):
    a = rows_of(scal, j)
    s1_o = base[j] + (time_step * a[0]) * (cx[0, 0] * halo[0])
    msg[0] = s1_o
    msg[1] = base_q[j] + 0.25 * (s1_o + time_step * (in_plane(s1_o, a, cy, cz, 0) - dg[j, 0] * s1_o))


def second_inner(core, scal, own, far, msg_own, msg_far, s1_in, s1_far, cx, cy, cz, dg, ctl, s2_in):
    for j, (c, msg) in enumerate(((own, msg_own), (far, msg_far))):
        a = rows_of(scal, j)
        s1_i = s1_in[j]
        l_i = a[0] * (cx[0, 1] * msg[0] + cx[1, 1] * s1_far[1 - j]) + in_plane(s1_i, a, cy, cz, 1) - dg[j, 1] * s1_i
        s2_in[j] = 0.75 * c[0, 1 + core[0]] + 0.25 * (s1_i + time_step * (l_i + a[4] * ctl[1]))


def third_stage(core, scal, own, far, msg_own, msg_far, s2_in, s2_far, near_edge, cx, cy, cz, dg, ctl, base):
    me = core[0]
    for j, (c, msg) in enumerate(((own, msg_own), (far, msg_far))):
        a = rows_of(scal, j)
        q, s2_i = msg[1], s2_in[j]
        back = (0.25 * time_step * a[0]) * (near_edge[...] * msg[0])
        l_o = a[0] * (cx[0, 0] * back + cx[1, 0] * s2_i) + in_plane(q, a, cy, cz, 0) - dg[j, 0] * q
        l_i = a[0] * (cx[0, 1] * q + cx[1, 1] * s2_far[1 - j]) + in_plane(s2_i, a, cy, cz, 1) - dg[j, 1] * s2_i
        base[j, 0] = c[0, 3 * me] / 3.0 + 2.0 / 3.0 * (q + time_step * (l_o + a[4] * ctl[0]))
        base[j, 1] = c[0, 1 + me] / 3.0 + 2.0 / 3.0 * (s2_i + time_step * (l_i + a[4] * ctl[1]))


def finals(j, scal, halo, base, cx, cy, cz, dg):
    a = rows_of(scal, j)
    step = (0.25 * time_step * a[0]) * (cx[0, 0] * halo[0])
    change = in_plane(step, a, cy, cz, 0) - dg[j, 0] * step + a[0] * (cx[0, 0] * halo[1])
    outer = base[j, 0] + 2.0 / 3.0 * (step + time_step * change)
    inner = base[j, 1] + (2.0 / 3.0 * time_step * a[0]) * (cx[0, 1] * step)
    return outer, inner


def third_edge(scal, halo, base, cx, cy, cz, dg, final):
    final[0], final[1] = finals(0, scal, halo, base, cx, cy, cz, dg)


def back_edge(j, final, first, after, scal, cx, cy, cz, dg, goals, term, msg, partial):
    a = rows_of(scal, j)
    u = []
    for k in range(2):
        t = after[k] + goals[k] * a[5] * (1.0 + 2.0 * variance_gain * (final[k] - first[k]))
        term[k] = t
        u.append(2.0 / 3.0 * t)
    msg[0] = a[0] * (cx[0, 0] * u[0])
    spread = a[0] * (cx[0, 1] * u[1]) + in_plane_back(u[0], a, cy, cz, 0) - dg[j, 0] * u[0]
    value = u[0] + time_step * spread
    partial[...] = value
    msg[1] = a[0] * (cx[0, 0] * value)
    return u


def turn_far(scal, halo, base, final_own, cx, cy, cz, dg, goals, after, final, term, msg, partial):
    final[0], final[1] = finals(1, scal, halo, base, cx, cy, cz, dg)
    first = [scal[0, 5] * final_own[k] + scal[1, 5] * final[k] for k in range(2)]
    back_edge(1, final, first, after, scal, cx, cy, cz, dg, goals, term, msg, partial)


def turn_own(scal, final_own, final_far, cx, cy, cz, dg, goals, after, term_far, term, msg, partial, cost, pin):
    first, total = [], 0.0
    for k in range(2):
        own, far = scal[0, 5] * final_own[k], scal[1, 5] * final_far[k]
        first.append(own + far)
        second = own * final_own[k] + far * final_far[k]
        total = total + goals[k] * (first[k] + variance_gain * (second - first[k] * first[k]))
    u = back_edge(0, final_own, first, after, scal, cx, cy, cz, dg, goals, term, msg, partial)
    rows, columns = total.shape
    total = sum(total[8 * r : 8 * r + 8] for r in range(rows // 8))
    cost[...] = sum(total[:, 128 * k : 128 * k + 128] for k in range(columns // 128))
    pin[0] = scal[0, 0] * (cx[1, 1] * u[1])
    pin[1] = scal[1, 0] * (cx[1, 1] * (2.0 / 3.0 * term_far[1]))


def back_inner(scal, term_own, term_far, pin_far, cx, cy, cz, dg, a2, pin2):
    for j, term in enumerate((term_own, term_far)):
        a = rows_of(scal, j)
        u = [2.0 / 3.0 * term[k] for k in range(2)]
        spread = a[0] * (cx[1, 0] * u[0]) + in_plane_back(u[1], a, cy, cz, 1) - dg[j, 1] * u[1] + pin_far[1 - j]
        a2_i = u[1] + time_step * spread
        a2[j] = a2_i
        pin2[j] = (0.25 * a[0]) * (cx[1, 1] * a2_i)


def back_second(scal, msg_own, msg_far, partial_own, partial_far, a2, pin_far, near_edge, cx, cy, cz, dg, base):
    for j, (msg, partial) in enumerate(((msg_own, partial_own), (msg_far, partial_far))):
        a = rows_of(scal, j)
        u_o, u_i = 0.25 * partial[...], 0.25 * a2[j]
        back = (0.25 * time_step * a[0]) * (near_edge[...] * msg[0])
        spread = a[0] * (cx[0, 1] * u_i) + in_plane_back(u_o, a, cy, cz, 0) - dg[j, 0] * u_o + back
        base[j, 0] = u_o + time_step * spread
        spread = a[0] * (cx[1, 0] * u_o) + in_plane_back(u_i, a, cy, cz, 1) - dg[j, 1] * u_i + pin_far[1 - j]
        base[j, 1] = u_i + time_step * spread


def second_back_edge(j, scal, halo, base, cx, cy, cz, dg, a1_o, msg):
    a = rows_of(scal, j)
    step = (0.25 * time_step) * halo[0]
    value = base[j, 0] + step + time_step * (in_plane_back(step, a, cy, cz, 0) - dg[j, 0] * step + 0.25 * halo[1])
    a1_o[...] = value
    msg[0] = a[0] * (cx[0, 0] * value)


def close(core, scal, terms, partials, halos, a1s, a2, base, cx, cy, cz, dg, ctl, pin3, keep, give, part, a1_in):
    sources = [0.0, 0.0]
    for j in range(2):
        a = rows_of(scal, j)
        term, halo, a1_o = terms[j], halos[j], a1s[j][...]
        a1_i = base[j, 1] + (0.25 * time_step * time_step * a[0]) * (cx[1, 0] * halo[0])
        a2_o = partials[j][...] + time_step * halo[0]
        a1_in[j] = a1_i
        pin3[j] = a[0] * (cx[1, 1] * a1_i)
        for k, (u2, last) in enumerate(((0.25 * a2_o, a1_o), (0.25 * a2[j], a1_i))):
            sources[k] = sources[k] + a[4] * (2.0 / 3.0 * term[k] + u2 + last)
        spread = a[0] * (cx[0, 1] * a1_i) + in_plane_back(a1_o, a, cy, cz, 0) - dg[j, 0] * a1_o
        part[j] = term[0] / 3.0 + 0.75 * a2_o + (a1_o + time_step * spread)
    half = ctl.shape[2] // 2
    zero = core[0] == 0
    for k in range(2):
        gradient = time_step * sources[k] + penalty * ctl[k]
        low, high = gradient[:, :half], gradient[:, half:]
        keep[k] = jnp.where(zero, low, high)
        give[k] = jnp.where(zero, high, low)


def close_all(core, scal, term_own, term_far, partial_own, partial_far, halo_own, halo_far, a1_own, a1_far, *rest):
    close(core, scal, (term_own, term_far), (partial_own, partial_far), (halo_own, halo_far), (a1_own, a1_far), *rest)


def last_inner(core, scal, term_own, term_far, a2, a1_own, a1_far, a1_in, pin_far, keep, taken, cx, cy, cz, dg, adj_in, adj_out, gradient):
    me = core[0]
    for j, (term, a1_o, out) in enumerate(((term_own, a1_own, adj_in), (term_far, a1_far, adj_out))):
        a = rows_of(scal, j)
        x = a1_in[j]
        spread = a[0] * (cx[1, 0] * a1_o[...]) + in_plane_back(x, a, cy, cz, 1) - dg[j, 1] * x + pin_far[1 - j]
        out[...] = term[1] / 3.0 + 0.75 * a2[j] + (x + time_step * spread)
    gradient[3 * me] = keep[0]
    gradient[1 + me] = keep[1]
    gradient[3 - 3 * me] = taken[0]
    gradient[2 - me] = taken[1]


def last_outer(part, halo, give):
    give[...] = part[1] + time_step * halo[0]


def assemble(core, part, halo, taken, adj_in, adj_taken, out):
    me = core[0]
    out[0, 3 * me] = part[0] + time_step * halo[0]
    out[0, 1 + me] = adj_in[...]
    out[0, 3 - 3 * me] = taken[...]
    out[0, 2 - me] = adj_taken[...]


def on_core(body, outs, scalars, arrays, hbm_out=(), after=(), name=None):
    out_shape = [
        jax.ShapeDtypeStruct(s, jnp.float32) if i in hbm_out else pltpu.VMEM(s, jnp.float32)
        for i, s in enumerate(outs)
    ]
    held = [pltpu.with_memory_space_constraint(x, pltpu.SMEM) for x in scalars]
    held += [pltpu.with_memory_space_constraint(x, pltpu.VMEM) for x in arrays]
    count, waits = len(held), len(after)

    def run(*refs):
        body(*refs[:count], *refs[count + waits :])

    return pl.pallas_call(
        run,
        out_shape=out_shape,
        in_specs=[pl.BlockSpec(memory_space=pltpu.SMEM)] * len(scalars)
        + [pl.BlockSpec(memory_space=pltpu.VMEM)] * len(arrays)
        + [pl.BlockSpec(memory_space=pl.ANY)] * waits,
        out_specs=[pl.BlockSpec(memory_space=pltpu.VMEM)] * len(outs),
        compiler_params=pltpu.CompilerParams(vmem_limit_bytes=VMEM_LIMIT),
        name=name or body.__name__,
    )(*held, *after)


def shards(
    concentration,
    adjoint_next,
    speed,
    direction_mask,
    decay_rate,
    control,
    goal_weight,
    node_index,
    weight_num,
    step_index,
):
    sections = lax.axis_size("space")
    ranks = sections * lax.axis_size("node")
    within = [(i, i ^ 1) for i in range(ranks)]
    across = [p for i in range(1, ranks - 1, 2) for p in ((i, i + 1), (i + 1, i))]
    swap = lambda x: lax.ppermute(x, AXES, within)
    pass_on = lambda x: lax.ppermute(x, AXES, across)

    _, layers, rows, columns = concentration.shape
    me = lax.axis_index("node").astype(jnp.int32)
    core = jnp.reshape(me, (1,))
    raw = jnp.concatenate(
        [
            node_index.astype(jnp.float32),
            weight_num.astype(jnp.float32)[:, None],
            step_index.astype(jnp.float32)[:, None],
            jnp.zeros((1, 118), jnp.float32),
        ],
        1,
    )
    far_raw = swap(raw)

    far = swap(concentration)
    take = lambda x: lax.dynamic_slice_in_dim(x, 3 * me, 1, axis=1)[0]
    far_halo = pass_on(take(concentration))
    own_halo = pass_on(take(far))

    plane = (rows, columns)
    pair = (2,) + plane
    four = (2,) + pair
    specs = [
        pl.BlockSpec(memory_space=pltpu.VMEM),
        pl.BlockSpec(memory_space=pltpu.VMEM),
        pl.BlockSpec((3, 2, rows, columns), lambda g, c: (0, c[0], 0, 0)),
        pl.BlockSpec((3, 2, rows, direction_mask.shape[3]), lambda g, c: (0, c[0], 0, 0)),
        pl.BlockSpec((2, rows, columns), lambda g, c: (c[0], 0, 0)),
        pl.BlockSpec((2, rows, columns), lambda g, c: (c[0], 0, 0)),
        pl.BlockSpec((2, rows, columns), lambda g, c: (c[0], 0, 0)),
        pl.BlockSpec((1, 2, rows, columns), lambda g, c: (0, c[0], 0, 0)),
        pl.BlockSpec((1, 2, rows, columns), lambda g, c: (0, 1 - c[0], 0, 0)),
    ]
    shapes = [four, four, four, four, plane, pair, pair, pair, pair]
    far_off = [
        pltpu.with_memory_space_constraint(x, pltpu.HBM)
        for x in (speed, direction_mask, decay_rate, control, goal_weight, adjoint_next, adjoint_next)
    ]
    scal, cx, cy, cz, dg, edge, ctl, goals, adj, adj_out = pl.pallas_call(
        prepare,
        out_shape=[pltpu.SMEM((2, 8), jnp.float32)] + [pltpu.VMEM(s, jnp.float32) for s in shapes],
        grid_spec=pltpu.PrefetchScalarGridSpec(
            num_scalar_prefetch=1,
            grid=(1,),
            in_specs=specs,
            out_specs=[pl.BlockSpec(memory_space=pltpu.SMEM)]
            + [pl.BlockSpec(memory_space=pltpu.VMEM)] * len(shapes),
        ),
        compiler_params=pltpu.CompilerParams(vmem_limit_bytes=VMEM_LIMIT),
        name="prepare",
    )(core, raw, far_raw, *far_off)
    near_edge = pass_on(edge)
    adj_far = swap(adj_out)

    fields = [cx, cy, cz, dg]
    both = [core, scal]
    states = [concentration, far]
    base, base_q, s1_in = on_core(first_stage, [pair, pair, pair], both, states + fields + [ctl])
    s1_far = swap(s1_in)
    edge_of = lambda j, halo: on_core(
        functools.partial(first_edge, j), [pair], [scal], [halo, base, base_q] + fields, name="first_edge"
    )[0]
    msg_far = edge_of(1, far_halo)
    halo2_own = pass_on(msg_far)
    msg_own = edge_of(0, own_halo)
    halo2_far = pass_on(msg_own)

    msgs = [msg_own, msg_far]
    (s2_in,) = on_core(second_inner, [pair], both, states + msgs + [s1_in, s1_far] + fields + [ctl])
    s2_far = swap(s2_in)
    (base,) = on_core(third_stage, [four], both, states + msgs + [s2_in, s2_far, near_edge] + fields + [ctl])
    (final_own,) = on_core(third_edge, [pair], [scal], [halo2_own, base] + fields)
    final_far, term_far, msg3_far, partial_far = on_core(
        turn_far, [pair, pair, pair, plane], [scal], [halo2_far, base, final_own] + fields + [goals, adj_far]
    )
    halo3_own = pass_on(msg3_far)
    term_own, msg3_own, partial_own, cost, pin = on_core(
        turn_own,
        [pair, pair, plane, (8, 128), pair],
        [scal],
        [final_own, final_far] + fields + [goals, adj, term_far],
    )
    halo3_far = pass_on(msg3_own)
    pin_far = swap(pin)
    terms, partials = [term_own, term_far], [partial_own, partial_far]
    a2, pin2 = on_core(back_inner, [pair, pair], [scal], terms + [pin_far] + fields)
    pin2_far = swap(pin2)
    (base,) = on_core(
        back_second, [four], [scal], [msg3_own, msg3_far] + partials + [a2, pin2_far, near_edge] + fields
    )
    edge_of = lambda j, halo: on_core(
        functools.partial(second_back_edge, j),
        [plane, (1,) + plane],
        [scal],
        [halo, base] + fields,
        name="second_back_edge",
    )
    a1_own, msg4_own = edge_of(0, halo3_own)
    halo4_far = pass_on(msg4_own)
    a1_far, msg4_far = edge_of(1, halo3_far)
    halo4_own = pass_on(msg4_far)
    half = (2, rows, columns // 2)
    pin3, keep, give, part, a1_in = on_core(
        close_all,
        [pair, half, half, pair, pair],
        both,
        terms + partials + [halo3_own, halo3_far, a1_own, a1_far, a2, base] + fields + [ctl],
    )
    pin3_far = swap(pin3)
    taken = swap(give)
    adj_in, adj_give, gradient = on_core(
        last_inner,
        [plane, plane, (layers, rows, columns // 2)],
        both,
        terms + [a2, a1_own, a1_far, a1_in, pin3_far, keep, taken] + fields,
        hbm_out=(2,),
    )
    adj_taken = swap(adj_give)
    (edge_give,) = on_core(last_outer, [plane], [], [part, halo4_far])
    edge_taken = swap(edge_give)
    (adjoint,) = on_core(
        assemble,
        [(1, layers, rows, columns)],
        [core],
        [part, halo4_own, edge_taken, adj_in, adj_taken],
        hbm_out=(0,),
    )

    if ranks & (ranks - 1):
        cost = lax.psum(cost, AXES)
    else:
        steps = [1 << k for k in range(ranks.bit_length() - 1)]
        for step in steps[:1] + steps[2:] + steps[1:2]:
            cost = cost + lax.ppermute(cost, AXES, [(i, i ^ step) for i in range(ranks)])
    cells = sections * layers * rows * columns
    objective = jnp.reshape(jnp.sum(cost) / cells, (1,))
    return (adjoint, gradient, objective)


def solution(mesh):
    return jax.shard_map(
        shards,
        mesh=mesh,
        in_specs=(
            P("node", ("groups", "space"), None, None),
            P("node", ("groups", "space"), None, None),
            P(None, ("groups", "space"), None, None),
            P(None, ("groups", "space"), None, None),
            P(("groups", "space"), None, None),
            P(("groups", "space"), None, None),
            P(("groups", "space"), None, None),
            P("node", None),
            P("node"),
            P("groups"),
        ),
        out_specs=(
            P("node", ("groups", "space"), None, None),
            P(("groups", "space"), None, "node"),
            P("groups"),
        ),
        check_vma=False,
    )
```

time: 91.2 us -> 85.6 us (0.939)
  starting transfers between devices: 53.7 us -> 62.2 us
  local copies, waits for them, and re-layouts: 5.96 us -> 0.68 us
  between operations: 9.08 us -> 4.04 us
  Pallas kernels: 11 us -> 9.06 us
  waiting for transfers between devices: 10.2 us -> 8.57 us
    ppermute x11, starting transfers between devices: 42.1 us -> 49.2 us  [shards(): swap = lambda x: lax.ppermute(x, AXES, within)]
    unnamed x16 -> x4, local copies, waits for them, and re-layouts: 4.2 us -> 0.65 us
    ppermute x11, waiting for transfers between devices: 4.3 us -> 2.25 us  [shards(): swap = lambda x: lax.ppermute(x, AXES, within)]
    ppermute x6 -> x9, starting transfers between devices: 4.03 us -> 5.99 us  [shards(): pass_on = lambda x: lax.ppermute(x, AXES, across)]
    pallas_call x9 -> x17, Pallas kernels: 11 us -> 9.06 us  [the longest x16 7.19 us: on_core(): pl.pallas_call(run, out_shape=out_shape, in_specs=[pl.BlockSpec(memory_sp...]
    squeeze x2, local copies, waits for them, and re-layouts: 0.98 us -> 0.03 us  [shards(): take = lambda x: lax.dynamic_slice_in_dim(x, 3 * me, 1, axis=1)[0]]
  transfers between devices with their start and end apart: 21 -> 24, of which waited for: 9 -> 6; matrix products, arithmetic and copies ran while one was open for 3% -> 1% of each run, Pallas kernels for 6% -> 6%
where the time goes in v2:
time: 85.6 us; the launch traced here: 85.2 us
  starting transfers between devices  62.2 us (73%)
  Pallas kernels  9.06 us (11%)
  waiting for transfers between devices  8.57 us (10%)
  between operations  4.04 us (5%)
    ppermute x11, starting transfers between devices, shards(): swap = lambda x: lax.ppermute(x, AXES, within)  49.2 us
    pallas_call x16, Pallas kernels, on_core(): pl.pallas_call(run, out_shape=out_shape, in_specs=[pl.BlockSpec(memory_sp...  7.19 us
    ppermute x4, starting transfers between devices, shards(): lax.ppermute(cost, AXES, [(i, i ^ step) for i in range(ranks)])  6.96 us
    ppermute x4, waiting for transfers between devices, shards(): lax.ppermute(cost, AXES, [(i, i ^ step) for i in range(ranks)])  6.29 us
    ppermute x9, starting transfers between devices, shards(): pass_on = lambda x: lax.ppermute(x, AXES, across)  5.99 us
    ppermute x11, waiting for transfers between devices, shards(): swap = lambda x: lax.ppermute(x, AXES, within)  2.25 us
    pallas_call x1, Pallas kernels, shards(): pl.pallas_call(prepare, out_shape=[pltpu.SMEM((2, 8), jnp.float32)] + [pl...  1.87 us
  transfers between devices with their start and end apart: 24, of which 6 were waited for; matrix products, arithmetic and copies ran while one was open for 1% of the time, Pallas kernels for 6%

profile of v2, /device:TPU:0, one launch (start us, length us, event | category | flops | bytes accessed | tf_op | source)
XLA Modules:
  0.0 85.2 jit_solution(5754369477187309)
XLA Ops:
  2.5 0.6 copy-done.1
  3.2 1.1 %collective-permute-done.far_raw = f32[1,128]{1,0:T(1,128)S(1)} collective-permute-done((f32[1,128]{1,0:T(1,128)S(1)}, f32[1,128]{1,0:T(1,128)S(1)}, u32[]{:S(2)}, u32[]{:S(2)}) %collective-permute-start) | collective-permute-done | bytes 544 | tf_op jit(solution)/shard_map/ppermute | solution.py:308
  4.3 1.9 %prepare.1 = (f32[2,8]{1,0:T(2,128)S(4)}, f32[2,2,64,512]{3,2,1,0:T(8,128)S(1)}, f32[2,2,64,512]{3,2,1,0:T(8,128)S(1)}, f32[2,2,64,512]{3,2,1,0:T(8,128)S(1)}, f...) custom-call(s32[1]{0:T(128)} %bitcast.core.refs_0_, ...), custom_call_target="tpu_custom_call" | custom-call | tf_op jit(solution)/shard_map/prepare/pallas_call | solution.py:349
  6.2 0.7 first_stage.1
  7.2 0.7 collective-permute-start.1
  7.9 0.7 collective-permute-start.4
  9.4 9.6 %collective-permute-start.6 = (f32[2,64,512]{2,1,0:T(8,128)S(1)}, f32[2,64,512]{2,1,0:T(8,128)S(1)}, u32[]{:S(2)}, u32[]{:S(2)}) collective-permute-start(f32[2,64,512]{2,1,0:T(8,128)S(1)} %second_inner.1.refs_6_), channel_id=1, source_target_pairs={{0,1},{1,0},{2,3},{3,2},{4,5},{5,4},{6,7},{7,6},{8,9},{9,8},{10,11... | collective-permute-start | bytes 786440 | tf_op jit(solution)/shard_map/ppermute | solution.py:308
  19.0 0.7 collective-permute-start.3
  19.7 3.9 %collective-permute-start.9 = (f32[2,64,512]{2,1,0:T(8,128)S(1)}, f32[2,64,512]{2,1,0:T(8,128)S(1)}, u32[]{:S(2)}, u32[]{:S(2)}) collective-permute-start(f32[2,64,512]{2,1,0:T(8,128)S(1)} %get-tuple-element.50), channel_id=1, source_target_pairs={{0,1},{1,0},{2,3},{3,2},{4,5},{5,4},{6,7},{7,6},{8,9},{9,8},{10,11... | collective-permute-start | bytes 786440 | tf_op jit(solution)/shard_map/ppermute | solution.py:308
  23.6 0.7 collective-permute-start.8
  24.2 0.7 collective-permute-start.7
  24.9 0.8 third_stage.1.refs_2_
  26.8 13.2 %collective-permute-start.12 = (f32[2,64,512]{2,1,0:T(8,128)S(1)}, f32[2,64,512]{2,1,0:T(8,128)S(1)}, u32[]{:S(2)}, u32[]{:S(2)}) collective-permute-start(f32[2,64,512]{2,1,0:T(8,128)S(1)} %get-tuple-element.59), channel_id=1, source_target_pairs={{0,1},{1,0},{2,3},{3,2},{4,5},{5,4},{6,7},{7,6},{8,9},{9,8},{10,11... | collective-permute-start | bytes 786440 | tf_op jit(solution)/shard_map/ppermute | solution.py:308
  39.9 1.2 %collective-permute-done.12.refs_3_ = f32[2,64,512]{2,1,0:T(8,128)S(1)} collective-permute-done((f32[2,64,512]{2,1,0:T(8,128)S(1)}, f32[2,64,512]{2,1,0:T(8,128)S(1)}, u32[]{:S(2)}, u32[]{:S(2)}) %collective-permute-start.12) | collective-permute-done | bytes 262176 | tf_op jit(solution)/shard_map/ppermute | solution.py:308
  41.9 0.7 collective-permute-start.11
  42.6 0.7 collective-permute-start.10
  43.3 0.7 back_second.1.refs_2_.refs_11_
  45.0 14.0 %collective-permute-start.17 = (f32[2,64,512]{2,1,0:T(8,128)S(1)}, f32[2,64,512]{2,1,0:T(8,128)S(1)}, u32[]{:S(2)}, u32[]{:S(2)}) collective-permute-start(f32[2,64,512]{2,1,0:T(8,128)S(1)} %get-tuple-element.68), channel_id=1, source_target_pairs={{0,1},{1,0},{2,3},{3,2},{4,5},{5,4},{6,7},{7,6},{8,9},{9,8},{10,11... | collective-permute-start | bytes 786440 | tf_op jit(solution)/shard_map/ppermute | solution.py:308
  59.0 0.7 collective-permute-start.15
  59.7 3.8 %collective-permute-start.18 = (f32[2,64,256]{2,1,0:T(8,128)S(1)}, f32[2,64,256]{2,1,0:T(8,128)S(1)}, u32[]{:S(2)}, u32[]{:S(2)}) collective-permute-start(f32[2,64,256]{2,1,0:T(8,128)S(1)} %get-tuple-element.70), channel_id=1, source_target_pairs={{0,1},{1,0},{2,3},{3,2},{4,5},{5,4},{6,7},{7,6},{8,9},{9,8},{10,11... | collective-permute-start | bytes 393224 | tf_op jit(solution)/shard_map/ppermute | solution.py:308
  63.5 0.7 collective-permute-start.14
  64.2 3.4 %collective-permute-start.16 = (f32[64,512]{1,0:T(8,128)S(1)}, f32[64,512]{1,0:T(8,128)S(1)}, u32[]{:S(2)}, u32[]{:S(2)}) collective-permute-start(f32[64,512]{1,0:T(8,128)S(1)} %last_outer.1), channel_id=1, source_target_pairs={{0,1},{1,0},{2,3},{3,2},{4,5},{5,4},{6,7},{7,6},{8,9},{9,8},{10,11... | collective-permute-start | bytes 393224 | tf_op jit(solution)/shard_map/ppermute | solution.py:308
  67.6 1.0 %last_inner.1 = (f32[64,512]{1,0:T(8,128)S(1)}, f32[64,512]{1,0:T(8,128)S(1)}, f32[4,64,256]{2,1,0:T(8,128)}) custom-call(s32[1]{0:T(128)} %bitcast.core.refs_0_, f32[2,8]{1,0:T(2,128)S(4)} %get-tuple-element.39.refs_1_.refs_0_, f32[2,64,512]{2,1,0:T(8,128)S(1)} %get-tuple-element.54.refs_1_.refs_2_, ...), custom_call_target="tpu_custom_call" | custom-call | tf_op jit(solution)/shard_map/last_inner/pallas_call | solution.py:280
  69.2 0.8 collective-permute-done.20
  70.0 2.1 %collective-permute-start.21 = (f32[8,128]{1,0:T(8,128)S(1)}, f32[8,128]{1,0:T(8,128)S(1)}, u32[]{:S(2)}, u32[]{:S(2)}) collective-permute-start(f32[8,128]{1,0:T(8,128)S(1)} %add.17), channel_id=1, source_target_pairs={{0,4},{1,5},{2,6},{3,7},{4,0},{5,1},{6,2},{7,3},{8,12},{9,13},{10,... | collective-permute-start | bytes 12296 | tf_op jit(solution)/shard_map/ppermute | solution.py:444
  72.1 1.6 %collective-permute-done.21 = f32[8,128]{1,0:T(8,128)S(1)} collective-permute-done((f32[8,128]{1,0:T(8,128)S(1)}, f32[8,128]{1,0:T(8,128)S(1)}, u32[]{:S(2)}, u32[]{:S(2)}) %collective-permute-start.21) | collective-permute-done | bytes 4128 | tf_op jit(solution)/shard_map/ppermute | solution.py:444
  73.7 3.0 %collective-permute-start.22 = (f32[8,128]{1,0:T(8,128)S(1)}, f32[8,128]{1,0:T(8,128)S(1)}, u32[]{:S(2)}, u32[]{:S(2)}) collective-permute-start(f32[8,128]{1,0:T(8,128)S(1)} %add.18), channel_id=1, source_target_pairs={{0,8},{1,9},{2,10},{3,11},{4,12},{5,13},{6,14},{7,15},{8,0},{9,1},... | collective-permute-start | bytes 12296 | tf_op jit(solution)/shard_map/ppermute | solution.py:444
  76.7 1.6 %collective-permute-done.22 = f32[8,128]{1,0:T(8,128)S(1)} collective-permute-done((f32[8,128]{1,0:T(8,128)S(1)}, f32[8,128]{1,0:T(8,128)S(1)}, u32[]{:S(2)}, u32[]{:S(2)}) %collective-permute-start.22) | collective-permute-done | bytes 4128 | tf_op jit(solution)/shard_map/ppermute | solution.py:444
  78.3 1.3 %collective-permute-start.23 = (f32[8,128]{1,0:T(8,128)S(1)}, f32[8,128]{1,0:T(8,128)S(1)}, u32[]{:S(2)}, u32[]{:S(2)}) collective-permute-start(f32[8,128]{1,0:T(8,128)S(1)} %add.19), channel_id=1, source_target_pairs={{0,2},{1,3},{2,0},{3,1},{4,6},{5,7},{6,4},{7,5},{8,10},{9,11},{10,... | collective-permute-start | bytes 12296 | tf_op jit(solution)/shard_map/ppermute | solution.py:444
  79.7 2.3 %collective-permute-done.23 = f32[8,128]{1,0:T(8,128)S(1)} collective-permute-done((f32[8,128]{1,0:T(8,128)S(1)}, f32[8,128]{1,0:T(8,128)S(1)}, u32[]{:S(2)}, u32[]{:S(2)}) %collective-permute-start.23) | collective-permute-done | bytes 4128 | tf_op jit(solution)/shard_map/ppermute | solution.py:444
  81.9 0.6 add_reduce_fusion
  83.2 0.8 assemble.1
  (46 shorter events, 5.1 us)
Async XLA Ops:
  0.6 5.6 %collective-permute-start.2 = (f32[1,4,64,512]{3,2,1,0:T(8,128)}, f32[1,4,64,512]{3,2,1,0:T(8,128)S(1)}, u32[]{:S(2)}, u32[]{:S(2)}) collective-permute-start(f32[1,4,64,512]{3,2,1,0:T(8,128)} %refs_2_.5), channel_id=1, source_target_pairs={{0,1},{1,0},{2,3},{3,2},{4,5},{5,4},{6,7},{7,6},{8,9},{9,8},{10,11... | collective-permute-start | bytes 1572872 | tf_op jit(solution)/shard_map/ppermute | solution.py:308
  2.4 0.7 copy-start.1
  3.2 1.1 %collective-permute-start = (f32[1,128]{1,0:T(1,128)S(1)}, f32[1,128]{1,0:T(1,128)S(1)}, u32[]{:S(2)}, u32[]{:S(2)}) collective-permute-start(f32[1,128]{1,0:T(1,128)S(1)} %bitcast_maximum_fusion.own_raw), channel_id=1, source_target_pairs={{0,1},{1,0},{2,3},{3,2},{4,5},{5,4},{6,7},{7,6},{8,9},{9,8},{10,11... | collective-permute-start | bytes 1544 | tf_op jit(solution)/shard_map/ppermute | solution.py:308
  4.3 1.9 %copy-start = (f32[1,4,64,512]{3,2,1,0:T(8,128)S(1)}, f32[1,4,64,512]{3,2,1,0:T(8,128)}, u32[]{:S(2)}) copy-start(f32[1,4,64,512]{3,2,1,0:T(8,128)} %refs_2_.5) | copy-start | bytes 1572868
  6.9 2.1 %collective-permute-start.5 = (f32[2,64,512]{2,1,0:T(8,128)S(1)}, f32[2,64,512]{2,1,0:T(8,128)S(1)}, u32[]{:S(2)}, u32[]{:S(2)}) collective-permute-start(f32[2,64,512]{2,1,0:T(8,128)S(1)} %get-tuple-element.47.refs_6_), channel_id=1, source_target_pairs={{0,1},{1,0},{2,3},{3,2},{4,5},{5,4},{6,7},{7,6},{8,9},{9,8},{10,11... | collective-permute-start | bytes 786440 | tf_op jit(solution)/shard_map/ppermute | solution.py:308
  7.2 1.4 %collective-permute-start.1 = (f32[1,64,512]{2,1,0:T(8,128)S(1)}, f32[1,64,512]{2,1,0:T(8,128)S(1)}, u32[]{:S(2)}, u32[]{:S(2)}) collective-permute-start(f32[1,64,512]{2,1,0:T(8,128)S(1)} %dynamic-slice_bitcast_fusion.1), channel_id=1, source_target_pairs={{1,2},{2,1},{3,4},{4,3},{5,6},{6,5},{7,8},{8,7},{9,10},{10,9},{11,... | collective-permute-start | bytes 393224 | tf_op jit(solution)/shard_map/ppermute | solution.py:309
  7.9 0.9 %collective-permute-start.4 = (f32[1,64,512]{2,1,0:T(8,128)S(1)}, f32[1,64,512]{2,1,0:T(8,128)S(1)}, u32[]{:S(2)}, u32[]{:S(2)}) collective-permute-start(f32[1,64,512]{2,1,0:T(8,128)S(1)} %dynamic-slice_bitcast_fusion), channel_id=1, source_target_pairs={{1,2},{2,1},{3,4},{4,3},{5,6},{6,5},{7,8},{8,7},{9,10},{10,9},{11,... | collective-permute-start | bytes 393224 | tf_op jit(solution)/shard_map/ppermute | solution.py:309
  9.4 15.5 %collective-permute-start.6 = (f32[2,64,512]{2,1,0:T(8,128)S(1)}, f32[2,64,512]{2,1,0:T(8,128)S(1)}, u32[]{:S(2)}, u32[]{:S(2)}) collective-permute-start(f32[2,64,512]{2,1,0:T(8,128)S(1)} %second_inner.1.refs_6_), channel_id=1, source_target_pairs={{0,1},{1,0},{2,3},{3,2},{4,5},{5,4},{6,7},{7,6},{8,9},{9,8},{10,11... | collective-permute-start | bytes 786440 | tf_op jit(solution)/shard_map/ppermute | solution.py:308
  19.0 6.7 %collective-permute-start.3 = (f32[2,64,512]{2,1,0:T(8,128)S(1)}, f32[2,64,512]{2,1,0:T(8,128)S(1)}, u32[]{:S(2)}, u32[]{:S(2)}) collective-permute-start(f32[2,64,512]{2,1,0:T(8,128)S(1)} %first_edge.2.refs_5_), channel_id=1, source_target_pairs={{1,2},{2,1},{3,4},{4,3},{5,6},{6,5},{7,8},{8,7},{9,10},{10,9},{11,... | collective-permute-start | bytes 786440 | tf_op jit(solution)/shard_map/ppermute | solution.py:309
  19.7 6.2 %collective-permute-start.9 = (f32[2,64,512]{2,1,0:T(8,128)S(1)}, f32[2,64,512]{2,1,0:T(8,128)S(1)}, u32[]{:S(2)}, u32[]{:S(2)}) collective-permute-start(f32[2,64,512]{2,1,0:T(8,128)S(1)} %get-tuple-element.50), channel_id=1, source_target_pairs={{0,1},{1,0},{2,3},{3,2},{4,5},{5,4},{6,7},{7,6},{8,9},{9,8},{10,11... | collective-permute-start | bytes 786440 | tf_op jit(solution)/shard_map/ppermute | solution.py:308
  23.6 2.4 %collective-permute-start.8 = (f32[2,64,512]{2,1,0:T(8,128)S(1)}, f32[2,64,512]{2,1,0:T(8,128)S(1)}, u32[]{:S(2)}, u32[]{:S(2)}) collective-permute-start(f32[2,64,512]{2,1,0:T(8,128)S(1)} %first_edge.3.refs_4_), channel_id=1, source_target_pairs={{1,2},{2,1},{3,4},{4,3},{5,6},{6,5},{7,8},{8,7},{9,10},{10,9},{11,... | collective-permute-start | bytes 786440 | tf_op jit(solution)/shard_map/ppermute | solution.py:309
  24.2 0.7 collective-permute-start.7
  26.8 14.3 %collective-permute-start.12 = (f32[2,64,512]{2,1,0:T(8,128)S(1)}, f32[2,64,512]{2,1,0:T(8,128)S(1)}, u32[]{:S(2)}, u32[]{:S(2)}) collective-permute-start(f32[2,64,512]{2,1,0:T(8,128)S(1)} %get-tuple-element.59), channel_id=1, source_target_pairs={{0,1},{1,0},{2,3},{3,2},{4,5},{5,4},{6,7},{7,6},{8,9},{9,8},{10,11... | collective-permute-start | bytes 786440 | tf_op jit(solution)/shard_map/ppermute | solution.py:308
  41.5 1.8 %collective-permute-start.13 = (f32[2,64,512]{2,1,0:T(8,128)S(1)}, f32[2,64,512]{2,1,0:T(8,128)S(1)}, u32[]{:S(2)}, u32[]{:S(2)}) collective-permute-start(f32[2,64,512]{2,1,0:T(8,128)S(1)} %get-tuple-element.61), channel_id=1, source_target_pairs={{0,1},{1,0},{2,3},{3,2},{4,5},{5,4},{6,7},{7,6},{8,9},{9,8},{10,11... | collective-permute-start | bytes 786440 | tf_op jit(solution)/shard_map/ppermute | solution.py:308
  41.9 2.1 %collective-permute-start.11 = (f32[2,64,512]{2,1,0:T(8,128)S(1)}, f32[2,64,512]{2,1,0:T(8,128)S(1)}, u32[]{:S(2)}, u32[]{:S(2)}) collective-permute-start(f32[2,64,512]{2,1,0:T(8,128)S(1)} %get-tuple-element.58.refs_1_), channel_id=1, source_target_pairs={{1,2},{2,1},{3,4},{4,3},{5,6},{6,5},{7,8},{8,7},{9,10},{10,9},{11,... | collective-permute-start | bytes 786440 | tf_op jit(solution)/shard_map/ppermute | solution.py:309
  42.6 1.6 %collective-permute-start.10 = (f32[2,64,512]{2,1,0:T(8,128)S(1)}, f32[2,64,512]{2,1,0:T(8,128)S(1)}, u32[]{:S(2)}, u32[]{:S(2)}) collective-permute-start(f32[2,64,512]{2,1,0:T(8,128)S(1)} %get-tuple-element.57.refs_2_), channel_id=1, source_target_pairs={{1,2},{2,1},{3,4},{4,3},{5,6},{6,5},{7,8},{8,7},{9,10},{10,9},{11,... | collective-permute-start | bytes 786440 | tf_op jit(solution)/shard_map/ppermute | solution.py:309
  45.0 22.6 %collective-permute-start.17 = (f32[2,64,512]{2,1,0:T(8,128)S(1)}, f32[2,64,512]{2,1,0:T(8,128)S(1)}, u32[]{:S(2)}, u32[]{:S(2)}) collective-permute-start(f32[2,64,512]{2,1,0:T(8,128)S(1)} %get-tuple-element.68), channel_id=1, source_target_pairs={{0,1},{1,0},{2,3},{3,2},{4,5},{5,4},{6,7},{7,6},{8,9},{9,8},{10,11... | collective-permute-start | bytes 786440 | tf_op jit(solution)/shard_map/ppermute | solution.py:308
  59.0 5.1 %collective-permute-start.15 = (f32[1,64,512]{2,1,0:T(8,128)S(1)}, f32[1,64,512]{2,1,0:T(8,128)S(1)}, u32[]{:S(2)}, u32[]{:S(2)}) collective-permute-start(f32[1,64,512]{2,1,0:T(8,128)S(1)} %get-tuple-element.66), channel_id=1, source_target_pairs={{1,2},{2,1},{3,4},{4,3},{5,6},{6,5},{7,8},{8,7},{9,10},{10,9},{11,... | collective-permute-start | bytes 393224 | tf_op jit(solution)/shard_map/ppermute | solution.py:309
  59.7 7.9 %collective-permute-start.18 = (f32[2,64,256]{2,1,0:T(8,128)S(1)}, f32[2,64,256]{2,1,0:T(8,128)S(1)}, u32[]{:S(2)}, u32[]{:S(2)}) collective-permute-start(f32[2,64,256]{2,1,0:T(8,128)S(1)} %get-tuple-element.70), channel_id=1, source_target_pairs={{0,1},{1,0},{2,3},{3,2},{4,5},{5,4},{6,7},{7,6},{8,9},{9,8},{10,11... | collective-permute-start | bytes 393224 | tf_op jit(solution)/shard_map/ppermute | solution.py:308
  63.5 19.7 %collective-permute-start.14 = (f32[1,64,512]{2,1,0:T(8,128)S(1)}, f32[1,64,512]{2,1,0:T(8,128)S(1)}, u32[]{:S(2)}, u32[]{:S(2)}) collective-permute-start(f32[1,64,512]{2,1,0:T(8,128)S(1)} %get-tuple-element.65), channel_id=1, source_target_pairs={{1,2},{2,1},{3,4},{4,3},{5,6},{6,5},{7,8},{8,7},{9,10},{10,9},{11,... | collective-permute-start | bytes 393224 | tf_op jit(solution)/shard_map/ppermute | solution.py:309
  64.2 19.0 %collective-permute-start.16 = (f32[64,512]{1,0:T(8,128)S(1)}, f32[64,512]{1,0:T(8,128)S(1)}, u32[]{:S(2)}, u32[]{:S(2)}) collective-permute-start(f32[64,512]{1,0:T(8,128)S(1)} %last_outer.1), channel_id=1, source_target_pairs={{0,1},{1,0},{2,3},{3,2},{4,5},{5,4},{6,7},{7,6},{8,9},{9,8},{10,11... | collective-permute-start | bytes 393224 | tf_op jit(solution)/shard_map/ppermute | solution.py:308
  68.6 14.6 %collective-permute-start.19 = (f32[64,512]{1,0:T(8,128)S(1)}, f32[64,512]{1,0:T(8,128)S(1)}, u32[]{:S(2)}, u32[]{:S(2)}) collective-permute-start(f32[64,512]{1,0:T(8,128)S(1)} %get-tuple-element.72), channel_id=1, source_target_pairs={{0,1},{1,0},{2,3},{3,2},{4,5},{5,4},{6,7},{7,6},{8,9},{9,8},{10,11... | collective-permute-start | bytes 393224 | tf_op jit(solution)/shard_map/ppermute | solution.py:308
  68.7 1.3 %collective-permute-start.20 = (f32[8,128]{1,0:T(8,128)S(1)}, f32[8,128]{1,0:T(8,128)S(1)}, u32[]{:S(2)}, u32[]{:S(2)}) collective-permute-start(f32[8,128]{1,0:T(8,128)S(1)} %get-tuple-element.74), channel_id=1, source_target_pairs={{0,1},{1,0},{2,3},{3,2},{4,5},{5,4},{6,7},{7,6},{8,9},{9,8},{10,11... | collective-permute-start | bytes 12296 | tf_op jit(solution)/shard_map/ppermute | solution.py:444
  70.0 3.7 %collective-permute-start.21 = (f32[8,128]{1,0:T(8,128)S(1)}, f32[8,128]{1,0:T(8,128)S(1)}, u32[]{:S(2)}, u32[]{:S(2)}) collective-permute-start(f32[8,128]{1,0:T(8,128)S(1)} %add.17), channel_id=1, source_target_pairs={{0,4},{1,5},{2,6},{3,7},{4,0},{5,1},{6,2},{7,3},{8,12},{9,13},{10,... | collective-permute-start | bytes 12296 | tf_op jit(solution)/shard_map/ppermute | solution.py:444
  73.7 4.6 %collective-permute-start.22 = (f32[8,128]{1,0:T(8,128)S(1)}, f32[8,128]{1,0:T(8,128)S(1)}, u32[]{:S(2)}, u32[]{:S(2)}) collective-permute-start(f32[8,128]{1,0:T(8,128)S(1)} %add.18), channel_id=1, source_target_pairs={{0,8},{1,9},{2,10},{3,11},{4,12},{5,13},{6,14},{7,15},{8,0},{9,1},... | collective-permute-start | bytes 12296 | tf_op jit(solution)/shard_map/ppermute | solution.py:444
  78.3 3.6 %collective-permute-start.23 = (f32[8,128]{1,0:T(8,128)S(1)}, f32[8,128]{1,0:T(8,128)S(1)}, u32[]{:S(2)}, u32[]{:S(2)}) collective-permute-start(f32[8,128]{1,0:T(8,128)S(1)} %add.19), channel_id=1, source_target_pairs={{0,2},{1,3},{2,0},{3,1},{4,6},{5,7},{6,4},{7,5},{8,10},{9,11},{10,... | collective-permute-start | bytes 12296 | tf_op jit(solution)/shard_map/ppermute | solution.py:444

commit v3 on v2

v3 whole, which is shorter than its diff:
```python
import functools
import math

import jax
import jax.numpy as jnp
from jax import lax
from jax.experimental import pallas as pl
from jax.experimental.pallas import tpu as pltpu
from jax.sharding import PartitionSpec as P

time_step = 0.6
variance_gain = 0.5
penalty = 0.1
weight_denominator = 16.0

VMEM_LIMIT = 24 * 1024 * 1024
AXES = ("space", "node")
LONG = 40


def roll(value, steps, axis):
    return pltpu.roll(value, steps % value.shape[axis], axis)


def in_plane(value, a, cy, cz, k):
    return a[1] * (cy[0, k] * roll(value, 1, 0) + cy[1, k] * roll(value, -1, 0)) + a[2] * (
        cz[0, k] * roll(value, 1, 1) + cz[1, k] * roll(value, -1, 1)
    )


def in_plane_back(value, a, cy, cz, k):
    return a[1] * (roll(cy[0, k] * value, -1, 0) + roll(cy[1, k] * value, 1, 0)) + a[2] * (
        roll(cz[0, k] * value, -1, 1) + roll(cz[1, k] * value, 1, 1)
    )


def rows_of(scal, j):
    return [scal[j, k] for k in range(6)]


def node_scales(own_index, far_index, own_weight, far_weight, step_index, scal):
    lane = lax.broadcasted_iota(jnp.int32, (8, 128), 1)
    row = lax.broadcasted_iota(jnp.int32, (8, 128), 0)
    raw = jnp.zeros((8, 128), jnp.int32)
    for j, (index, weight) in enumerate(((own_index, own_weight), (far_index, far_weight))):
        for k, number in enumerate([index[0, k] for k in range(8)] + [weight[0], step_index[0]]):
            raw = jnp.where((lane == k) & (row == j), number, raw)
    raw = raw.astype(jnp.float32)
    points = -jnp.cos(math.pi * raw / 8.0)
    phase = 1.0 + 0.5 * jnp.sin(2.0 * math.pi * raw / 64.0)
    factor = 1.0 + 0.3 * points
    third = factor * (1.0 + 0.2 * roll(points, -5, 1))
    kappa = jnp.exp(0.5 * (points + 0.5 * roll(points, -2, 1)))
    source = (factor + 0.2 * roll(points, -2, 1)) * roll(phase, -5, 1)
    weight = roll(raw, -3, 1) / weight_denominator
    for j in range(2):
        for k, value in enumerate((factor, factor, third, kappa, source, weight)):
            scal[j, k] = jnp.sum(jnp.where((lane == k) & (row == j), value, 0.0))


def prepare(core, own_index, far_index, own_weight, far_weight, step_index, speed, mask, decay, control, goal, adjoint, scal, cx, cy, cz, dg, edge, ctl, goals, adj, adj_out_o, adj_out_i):
    me = core[0]
    node_scales(own_index, far_index, own_weight, far_weight, step_index, scal)
    rows, columns = speed.shape[2:]
    blocks = mask.shape[3]
    spread = (
        lax.broadcasted_iota(jnp.int32, (blocks, columns), 1) // (columns // blocks)
        == lax.broadcasted_iota(jnp.int32, (blocks, columns), 0)
    ).astype(jnp.bfloat16)
    row = lax.broadcasted_iota(jnp.int32, (rows, columns), 0)
    column = lax.broadcasted_iota(jnp.int32, (rows, columns), 1)
    flip = (me == 1).astype(jnp.float32)
    for k, at in enumerate((3 * me, 1 + me, 2 - me)):
        s, up = [], []
        for d in range(3):
            bits = mask[d, at].astype(jnp.float32).astype(jnp.bfloat16)
            up.append(jnp.dot(bits, spread, preferred_element_type=jnp.float32))
            s.append(speed[d, at].astype(jnp.float32))
        toward_outer = up[0] + flip - 2.0 * flip * up[0]
        outer = s[0] * toward_outer
        cx[0, k] = outer
        cx[1, k] = s[0] - outer
        if k == 0:
            edge[...] = outer
        lower = s[1] * up[1]
        cy[0, k] = jnp.where(row == 0, 0.0, lower)
        cy[1, k] = jnp.where(row == rows - 1, 0.0, s[1] - lower)
        lower = s[2] * up[2]
        cz[0, k] = jnp.where(column == 0, 0.0, lower)
        cz[1, k] = jnp.where(column == columns - 1, 0.0, s[2] - lower)
        rate = decay[at].astype(jnp.float32)
        for j in range(2):
            a = rows_of(scal, j)
            dg[j, k] = a[0] * s[0] + a[1] * s[1] + a[2] * s[2] + a[3] * rate
        ctl[k] = control[at]
        if k < 2:
            goals[k] = goal[at].astype(jnp.float32)
            adj[k] = adjoint[0, at].astype(jnp.float32)
    adj_out_o[...] = adjoint[0, 3 - 3 * me].astype(jnp.float32)
    adj_out_i[...] = adjoint[0, 2 - me].astype(jnp.float32)


def first_stage(core, scal, own, far, cx, cy, cz, dg, ctl, base, base_q, s1_in, s1_next):
    me = core[0]
    for j, c in enumerate((own, far)):
        a = rows_of(scal, j)
        c_o, c_i, c_n, c_f = c[0, 3 * me], c[0, 1 + me], c[0, 2 - me], c[0, 3 - 3 * me]
        push = [a[4] * ctl[k] for k in range(3)]
        l_i = a[0] * (cx[0, 1] * c_o + cx[1, 1] * c_n) + in_plane(c_i, a, cy, cz, 1) - dg[j, 1] * c_i
        s1_i = c_i + time_step * (l_i + push[1])
        s1_in[j] = s1_i
        l_o = a[0] * (cx[1, 0] * c_i) + in_plane(c_o, a, cy, cz, 0) - dg[j, 0] * c_o
        base[j] = c_o + time_step * (l_o + push[0])
        base_q[j] = 0.75 * c_o + (0.25 * time_step) * (a[0] * (cx[1, 0] * s1_i) + push[0])
        l_n = a[0] * (cx[0, 2] * c_i + cx[1, 2] * c_f) + in_plane(c_n, a, cy, cz, 2) - dg[j, 2] * c_n
        s1_next[j] = c_n + time_step * (l_n + push[2])


def first_edge(j, scal, halo, base, base_q, cx, cy, cz, dg, msg):
    a = rows_of(scal, j)
    s1_o = base[j] + (time_step * a[0]) * (cx[0, 0] * halo[0])
    msg[0] = s1_o
    msg[1] = base_q[j] + 0.25 * (s1_o + time_step * (in_plane(s1_o, a, cy, cz, 0) - dg[j, 0] * s1_o))


def second_inner(core, scal, own, far, msg_own, msg_far, s1_in, s1_next, cx, cy, cz, dg, ctl, s2_own, s2_far):
    for j, (c, msg, out) in enumerate(((own, msg_own, s2_own), (far, msg_far, s2_far))):
        a = rows_of(scal, j)
        s1_i = s1_in[j]
        l_i = a[0] * (cx[0, 1] * msg[0] + cx[1, 1] * s1_next[j]) + in_plane(s1_i, a, cy, cz, 1) - dg[j, 1] * s1_i
        out[...] = 0.75 * c[0, 1 + core[0]] + 0.25 * (s1_i + time_step * (l_i + a[4] * ctl[1]))


def third_stage(core, scal, own, far, msg_own, msg_far, s2_own, s2_far, next_own, next_far, near_edge, cx, cy, cz, dg, ctl, base):
    me = core[0]
    parts = ((own, msg_own, s2_own, next_own), (far, msg_far, s2_far, next_far))
    for j, (c, msg, s2, s2_next) in enumerate(parts):
        a = rows_of(scal, j)
        q, s2_i = msg[1], s2[...]
        back = (0.25 * time_step * a[0]) * (near_edge[...] * msg[0])
        l_o = a[0] * (cx[0, 0] * back + cx[1, 0] * s2_i) + in_plane(q, a, cy, cz, 0) - dg[j, 0] * q
        l_i = a[0] * (cx[0, 1] * q + cx[1, 1] * s2_next[...]) + in_plane(s2_i, a, cy, cz, 1) - dg[j, 1] * s2_i
        base[j, 0] = c[0, 3 * me] / 3.0 + 2.0 / 3.0 * (q + time_step * (l_o + a[4] * ctl[0]))
        base[j, 1] = c[0, 1 + me] / 3.0 + 2.0 / 3.0 * (s2_i + time_step * (l_i + a[4] * ctl[1]))


def finals(j, scal, halo, base, cx, cy, cz, dg):
    a = rows_of(scal, j)
    step = (0.25 * time_step * a[0]) * (cx[0, 0] * halo[0])
    change = in_plane(step, a, cy, cz, 0) - dg[j, 0] * step + a[0] * (cx[0, 0] * halo[1])
    outer = base[j, 0] + 2.0 / 3.0 * (step + time_step * change)
    inner = base[j, 1] + (2.0 / 3.0 * time_step * a[0]) * (cx[0, 1] * step)
    return outer, inner


def third_edge(scal, halo, base, cx, cy, cz, dg, final):
    final[0], final[1] = finals(0, scal, halo, base, cx, cy, cz, dg)


def back_edge(j, final, first, after, scal, cx, cy, cz, dg, goals, term, msg, partial):
    a = rows_of(scal, j)
    u = []
    for k in range(2):
        t = after[k] + goals[k] * a[5] * (1.0 + 2.0 * variance_gain * (final[k] - first[k]))
        term[k] = t
        u.append(2.0 / 3.0 * t)
    msg[0] = a[0] * (cx[0, 0] * u[0])
    spread = a[0] * (cx[0, 1] * u[1]) + in_plane_back(u[0], a, cy, cz, 0) - dg[j, 0] * u[0]
    value = u[0] + time_step * spread
    partial[...] = value
    msg[1] = a[0] * (cx[0, 0] * value)


def turn_far(scal, halo, base, final_own, cx, cy, cz, dg, goals, after_o, after_i, final, term, msg, partial):
    final[0], final[1] = finals(1, scal, halo, base, cx, cy, cz, dg)
    first = [scal[0, 5] * final_own[k] + scal[1, 5] * final[k] for k in range(2)]
    after = (after_o[...], after_i[...])
    back_edge(1, final, first, after, scal, cx, cy, cz, dg, goals, term, msg, partial)


def turn_own(scal, final_own, final_far, cx, cy, cz, dg, goals, after, term, msg, partial):
    first = [scal[0, 5] * final_own[k] + scal[1, 5] * final_far[k] for k in range(2)]
    back_edge(0, final_own, first, after, scal, cx, cy, cz, dg, goals, term, msg, partial)


def put(refs, values):
    start, whole = 0, jnp.concatenate(values, 0)
    for ref in refs:
        ref[...] = whole[start : start + ref.shape[0]]
        start += ref.shape[0]


def get(refs, count):
    whole = jnp.concatenate([ref[...] for ref in refs], 0)
    rows = whole.shape[0] // count
    return [whole[rows * k : rows * k + rows] for k in range(count)]


def cut(rows, pieces):
    tiles = rows // 8
    return [8 * (tiles // pieces + (k < tiles % pieces)) for k in range(pieces)]


def turn_inner(scal, final_own, final_far, term_own, term_far, cx, cy, cz, dg, goals, cost, part, *pins):
    total = 0.0
    for k in range(2):
        own, far = scal[0, 5] * final_own[k], scal[1, 5] * final_far[k]
        first = own + far
        second = own * final_own[k] + far * final_far[k]
        total = total + goals[k] * (first + variance_gain * (second - first * first))
    rows, columns = total.shape
    total = sum(total[8 * r : 8 * r + 8] for r in range(rows // 8))
    cost[...] = sum(total[:, 128 * k : 128 * k + 128] for k in range(columns // 128))
    products = []
    for j, term in enumerate((term_own, term_far)):
        a = rows_of(scal, j)
        u = [2.0 / 3.0 * term[k] for k in range(2)]
        spread = a[0] * (cx[1, 0] * u[0]) + in_plane_back(u[1], a, cy, cz, 1) - dg[j, 1] * u[1]
        value = u[1] + time_step * spread
        part[j] = value
        products += [a[0] * (cx[1, 1] * u[1]), a[0] * (cx[1, 1] * value)]
    put(pins, products)


def back_second(scal, msg_own, msg_far, partial_own, partial_far, part, near_edge, cx, cy, cz, dg, *rest):
    (cost, cost_far), (base, a2, total) = rest[:2], rest[-3:]
    count = (len(rest) - 5) // 2
    mine, theirs = get(rest[2 : 2 + count], 4), get(rest[2 + count : -3], 4)
    total[...] = cost[...] + cost_far[...]
    for j, (msg, partial) in enumerate(((msg_own, partial_own), (msg_far, partial_far))):
        a = rows_of(scal, j)
        pin, pin2 = theirs[2 - 2 * j], theirs[3 - 2 * j]
        pin2 = 0.25 * (pin2 + (time_step * a[0]) * (cx[0, 2] * mine[2 * j]))
        a2_i = part[j] + time_step * pin
        a2[j] = a2_i
        u_o, u_i = 0.25 * partial[...], 0.25 * a2_i
        back = (0.25 * time_step * a[0]) * (near_edge[...] * msg[0])
        spread = a[0] * (cx[0, 1] * u_i) + in_plane_back(u_o, a, cy, cz, 0) - dg[j, 0] * u_o + back
        base[j, 0] = u_o + time_step * spread
        spread = a[0] * (cx[1, 0] * u_o) + in_plane_back(u_i, a, cy, cz, 1) - dg[j, 1] * u_i + pin2
        base[j, 1] = u_i + time_step * spread


def second_back_edge(j, scal, halo, base, cx, cy, cz, dg, a1_o, msg):
    a = rows_of(scal, j)
    step = (0.25 * time_step) * halo[0]
    value = base[j, 0] + step + time_step * (in_plane_back(step, a, cy, cz, 0) - dg[j, 0] * step + 0.25 * halo[1])
    a1_o[...] = value
    msg[...] = a[0] * (cx[0, 0] * value)


def close(core, scal, term_own, term_far, partial_own, partial_far, halo_own, halo_far, a1_own, a1_far, a2, base, cx, cy, cz, dg, ctl, keep, part, *out):
    give, send = out[0], out[1:]
    sources = [0.0, 0.0]
    parts = ((term_own, partial_own, halo_own, a1_own), (term_far, partial_far, halo_far, a1_far))
    for j, (term, partial, halo, a1) in enumerate(parts):
        a = rows_of(scal, j)
        x = [a1[...], base[j, 1] + (0.25 * time_step * time_step * a[0]) * (cx[1, 0] * halo[0])]
        a2_o = partial[...] + time_step * halo[0]
        for k, second in enumerate((a2_o, a2[j])):
            sources[k] = sources[k] + a[4] * (2.0 / 3.0 * term[k] + 0.25 * second + x[k])
        spread = a[0] * (cx[0, 1] * x[1]) + in_plane_back(x[0], a, cy, cz, 0) - dg[j, 0] * x[0]
        outer = term[0] / 3.0 + 0.75 * a2_o + (x[0] + time_step * spread)
        spread = a[0] * (cx[1, 0] * x[0]) + in_plane_back(x[1], a, cy, cz, 1) - dg[j, 1] * x[1]
        inner = term[1] / 3.0 + 0.75 * a2[j] + (x[1] + time_step * spread)
        pin = a[0] * (cx[1, 1] * x[1])
        if j == 0:
            part[0], part[1], part[2] = outer, inner, pin
        else:
            put(send, [outer, inner, pin])
    half = ctl.shape[2] // 2
    zero = core[0] == 0
    for k in range(2):
        gradient = time_step * sources[k] + penalty * ctl[k]
        low, high = gradient[:, :half], gradient[:, half:]
        keep[k] = jnp.where(zero, low, high)
        give[k] = jnp.where(zero, high, low)


def place_gradient(core, keep, taken, gradient):
    me = core[0]
    gradient[3 * me] = keep[0]
    gradient[1 + me] = keep[1]
    gradient[3 - 3 * me] = taken[0]
    gradient[2 - me] = taken[1]


def last_edge(halo, halo_far, part, outer, add):
    outer[...] = part[0] + time_step * halo[...]
    add[...] = time_step * halo_far[...]


def assemble(cells, core, part, outer, add, cost, *rest):
    taken, (out, objective) = get(rest[:-2], 3), rest[-2:]
    me = core[0]
    out[0, 3 * me] = outer[...]
    out[0, 1 + me] = part[1] + time_step * taken[2]
    out[0, 3 - 3 * me] = taken[0] + add[...]
    out[0, 2 - me] = taken[1] + time_step * part[2]
    objective[0] = jnp.sum(cost[...]) / cells


def on_core(body, outs, scalars, arrays, hbm_out=(), smem_out=(), after=(), cost=0, name=None):
    hbm_out = tuple(hbm_out) + tuple(smem_out)
    out_shape = [
        jax.ShapeDtypeStruct(s, jnp.float32) if i in hbm_out else pltpu.VMEM(s, jnp.float32)
        for i, s in enumerate(outs)
    ]
    held = [pltpu.with_memory_space_constraint(x, pltpu.SMEM) for x in scalars]
    held += [pltpu.with_memory_space_constraint(x, pltpu.VMEM) for x in arrays]
    count, waits = len(held), len(after)

    def run(*refs):
        body(*refs[:count], *refs[count + waits :])

    return pl.pallas_call(
        run,
        out_shape=out_shape,
        in_specs=[pl.BlockSpec(memory_space=pltpu.SMEM)] * len(scalars)
        + [pl.BlockSpec(memory_space=pltpu.VMEM)] * len(arrays)
        + [pl.BlockSpec(memory_space=pl.ANY)] * waits,
        out_specs=[
            pl.BlockSpec(memory_space=pltpu.SMEM if i in smem_out else pltpu.VMEM) for i in range(len(outs))
        ],
        compiler_params=pltpu.CompilerParams(vmem_limit_bytes=VMEM_LIMIT),
        cost_estimate=pl.CostEstimate(flops=cost * 1_000_000_000, bytes_accessed=cost * 3_000_000, transcendentals=0) if cost else None,
        name=name or body.__name__,
    )(*held, *after)


def shards(
    concentration,
    adjoint_next,
    speed,
    direction_mask,
    decay_rate,
    control,
    goal_weight,
    node_index,
    weight_num,
    step_index,
):
    sections = lax.axis_size("space")
    ranks = sections * lax.axis_size("node")
    within = [(i, i ^ 1) for i in range(ranks)]
    across = [p for i in range(1, ranks - 1, 2) for p in ((i, i + 1), (i + 1, i))]
    along = [p for i in range(0, ranks - 2, 2) for p in ((i + 1, i + 3), (i + 2, i))]

    def swap(x, what):
        with jax.named_scope("swap_" + what):
            return lax.ppermute(x, AXES, within)

    def pass_on(x, what, pairs=across):
        with jax.named_scope("pass_" + what):
            return lax.ppermute(x, AXES, pairs)

    _, layers, rows, columns = concentration.shape
    me = lax.axis_index("node").astype(jnp.int32)
    core = jnp.reshape(me, (1,))
    far_index, far_weight = swap(node_index, "node_index"), swap(weight_num, "weight_num")

    far = swap(concentration, "state")
    take = lambda x: lax.dynamic_slice_in_dim(x, 3 * me, 1, axis=1)[0]
    far_halo = pass_on(take(concentration), "state_own")
    own_halo = pass_on(take(far), "state_far")

    plane = (rows, columns)
    pair, three = (2,) + plane, (3,) + plane
    four, six = (2,) + pair, (2,) + three
    sides = (2, rows, columns // 2)
    shapes = [six, six, six, six, plane, three, pair, pair, plane, plane]
    far_off = [
        pltpu.with_memory_space_constraint(x, pltpu.HBM)
        for x in (speed, direction_mask, decay_rate, control, goal_weight, adjoint_next)
    ]
    scal, cx, cy, cz, dg, edge, ctl, goals, adj, adj_out_o, adj_out_i = pl.pallas_call(
        prepare,
        out_shape=[pltpu.SMEM((2, 8), jnp.float32)] + [pltpu.VMEM(s, jnp.float32) for s in shapes],
        in_specs=[pl.BlockSpec(memory_space=pltpu.SMEM)] * 6 + [pl.BlockSpec(memory_space=pltpu.VMEM)] * 6,
        out_specs=[pl.BlockSpec(memory_space=pltpu.SMEM)] + [pl.BlockSpec(memory_space=pltpu.VMEM)] * len(shapes),
        compiler_params=pltpu.CompilerParams(vmem_limit_bytes=VMEM_LIMIT),
        name="prepare",
    )(core, node_index, far_index, weight_num, far_weight, step_index, *far_off)
    near_edge = pass_on(edge, "edge")
    after_o, after_i = swap(adj_out_o, "after_o"), swap(adj_out_i, "after_i")

    fields = [cx, cy, cz, dg]
    both = [core, scal]
    states = [concentration, far]
    base, base_q, s1_in, s1_next = on_core(first_stage, [pair] * 4, both, states + fields + [ctl])
    edge_of = lambda j, halo, after=(): on_core(
        functools.partial(first_edge, j), [pair], [scal], [halo, base, base_q] + fields, after=after, cost=LONG, name="first_edge"
    )[0]
    msg_far = edge_of(1, far_halo)
    halo2_own = pass_on(msg_far, "stage2_far")
    msg_own = edge_of(0, own_halo)
    halo2_far = pass_on(msg_own, "stage2_own")

    msgs = [msg_own, msg_far]
    s2 = list(on_core(second_inner, [plane] * 2, both, states + msgs + [s1_in, s1_next] + fields + [ctl], after=[near_edge, after_o, after_i]))
    s2_next = [swap(s2[1], "s2_far"), swap(s2[0], "s2_own")]
    (base,) = on_core(third_stage, [four], both, states + msgs + s2 + s2_next + [near_edge] + fields + [ctl])
    (final_own,) = on_core(third_edge, [pair], [scal], [halo2_own, base] + fields)
    final_far, term_far, msg3_far, partial_far = on_core(
        turn_far, [pair, pair, pair, plane], [scal], [halo2_far, base, final_own] + fields + [goals, after_o, after_i]
    )
    halo3_own = pass_on(msg3_far, "back2_far")
    term_own, msg3_own, partial_own = on_core(
        turn_own, [pair, pair, plane], [scal], [final_own, final_far] + fields + [goals, adj]
    )
    halo3_far = pass_on(msg3_own, "back2_own")
    terms, partials = [term_own, term_far], [partial_own, partial_far]
    cost, part, *pins = on_core(
        turn_inner, [(8, 128), pair] + [(r, columns) for r in cut(4 * rows, 3)], [scal], [final_own, final_far] + terms + fields + [goals]
    )
    theirs = [swap(x, "pin") for x in pins]
    base, a2, cost = on_core(
        back_second,
        [four, pair, (8, 128)],
        [scal],
        [msg3_own, msg3_far] + partials + [part, near_edge] + fields + [cost, swap(cost, "goal_sum")] + pins + theirs,
    )
    sums = [cost]
    if sections & (sections - 1):
        sums.append(lax.psum(cost, "space"))
    else:
        steps = [1 << k for k in range(sections.bit_length() - 1)]
        for step in steps[1:] + steps[:1]:
            with jax.named_scope("goal_sum"):
                sums.append(sums[-1] + lax.ppermute(sums[-1], "space", [(i, i ^ step) for i in range(sections)]))
    sum_at = lambda k: sums[min(k, len(sums) - 1)]

    edge_of = lambda j, halo, last: on_core(
        functools.partial(second_back_edge, j),
        [plane, plane],
        [scal],
        [halo, base] + fields,
        after=[last],
        cost=LONG,
        name="second_back_edge",
    )
    a1_own, msg4_own = edge_of(0, halo3_own, sum_at(1))
    halo4_far = pass_on(msg4_own, "back1_own", along)
    a1_far, msg4_far = edge_of(1, halo3_far, a1_own)
    halo4_own = pass_on(msg4_far, "back1_far")
    keep, part, *out = on_core(
        close,
        [sides, three, sides] + [(r, columns) for r in cut(3 * rows, 2)],
        both,
        terms + partials + [halo3_own, halo3_far, a1_own, a1_far, a2, base] + fields + [ctl],
        after=[sum_at(2)],
        cost=LONG,
    )
    parts = [swap(x, "adjoint") for x in out[1:]]
    taken = swap(out[0], "gradient")
    (gradient,) = on_core(
        place_gradient, [(layers, rows, columns // 2)], [core], [keep, taken], hbm_out=(0,)
    )
    outer, add = on_core(last_edge, [plane] * 2, [], [halo4_own, halo4_far, part], after=[sums[-1]], cost=LONG)
    adjoint, objective = on_core(
        functools.partial(assemble, sections * layers * rows * columns),
        [(1, layers, rows, columns), (1,)],
        [core],
        [part, outer, add, sums[-1]] + parts,
        hbm_out=(0,),
        smem_out=(1,),
        name="assemble",
    )
    return (adjoint, gradient, objective)


def solution(mesh):
    return jax.shard_map(
        shards,
        mesh=mesh,
        in_specs=(
            P("node", ("groups", "space"), None, None),
            P("node", ("groups", "space"), None, None),
            P(None, ("groups", "space"), None, None),
            P(None, ("groups", "space"), None, None),
            P(("groups", "space"), None, None),
            P(("groups", "space"), None, None),
            P(("groups", "space"), None, None),
            P("node", None),
            P("node"),
            P("groups"),
        ),
        out_specs=(
            P("node", ("groups", "space"), None, None),
            P(("groups", "space"), None, "node"),
            P("groups"),
        ),
        check_vma=False,
    )
```

time: 85.6 us -> 72.5 us (0.85)
  starting transfers between devices: 62.2 us -> 48.6 us
  between operations: 4.04 us -> 2.22 us
  Pallas kernels: 9.06 us -> 10.6 us
    ppermute x24 -> x26, starting transfers between devices: 62.2 us -> 48.6 us  [the longest x14 36.4 us: swap(): return lax.ppermute(x, AXES, within)]
    pallas_call x1, Pallas kernels: 1.87 us -> 2.97 us  [shards(): pl.pallas_call(prepare, out_shape=[pltpu.SMEM((2, 8), jnp.float32)] + [pl...]
    squeeze x2, local copies, waits for them, and re-layouts: 0.03 us -> 0.94 us  [shards(): take = lambda x: lax.dynamic_slice_in_dim(x, 3 * me, 1, axis=1)[0]]
    ppermute x24 -> x26, waiting for transfers between devices: 8.57 us -> 8.91 us  [the longest x3 5.61 us: shards(): lax.ppermute(sums[-1], 'space', [(i, i ^ step) for i in range(sections)])]
  transfers between devices with their start and end apart: 24 -> 26, of which waited for: 6 -> 7; matrix products, arithmetic and copies ran while one was open for 1% -> 1% of each run, Pallas kernels for 6% -> 13%
where the time goes in v3:
time: 72.5 us; the launch traced here: 71.3 us
  starting transfers between devices  48.6 us (67%)
  Pallas kernels  10.6 us (15%)
  waiting for transfers between devices  8.91 us (12%)
  between operations  2.22 us (3%)
  local copies, waits for them, and re-layouts  0.95 us (1%)
    ppermute x14, starting transfers between devices, swap(): return lax.ppermute(x, AXES, within)  36.4 us
    pallas_call x16, Pallas kernels, on_core(): pl.pallas_call(run, out_shape=out_shape, in_specs=[pl.BlockSpec(memory_sp...  7.63 us
    ppermute x9, starting transfers between devices, pass_on(): return lax.ppermute(x, AXES, pairs)  6.67 us
    ppermute x3, waiting for transfers between devices, shards(): lax.ppermute(sums[-1], 'space', [(i, i ^ step) for i in range(sections)])  5.61 us
    ppermute x3, starting transfers between devices, shards(): lax.ppermute(sums[-1], 'space', [(i, i ^ step) for i in range(sections)])  5.5 us
    pallas_call x1, Pallas kernels, shards(): pl.pallas_call(prepare, out_shape=[pltpu.SMEM((2, 8), jnp.float32)] + [pl...  2.97 us
    ppermute x14, waiting for transfers between devices, swap(): return lax.ppermute(x, AXES, within)  2.39 us
  transfers between devices with their start and end apart: 26, of which 7 were waited for; matrix products, arithmetic and copies ran while one was open for 1% of the time, Pallas kernels for 13%

profile of v3, /device:TPU:0, one launch (start us, length us, event | category | flops | bytes accessed | tf_op | source)
XLA Modules:
  0.0 71.3 jit_solution(12357560001579928933)
XLA Ops:
  1.1 0.9 %dynamic-slice_bitcast_fusion.1 = f32[1,64,512]{2,1,0:T(8,128)S(1)} fusion(f32[1,4,64,512]{3,2,1,0:T(8,128)} %refs_2_.5, s32[]{:T(128)S(6)} %select_n.4), kind=kLoop, calls=%fused_computation.1 | loop fusion | bytes 262148 | tf_op jit(solution)/shard_map/squeeze | solution.py:363
  2.1 0.7 collective-permute-start.2
  2.8 3.9 %collective-permute-start = (s32[1,8]{1,0:T(1,128)S(1)}, s32[1,8]{1,0:T(1,128)S(1)}, u32[]{:S(2)}, u32[]{:S(2)}) collective-permute-start(s32[1,8]{1,0:T(1,128)S(1)} %copy-done.1), channel_id=1, source_target_pairs={{0,1},{1,0},{2,3},{3,2},{4,5},{5,4},{6,7},{7,6},{8,9},{9,8},{10,11... | collective-permute-start | bytes 104 | tf_op jit(solution)/shard_map/swap_node_index/ppermute | solution.py:351
  8.1 3.0 %prepare.1 = (f32[2,8]{1,0:T(2,128)S(4)}, f32[2,3,64,512]{3,2,1,0:T(8,128)S(1)}, f32[2,3,64,512]{3,2,1,0:T(8,128)S(1)}, f32[2,3,64,512]{3,2,1,0:T(8,128)S(1)}, f...) custom-call(s32[1]{0:T(128)} %bitcast.core.refs_0_, ...), custom_call_target="tpu_custom_call" | custom-call | tf_op jit(solution)/shard_map/prepare/pallas_call | solution.py:376
  11.1 0.7 collective-permute-start.6
  11.8 3.0 %collective-permute-start.7 = (f32[64,512]{1,0:T(8,128)S(1)}, f32[64,512]{1,0:T(8,128)S(1)}, u32[]{:S(2)}, u32[]{:S(2)}) collective-permute-start(f32[64,512]{1,0:T(8,128)S(1)} %get-tuple-element.59), channel_id=1, source_target_pairs={{0,1},{1,0},{2,3},{3,2},{4,5},{5,4},{6,7},{7,6},{8,9},{9,8},{10,11... | collective-permute-start | bytes 393224 | tf_op jit(solution)/shard_map/swap_after_o/ppermute | solution.py:351
  14.8 0.7 collective-permute-start.5
  15.5 1.0 %first_stage.1 = (f32[2,64,512]{2,1,0:T(8,128)S(1)}, f32[2,64,512]{2,1,0:T(8,128)S(1)}, f32[2,64,512]{2,1,0:T(8,128)S(1)}, f32[2,64,512]{2,1,0:T(8,128)S(1)}) custom-call(s32[1]{0:T(128)} %bitcast.core.refs_0_, f32[2,8]{1,0:T(2,128)S(4)} %get-tuple-element.48.refs_1_.refs_0_, f32[1,4,64,512]{3,2,1,0:T(8,128)S(1)} %copy-done, ...), custom_call_target="tpu_custom_call" | custom-call | tf_op jit(solution)/shard_map/first_stage/pallas_call | solution.py:316
  16.7 0.7 collective-permute-start.4
  17.6 0.7 collective-permute-start.11
  18.8 7.4 %collective-permute-start.10 = (f32[64,512]{1,0:T(8,128)S(1)}, f32[64,512]{1,0:T(8,128)S(1)}, u32[]{:S(2)}, u32[]{:S(2)}) collective-permute-start(f32[64,512]{1,0:T(8,128)S(1)} %get-tuple-element.61.refs_6_), channel_id=1, source_target_pairs={{0,1},{1,0},{2,3},{3,2},{4,5},{5,4},{6,7},{7,6},{8,9},{9,8},{10,11... | collective-permute-start | bytes 393224 | tf_op jit(solution)/shard_map/swap_s2_own/ppermute | solution.py:351
  26.3 0.9 %collective-permute-done.10.refs_9_ = f32[64,512]{1,0:T(8,128)S(1)} collective-permute-done((f32[64,512]{1,0:T(8,128)S(1)}, f32[64,512]{1,0:T(8,128)S(1)}, u32[]{:S(2)}, u32[]{:S(2)}) %collective-permute-start.10) | collective-permute-done | bytes 131104 | tf_op jit(solution)/shard_map/swap_s2_own/ppermute | solution.py:351
  27.5 0.8 %third_stage.1.refs_2_ = f32[2,2,64,512]{3,2,1,0:T(8,128)S(1)} custom-call(s32[1]{0:T(128)} %bitcast.core.refs_0_, f32[2,8]{1,0:T(2,128)S(4)} %get-tuple-element.48.refs_1_.refs_0_, f32[1,4,64,512]{3,2,1,0:T(8,128)S(1)} %copy-done, f32[1,4,64,512]{3,2,1,0:T(8,128)S(1)} %collective-permute-done.3.refs_3_, f32[2,64,512]{2,1,0:T(8,128)S(1)} %first_edge.3.refs_4_, ...), custom_call_target="tpu_custom_call" | custom-call | tf_op jit(solution)/shard_map/third_stage/pallas_call | solution.py:316
  29.0 0.7 collective-permute-start.12
  29.9 0.5 turn_inner.1
  30.5 9.0 %collective-permute-start.15 = (f32[88,512]{1,0:T(8,128)S(1)}, f32[88,512]{1,0:T(8,128)S(1)}, u32[]{:S(2)}, u32[]{:S(2)}) collective-permute-start(f32[88,512]{1,0:T(8,128)S(1)} %get-tuple-element.74.refs_13_), channel_id=1, source_target_pairs={{0,1},{1,0},{2,3},{3,2},{4,5},{5,4},{6,7},{7,6},{8,9},{9,8},{10,11... | collective-permute-start | bytes 540680 | tf_op jit(solution)/shard_map/swap_pin/ppermute | solution.py:351
  40.1 1.1 %collective-permute-done.14.refs_12_ = f32[8,128]{1,0:T(8,128)S(1)} collective-permute-done((f32[8,128]{1,0:T(8,128)S(1)}, f32[8,128]{1,0:T(8,128)S(1)}, u32[]{:S(2)}, u32[]{:S(2)}) %collective-permute-start.14) | collective-permute-done | bytes 4128 | tf_op jit(solution)/shard_map/swap_goal_sum/ppermute | solution.py:351
  41.2 0.8 %back_second.1 = (f32[2,2,64,512]{3,2,1,0:T(8,128)S(1)}, f32[2,64,512]{2,1,0:T(8,128)S(1)}, f32[8,128]{1,0:T(8,128)S(1)}) custom-call(f32[2,8]{1,0:T(2,128)S(4)} %get-tuple-element.48.refs_1_.refs_0_, f32[2,64,512]{2,1,0:T(8,128)S(1)} %get-tuple-element.71.refs_1_, f32[2,64,512]{2,1,0:T(8,128)S(1)} %get-tuple-element.70.refs_2_, ...), custom_call_target="tpu_custom_call" | custom-call | tf_op jit(solution)/shard_map/back_second/pallas_call | solution.py:316
  42.0 1.6 %collective-permute-start.18 = (f32[8,128]{1,0:T(8,128)S(1)}, f32[8,128]{1,0:T(8,128)S(1)}, u32[]{:S(2)}, u32[]{:S(2)}) collective-permute-start(f32[8,128]{1,0:T(8,128)S(1)} %get-tuple-element.78), channel_id=1, source_target_pairs={{0,4},{2,6},{4,0},{6,2},{8,12},{10,14},{12,8},{14,10},{1,5},{3,7},... | collective-permute-start | bytes 12296 | tf_op jit(solution)/shard_map/goal_sum/ppermute | solution.py:430
  43.6 2.0 %collective-permute-done.18 = f32[8,128]{1,0:T(8,128)S(1)} collective-permute-done((f32[8,128]{1,0:T(8,128)S(1)}, f32[8,128]{1,0:T(8,128)S(1)}, u32[]{:S(2)}, u32[]{:S(2)}) %collective-permute-start.18) | collective-permute-done | bytes 4128 | tf_op jit(solution)/shard_map/goal_sum/ppermute | solution.py:430
  45.7 2.6 %collective-permute-start.19 = (f32[8,128]{1,0:T(8,128)S(1)}, f32[8,128]{1,0:T(8,128)S(1)}, u32[]{:S(2)}, u32[]{:S(2)}) collective-permute-start(f32[8,128]{1,0:T(8,128)S(1)} %add.14.refs_7_), channel_id=1, source_target_pairs={{0,8},{2,10},{4,12},{6,14},{8,0},{10,2},{12,4},{14,6},{1,9},{3,11}... | collective-permute-start | bytes 12296 | tf_op jit(solution)/shard_map/goal_sum/ppermute | solution.py:430
  48.2 1.9 %collective-permute-done.19 = f32[8,128]{1,0:T(8,128)S(1)} collective-permute-done((f32[8,128]{1,0:T(8,128)S(1)}, f32[8,128]{1,0:T(8,128)S(1)}, u32[]{:S(2)}, u32[]{:S(2)}) %collective-permute-start.19) | collective-permute-done | bytes 4128 | tf_op jit(solution)/shard_map/goal_sum/ppermute | solution.py:430
  50.2 1.3 %collective-permute-start.22 = (f32[8,128]{1,0:T(8,128)S(1)}, f32[8,128]{1,0:T(8,128)S(1)}, u32[]{:S(2)}, u32[]{:S(2)}) collective-permute-start(f32[8,128]{1,0:T(8,128)S(1)} %add.15.refs_17_), channel_id=1, source_target_pairs={{0,2},{2,0},{4,6},{6,4},{8,10},{10,8},{12,14},{14,12},{1,3},{3,1},... | collective-permute-start | bytes 12296 | tf_op jit(solution)/shard_map/goal_sum/ppermute | solution.py:430
  51.4 0.7 collective-permute-start.13
  52.1 1.7 %collective-permute-done.22 = f32[8,128]{1,0:T(8,128)S(1)} collective-permute-done((f32[8,128]{1,0:T(8,128)S(1)}, f32[8,128]{1,0:T(8,128)S(1)}, u32[]{:S(2)}, u32[]{:S(2)}) %collective-permute-start.22) | collective-permute-done | bytes 4128 | tf_op jit(solution)/shard_map/goal_sum/ppermute | solution.py:430
  54.2 0.7 collective-permute-start.20
  54.9 1.3 %collective-permute-start.21 = (f32[64,512]{1,0:T(8,128)S(1)}, f32[64,512]{1,0:T(8,128)S(1)}, u32[]{:S(2)}, u32[]{:S(2)}) collective-permute-start(f32[64,512]{1,0:T(8,128)S(1)} %get-tuple-element.84), channel_id=1, source_target_pairs={{1,3},{2,0},{3,5},{4,2},{5,7},{6,4},{7,9},{8,6},{9,11},{10,8},{11,... | collective-permute-start | bytes 393224 | tf_op jit(solution)/shard_map/pass_back1_own/ppermute | solution.py:355
  56.2 0.8 %close.1 = (f32[2,64,256]{2,1,0:T(8,128)S(1)}, f32[3,64,512]{2,1,0:T(8,128)S(1)}, f32[2,64,256]{2,1,0:T(8,128)S(1)}, f32[96,512]{1,0:T(8,128)S(1)}, f32[96,512]{1,0:T(8,128)S(1)}) custom-call(s32[1]{0:T(128)} %bitcast.core.refs_0_, f32[2,8]{1,0:T(2,128)S(4)} %get-tuple-element.48.refs_1_.refs_0_, f32[2,64,512]{2,1,0:T(8,128)S(1)} %get-tuple-element.66.refs_3_.refs_2_, ...), custom_call_target="tpu_custom_call" | custom-call | flops 40000000000 | bytes 120000000 | tf_op jit(solution)/shard_map/close/pallas_call | solution.py:316
  57.0 11.2 %collective-permute-start.25 = (f32[2,64,256]{2,1,0:T(8,128)S(1)}, f32[2,64,256]{2,1,0:T(8,128)S(1)}, u32[]{:S(2)}, u32[]{:S(2)}) collective-permute-start(f32[2,64,256]{2,1,0:T(8,128)S(1)} %get-tuple-element.91), channel_id=1, source_target_pairs={{0,1},{1,0},{2,3},{3,2},{4,5},{5,4},{6,7},{7,6},{8,9},{9,8},{10,11... | collective-permute-start | bytes 393224 | tf_op jit(solution)/shard_map/swap_gradient/ppermute | solution.py:351
  68.8 0.9 %collective-permute-done.21.refs_1_ = f32[64,512]{1,0:T(8,128)S(1)} collective-permute-done((f32[64,512]{1,0:T(8,128)S(1)}, f32[64,512]{1,0:T(8,128)S(1)}, u32[]{:S(2)}, u32[]{:S(2)}) %collective-permute-start.21) | collective-permute-done | bytes 131104 | tf_op jit(solution)/shard_map/pass_back1_own/ppermute | solution.py:355
  69.7 0.7 %place_gradient.1 = f32[4,64,256]{2,1,0:T(8,128)} custom-call(s32[1]{0:T(128)} %bitcast.core.refs_0_, f32[2,64,256]{2,1,0:T(8,128)S(1)} %get-tuple-element.90.refs_1_, f32[2,64,256]{2,1,0:T(8,128)S(1)} %collective-permute-done.25.refs_2_), custom_call_target="tpu_custom_call" | custom-call | tf_op jit(solution)/shard_map/place_gradient/pallas_call | solution.py:316
  70.4 0.9 %assemble.1 = (f32[1,4,64,512]{3,2,1,0:T(8,128)}, f32[1]{0:T(128)}) custom-call(s32[1]{0:T(128)} %bitcast.core.refs_0_, f32[3,64,512]{2,1,0:T(8,128)S(1)} %get-tuple-element.82.refs_2_.refs_1_, f32[64,512]{1,0:T(8,128)S(1)} %get-tuple-element.85.refs_2_, f32[64,512]{1,0:T(8,128)S(1)} %get-tuple-element.86.refs_3_, f32[8,128]{1,0:T(8,128)S(1)} %add.16.refs_3_.refs_4_, ...), custom_call_target="tpu_custom_call" | custom-call | tf_op jit(solution)/shard_map/assemble/pallas_call | solution.py:316
  (46 shorter events, 4.4 us)
Async XLA Ops:
  0.6 14.2 %collective-permute-start.3 = (f32[1,4,64,512]{3,2,1,0:T(8,128)}, f32[1,4,64,512]{3,2,1,0:T(8,128)S(1)}, u32[]{:S(2)}, u32[]{:S(2)}) collective-permute-start(f32[1,4,64,512]{3,2,1,0:T(8,128)} %refs_2_.5), channel_id=1, source_target_pairs={{0,1},{1,0},{2,3},{3,2},{4,5},{5,4},{6,7},{7,6},{8,9},{9,8},{10,11... | collective-permute-start | bytes 1572872 | tf_op jit(solution)/shard_map/swap_state/ppermute | solution.py:351
  1.1 1.6 %copy-start.1 = (s32[1,8]{1,0:T(1,128)S(1)}, s32[1,8]{1,0:T(1,128)}, u32[]{:S(2)}) copy-start(s32[1,8]{1,0:T(1,128)} %own_index.1) | copy-start | bytes 100
  2.1 14.5 %collective-permute-start.2 = (f32[1,64,512]{2,1,0:T(8,128)S(1)}, f32[1,64,512]{2,1,0:T(8,128)S(1)}, u32[]{:S(2)}, u32[]{:S(2)}) collective-permute-start(f32[1,64,512]{2,1,0:T(8,128)S(1)} %dynamic-slice_bitcast_fusion.1), channel_id=1, source_target_pairs={{1,2},{2,1},{3,4},{4,3},{5,6},{6,5},{7,8},{8,7},{9,10},{10,9},{11,... | collective-permute-start | bytes 393224 | tf_op jit(solution)/shard_map/pass_state_own/ppermute | solution.py:355
  2.8 5.3 %collective-permute-start = (s32[1,8]{1,0:T(1,128)S(1)}, s32[1,8]{1,0:T(1,128)S(1)}, u32[]{:S(2)}, u32[]{:S(2)}) collective-permute-start(s32[1,8]{1,0:T(1,128)S(1)} %copy-done.1), channel_id=1, source_target_pairs={{0,1},{1,0},{2,3},{3,2},{4,5},{5,4},{6,7},{7,6},{8,9},{9,8},{10,11... | collective-permute-start | bytes 104 | tf_op jit(solution)/shard_map/swap_node_index/ppermute | solution.py:351
  6.7 1.4 %collective-permute-start.1 = (s32[1]{0:T(128)}, s32[1]{0:T(128)}, u32[]{:S(2)}, u32[]{:S(2)}) collective-permute-start(s32[1]{0:T(128)} %param.18), channel_id=1, source_target_pairs={{0,1},{1,0},{2,3},{3,2},{4,5},{5,4},{6,7},{7,6},{8,9},{9,8},{10,11... | collective-permute-start | bytes 20 | tf_op jit(solution)/shard_map/swap_weight_num/ppermute | solution.py:351
  8.1 7.4 %copy-start = (f32[1,4,64,512]{3,2,1,0:T(8,128)S(1)}, f32[1,4,64,512]{3,2,1,0:T(8,128)}, u32[]{:S(2)}) copy-start(f32[1,4,64,512]{3,2,1,0:T(8,128)} %refs_2_.5) | copy-start | bytes 1572868
  11.1 7.2 %collective-permute-start.6 = (f32[64,512]{1,0:T(8,128)S(1)}, f32[64,512]{1,0:T(8,128)S(1)}, u32[]{:S(2)}, u32[]{:S(2)}) collective-permute-start(f32[64,512]{1,0:T(8,128)S(1)} %get-tuple-element.58), channel_id=1, source_target_pairs={{1,2},{2,1},{3,4},{4,3},{5,6},{6,5},{7,8},{8,7},{9,10},{10,9},{11,... | collective-permute-start | bytes 393224 | tf_op jit(solution)/shard_map/pass_edge/ppermute | solution.py:355
  11.8 6.6 %collective-permute-start.7 = (f32[64,512]{1,0:T(8,128)S(1)}, f32[64,512]{1,0:T(8,128)S(1)}, u32[]{:S(2)}, u32[]{:S(2)}) collective-permute-start(f32[64,512]{1,0:T(8,128)S(1)} %get-tuple-element.59), channel_id=1, source_target_pairs={{0,1},{1,0},{2,3},{3,2},{4,5},{5,4},{6,7},{7,6},{8,9},{9,8},{10,11... | collective-permute-start | bytes 393224 | tf_op jit(solution)/shard_map/swap_after_o/ppermute | solution.py:351
  14.7 3.6 %collective-permute-start.8 = (f32[64,512]{1,0:T(8,128)S(1)}, f32[64,512]{1,0:T(8,128)S(1)}, u32[]{:S(2)}, u32[]{:S(2)}) collective-permute-start(f32[64,512]{1,0:T(8,128)S(1)} %get-tuple-element.60), channel_id=1, source_target_pairs={{0,1},{1,0},{2,3},{3,2},{4,5},{5,4},{6,7},{7,6},{8,9},{9,8},{10,11... | collective-permute-start | bytes 393224 | tf_op jit(solution)/shard_map/swap_after_i/ppermute | solution.py:351
  14.8 2.6 %collective-permute-start.5 = (f32[1,64,512]{2,1,0:T(8,128)S(1)}, f32[1,64,512]{2,1,0:T(8,128)S(1)}, u32[]{:S(2)}, u32[]{:S(2)}) collective-permute-start(f32[1,64,512]{2,1,0:T(8,128)S(1)} %dynamic-slice_bitcast_fusion), channel_id=1, source_target_pairs={{1,2},{2,1},{3,4},{4,3},{5,6},{6,5},{7,8},{8,7},{9,10},{10,9},{11,... | collective-permute-start | bytes 393224 | tf_op jit(solution)/shard_map/pass_state_far/ppermute | solution.py:355
  16.7 11.6 %collective-permute-start.4 = (f32[2,64,512]{2,1,0:T(8,128)S(1)}, f32[2,64,512]{2,1,0:T(8,128)S(1)}, u32[]{:S(2)}, u32[]{:S(2)}) collective-permute-start(f32[2,64,512]{2,1,0:T(8,128)S(1)} %first_edge.2.refs_5_), channel_id=1, source_target_pairs={{1,2},{2,1},{3,4},{4,3},{5,6},{6,5},{7,8},{8,7},{9,10},{10,9},{11,... | collective-permute-start | bytes 786440 | tf_op jit(solution)/shard_map/pass_stage2_far/ppermute | solution.py:355
  17.6 10.9 %collective-permute-start.11 = (f32[2,64,512]{2,1,0:T(8,128)S(1)}, f32[2,64,512]{2,1,0:T(8,128)S(1)}, u32[]{:S(2)}, u32[]{:S(2)}) collective-permute-start(f32[2,64,512]{2,1,0:T(8,128)S(1)} %first_edge.3.refs_4_), channel_id=1, source_target_pairs={{1,2},{2,1},{3,4},{4,3},{5,6},{6,5},{7,8},{8,7},{9,10},{10,9},{11,... | collective-permute-start | bytes 786440 | tf_op jit(solution)/shard_map/pass_stage2_own/ppermute | solution.py:355
  18.8 8.4 %collective-permute-start.10 = (f32[64,512]{1,0:T(8,128)S(1)}, f32[64,512]{1,0:T(8,128)S(1)}, u32[]{:S(2)}, u32[]{:S(2)}) collective-permute-start(f32[64,512]{1,0:T(8,128)S(1)} %get-tuple-element.61.refs_6_), channel_id=1, source_target_pairs={{0,1},{1,0},{2,3},{3,2},{4,5},{5,4},{6,7},{7,6},{8,9},{9,8},{10,11... | collective-permute-start | bytes 393224 | tf_op jit(solution)/shard_map/swap_s2_own/ppermute | solution.py:351
  26.2 1.3 %collective-permute-start.9 = (f32[64,512]{1,0:T(8,128)S(1)}, f32[64,512]{1,0:T(8,128)S(1)}, u32[]{:S(2)}, u32[]{:S(2)}) collective-permute-start(f32[64,512]{1,0:T(8,128)S(1)} %get-tuple-element.62.refs_7_), channel_id=1, source_target_pairs={{0,1},{1,0},{2,3},{3,2},{4,5},{5,4},{6,7},{7,6},{8,9},{9,8},{10,11... | collective-permute-start | bytes 393224 | tf_op jit(solution)/shard_map/swap_s2_far/ppermute | solution.py:351
  29.0 24.8 %collective-permute-start.12 = (f32[2,64,512]{2,1,0:T(8,128)S(1)}, f32[2,64,512]{2,1,0:T(8,128)S(1)}, u32[]{:S(2)}, u32[]{:S(2)}) collective-permute-start(f32[2,64,512]{2,1,0:T(8,128)S(1)} %get-tuple-element.70.refs_2_), channel_id=1, source_target_pairs={{1,2},{2,1},{3,4},{4,3},{5,6},{6,5},{7,8},{8,7},{9,10},{10,9},{11,... | collective-permute-start | bytes 786440 | tf_op jit(solution)/shard_map/pass_back2_far/ppermute | solution.py:355
  30.5 10.7 %collective-permute-start.15 = (f32[88,512]{1,0:T(8,128)S(1)}, f32[88,512]{1,0:T(8,128)S(1)}, u32[]{:S(2)}, u32[]{:S(2)}) collective-permute-start(f32[88,512]{1,0:T(8,128)S(1)} %get-tuple-element.74.refs_13_), channel_id=1, source_target_pairs={{0,1},{1,0},{2,3},{3,2},{4,5},{5,4},{6,7},{7,6},{8,9},{9,8},{10,11... | collective-permute-start | bytes 540680 | tf_op jit(solution)/shard_map/swap_pin/ppermute | solution.py:351
  39.5 1.7 %collective-permute-start.16 = (f32[88,512]{1,0:T(8,128)S(1)}, f32[88,512]{1,0:T(8,128)S(1)}, u32[]{:S(2)}, u32[]{:S(2)}) collective-permute-start(f32[88,512]{1,0:T(8,128)S(1)} %get-tuple-element.75.refs_14_), channel_id=1, source_target_pairs={{0,1},{1,0},{2,3},{3,2},{4,5},{5,4},{6,7},{7,6},{8,9},{9,8},{10,11... | collective-permute-start | bytes 540680 | tf_op jit(solution)/shard_map/swap_pin/ppermute | solution.py:351
  39.6 1.6 %collective-permute-start.17 = (f32[80,512]{1,0:T(8,128)S(1)}, f32[80,512]{1,0:T(8,128)S(1)}, u32[]{:S(2)}, u32[]{:S(2)}) collective-permute-start(f32[80,512]{1,0:T(8,128)S(1)} %get-tuple-element.76.refs_15_), channel_id=1, source_target_pairs={{0,1},{1,0},{2,3},{3,2},{4,5},{5,4},{6,7},{7,6},{8,9},{9,8},{10,11... | collective-permute-start | bytes 491528 | tf_op jit(solution)/shard_map/swap_pin/ppermute | solution.py:351
  40.0 1.2 %collective-permute-start.14 = (f32[8,128]{1,0:T(8,128)S(1)}, f32[8,128]{1,0:T(8,128)S(1)}, u32[]{:S(2)}, u32[]{:S(2)}) collective-permute-start(f32[8,128]{1,0:T(8,128)S(1)} %get-tuple-element.73.refs_11_), channel_id=1, source_target_pairs={{0,1},{1,0},{2,3},{3,2},{4,5},{5,4},{6,7},{7,6},{8,9},{9,8},{10,11... | collective-permute-start | bytes 12296 | tf_op jit(solution)/shard_map/swap_goal_sum/ppermute | solution.py:351
  42.0 3.7 %collective-permute-start.18 = (f32[8,128]{1,0:T(8,128)S(1)}, f32[8,128]{1,0:T(8,128)S(1)}, u32[]{:S(2)}, u32[]{:S(2)}) collective-permute-start(f32[8,128]{1,0:T(8,128)S(1)} %get-tuple-element.78), channel_id=1, source_target_pairs={{0,4},{2,6},{4,0},{6,2},{8,12},{10,14},{12,8},{14,10},{1,5},{3,7},... | collective-permute-start | bytes 12296 | tf_op jit(solution)/shard_map/goal_sum/ppermute | solution.py:430
  45.7 4.5 %collective-permute-start.19 = (f32[8,128]{1,0:T(8,128)S(1)}, f32[8,128]{1,0:T(8,128)S(1)}, u32[]{:S(2)}, u32[]{:S(2)}) collective-permute-start(f32[8,128]{1,0:T(8,128)S(1)} %add.14.refs_7_), channel_id=1, source_target_pairs={{0,8},{2,10},{4,12},{6,14},{8,0},{10,2},{12,4},{14,6},{1,9},{3,11}... | collective-permute-start | bytes 12296 | tf_op jit(solution)/shard_map/goal_sum/ppermute | solution.py:430
  50.2 3.6 %collective-permute-start.22 = (f32[8,128]{1,0:T(8,128)S(1)}, f32[8,128]{1,0:T(8,128)S(1)}, u32[]{:S(2)}, u32[]{:S(2)}) collective-permute-start(f32[8,128]{1,0:T(8,128)S(1)} %add.15.refs_17_), channel_id=1, source_target_pairs={{0,2},{2,0},{4,6},{6,4},{8,10},{10,8},{12,14},{14,12},{1,3},{3,1},... | collective-permute-start | bytes 12296 | tf_op jit(solution)/shard_map/goal_sum/ppermute | solution.py:430
  51.4 2.6 %collective-permute-start.13 = (f32[2,64,512]{2,1,0:T(8,128)S(1)}, f32[2,64,512]{2,1,0:T(8,128)S(1)}, u32[]{:S(2)}, u32[]{:S(2)}) collective-permute-start(f32[2,64,512]{2,1,0:T(8,128)S(1)} %get-tuple-element.71.refs_1_), channel_id=1, source_target_pairs={{1,2},{2,1},{3,4},{4,3},{5,6},{6,5},{7,8},{8,7},{9,10},{10,9},{11,... | collective-permute-start | bytes 786440 | tf_op jit(solution)/shard_map/pass_back2_own/ppermute | solution.py:355
  54.2 14.6 %collective-permute-start.20 = (f32[64,512]{1,0:T(8,128)S(1)}, f32[64,512]{1,0:T(8,128)S(1)}, u32[]{:S(2)}, u32[]{:S(2)}) collective-permute-start(f32[64,512]{1,0:T(8,128)S(1)} %get-tuple-element.83), channel_id=1, source_target_pairs={{1,2},{2,1},{3,4},{4,3},{5,6},{6,5},{7,8},{8,7},{9,10},{10,9},{11,... | collective-permute-start | bytes 393224 | tf_op jit(solution)/shard_map/pass_back1_far/ppermute | solution.py:355
  54.9 14.8 %collective-permute-start.21 = (f32[64,512]{1,0:T(8,128)S(1)}, f32[64,512]{1,0:T(8,128)S(1)}, u32[]{:S(2)}, u32[]{:S(2)}) collective-permute-start(f32[64,512]{1,0:T(8,128)S(1)} %get-tuple-element.84), channel_id=1, source_target_pairs={{1,3},{2,0},{3,5},{4,2},{5,7},{6,4},{7,9},{8,6},{9,11},{10,8},{11,... | collective-permute-start | bytes 393224 | tf_op jit(solution)/shard_map/pass_back1_own/ppermute | solution.py:355
  57.0 12.7 %collective-permute-start.25 = (f32[2,64,256]{2,1,0:T(8,128)S(1)}, f32[2,64,256]{2,1,0:T(8,128)S(1)}, u32[]{:S(2)}, u32[]{:S(2)}) collective-permute-start(f32[2,64,256]{2,1,0:T(8,128)S(1)} %get-tuple-element.91), channel_id=1, source_target_pairs={{0,1},{1,0},{2,3},{3,2},{4,5},{5,4},{6,7},{7,6},{8,9},{9,8},{10,11... | collective-permute-start | bytes 393224 | tf_op jit(solution)/shard_map/swap_gradient/ppermute | solution.py:351
  68.3 2.2 %collective-permute-start.23 = (f32[96,512]{1,0:T(8,128)S(1)}, f32[96,512]{1,0:T(8,128)S(1)}, u32[]{:S(2)}, u32[]{:S(2)}) collective-permute-start(f32[96,512]{1,0:T(8,128)S(1)} %get-tuple-element.87), channel_id=1, source_target_pairs={{0,1},{1,0},{2,3},{3,2},{4,5},{5,4},{6,7},{7,6},{8,9},{9,8},{10,11... | collective-permute-start | bytes 589832 | tf_op jit(solution)/shard_map/swap_adjoint/ppermute | solution.py:351
  68.3 2.1 %collective-permute-start.24 = (f32[96,512]{1,0:T(8,128)S(1)}, f32[96,512]{1,0:T(8,128)S(1)}, u32[]{:S(2)}, u32[]{:S(2)}) collective-permute-start(f32[96,512]{1,0:T(8,128)S(1)} %get-tuple-element.88), channel_id=1, source_target_pairs={{0,1},{1,0},{2,3},{3,2},{4,5},{5,4},{6,7},{7,6},{8,9},{9,8},{10,11... | collective-permute-start | bytes 589832 | tf_op jit(solution)/shard_map/swap_adjoint/ppermute | solution.py:351

commit v4 on v3

v4 whole, which is shorter than its diff:
```python
import functools
import math

import jax
import jax.numpy as jnp
from jax import lax
from jax.experimental import pallas as pl
from jax.experimental.pallas import tpu as pltpu
from jax.sharding import PartitionSpec as P

time_step = 0.6
variance_gain = 0.5
penalty = 0.1
weight_denominator = 16.0

VMEM_LIMIT = 24 * 1024 * 1024
AXES = ("space", "node")
LONG = 40


def cost_of(us):
    return pl.CostEstimate(flops=us * 1_000_000_000, bytes_accessed=us * 3_000_000, transcendentals=0)


def roll(value, steps, axis):
    return pltpu.roll(value, steps % value.shape[axis], axis)


def in_plane(value, a, cy, cz, k):
    return a[1] * (cy[0, k] * roll(value, 1, 0) + cy[1, k] * roll(value, -1, 0)) + a[2] * (
        cz[0, k] * roll(value, 1, 1) + cz[1, k] * roll(value, -1, 1)
    )


def in_plane_back(value, a, cy, cz, k):
    return a[1] * (roll(cy[0, k] * value, -1, 0) + roll(cy[1, k] * value, 1, 0)) + a[2] * (
        roll(cz[0, k] * value, -1, 1) + roll(cz[1, k] * value, 1, 1)
    )


def rows_of(scal, j):
    return [scal[j, k] for k in range(5)]


def pick(values, index):
    result = jnp.float32(values[-1])
    for k, value in enumerate(values[:-1]):
        result = jnp.where(index == k, jnp.float32(value), result)
    return result


def node_scales(indices, step, scal):
    levels = [-math.cos(math.pi * k / 8.0) for k in range(9)]
    half = step[0] & 31
    wave = pick([math.sin(2.0 * math.pi * k / 64.0) for k in range(17)], jnp.minimum(half, 32 - half))
    phase = 1.0 + jnp.where(step[0] < 32, 0.5, -0.5) * wave
    for j, index in enumerate(indices):
        p = {k: pick(levels, index[0, k]) for k in (0, 1, 2, 4, 6, 7)}
        scal[j, 0] = 1.0 + 0.3 * p[0]
        scal[j, 1] = 1.0 + 0.3 * p[1]
        scal[j, 2] = (1.0 + 0.3 * p[2]) * (1.0 + 0.2 * p[7])
        scal[j, 3] = pick([math.exp(0.5 * p) for p in levels], index[0, 3]) * pick(
            [math.exp(0.25 * p) for p in levels], index[0, 5]
        )
        scal[j, 4] = (1.0 + 0.3 * p[4] + 0.2 * p[6]) * phase


def expand(bits, columns):
    blocks = bits.shape[1]
    spread = (
        lax.broadcasted_iota(jnp.int32, (blocks, columns), 1) // (columns // blocks)
        == lax.broadcasted_iota(jnp.int32, (blocks, columns), 0)
    ).astype(jnp.bfloat16)
    return jnp.dot(bits.astype(jnp.float32).astype(jnp.bfloat16), spread, preferred_element_type=jnp.float32)


def toward_outer(up, me):
    flip = (me == 1).astype(jnp.float32)
    return up + flip - 2.0 * flip * up


def pack(core, own, far, out):
    out[0] = own[0, 0]
    out[1] = far[0, 3 * core[0]]


def fields_of(k, at, me, speeds, masks, cx, cy, cz):
    rows, columns = speeds.shape[2:]
    row = lax.broadcasted_iota(jnp.int32, (rows, columns), 0)
    column = lax.broadcasted_iota(jnp.int32, (rows, columns), 1)
    up = [expand(masks[d, at], columns) for d in range(3)]
    s = [speeds[d, at].astype(jnp.float32) for d in range(3)]
    outer = s[0] * toward_outer(up[0], me)
    cx[0, k] = outer
    cx[1, k] = s[0] - outer
    lower = s[1] * up[1]
    cy[0, k] = jnp.where(row == 0, 0.0, lower)
    cy[1, k] = jnp.where(row == rows - 1, 0.0, s[1] - lower)
    lower = s[2] * up[2]
    cz[0, k] = jnp.where(column == 0, 0.0, lower)
    cz[1, k] = jnp.where(column == columns - 1, 0.0, s[2] - lower)


def own_of(k, at, rates, speeds, scal, dg):
    s = [speeds[d, at].astype(jnp.float32) for d in range(3)] + [rates[at].astype(jnp.float32)]
    for j in range(2):
        dg[j, k] = sum(scal[j, d] * s[d] for d in range(4))


def prepare(core, own_index, far_index, step_index, speed, mask, decay, control, scal, cx, cy, cz, dg, ctl, edge, own_ids, far_ids, step, few):
    me = core[0]
    small = [(own_index, own_ids), (far_index, far_ids), (step_index, step)]
    small = [pltpu.make_async_copy(source, target, few.at[n]) for n, (source, target) in enumerate(small)]
    for copy in small:
        copy.start()
    for k, at in enumerate((3 * me, 1 + me)):
        fields_of(k, at, me, speed, mask, cx, cy, cz)
        ctl[k] = control[at]
    edge[...] = cx[0, 0]
    for copy in small:
        copy.wait()
    node_scales((own_ids, far_ids), step, scal)
    for k, at in enumerate((3 * me, 1 + me)):
        own_of(k, at, decay, speed, scal, dg)


def prepare_next(core, scal, speed, mask, decay, control, own, far, _, __, s1_next, near, cx, cy, cz, dg):
    me = core[0]
    at = 2 - me
    fields_of(0, at, me, speed, mask, cx, cy, cz)
    own_of(0, at, decay, speed, scal, dg)
    near[...] = cx[0, 0]
    for j, c in enumerate((own, far)):
        a = rows_of(scal, j)
        value = c[0, at]
        l = a[0] * (cx[0, 0] * c[0, 1 + me] + cx[1, 0] * c[0, 3 - 3 * me]) + in_plane(value, a, cy, cz, 0) - dg[j, 0] * value
        s1_next[j] = value + time_step * (l + a[4] * control[at])


def prepare_back(core, own_weight, far_weight, goal, adjoint, weights, goals, adj, adj_out_o, adj_out_i):
    me = core[0]
    weights[0] = own_weight[0].astype(jnp.float32) * (1.0 / weight_denominator)
    weights[1] = far_weight[0].astype(jnp.float32) * (1.0 / weight_denominator)
    for k, at in enumerate((3 * me, 1 + me)):
        goals[k] = goal[at].astype(jnp.float32)
        adj[k] = adjoint[0, at].astype(jnp.float32)
    adj_out_o[...] = adjoint[0, 3 - 3 * me].astype(jnp.float32)
    adj_out_i[...] = adjoint[0, 2 - me].astype(jnp.float32)


def first_stage(core, scal, own, far, cx, cy, cz, dg, ctl, base, base_q, s1_in):
    me = core[0]
    for j, c in enumerate((own, far)):
        a = rows_of(scal, j)
        c_o, c_i = c[0, 3 * me], c[0, 1 + me]
        push = [a[4] * ctl[k] for k in range(2)]
        l_i = a[0] * (cx[0, 1] * c_o + cx[1, 1] * c[0, 2 - me]) + in_plane(c_i, a, cy, cz, 1) - dg[j, 1] * c_i
        s1_i = c_i + time_step * (l_i + push[1])
        s1_in[j] = s1_i
        l_o = a[0] * (cx[1, 0] * c_i) + in_plane(c_o, a, cy, cz, 0) - dg[j, 0] * c_o
        base[j] = c_o + time_step * (l_o + push[0])
        base_q[j] = 0.75 * c_o + (0.25 * time_step) * (a[0] * (cx[1, 0] * s1_i) + push[0])


def first_edge(scal, halo, base, base_q, cx, cy, cz, dg, msg):
    for j in range(2):
        a = rows_of(scal, j)
        s1_o = base[j] + (time_step * a[0]) * (cx[0, 0] * halo[1 - j])
        msg[j, 0] = s1_o
        msg[j, 1] = base_q[j] + 0.25 * (s1_o + time_step * (in_plane(s1_o, a, cy, cz, 0) - dg[j, 0] * s1_o))


def second_inner(core, scal, own, far, msg, s1_in, s1_next, cx, cy, cz, dg, ctl, s2_own, s2_far):
    for j, (c, out) in enumerate(((own, s2_own), (far, s2_far))):
        a = rows_of(scal, j)
        s1_i = s1_in[j]
        l_i = a[0] * (cx[0, 1] * msg[j, 0] + cx[1, 1] * s1_next[j]) + in_plane(s1_i, a, cy, cz, 1) - dg[j, 1] * s1_i
        out[...] = 0.75 * c[0, 1 + core[0]] + 0.25 * (s1_i + time_step * (l_i + a[4] * ctl[1]))


def third_stage(core, scal, own, far, msg, s2_own, s2_far, next_own, next_far, near_edge, cx, cy, cz, dg, ctl, base):
    me = core[0]
    parts = ((own, s2_own, next_own), (far, s2_far, next_far))
    for j, (c, s2, s2_next) in enumerate(parts):
        a = rows_of(scal, j)
        q, s2_i = msg[j, 1], s2[...]
        back = (0.25 * time_step * a[0]) * (near_edge[...] * msg[j, 0])
        l_o = a[0] * (cx[0, 0] * back + cx[1, 0] * s2_i) + in_plane(q, a, cy, cz, 0) - dg[j, 0] * q
        l_i = a[0] * (cx[0, 1] * q + cx[1, 1] * s2_next[...]) + in_plane(s2_i, a, cy, cz, 1) - dg[j, 1] * s2_i
        base[j, 0] = c[0, 3 * me] / 3.0 + 2.0 / 3.0 * (q + time_step * (l_o + a[4] * ctl[0]))
        base[j, 1] = c[0, 1 + me] / 3.0 + 2.0 / 3.0 * (s2_i + time_step * (l_i + a[4] * ctl[1]))


def finals(j, scal, halo, base, cx, cy, cz, dg):
    a = rows_of(scal, j)
    step = (0.25 * time_step * a[0]) * (cx[0, 0] * halo[1 - j, 0])
    change = in_plane(step, a, cy, cz, 0) - dg[j, 0] * step + a[0] * (cx[0, 0] * halo[1 - j, 1])
    outer = base[j, 0] + 2.0 / 3.0 * (step + time_step * change)
    inner = base[j, 1] + (2.0 / 3.0 * time_step * a[0]) * (cx[0, 1] * step)
    return outer, inner


def turn(scal, weights, halo, base, cx, cy, cz, dg, goals, adj, after_o, after_i, final_own, final_far, term, msg, partial):
    final_own[0], final_own[1] = finals(0, scal, halo, base, cx, cy, cz, dg)
    final_far[0], final_far[1] = finals(1, scal, halo, base, cx, cy, cz, dg)
    first = [weights[0] * final_own[k] + weights[1] * final_far[k] for k in range(2)]
    for j, (final, after) in enumerate(((final_own, (adj[0], adj[1])), (final_far, (after_o[...], after_i[...])))):
        a = rows_of(scal, j)
        u = []
        for k in range(2):
            t = after[k] + goals[k] * weights[j] * (1.0 + 2.0 * variance_gain * (final[k] - first[k]))
            term[j, k] = t
            u.append(2.0 / 3.0 * t)
        msg[j, 0] = a[0] * (cx[0, 0] * u[0])
        spread = a[0] * (cx[0, 1] * u[1]) + in_plane_back(u[0], a, cy, cz, 0) - dg[j, 0] * u[0]
        value = u[0] + time_step * spread
        partial[j] = value
        msg[j, 1] = a[0] * (cx[0, 0] * value)


class Laid:
    def __init__(self, refs):
        self.left = [(ref, start) for ref in refs for start in range(0, ref.shape[0], 8)]

    def put(self, value):
        for start in range(0, value.shape[0], 8):
            ref, at = self.left.pop(0)
            ref[at : at + 8] = value[start : start + 8]


def get(refs, count, rows):
    whole = jnp.concatenate([ref[...] for ref in refs], 0)
    return [whole[rows * k : rows * k + rows] for k in range(count)] + [whole[rows * count :]]


def cut(rows, pieces):
    tiles = rows // 8
    return [8 * (tiles // pieces + (k < tiles % pieces)) for k in range(pieces)]


def turn_inner(scal, weights, final_own, final_far, terms, cx, cy, cz, dg, goals, part, cost, *pins):
    laid = Laid(pins)
    for j in range(2):
        a = rows_of(scal, j)
        u = [2.0 / 3.0 * terms[j, k] for k in range(2)]
        laid.put(a[0] * (cx[1, 1] * u[1]))
        spread = a[0] * (cx[1, 0] * u[0]) + in_plane_back(u[1], a, cy, cz, 1) - dg[j, 1] * u[1]
        value = u[1] + time_step * spread
        part[j] = value
        laid.put(a[0] * (cx[1, 1] * value))
    total = 0.0
    for k in range(2):
        own, far = weights[0] * final_own[k], weights[1] * final_far[k]
        first = own + far
        second = own * final_own[k] + far * final_far[k]
        total = total + goals[k] * (first + variance_gain * (second - first * first))
    rows = total.shape[0]
    total = sum(total[8 * r : 8 * r + 8] for r in range(rows // 8))
    cost[...] = total
    laid.put(total)


def back_second(scal, msgs, partials, part, near_edge, near, cx, cy, cz, dg, cost_own, *rest):
    base, a2, total = rest[-3:]
    count, rows = (len(rest) - 3) // 2, msgs.shape[2]
    mine, theirs = get(rest[:count], 4, rows), get(rest[count:-3], 4, rows)
    cost = cost_own[...] + theirs[4]
    total[...] = sum(cost[:, 128 * k : 128 * k + 128] for k in range(cost.shape[1] // 128))
    for j in range(2):
        a = rows_of(scal, j)
        pin, pin2 = theirs[2 - 2 * j], theirs[3 - 2 * j]
        pin2 = 0.25 * (pin2 + (time_step * a[0]) * (near[...] * mine[2 * j]))
        a2_i = part[j] + time_step * pin
        a2[j] = a2_i
        u_o, u_i = 0.25 * partials[j], 0.25 * a2_i
        back = (0.25 * time_step * a[0]) * (near_edge[...] * msgs[j, 0])
        spread = a[0] * (cx[0, 1] * u_i) + in_plane_back(u_o, a, cy, cz, 0) - dg[j, 0] * u_o + back
        base[j, 0] = u_o + time_step * spread
        spread = a[0] * (cx[1, 0] * u_o) + in_plane_back(u_i, a, cy, cz, 1) - dg[j, 1] * u_i + pin2
        base[j, 1] = u_i + time_step * spread


def second_back_edge(scal, halo, base, cx, cy, cz, dg, cost, cost_far, a1, msg_far, msg_own, total):
    total[...] = cost[...] + cost_far[...]
    for j, msg in ((1, msg_far), (0, msg_own)):
        a = rows_of(scal, j)
        step = (0.25 * time_step) * halo[1 - j, 0]
        spread = in_plane_back(step, a, cy, cz, 0) - dg[j, 0] * step + 0.25 * halo[1 - j, 1]
        value = base[j, 0] + step + time_step * spread
        a1[j] = value
        msg[...] = a[0] * (cx[0, 0] * value)


def close(core, scal, terms, partials, halo, a1, a2, base, cx, cy, cz, dg, ctl, keep, part, give, *send):
    laid = Laid(send)
    sources = [0.0, 0.0]
    for j in range(2):
        a = rows_of(scal, j)
        first = halo[1 - j, 0]
        x = [a1[j], base[j, 1] + (0.25 * time_step * time_step * a[0]) * (cx[1, 0] * first)]
        a2_o = partials[j] + time_step * first
        for k, second in enumerate((a2_o, a2[j])):
            sources[k] = sources[k] + a[4] * (2.0 / 3.0 * terms[j, k] + 0.25 * second + x[k])
        spread = a[0] * (cx[0, 1] * x[1]) + in_plane_back(x[0], a, cy, cz, 0) - dg[j, 0] * x[0]
        outer = terms[j, 0] / 3.0 + 0.75 * a2_o + (x[0] + time_step * spread)
        spread = a[0] * (cx[1, 0] * x[0]) + in_plane_back(x[1], a, cy, cz, 1) - dg[j, 1] * x[1]
        inner = terms[j, 1] / 3.0 + 0.75 * a2[j] + (x[1] + time_step * spread)
        for k, value in enumerate((outer, inner, a[0] * (cx[1, 1] * x[1]))):
            if j == 0:
                part[k] = value
            else:
                laid.put(value)
    half = ctl.shape[2] // 2
    zero = core[0] == 0
    for k in range(2):
        gradient = time_step * sources[k] + penalty * ctl[k]
        low, high = gradient[:, :half], gradient[:, half:]
        keep[k] = jnp.where(zero, low, high)
        give[k] = jnp.where(zero, high, low)


def last_edge(halo_own, halo_far, part, cost, cost_far, outer, add, total):
    total[...] = cost[...] + cost_far[...]
    outer[...] = part[0] + time_step * halo_own[...]
    add[...] = time_step * halo_far[...]


def assemble(cells, core, part, outer, add, cost, keep, taken, *rest):
    theirs, (out, gradient, objective) = get(rest[:-3], 3, part.shape[1]), rest[-3:]
    me = core[0]
    out[0, 3 * me] = outer[...]
    out[0, 1 + me] = part[1] + time_step * theirs[2]
    out[0, 3 - 3 * me] = theirs[0] + add[...]
    out[0, 2 - me] = theirs[1] + time_step * part[2]
    gradient[3 * me] = keep[0]
    gradient[1 + me] = keep[1]
    gradient[3 - 3 * me] = taken[0]
    gradient[2 - me] = taken[1]
    objective[0] = jnp.sum(cost[...]) / cells


def on_core(body, outs, scalars, arrays, hbm_out=(), smem_out=(), after=(), cost=0, name=None):
    hbm_out = tuple(hbm_out) + tuple(smem_out)
    out_shape = [
        jax.ShapeDtypeStruct(s, jnp.float32) if i in hbm_out else pltpu.VMEM(s, jnp.float32)
        for i, s in enumerate(outs)
    ]
    held = [pltpu.with_memory_space_constraint(x, pltpu.SMEM) for x in scalars]
    held += [pltpu.with_memory_space_constraint(x, pltpu.VMEM) for x in arrays]
    count, waits = len(held), len(after)

    def run(*refs):
        body(*refs[:count], *refs[count + waits :])

    return pl.pallas_call(
        run,
        out_shape=out_shape,
        in_specs=[pl.BlockSpec(memory_space=pltpu.SMEM)] * len(scalars)
        + [pl.BlockSpec(memory_space=pltpu.VMEM)] * len(arrays)
        + [pl.BlockSpec(memory_space=pl.ANY)] * waits,
        out_specs=[
            pl.BlockSpec(memory_space=pltpu.SMEM if i in smem_out else pltpu.VMEM) for i in range(len(outs))
        ],
        compiler_params=pltpu.CompilerParams(vmem_limit_bytes=VMEM_LIMIT),
        cost_estimate=cost_of(cost) if cost else None,
        name=name or body.__name__,
    )(*held, *after)


def shards(
    concentration,
    adjoint_next,
    speed,
    direction_mask,
    decay_rate,
    control,
    goal_weight,
    node_index,
    weight_num,
    step_index,
):
    sections = lax.axis_size("space")
    ranks = sections * lax.axis_size("node")
    within = [(i, i ^ 1) for i in range(ranks)]
    across = [p for i in range(1, ranks - 1, 2) for p in ((i, i + 1), (i + 1, i))]
    along = [p for i in range(0, ranks - 2, 2) for p in ((i + 1, i + 3), (i + 2, i))]

    def swap(x, what):
        with jax.named_scope("swap_" + what):
            return lax.ppermute(x, AXES, within)

    def pass_on(x, what, pairs=across):
        with jax.named_scope("pass_" + what):
            return lax.ppermute(x, AXES, pairs)

    _, layers, rows, columns = concentration.shape
    me = lax.axis_index("node").astype(jnp.int32)
    core = jnp.reshape(me, (1,))
    far_index, far_weight, step = swap(node_index, "node_index"), swap(weight_num, "weight_num"), swap(step_index, "step")

    far = swap(concentration, "state")
    plane = (rows, columns)
    pair, three = (2,) + plane, (3,) + plane
    four = (2,) + pair
    sides = (2, rows, columns // 2)
    held = lambda x, space: pltpu.with_memory_space_constraint(x, space)
    packed = pl.pallas_call(
        pack,
        out_shape=pltpu.VMEM(pair, jnp.float32),
        grid_spec=pltpu.PrefetchScalarGridSpec(
            num_scalar_prefetch=1,
            grid=(1,),
            in_specs=[
                pl.BlockSpec((1, 1) + plane, lambda g, c: (0, 3 * c[0], 0, 0)),
                pl.BlockSpec(memory_space=pltpu.VMEM),
            ],
            out_specs=pl.BlockSpec(memory_space=pltpu.VMEM),
        ),
        compiler_params=pltpu.CompilerParams(vmem_limit_bytes=VMEM_LIMIT),
        cost_estimate=cost_of(LONG),
        name="pack",
    )(core, held(concentration, pltpu.HBM), held(far, pltpu.VMEM))
    halo = pass_on(packed, "state")

    shapes = [four, four, four, four, pair, plane]
    scal, cx, cy, cz, dg, ctl, edge = pl.pallas_call(
        prepare,
        out_shape=[pltpu.SMEM((2, 8), jnp.float32)] + [pltpu.VMEM(s, jnp.float32) for s in shapes],
        in_specs=[pl.BlockSpec(memory_space=pltpu.SMEM)]
        + [pl.BlockSpec(memory_space=pl.ANY)] * 3
        + [pl.BlockSpec(memory_space=pltpu.VMEM)] * 4,
        out_specs=[pl.BlockSpec(memory_space=pltpu.SMEM)] + [pl.BlockSpec(memory_space=pltpu.VMEM)] * len(shapes),
        scratch_shapes=[
            pltpu.SMEM(node_index.shape, jnp.int32),
            pltpu.SMEM(node_index.shape, jnp.int32),
            pltpu.SMEM((1,), jnp.int32),
            pltpu.SemaphoreType.DMA((3,)),
        ],
        compiler_params=pltpu.CompilerParams(vmem_limit_bytes=VMEM_LIMIT),
        cost_estimate=cost_of(LONG),
        name="prepare",
    )(
        core,
        held(node_index, pltpu.HBM),
        *(far_index, step),
        *[held(x, pltpu.VMEM) for x in (speed, direction_mask, decay_rate, control)],
    )
    near_edge = pass_on(edge, "edge")
    fields = [cx, cy, cz, dg]
    both = [core, scal]
    states = [concentration, far]
    base, base_q, s1_in = on_core(first_stage, [pair] * 3, both, states + fields + [ctl])
    (msg,) = on_core(first_edge, [four], [scal], [halo, base, base_q] + fields, cost=LONG)
    halo2 = pass_on(msg, "stage2")

    weights, goals, adj, adj_out_o, adj_out_i = pl.pallas_call(
        lambda *refs: prepare_back(*refs[:5], *refs[6:]),
        out_shape=[pltpu.SMEM((2,), jnp.float32)]
        + [pltpu.VMEM(s, jnp.float32) for s in (pair, pair, plane, plane)],
        in_specs=[pl.BlockSpec(memory_space=pltpu.SMEM)] * 3
        + [pl.BlockSpec(memory_space=pltpu.VMEM)] * 2
        + [pl.BlockSpec(memory_space=pl.ANY)],
        out_specs=[pl.BlockSpec(memory_space=pltpu.SMEM)] + [pl.BlockSpec(memory_space=pltpu.VMEM)] * 4,
        compiler_params=pltpu.CompilerParams(vmem_limit_bytes=VMEM_LIMIT),
        name="prepare_back",
    )(core, swap(far_weight, "weight_num"), far_weight, held(goal_weight, pltpu.HBM), held(adjoint_next, pltpu.HBM), msg)
    after_o, after_i = swap(adj_out_o, "after_o"), swap(adj_out_i, "after_i")

    s1_next, near = pl.pallas_call(
        prepare_next,
        out_shape=[pltpu.VMEM(pair, jnp.float32), pltpu.VMEM(plane, jnp.float32)],
        in_specs=[pl.BlockSpec(memory_space=pltpu.SMEM)] * 2
        + [pl.BlockSpec(memory_space=pltpu.VMEM)] * 6
        + [pl.BlockSpec(memory_space=pl.ANY)] * 2,
        out_specs=[pl.BlockSpec(memory_space=pltpu.VMEM)] * 2,
        scratch_shapes=[pltpu.VMEM((2, 1) + plane, jnp.float32)] * 4,
        compiler_params=pltpu.CompilerParams(vmem_limit_bytes=VMEM_LIMIT),
        cost_estimate=cost_of(LONG),
        name="prepare_next",
    )(
        core,
        held(scal, pltpu.SMEM),
        *[held(x, pltpu.VMEM) for x in (speed, direction_mask, decay_rate, control)],
        *[held(x, pltpu.VMEM) for x in states],
        msg,
        near_edge,
    )

    s2 = list(on_core(second_inner, [plane] * 2, both, states + [msg, s1_in, s1_next] + fields + [ctl]))
    s2_next = [swap(s2[1], "s2_far"), swap(s2[0], "s2_own")]
    (base,) = on_core(third_stage, [four], both, states + [msg] + s2 + s2_next + [near_edge] + fields + [ctl])
    final_own, final_far, terms, msg3, partials = on_core(
        turn,
        [pair, pair, four, four, pair],
        [scal, weights],
        [halo2, base] + fields + [goals, adj, after_o, after_i],
    )
    halo3 = pass_on(msg3, "back2")
    part, cost, *pins = on_core(
        turn_inner,
        [pair, (8, columns)] + [(r, columns) for r in cut(4 * rows + 8, 3)],
        [scal, weights],
        [final_own, final_far, terms] + fields + [goals],
    )
    theirs = [swap(x, "pin") for x in pins]
    base, a2, cost = on_core(
        back_second,
        [four, pair, (8, 128)],
        [scal],
        [msg3, partials, part, near_edge, near] + fields + [cost] + pins + theirs,
    )
    whole = sections & (sections - 1) == 0
    steps = [1 << k for k in range(sections.bit_length() - 1)] if whole else []
    steps = steps[1:] + steps[:1]

    def from_pair(x, k):
        with jax.named_scope("goal_sum"):
            if k >= len(steps):
                return jnp.zeros_like(x)
            return lax.ppermute(x, "space", [(i, i ^ steps[k]) for i in range(sections)])

    for k in range(len(steps) - 2):
        cost = cost + from_pair(cost, k)
    a1, msg4_far, msg4_own, cost = on_core(
        second_back_edge,
        [pair, plane, plane, (8, 128)],
        [scal],
        [halo3, base] + fields + [cost, from_pair(cost, max(0, len(steps) - 2))],
    )
    halo4_own = pass_on(msg4_far, "back1_far")
    halo4_far = pass_on(msg4_own, "back1_own", along)
    keep, part, *out = on_core(
        close,
        [sides, three, sides] + [(r, columns) for r in cut(3 * rows, 2)],
        both,
        [terms, partials, halo3, a1, a2, base] + fields + [ctl],
    )
    parts = [swap(x, "adjoint") for x in out[1:]]
    taken = swap(out[0], "gradient")
    outer, add, cost = on_core(
        last_edge,
        [plane, plane, (8, 128)],
        [],
        [halo4_own, halo4_far, part, cost, from_pair(cost, max(1, len(steps) - 1))],
        cost=LONG,
    )
    if not whole:
        cost = lax.psum(cost, "space")
    adjoint, gradient, objective = on_core(
        functools.partial(assemble, sections * layers * rows * columns),
        [(1, layers, rows, columns), (layers, rows, columns // 2), (1,)],
        [core],
        [part, outer, add, cost, keep, taken] + parts,
        hbm_out=(0, 1),
        smem_out=(2,),
        name="assemble",
    )
    return (adjoint, gradient, objective)


def solution(mesh):
    return jax.shard_map(
        shards,
        mesh=mesh,
        in_specs=(
            P("node", ("groups", "space"), None, None),
            P("node", ("groups", "space"), None, None),
            P(None, ("groups", "space"), None, None),
            P(None, ("groups", "space"), None, None),
            P(("groups", "space"), None, None),
            P(("groups", "space"), None, None),
            P(("groups", "space"), None, None),
            P("node", None),
            P("node"),
            P("groups"),
        ),
        out_specs=(
            P("node", ("groups", "space"), None, None),
            P(("groups", "space"), None, "node"),
            P("groups"),
        ),
        check_vma=False,
    )
```

time: 72.5 us -> 60.2 us (0.83)
  starting transfers between devices: 48.6 us -> 38.8 us
  Pallas kernels: 10.6 us -> 12.2 us
  between operations: 2.22 us -> 0.89 us
  waiting for transfers between devices: 8.91 us -> 7.72 us
  local copies, waits for them, and re-layouts: 0.95 us -> 0.02 us
    ppermute x14 -> x15, starting transfers between devices: 36.4 us -> 27.1 us  [swap(): return lax.ppermute(x, AXES, within)]
    pallas_call x0 -> x3, Pallas kernels: none -> 3.88 us  [the longest x1 2.28 us: shards(): pl.pallas_call(lambda *refs: prepare_back(*refs[:5], *refs[6:]), out_shap...]
    ppermute x9 -> x6, starting transfers between devices: 6.67 us -> 4.83 us  [pass_on(): return lax.ppermute(x, AXES, pairs)]
    ppermute x3, waiting for transfers between devices: 5.61 us -> 3.95 us  [from_pair(): lax.ppermute(x, 'space', [(i, i ^ steps[k]) for i in range(sections)])]
    ppermute x3, starting transfers between devices: 5.5 us -> 6.93 us  [from_pair(): lax.ppermute(x, 'space', [(i, i ^ steps[k]) for i in range(sections)])]
    ppermute x14 -> x15, waiting for transfers between devices: 2.39 us -> 3.75 us  [swap(): return lax.ppermute(x, AXES, within)]
    pallas_call x1, Pallas kernels: 2.97 us -> 1.71 us  [shards(): pl.pallas_call(prepare, out_shape=[pltpu.SMEM((2, 8), jnp.float32)] + [pl...]
    pallas_call x16 -> x11, Pallas kernels: 7.63 us -> 6.58 us  [on_core(): pl.pallas_call(run, out_shape=out_shape, in_specs=[pl.BlockSpec(memory_sp...]
  transfers between devices with their start and end apart: 26 -> 24, of which waited for: 7 -> 9; matrix products, arithmetic and copies ran while one was open for 1% -> 0% of each run, Pallas kernels for 13% -> 17%
where the time goes in v4:
time: 60.2 us; the launch traced here: 59.6 us
  starting transfers between devices  38.8 us (64%)
  Pallas kernels  12.2 us (20%)
  waiting for transfers between devices  7.72 us (13%)
  between operations  0.89 us (1%)
    ppermute x15, starting transfers between devices, swap(): return lax.ppermute(x, AXES, within)  27.1 us
    ppermute x3, starting transfers between devices, from_pair(): lax.ppermute(x, 'space', [(i, i ^ steps[k]) for i in range(sections)])  6.93 us
    pallas_call x11, Pallas kernels, on_core(): pl.pallas_call(run, out_shape=out_shape, in_specs=[pl.BlockSpec(memory_sp...  6.58 us
    ppermute x6, starting transfers between devices, pass_on(): return lax.ppermute(x, AXES, pairs)  4.83 us
    ppermute x3, waiting for transfers between devices, from_pair(): lax.ppermute(x, 'space', [(i, i ^ steps[k]) for i in range(sections)])  3.95 us
    ppermute x15, waiting for transfers between devices, swap(): return lax.ppermute(x, AXES, within)  3.75 us
    pallas_call x1, Pallas kernels, shards(): pl.pallas_call(lambda *refs: prepare_back(*refs[:5], *refs[6:]), out_shap...  2.28 us
    pallas_call x1, Pallas kernels, shards(): pl.pallas_call(prepare, out_shape=[pltpu.SMEM((2, 8), jnp.float32)] + [pl...  1.71 us
  transfers between devices with their start and end apart: 24, of which 9 were waited for; matrix products, arithmetic and copies ran while one was open for 0% of the time, Pallas kernels for 17%

profile of v4, /device:TPU:0, one launch (start us, length us, event | category | flops | bytes accessed | tf_op | source)
XLA Modules:
  0.0 59.6 jit_solution(12418290873549243711)
XLA Ops:
  0.6 0.5 collective-permute-start.4
  1.7 1.1 %collective-permute-done.2.refs_2_ = s32[1]{0:T(128)} collective-permute-done((s32[1]{0:T(128)}, s32[1]{0:T(128)}, u32[]{:S(2)}, u32[]{:S(2)}) %collective-permute-start.2) | collective-permute-done | bytes 36 | tf_op jit(solution)/shard_map/swap_weight_num/ppermute | solution.py:390
  3.2 1.1 %pack.1 = f32[2,64,512]{2,1,0:T(8,128)S(1)} custom-call(s32[1]{0:T(128)} %bitcast.core.refs_0_, f32[1,4,64,512]{3,2,1,0:T(8,128)} %refs_2_.5, f32[1,4,64,512]{3,2,1,0:T(8,128)S(1)} %collective-permute-done.4.far.refs_3_), custom_call_target="tpu_custom_call" | custom-call | flops 40000000000 | bytes 120000000 | tf_op jit(solution)/shard_map/pack/pallas_call | solution.py:407
  4.2 0.8 %collective-permute-start.5 = (f32[2,64,512]{2,1,0:T(8,128)S(1)}, f32[2,64,512]{2,1,0:T(8,128)S(1)}, u32[]{:S(2)}, u32[]{:S(2)}) collective-permute-start(f32[2,64,512]{2,1,0:T(8,128)S(1)} %pack.1), channel_id=1, source_target_pairs={{1,2},{2,1},{3,4},{4,3},{5,6},{6,5},{7,8},{8,7},{9,10},{10,9},{11,... | collective-permute-start | bytes 786440 | tf_op jit(solution)/shard_map/pass_state/ppermute | solution.py:394
  5.1 1.7 %prepare.1 = (f32[2,8]{1,0:T(2,128)S(4)}, f32[2,2,64,512]{3,2,1,0:T(8,128)S(1)}, f32[2,2,64,512]{3,2,1,0:T(8,128)S(1)}, f32[2,2,64,512]{3,2,1,0:T(8,128)S(1)}, f...) custom-call(s32[1]{0:T(128)} %bitcast.core.refs_0_, s32[1,8]{1,0:T(1,128)} %own_index.1, ...), custom_call_target="tpu_custom_call" | custom-call | flops 40000000000 | bytes 120000000 | tf_op jit(solution)/shard_map/prepare/pallas_call | solution.py:426
  6.8 0.7 %collective-permute-start.7 = (f32[64,512]{1,0:T(8,128)S(1)}, f32[64,512]{1,0:T(8,128)S(1)}, u32[]{:S(2)}, u32[]{:S(2)}) collective-permute-start(f32[64,512]{1,0:T(8,128)S(1)} %get-tuple-element.57), channel_id=1, source_target_pairs={{1,2},{2,1},{3,4},{4,3},{5,6},{6,5},{7,8},{8,7},{9,10},{10,9},{11,... | collective-permute-start | bytes 393224 | tf_op jit(solution)/shard_map/pass_edge/ppermute | solution.py:394
  7.5 0.7 %first_stage.1 = (f32[2,64,512]{2,1,0:T(8,128)S(1)}, f32[2,64,512]{2,1,0:T(8,128)S(1)}, f32[2,64,512]{2,1,0:T(8,128)S(1)}) custom-call(s32[1]{0:T(128)} %bitcast.core.refs_0_, f32[2,8]{1,0:T(2,128)S(4)} %get-tuple-element.47.refs_1_.refs_0_.scal, f32[1,4,64,512]{3,2,1,0:T(8,128)S(1)} %copy-done, f32[1,4,64,512]{3,2,1,0:T(8,128)S(1)} %collective-permute-done.4.far.refs_3_, ...), custom_call_target="tpu_custom_call" | custom-call | tf_op jit(solution)/shard_map/first_stage/pallas_call | solution.py:355
  8.6 0.7 %collective-permute-start.6 = (f32[2,2,64,512]{3,2,1,0:T(8,128)S(1)}, f32[2,2,64,512]{3,2,1,0:T(8,128)S(1)}, u32[]{:S(2)}, u32[]{:S(2)}) collective-permute-start(f32[2,2,64,512]{3,2,1,0:T(8,128)S(1)} %first_edge.1.refs_5_._.refs_4_), channel_id=1, source_target_pairs={{1,2},{2,1},{3,4},{4,3},{5,6},{6,5},{7,8},{8,7},{9,10},{10,9},{11,... | collective-permute-start | bytes 1572872 | tf_op jit(solution)/shard_map/pass_stage2/ppermute | solution.py:394
  9.3 0.5 prepare_next.1
  10.2 10.7 %collective-permute-start.9 = (f32[64,512]{1,0:T(8,128)S(1)}, f32[64,512]{1,0:T(8,128)S(1)}, u32[]{:S(2)}, u32[]{:S(2)}) collective-permute-start(f32[64,512]{1,0:T(8,128)S(1)} %get-tuple-element.59.refs_5_), channel_id=1, source_target_pairs={{0,1},{1,0},{2,3},{3,2},{4,5},{5,4},{6,7},{7,6},{8,9},{9,8},{10,11... | collective-permute-start | bytes 393224 | tf_op jit(solution)/shard_map/swap_s2_own/ppermute | solution.py:390
  21.0 2.3 %prepare_back.1 = (f32[2]{0:T(128)S(4)}, f32[2,64,512]{2,1,0:T(8,128)S(1)}, f32[2,64,512]{2,1,0:T(8,128)S(1)}, f32[64,512]{1,0:T(8,128)S(1)}, f32[64,512]{1,0:T(8,128)S(1)}) custom-call(s32[1]{0:T(128)} %bitcast.core.refs_0_, s32[1]{0:T(128)} %collective-permute-done.3.refs_1_, s32[1]{0:T(128)} %collective-permute-done.2.refs_2_, ...), custom_call_target="tpu_custom_call" | custom-call | tf_op jit(solution)/shard_map/prepare_back/pallas_call | solution.py:456
  23.3 0.5 collective-permute-start.10
  23.9 0.8 %third_stage.1.refs_3_ = f32[2,2,64,512]{3,2,1,0:T(8,128)S(1)} custom-call(s32[1]{0:T(128)} %bitcast.core.refs_0_, f32[2,8]{1,0:T(2,128)S(4)} %get-tuple-element.47.refs_1_.refs_0_.scal, f32[1,4,64,512]{3,2,1,0:T(8,128)S(1)} %copy-done, f32[1,4,64,512]{3,2,1,0:T(8,128)S(1)} %collective-permute-done.4.far.refs_3_, ...), custom_call_target="tpu_custom_call" | custom-call | tf_op jit(solution)/shard_map/third_stage/pallas_call | solution.py:355
  25.2 0.9 %turn.1 = (f32[2,64,512]{2,1,0:T(8,128)S(1)}, f32[2,64,512]{2,1,0:T(8,128)S(1)}, f32[2,2,64,512]{3,2,1,0:T(8,128)S(1)}, f32[2,2,64,512]{3,2,1,0:T(8,128)S(1)}, f32[2,64,512]{2,1,0:T(8,128)S(1)}) custom-call(f32[2,8]{1,0:T(2,128)S(4)} %get-tuple-element.47.refs_1_.refs_0_.scal, f32[2]{0:T(128)S(4)} %get-tuple-element.55.refs_1_, ...), custom_call_target="tpu_custom_call" | custom-call | tf_op jit(solution)/shard_map/turn/pallas_call | solution.py:355
  26.0 0.7 %collective-permute-start.12 = (f32[2,2,64,512]{3,2,1,0:T(8,128)S(1)}, f32[2,2,64,512]{3,2,1,0:T(8,128)S(1)}, u32[]{:S(2)}, u32[]{:S(2)}) collective-permute-start(f32[2,2,64,512]{3,2,1,0:T(8,128)S(1)} %get-tuple-element.67.refs_1_), channel_id=1, source_target_pairs={{1,2},{2,1},{3,4},{4,3},{5,6},{6,5},{7,8},{8,7},{9,10},{10,9},{11,... | collective-permute-start | bytes 1572872 | tf_op jit(solution)/shard_map/pass_back2/ppermute | solution.py:394
  26.7 0.5 turn_inner.1
  27.3 10.1 %collective-permute-start.13 = (f32[88,512]{1,0:T(8,128)S(1)}, f32[88,512]{1,0:T(8,128)S(1)}, u32[]{:S(2)}, u32[]{:S(2)}) collective-permute-start(f32[88,512]{1,0:T(8,128)S(1)} %get-tuple-element.73.refs_11_), channel_id=1, source_target_pairs={{0,1},{1,0},{2,3},{3,2},{4,5},{5,4},{6,7},{7,6},{8,9},{9,8},{10,11... | collective-permute-start | bytes 540680 | tf_op jit(solution)/shard_map/swap_pin/ppermute | solution.py:390
  37.5 0.4 collective-permute-start.15
  37.9 0.5 collective-permute-done.13.refs_14_
  39.1 0.7 %back_second.1 = (f32[2,2,64,512]{3,2,1,0:T(8,128)S(1)}, f32[2,64,512]{2,1,0:T(8,128)S(1)}, f32[8,128]{1,0:T(8,128)S(1)}) custom-call(f32[2,8]{1,0:T(2,128)S(4)} %get-tuple-element.47.refs_1_.refs_0_.scal, f32[2,2,64,512]{3,2,1,0:T(8,128)S(1)} %get-tuple-element.67.refs_1_, f32[2,64,512]{2,1,0:T(8,128)S(1)} %get-tuple-element.66.refs_2_.refs_3_, ...), custom_call_target="tpu_custom_call" | custom-call | tf_op jit(solution)/shard_map/back_second/pallas_call | solution.py:355
  39.8 1.6 %collective-permute-start.16 = (f32[8,128]{1,0:T(8,128)S(1)}, f32[8,128]{1,0:T(8,128)S(1)}, u32[]{:S(2)}, u32[]{:S(2)}) collective-permute-start(f32[8,128]{1,0:T(8,128)S(1)} %get-tuple-element.77), channel_id=1, source_target_pairs={{0,4},{2,6},{4,0},{6,2},{8,12},{10,14},{12,8},{14,10},{1,5},{3,7},... | collective-permute-start | bytes 12296 | tf_op jit(solution)/shard_map/goal_sum/ppermute | solution.py:520
  41.5 2.0 %collective-permute-done.16 = f32[8,128]{1,0:T(8,128)S(1)} collective-permute-done((f32[8,128]{1,0:T(8,128)S(1)}, f32[8,128]{1,0:T(8,128)S(1)}, u32[]{:S(2)}, u32[]{:S(2)}) %collective-permute-start.16) | collective-permute-done | bytes 4128 | tf_op jit(solution)/shard_map/goal_sum/ppermute | solution.py:520
  43.5 2.6 %collective-permute-start.17 = (f32[8,128]{1,0:T(8,128)S(1)}, f32[8,128]{1,0:T(8,128)S(1)}, u32[]{:S(2)}, u32[]{:S(2)}) collective-permute-start(f32[8,128]{1,0:T(8,128)S(1)} %add.3.refs_7_), channel_id=1, source_target_pairs={{0,8},{2,10},{4,12},{6,14},{8,0},{10,2},{12,4},{14,6},{1,9},{3,11}... | collective-permute-start | bytes 12296 | tf_op jit(solution)/shard_map/goal_sum/ppermute | solution.py:520
  46.1 1.9 %collective-permute-done.17.refs_8_ = f32[8,128]{1,0:T(8,128)S(1)} collective-permute-done((f32[8,128]{1,0:T(8,128)S(1)}, f32[8,128]{1,0:T(8,128)S(1)}, u32[]{:S(2)}, u32[]{:S(2)}) %collective-permute-start.17) | collective-permute-done | bytes 4128 | tf_op jit(solution)/shard_map/goal_sum/ppermute | solution.py:520
  48.4 0.7 %collective-permute-start.18 = (f32[64,512]{1,0:T(8,128)S(1)}, f32[64,512]{1,0:T(8,128)S(1)}, u32[]{:S(2)}, u32[]{:S(2)}) collective-permute-start(f32[64,512]{1,0:T(8,128)S(1)} %get-tuple-element.81), channel_id=1, source_target_pairs={{1,2},{2,1},{3,4},{4,3},{5,6},{6,5},{7,8},{8,7},{9,10},{10,9},{11,... | collective-permute-start | bytes 393224 | tf_op jit(solution)/shard_map/pass_back1_far/ppermute | solution.py:394
  49.1 1.3 %collective-permute-start.19 = (f32[64,512]{1,0:T(8,128)S(1)}, f32[64,512]{1,0:T(8,128)S(1)}, u32[]{:S(2)}, u32[]{:S(2)}) collective-permute-start(f32[64,512]{1,0:T(8,128)S(1)} %get-tuple-element.82), channel_id=1, source_target_pairs={{1,3},{2,0},{3,5},{4,2},{5,7},{6,4},{7,9},{8,6},{9,11},{10,8},{11,... | collective-permute-start | bytes 393224 | tf_op jit(solution)/shard_map/pass_back1_own/ppermute | solution.py:394
  50.4 2.7 %collective-permute-start.20 = (f32[8,128]{1,0:T(8,128)S(1)}, f32[8,128]{1,0:T(8,128)S(1)}, u32[]{:S(2)}, u32[]{:S(2)}) collective-permute-start(f32[8,128]{1,0:T(8,128)S(1)} %get-tuple-element.83.refs_3_), channel_id=1, source_target_pairs={{0,2},{2,0},{4,6},{6,4},{8,10},{10,8},{12,14},{14,12},{1,3},{3,1},... | collective-permute-start | bytes 12296 | tf_op jit(solution)/shard_map/goal_sum/ppermute | solution.py:520
  53.1 0.9 %close.1 = (f32[2,64,256]{2,1,0:T(8,128)S(1)}, f32[3,64,512]{2,1,0:T(8,128)S(1)}, f32[2,64,256]{2,1,0:T(8,128)S(1)}, f32[96,512]{1,0:T(8,128)S(1)}, f32[96,512]{1,0:T(8,128)S(1)}) custom-call(s32[1]{0:T(128)} %bitcast.core.refs_0_, f32[2,8]{1,0:T(2,128)S(4)} %get-tuple-element.47.refs_1_.refs_0_.scal, ...), custom_call_target="tpu_custom_call" | custom-call | tf_op jit(solution)/shard_map/close/pallas_call | solution.py:355
  53.9 2.2 %collective-permute-start.21 = (f32[2,64,256]{2,1,0:T(8,128)S(1)}, f32[2,64,256]{2,1,0:T(8,128)S(1)}, u32[]{:S(2)}, u32[]{:S(2)}) collective-permute-start(f32[2,64,256]{2,1,0:T(8,128)S(1)} %get-tuple-element.88), channel_id=1, source_target_pairs={{0,1},{1,0},{2,3},{3,2},{4,5},{5,4},{6,7},{7,6},{8,9},{9,8},{10,11... | collective-permute-start | bytes 393224 | tf_op jit(solution)/shard_map/swap_gradient/ppermute | solution.py:390
  56.2 1.4 %collective-permute-start.23 = (f32[96,512]{1,0:T(8,128)S(1)}, f32[96,512]{1,0:T(8,128)S(1)}, u32[]{:S(2)}, u32[]{:S(2)}) collective-permute-start(f32[96,512]{1,0:T(8,128)S(1)} %get-tuple-element.90), channel_id=1, source_target_pairs={{0,1},{1,0},{2,3},{3,2},{4,5},{5,4},{6,7},{7,6},{8,9},{9,8},{10,11... | collective-permute-start | bytes 589832 | tf_op jit(solution)/shard_map/swap_adjoint/ppermute | solution.py:390
  57.7 1.0 %collective-permute-done.23.refs_8_ = f32[96,512]{1,0:T(8,128)S(1)} collective-permute-done((f32[96,512]{1,0:T(8,128)S(1)}, f32[96,512]{1,0:T(8,128)S(1)}, u32[]{:S(2)}, u32[]{:S(2)}) %collective-permute-start.23) | collective-permute-done | bytes 196640 | tf_op jit(solution)/shard_map/swap_adjoint/ppermute | solution.py:390
  58.7 1.0 %assemble.1 = (f32[1,4,64,512]{3,2,1,0:T(8,128)}, f32[4,64,256]{2,1,0:T(8,128)}, f32[1]{0:T(128)}) custom-call(s32[1]{0:T(128)} %bitcast.core.refs_0_, f32[3,64,512]{2,1,0:T(8,128)S(1)} %get-tuple-element.80.refs_2_.refs_1_, f32[64,512]{1,0:T(8,128)S(1)} %get-tuple-element.84.refs_2_, f32[64,512]{1,0:T(8,128)S(1)} %get-tuple-element.85.refs_3_, ...), custom_call_target="tpu_custom_call" | custom-call | tf_op jit(solution)/shard_map/assemble/pallas_call | solution.py:355
  (42 shorter events, 3.5 us)
Async XLA Ops:
  0.6 2.5 %collective-permute-start.4 = (f32[1,4,64,512]{3,2,1,0:T(8,128)}, f32[1,4,64,512]{3,2,1,0:T(8,128)S(1)}, u32[]{:S(2)}, u32[]{:S(2)}) collective-permute-start(f32[1,4,64,512]{3,2,1,0:T(8,128)} %refs_2_.5), channel_id=1, source_target_pairs={{0,1},{1,0},{2,3},{3,2},{4,5},{5,4},{6,7},{7,6},{8,9},{9,8},{10,11... | collective-permute-start | bytes 1572872 | tf_op jit(solution)/shard_map/swap_state/ppermute | solution.py:390
  1.2 3.9 %collective-permute-start = (s32[1,8]{1,0:T(1,128)}, s32[1,8]{1,0:T(1,128)S(1)}, u32[]{:S(2)}, u32[]{:S(2)}) collective-permute-start(s32[1,8]{1,0:T(1,128)} %own_index.1), channel_id=1, source_target_pairs={{0,1},{1,0},{2,3},{3,2},{4,5},{5,4},{6,7},{7,6},{8,9},{9,8},{10,11... | collective-permute-start | bytes 104 | tf_op jit(solution)/shard_map/swap_node_index/ppermute | solution.py:390
  1.2 1.6 %collective-permute-start.2 = (s32[1]{0:T(128)}, s32[1]{0:T(128)}, u32[]{:S(2)}, u32[]{:S(2)}) collective-permute-start(s32[1]{0:T(128)} %param.18), channel_id=1, source_target_pairs={{0,1},{1,0},{2,3},{3,2},{4,5},{5,4},{6,7},{7,6},{8,9},{9,8},{10,11... | collective-permute-start | bytes 20 | tf_op jit(solution)/shard_map/swap_weight_num/ppermute | solution.py:390
  1.7 3.4 %collective-permute-start.1 = (s32[1]{0:T(128)}, s32[1]{0:T(128)}, u32[]{:S(2)}, u32[]{:S(2)}) collective-permute-start(s32[1]{0:T(128)} %param.19), channel_id=1, source_target_pairs={{0,1},{1,0},{2,3},{3,2},{4,5},{5,4},{6,7},{7,6},{8,9},{9,8},{10,11... | collective-permute-start | bytes 20 | tf_op jit(solution)/shard_map/swap_step/ppermute | solution.py:390
  2.8 18.2 %collective-permute-start.3 = (s32[1]{0:T(128)}, s32[1]{0:T(128)}, u32[]{:S(2)}, u32[]{:S(2)}) collective-permute-start(s32[1]{0:T(128)} %collective-permute-done.2.refs_2_), channel_id=1, source_target_pairs={{0,1},{1,0},{2,3},{3,2},{4,5},{5,4},{6,7},{7,6},{8,9},{9,8},{10,11... | collective-permute-start | bytes 20 | tf_op jit(solution)/shard_map/swap_weight_num/ppermute | solution.py:390
  3.1 1.9 %copy-start.1 = (bf16[3,4,64,512]{3,2,1,0:T(8,128)(2,1)S(1)}, bf16[3,4,64,512]{3,2,1,0:T(8,128)(2,1)}, u32[]{:S(2)}) copy-start(bf16[3,4,64,512]{3,2,1,0:T(8,128)(2,1)} %speed.3) | copy-start | bytes 2359300
  3.1 1.9 %copy-start.2 = (f32[4,64,512]{2,1,0:T(8,128)S(1)}, f32[4,64,512]{2,1,0:T(8,128)}, u32[]{:S(2)}) copy-start(f32[4,64,512]{2,1,0:T(8,128)} %control.3) | copy-start | bytes 1572868
  3.1 2.0 %copy-start.3 = (s32[3,4,64,64]{3,2,1,0:T(8,128)S(1)}, s32[3,4,64,64]{3,2,1,0:T(8,128)}, u32[]{:S(2)}) copy-start(s32[3,4,64,64]{3,2,1,0:T(8,128)} %mask.3) | copy-start | bytes 589828
  3.1 2.0 %copy-start.4 = (bf16[4,64,512]{2,1,0:T(8,128)(2,1)S(1)}, bf16[4,64,512]{2,1,0:T(8,128)(2,1)}, u32[]{:S(2)}) copy-start(bf16[4,64,512]{2,1,0:T(8,128)(2,1)} %decay.3) | copy-start | bytes 786436
  4.2 3.3 %copy-start = (f32[1,4,64,512]{3,2,1,0:T(8,128)S(1)}, f32[1,4,64,512]{3,2,1,0:T(8,128)}, u32[]{:S(2)}) copy-start(f32[1,4,64,512]{3,2,1,0:T(8,128)} %refs_2_.5) | copy-start | bytes 1572868
  4.2 4.0 %collective-permute-start.5 = (f32[2,64,512]{2,1,0:T(8,128)S(1)}, f32[2,64,512]{2,1,0:T(8,128)S(1)}, u32[]{:S(2)}, u32[]{:S(2)}) collective-permute-start(f32[2,64,512]{2,1,0:T(8,128)S(1)} %pack.1), channel_id=1, source_target_pairs={{1,2},{2,1},{3,4},{4,3},{5,6},{6,5},{7,8},{8,7},{9,10},{10,9},{11,... | collective-permute-start | bytes 786440 | tf_op jit(solution)/shard_map/pass_state/ppermute | solution.py:394
  6.8 2.4 %collective-permute-start.7 = (f32[64,512]{1,0:T(8,128)S(1)}, f32[64,512]{1,0:T(8,128)S(1)}, u32[]{:S(2)}, u32[]{:S(2)}) collective-permute-start(f32[64,512]{1,0:T(8,128)S(1)} %get-tuple-element.57), channel_id=1, source_target_pairs={{1,2},{2,1},{3,4},{4,3},{5,6},{6,5},{7,8},{8,7},{9,10},{10,9},{11,... | collective-permute-start | bytes 393224 | tf_op jit(solution)/shard_map/pass_edge/ppermute | solution.py:394
  8.6 16.6 %collective-permute-start.6 = (f32[2,2,64,512]{3,2,1,0:T(8,128)S(1)}, f32[2,2,64,512]{3,2,1,0:T(8,128)S(1)}, u32[]{:S(2)}, u32[]{:S(2)}) collective-permute-start(f32[2,2,64,512]{3,2,1,0:T(8,128)S(1)} %first_edge.1.refs_5_._.refs_4_), channel_id=1, source_target_pairs={{1,2},{2,1},{3,4},{4,3},{5,6},{6,5},{7,8},{8,7},{9,10},{10,9},{11,... | collective-permute-start | bytes 1572872 | tf_op jit(solution)/shard_map/pass_stage2/ppermute | solution.py:394
  10.2 13.7 %collective-permute-start.9 = (f32[64,512]{1,0:T(8,128)S(1)}, f32[64,512]{1,0:T(8,128)S(1)}, u32[]{:S(2)}, u32[]{:S(2)}) collective-permute-start(f32[64,512]{1,0:T(8,128)S(1)} %get-tuple-element.59.refs_5_), channel_id=1, source_target_pairs={{0,1},{1,0},{2,3},{3,2},{4,5},{5,4},{6,7},{7,6},{8,9},{9,8},{10,11... | collective-permute-start | bytes 393224 | tf_op jit(solution)/shard_map/swap_s2_own/ppermute | solution.py:390
  21.0 2.9 %collective-permute-start.8 = (f32[64,512]{1,0:T(8,128)S(1)}, f32[64,512]{1,0:T(8,128)S(1)}, u32[]{:S(2)}, u32[]{:S(2)}) collective-permute-start(f32[64,512]{1,0:T(8,128)S(1)} %get-tuple-element.60.refs_6_), channel_id=1, source_target_pairs={{0,1},{1,0},{2,3},{3,2},{4,5},{5,4},{6,7},{7,6},{8,9},{9,8},{10,11... | collective-permute-start | bytes 393224 | tf_op jit(solution)/shard_map/swap_s2_far/ppermute | solution.py:390
  23.3 1.5 %collective-permute-start.10 = (f32[64,512]{1,0:T(8,128)S(1)}, f32[64,512]{1,0:T(8,128)S(1)}, u32[]{:S(2)}, u32[]{:S(2)}) collective-permute-start(f32[64,512]{1,0:T(8,128)S(1)} %get-tuple-element.63), channel_id=1, source_target_pairs={{0,1},{1,0},{2,3},{3,2},{4,5},{5,4},{6,7},{7,6},{8,9},{9,8},{10,11... | collective-permute-start | bytes 393224 | tf_op jit(solution)/shard_map/swap_after_o/ppermute | solution.py:390
  23.8 1.3 %collective-permute-start.11 = (f32[64,512]{1,0:T(8,128)S(1)}, f32[64,512]{1,0:T(8,128)S(1)}, u32[]{:S(2)}, u32[]{:S(2)}) collective-permute-start(f32[64,512]{1,0:T(8,128)S(1)} %get-tuple-element.64), channel_id=1, source_target_pairs={{0,1},{1,0},{2,3},{3,2},{4,5},{5,4},{6,7},{7,6},{8,9},{9,8},{10,11... | collective-permute-start | bytes 393224 | tf_op jit(solution)/shard_map/swap_after_i/ppermute | solution.py:390
  26.0 22.0 %collective-permute-start.12 = (f32[2,2,64,512]{3,2,1,0:T(8,128)S(1)}, f32[2,2,64,512]{3,2,1,0:T(8,128)S(1)}, u32[]{:S(2)}, u32[]{:S(2)}) collective-permute-start(f32[2,2,64,512]{3,2,1,0:T(8,128)S(1)} %get-tuple-element.67.refs_1_), channel_id=1, source_target_pairs={{1,2},{2,1},{3,4},{4,3},{5,6},{6,5},{7,8},{8,7},{9,10},{10,9},{11,... | collective-permute-start | bytes 1572872 | tf_op jit(solution)/shard_map/pass_back2/ppermute | solution.py:394
  27.3 11.1 %collective-permute-start.13 = (f32[88,512]{1,0:T(8,128)S(1)}, f32[88,512]{1,0:T(8,128)S(1)}, u32[]{:S(2)}, u32[]{:S(2)}) collective-permute-start(f32[88,512]{1,0:T(8,128)S(1)} %get-tuple-element.73.refs_11_), channel_id=1, source_target_pairs={{0,1},{1,0},{2,3},{3,2},{4,5},{5,4},{6,7},{7,6},{8,9},{9,8},{10,11... | collective-permute-start | bytes 540680 | tf_op jit(solution)/shard_map/swap_pin/ppermute | solution.py:390
  37.4 1.4 %collective-permute-start.14 = (f32[88,512]{1,0:T(8,128)S(1)}, f32[88,512]{1,0:T(8,128)S(1)}, u32[]{:S(2)}, u32[]{:S(2)}) collective-permute-start(f32[88,512]{1,0:T(8,128)S(1)} %get-tuple-element.74.refs_12_), channel_id=1, source_target_pairs={{0,1},{1,0},{2,3},{3,2},{4,5},{5,4},{6,7},{7,6},{8,9},{9,8},{10,11... | collective-permute-start | bytes 540680 | tf_op jit(solution)/shard_map/swap_pin/ppermute | solution.py:390
  37.5 1.6 %collective-permute-start.15 = (f32[88,512]{1,0:T(8,128)S(1)}, f32[88,512]{1,0:T(8,128)S(1)}, u32[]{:S(2)}, u32[]{:S(2)}) collective-permute-start(f32[88,512]{1,0:T(8,128)S(1)} %get-tuple-element.75.refs_13_), channel_id=1, source_target_pairs={{0,1},{1,0},{2,3},{3,2},{4,5},{5,4},{6,7},{7,6},{8,9},{9,8},{10,11... | collective-permute-start | bytes 540680 | tf_op jit(solution)/shard_map/swap_pin/ppermute | solution.py:390
  39.8 3.7 %collective-permute-start.16 = (f32[8,128]{1,0:T(8,128)S(1)}, f32[8,128]{1,0:T(8,128)S(1)}, u32[]{:S(2)}, u32[]{:S(2)}) collective-permute-start(f32[8,128]{1,0:T(8,128)S(1)} %get-tuple-element.77), channel_id=1, source_target_pairs={{0,4},{2,6},{4,0},{6,2},{8,12},{10,14},{12,8},{14,10},{1,5},{3,7},... | collective-permute-start | bytes 12296 | tf_op jit(solution)/shard_map/goal_sum/ppermute | solution.py:520
  43.5 4.5 %collective-permute-start.17 = (f32[8,128]{1,0:T(8,128)S(1)}, f32[8,128]{1,0:T(8,128)S(1)}, u32[]{:S(2)}, u32[]{:S(2)}) collective-permute-start(f32[8,128]{1,0:T(8,128)S(1)} %add.3.refs_7_), channel_id=1, source_target_pairs={{0,8},{2,10},{4,12},{6,14},{8,0},{10,2},{12,4},{14,6},{1,9},{3,11}... | collective-permute-start | bytes 12296 | tf_op jit(solution)/shard_map/goal_sum/ppermute | solution.py:520
  48.4 9.2 %collective-permute-start.18 = (f32[64,512]{1,0:T(8,128)S(1)}, f32[64,512]{1,0:T(8,128)S(1)}, u32[]{:S(2)}, u32[]{:S(2)}) collective-permute-start(f32[64,512]{1,0:T(8,128)S(1)} %get-tuple-element.81), channel_id=1, source_target_pairs={{1,2},{2,1},{3,4},{4,3},{5,6},{6,5},{7,8},{8,7},{9,10},{10,9},{11,... | collective-permute-start | bytes 393224 | tf_op jit(solution)/shard_map/pass_back1_far/ppermute | solution.py:394
  49.1 8.6 %collective-permute-start.19 = (f32[64,512]{1,0:T(8,128)S(1)}, f32[64,512]{1,0:T(8,128)S(1)}, u32[]{:S(2)}, u32[]{:S(2)}) collective-permute-start(f32[64,512]{1,0:T(8,128)S(1)} %get-tuple-element.82), channel_id=1, source_target_pairs={{1,3},{2,0},{3,5},{4,2},{5,7},{6,4},{7,9},{8,6},{9,11},{10,8},{11,... | collective-permute-start | bytes 393224 | tf_op jit(solution)/shard_map/pass_back1_own/ppermute | solution.py:394
  50.4 5.8 %collective-permute-start.20 = (f32[8,128]{1,0:T(8,128)S(1)}, f32[8,128]{1,0:T(8,128)S(1)}, u32[]{:S(2)}, u32[]{:S(2)}) collective-permute-start(f32[8,128]{1,0:T(8,128)S(1)} %get-tuple-element.83.refs_3_), channel_id=1, source_target_pairs={{0,2},{2,0},{4,6},{6,4},{8,10},{10,8},{12,14},{14,12},{1,3},{3,1},... | collective-permute-start | bytes 12296 | tf_op jit(solution)/shard_map/goal_sum/ppermute | solution.py:520
  53.9 3.7 %collective-permute-start.21 = (f32[2,64,256]{2,1,0:T(8,128)S(1)}, f32[2,64,256]{2,1,0:T(8,128)S(1)}, u32[]{:S(2)}, u32[]{:S(2)}) collective-permute-start(f32[2,64,256]{2,1,0:T(8,128)S(1)} %get-tuple-element.88), channel_id=1, source_target_pairs={{0,1},{1,0},{2,3},{3,2},{4,5},{5,4},{6,7},{7,6},{8,9},{9,8},{10,11... | collective-permute-start | bytes 393224 | tf_op jit(solution)/shard_map/swap_gradient/ppermute | solution.py:390
  56.1 1.6 %collective-permute-start.22 = (f32[96,512]{1,0:T(8,128)S(1)}, f32[96,512]{1,0:T(8,128)S(1)}, u32[]{:S(2)}, u32[]{:S(2)}) collective-permute-start(f32[96,512]{1,0:T(8,128)S(1)} %get-tuple-element.89), channel_id=1, source_target_pairs={{0,1},{1,0},{2,3},{3,2},{4,5},{5,4},{6,7},{7,6},{8,9},{9,8},{10,11... | collective-permute-start | bytes 589832 | tf_op jit(solution)/shard_map/swap_adjoint/ppermute | solution.py:390
  56.2 2.5 %collective-permute-start.23 = (f32[96,512]{1,0:T(8,128)S(1)}, f32[96,512]{1,0:T(8,128)S(1)}, u32[]{:S(2)}, u32[]{:S(2)}) collective-permute-start(f32[96,512]{1,0:T(8,128)S(1)} %get-tuple-element.90), channel_id=1, source_target_pairs={{0,1},{1,0},{2,3},{3,2},{4,5},{5,4},{6,7},{7,6},{8,9},{9,8},{10,11... | collective-permute-start | bytes 589832 | tf_op jit(solution)/shard_map/swap_adjoint/ppermute | solution.py:390

commit v5 on v4

--- a/solution.py
+++ b/solution.py
@@ -49,18 +49,19 @@
     return result
 
 
-def node_scales(indices, step, scal):
+def node_scales(tiles, scal):
     levels = [-math.cos(math.pi * k / 8.0) for k in range(9)]
-    half = step[0] & 31
+    step = tiles[0][0, 9].astype(jnp.int32)
+    half = step & 31
     wave = pick([math.sin(2.0 * math.pi * k / 64.0) for k in range(17)], jnp.minimum(half, 32 - half))
-    phase = 1.0 + jnp.where(step[0] < 32, 0.5, -0.5) * wave
-    for j, index in enumerate(indices):
-        p = {k: pick(levels, index[0, k]) for k in (0, 1, 2, 4, 6, 7)}
+    phase = 1.0 + jnp.where(step < 32, 0.5, -0.5) * wave
+    for j, tile in enumerate(tiles):
+        p = {k: pick(levels, tile[0, k]) for k in (0, 1, 2, 4, 6, 7)}
         scal[j, 0] = 1.0 + 0.3 * p[0]
         scal[j, 1] = 1.0 + 0.3 * p[1]
         scal[j, 2] = (1.0 + 0.3 * p[2]) * (1.0 + 0.2 * p[7])
-        scal[j, 3] = pick([math.exp(0.5 * p) for p in levels], index[0, 3]) * pick(
-            [math.exp(0.25 * p) for p in levels], index[0, 5]
+        scal[j, 3] = pick([math.exp(0.5 * p) for p in levels], tile[0, 3]) * pick(
+            [math.exp(0.25 * p) for p in levels], tile[0, 5]
         )
         scal[j, 4] = (1.0 + 0.3 * p[4] + 0.2 * p[6]) * phase
 
@@ -79,9 +80,23 @@
     return up + flip - 2.0 * flip * up
 
 
-def pack(core, own, far, out):
-    out[0] = own[0, 0]
-    out[1] = far[0, 3 * core[0]]
+def begin(out):
+    out[...] = jnp.zeros_like(out)
+
+
+def gather_numbers(index, weight, step, _, numbers):
+    lane = lax.broadcasted_iota(jnp.int32, numbers.shape, 1)
+    value = jnp.zeros(numbers.shape, jnp.int32)
+    for k, number in enumerate([index[0, k] for k in range(index.shape[1])] + [weight[0], step[0]]):
+        value = jnp.where(lane == k, number, value)
+    numbers[...] = value.astype(jnp.float32)
+
+
+def pack(core, own, far, speed, mask, out):
+    at = 3 * core[0]
+    out[0] = own[0, at]
+    out[1] = far[0, at]
+    out[2] = speed[0, at].astype(jnp.float32) * toward_outer(expand(mask[0, at], speed.shape[3]), core[0])
 
 
 def fields_of(k, at, me, speeds, masks, cx, cy, cz):
@@ -107,24 +122,17 @@
         dg[j, k] = sum(scal[j, d] * s[d] for d in range(4))
 
 
-def prepare(core, own_index, far_index, step_index, speed, mask, decay, control, scal, cx, cy, cz, dg, ctl, edge, own_ids, far_ids, step, few):
+def prepare(core, own_numbers, far_numbers, speed, mask, decay, control, scal, cx, cy, cz, dg, ctl):
     me = core[0]
-    small = [(own_index, own_ids), (far_index, far_ids), (step_index, step)]
-    small = [pltpu.make_async_copy(source, target, few.at[n]) for n, (source, target) in enumerate(small)]
-    for copy in small:
-        copy.start()
     for k, at in enumerate((3 * me, 1 + me)):
         fields_of(k, at, me, speed, mask, cx, cy, cz)
         ctl[k] = control[at]
-    edge[...] = cx[0, 0]
-    for copy in small:
-        copy.wait()
-    node_scales((own_ids, far_ids), step, scal)
+    node_scales((own_numbers[...], far_numbers[...]), scal)
     for k, at in enumerate((3 * me, 1 + me)):
         own_of(k, at, decay, speed, scal, dg)
 
 
-def prepare_next(core, scal, speed, mask, decay, control, own, far, _, __, s1_next, near, cx, cy, cz, dg):
+def prepare_next(core, scal, speed, mask, decay, control, own, far, _, s1_next, near, cx, cy, cz, dg):
     me = core[0]
     at = 2 - me
     fields_of(0, at, me, speed, mask, cx, cy, cz)
@@ -137,10 +145,10 @@
         s1_next[j] = value + time_step * (l + a[4] * control[at])
 
 
-def prepare_back(core, own_weight, far_weight, goal, adjoint, weights, goals, adj, adj_out_o, adj_out_i):
+def prepare_back(core, goal, own_numbers, far_numbers, adjoint, _, weights, goals, adj, adj_out_o, adj_out_i):
     me = core[0]
-    weights[0] = own_weight[0].astype(jnp.float32) * (1.0 / weight_denominator)
-    weights[1] = far_weight[0].astype(jnp.float32) * (1.0 / weight_denominator)
+    weights[0] = own_numbers[...][0, 8] * (1.0 / weight_denominator)
+    weights[1] = far_numbers[...][0, 8] * (1.0 / weight_denominator)
     for k, at in enumerate((3 * me, 1 + me)):
         goals[k] = goal[at].astype(jnp.float32)
         adj[k] = adjoint[0, at].astype(jnp.float32)
@@ -178,13 +186,13 @@
         out[...] = 0.75 * c[0, 1 + core[0]] + 0.25 * (s1_i + time_step * (l_i + a[4] * ctl[1]))
 
 
-def third_stage(core, scal, own, far, msg, s2_own, s2_far, next_own, next_far, near_edge, cx, cy, cz, dg, ctl, base):
+def third_stage(core, scal, own, far, msg, s2_own, s2_far, next_own, next_far, halo, cx, cy, cz, dg, ctl, base):
     me = core[0]
     parts = ((own, s2_own, next_own), (far, s2_far, next_far))
     for j, (c, s2, s2_next) in enumerate(parts):
         a = rows_of(scal, j)
         q, s2_i = msg[j, 1], s2[...]
-        back = (0.25 * time_step * a[0]) * (near_edge[...] * msg[j, 0])
+        back = (0.25 * time_step * a[0]) * (halo[2] * msg[j, 0])
         l_o = a[0] * (cx[0, 0] * back + cx[1, 0] * s2_i) + in_plane(q, a, cy, cz, 0) - dg[j, 0] * q
         l_i = a[0] * (cx[0, 1] * q + cx[1, 1] * s2_next[...]) + in_plane(s2_i, a, cy, cz, 1) - dg[j, 1] * s2_i
         base[j, 0] = c[0, 3 * me] / 3.0 + 2.0 / 3.0 * (q + time_step * (l_o + a[4] * ctl[0]))
@@ -260,7 +268,7 @@
     laid.put(total)
 
 
-def back_second(scal, msgs, partials, part, near_edge, near, cx, cy, cz, dg, cost_own, *rest):
+def back_second(scal, msgs, partials, part, halo, near, cx, cy, cz, dg, cost_own, *rest):
     base, a2, total = rest[-3:]
     count, rows = (len(rest) - 3) // 2, msgs.shape[2]
     mine, theirs = get(rest[:count], 4, rows), get(rest[count:-3], 4, rows)
@@ -273,25 +281,25 @@
         a2_i = part[j] + time_step * pin
         a2[j] = a2_i
         u_o, u_i = 0.25 * partials[j], 0.25 * a2_i
-        back = (0.25 * time_step * a[0]) * (near_edge[...] * msgs[j, 0])
+        back = (0.25 * time_step * a[0]) * (halo[2] * msgs[j, 0])
         spread = a[0] * (cx[0, 1] * u_i) + in_plane_back(u_o, a, cy, cz, 0) - dg[j, 0] * u_o + back
         base[j, 0] = u_o + time_step * spread
         spread = a[0] * (cx[1, 0] * u_o) + in_plane_back(u_i, a, cy, cz, 1) - dg[j, 1] * u_i + pin2
         base[j, 1] = u_i + time_step * spread
 
 
-def second_back_edge(scal, halo, base, cx, cy, cz, dg, cost, cost_far, a1, msg_far, msg_own, total):
-    total[...] = cost[...] + cost_far[...]
-    for j, msg in ((1, msg_far), (0, msg_own)):
+def second_back_edge(scal, halo, base, cx, cy, cz, dg, a1, msg):
+    for j in range(2):
         a = rows_of(scal, j)
         step = (0.25 * time_step) * halo[1 - j, 0]
         spread = in_plane_back(step, a, cy, cz, 0) - dg[j, 0] * step + 0.25 * halo[1 - j, 1]
         value = base[j, 0] + step + time_step * spread
         a1[j] = value
-        msg[...] = a[0] * (cx[0, 0] * value)
-
-
-def close(core, scal, terms, partials, halo, a1, a2, base, cx, cy, cz, dg, ctl, keep, part, give, *send):
+        msg[j] = a[0] * (cx[0, 0] * value)
+
+
+def close(core, scal, terms, partials, halo, a1, a2, base, cx, cy, cz, dg, ctl, cost, cost_far, keep, part, give, total, *send):
+    total[...] = cost[...] + cost_far[...]
     laid = Laid(send)
     sources = [0.0, 0.0]
     for j in range(2):
@@ -305,11 +313,13 @@
         outer = terms[j, 0] / 3.0 + 0.75 * a2_o + (x[0] + time_step * spread)
         spread = a[0] * (cx[1, 0] * x[0]) + in_plane_back(x[1], a, cy, cz, 1) - dg[j, 1] * x[1]
         inner = terms[j, 1] / 3.0 + 0.75 * a2[j] + (x[1] + time_step * spread)
-        for k, value in enumerate((outer, inner, a[0] * (cx[1, 1] * x[1]))):
-            if j == 0:
-                part[k] = value
-            else:
-                laid.put(value)
+        pin = a[0] * (cx[1, 1] * x[1])
+        part[j] = outer
+        if j == 0:
+            part[2], part[3] = inner, pin
+        else:
+            laid.put(inner)
+            laid.put(pin)
     half = ctl.shape[2] // 2
     zero = core[0] == 0
     for k in range(2):
@@ -319,23 +329,31 @@
         give[k] = jnp.where(zero, high, low)
 
 
-def last_edge(halo_own, halo_far, part, cost, cost_far, outer, add, total):
+def last_edge(halo, part, cost, cost_far, outer, give, total):
     total[...] = cost[...] + cost_far[...]
-    outer[...] = part[0] + time_step * halo_own[...]
-    add[...] = time_step * halo_far[...]
-
-
-def assemble(cells, core, part, outer, add, cost, keep, taken, *rest):
-    theirs, (out, gradient, objective) = get(rest[:-3], 3, part.shape[1]), rest[-3:]
+    give[...] = part[1] + time_step * halo[0]
+    outer[...] = part[0] + time_step * halo[1]
+
+
+def write_inner(core, part, keep, taken, *rest):
+    theirs, (out, gradient) = get(rest[:-2], 2, part.shape[1]), rest[-2:]
     me = core[0]
-    out[0, 3 * me] = outer[...]
-    out[0, 1 + me] = part[1] + time_step * theirs[2]
-    out[0, 3 - 3 * me] = theirs[0] + add[...]
-    out[0, 2 - me] = theirs[1] + time_step * part[2]
+    out[0, 1 + me] = part[2] + time_step * theirs[1]
+    out[0, 2 - me] = theirs[0] + time_step * part[3]
     gradient[3 * me] = keep[0]
     gradient[1 + me] = keep[1]
     gradient[3 - 3 * me] = taken[0]
     gradient[2 - me] = taken[1]
+
+
+def write_outer(far, core, value, _, out, sem):
+    at = 3 * core[0]
+    copy = pltpu.make_async_copy(value, out.at[0, 3 - at if far else at], sem)
+    copy.start()
+    copy.wait()
+
+
+def finish(cells, cost, objective):
     objective[0] = jnp.sum(cost[...]) / cells
 
 
@@ -383,99 +401,85 @@
     ranks = sections * lax.axis_size("node")
     within = [(i, i ^ 1) for i in range(ranks)]
     across = [p for i in range(1, ranks - 1, 2) for p in ((i, i + 1), (i + 1, i))]
-    along = [p for i in range(0, ranks - 2, 2) for p in ((i + 1, i + 3), (i + 2, i))]
 
     def swap(x, what):
         with jax.named_scope("swap_" + what):
             return lax.ppermute(x, AXES, within)
 
-    def pass_on(x, what, pairs=across):
+    def pass_on(x, what):
         with jax.named_scope("pass_" + what):
-            return lax.ppermute(x, AXES, pairs)
+            return lax.ppermute(x, AXES, across)
 
     _, layers, rows, columns = concentration.shape
     me = lax.axis_index("node").astype(jnp.int32)
     core = jnp.reshape(me, (1,))
-    far_index, far_weight, step = swap(node_index, "node_index"), swap(weight_num, "weight_num"), swap(step_index, "step")
-
     far = swap(concentration, "state")
     plane = (rows, columns)
-    pair, three = (2,) + plane, (3,) + plane
+    pair, four_planes = (2,) + plane, (4,) + plane
     four = (2,) + pair
     sides = (2, rows, columns // 2)
     held = lambda x, space: pltpu.with_memory_space_constraint(x, space)
-    packed = pl.pallas_call(
-        pack,
-        out_shape=pltpu.VMEM(pair, jnp.float32),
-        grid_spec=pltpu.PrefetchScalarGridSpec(
-            num_scalar_prefetch=1,
-            grid=(1,),
-            in_specs=[
-                pl.BlockSpec((1, 1) + plane, lambda g, c: (0, 3 * c[0], 0, 0)),
-                pl.BlockSpec(memory_space=pltpu.VMEM),
-            ],
-            out_specs=pl.BlockSpec(memory_space=pltpu.VMEM),
-        ),
-        compiler_params=pltpu.CompilerParams(vmem_limit_bytes=VMEM_LIMIT),
-        cost_estimate=cost_of(LONG),
-        name="pack",
-    )(core, held(concentration, pltpu.HBM), held(far, pltpu.VMEM))
+    (first,) = on_core(begin, [(8, 128)], [], [], cost=LONG)
+    (packed,) = on_core(
+        pack, [(3,) + plane], [core], [concentration, far, speed, direction_mask], after=[first]
+    )
     halo = pass_on(packed, "state")
-
-    shapes = [four, four, four, four, pair, plane]
-    scal, cx, cy, cz, dg, ctl, edge = pl.pallas_call(
+    numbers = pl.pallas_call(
+        gather_numbers,
+        out_shape=pltpu.VMEM((8, 128), jnp.float32),
+        in_specs=[pl.BlockSpec(memory_space=pltpu.SMEM)] * 3 + [pl.BlockSpec(memory_space=pl.ANY)],
+        out_specs=pl.BlockSpec(memory_space=pltpu.VMEM),
+        name="gather_numbers",
+    )(node_index, weight_num, step_index, packed)
+    far_numbers = swap(numbers, "numbers")
+
+    shapes = [four, four, four, four, pair]
+    scal, cx, cy, cz, dg, ctl = pl.pallas_call(
         prepare,
         out_shape=[pltpu.SMEM((2, 8), jnp.float32)] + [pltpu.VMEM(s, jnp.float32) for s in shapes],
         in_specs=[pl.BlockSpec(memory_space=pltpu.SMEM)]
-        + [pl.BlockSpec(memory_space=pl.ANY)] * 3
-        + [pl.BlockSpec(memory_space=pltpu.VMEM)] * 4,
+        + [pl.BlockSpec(memory_space=pltpu.VMEM)] * 6,
         out_specs=[pl.BlockSpec(memory_space=pltpu.SMEM)] + [pl.BlockSpec(memory_space=pltpu.VMEM)] * len(shapes),
-        scratch_shapes=[
-            pltpu.SMEM(node_index.shape, jnp.int32),
-            pltpu.SMEM(node_index.shape, jnp.int32),
-            pltpu.SMEM((1,), jnp.int32),
-            pltpu.SemaphoreType.DMA((3,)),
-        ],
         compiler_params=pltpu.CompilerParams(vmem_limit_bytes=VMEM_LIMIT),
-        cost_estimate=cost_of(LONG),
         name="prepare",
     )(
         core,
-        held(node_index, pltpu.HBM),
-        *(far_index, step),
-        *[held(x, pltpu.VMEM) for x in (speed, direction_mask, decay_rate, control)],
-    )
-    near_edge = pass_on(edge, "edge")
+        *[held(x, pltpu.VMEM) for x in (numbers, far_numbers, speed, direction_mask, decay_rate, control)],
+    )
     fields = [cx, cy, cz, dg]
     both = [core, scal]
     states = [concentration, far]
     base, base_q, s1_in = on_core(first_stage, [pair] * 3, both, states + fields + [ctl])
-    (msg,) = on_core(first_edge, [four], [scal], [halo, base, base_q] + fields, cost=LONG)
+    (msg,) = on_core(
+        first_edge, [four], [scal], [halo, base, base_q] + fields, cost=LONG
+    )
     halo2 = pass_on(msg, "stage2")
-
     weights, goals, adj, adj_out_o, adj_out_i = pl.pallas_call(
-        lambda *refs: prepare_back(*refs[:5], *refs[6:]),
+        prepare_back,
         out_shape=[pltpu.SMEM((2,), jnp.float32)]
         + [pltpu.VMEM(s, jnp.float32) for s in (pair, pair, plane, plane)],
-        in_specs=[pl.BlockSpec(memory_space=pltpu.SMEM)] * 3
-        + [pl.BlockSpec(memory_space=pltpu.VMEM)] * 2
+        in_specs=[pl.BlockSpec(memory_space=pltpu.SMEM)]
+        + [pl.BlockSpec(memory_space=pltpu.VMEM)] * 4
         + [pl.BlockSpec(memory_space=pl.ANY)],
         out_specs=[pl.BlockSpec(memory_space=pltpu.SMEM)] + [pl.BlockSpec(memory_space=pltpu.VMEM)] * 4,
         compiler_params=pltpu.CompilerParams(vmem_limit_bytes=VMEM_LIMIT),
         name="prepare_back",
-    )(core, swap(far_weight, "weight_num"), far_weight, held(goal_weight, pltpu.HBM), held(adjoint_next, pltpu.HBM), msg)
-    after_o, after_i = swap(adj_out_o, "after_o"), swap(adj_out_i, "after_i")
-
+    )(
+        core,
+        held(goal_weight, pltpu.HBM),
+        *[held(x, pltpu.VMEM) for x in (numbers, far_numbers)],
+        held(adjoint_next, pltpu.HBM),
+        msg,
+    )
     s1_next, near = pl.pallas_call(
         prepare_next,
         out_shape=[pltpu.VMEM(pair, jnp.float32), pltpu.VMEM(plane, jnp.float32)],
         in_specs=[pl.BlockSpec(memory_space=pltpu.SMEM)] * 2
         + [pl.BlockSpec(memory_space=pltpu.VMEM)] * 6
-        + [pl.BlockSpec(memory_space=pl.ANY)] * 2,
+        + [pl.BlockSpec(memory_space=pl.ANY)],
         out_specs=[pl.BlockSpec(memory_space=pltpu.VMEM)] * 2,
         scratch_shapes=[pltpu.VMEM((2, 1) + plane, jnp.float32)] * 4,
         compiler_params=pltpu.CompilerParams(vmem_limit_bytes=VMEM_LIMIT),
-        cost_estimate=cost_of(LONG),
         name="prepare_next",
     )(
         core,
@@ -483,12 +487,13 @@
         *[held(x, pltpu.VMEM) for x in (speed, direction_mask, decay_rate, control)],
         *[held(x, pltpu.VMEM) for x in states],
         msg,
-        near_edge,
-    )
+    )
+
+    after_o, after_i = swap(adj_out_o, "after_o"), swap(adj_out_i, "after_i")
 
     s2 = list(on_core(second_inner, [plane] * 2, both, states + [msg, s1_in, s1_next] + fields + [ctl]))
     s2_next = [swap(s2[1], "s2_far"), swap(s2[0], "s2_own")]
-    (base,) = on_core(third_stage, [four], both, states + [msg] + s2 + s2_next + [near_edge] + fields + [ctl])
+    (base,) = on_core(third_stage, [four], both, states + [msg] + s2 + s2_next + [halo] + fields + [ctl])
     final_own, final_far, terms, msg3, partials = on_core(
         turn,
         [pair, pair, four, four, pair],
@@ -507,7 +512,7 @@
         back_second,
         [four, pair, (8, 128)],
         [scal],
-        [msg3, partials, part, near_edge, near] + fields + [cost] + pins + theirs,
+        [msg3, partials, part, halo, near] + fields + [cost] + pins + theirs,
     )
     whole = sections & (sections - 1) == 0
     steps = [1 << k for k in range(sections.bit_length() - 1)] if whole else []
@@ -519,42 +524,54 @@
                 return jnp.zeros_like(x)
             return lax.ppermute(x, "space", [(i, i ^ steps[k]) for i in range(sections)])
 
-    for k in range(len(steps) - 2):
+    cost = cost + from_pair(cost, 0)
+    a1, msg4 = on_core(second_back_edge, [pair, pair], [scal], [halo3, base] + fields, after=[cost])
+    halo4 = pass_on(msg4, "back1")
+    keep, part, give, cost, *out = on_core(
+        close,
+        [sides, four_planes, sides, (8, 128)] + [(r, columns) for r in cut(2 * rows, 2)],
+        both,
+        [terms, partials, halo3, a1, a2, base] + fields + [ctl, cost, from_pair(cost, 1)],
+        cost=2 * LONG,
+    )
+    parts = [swap(x, "adjoint") for x in out]
+    taken = swap(give, "gradient")
+    adjoint, gradient = on_core(
+        write_inner,
+        [(1, layers, rows, columns), (layers, rows, columns // 2)],
+        [core],
+        [part, keep, taken] + parts,
+        hbm_out=(0, 1),
+    )
+    for k in range(2, len(steps) - 1):
         cost = cost + from_pair(cost, k)
-    a1, msg4_far, msg4_own, cost = on_core(
-        second_back_edge,
-        [pair, plane, plane, (8, 128)],
-        [scal],
-        [halo3, base] + fields + [cost, from_pair(cost, max(0, len(steps) - 2))],
-    )
-    halo4_own = pass_on(msg4_far, "back1_far")
-    halo4_far = pass_on(msg4_own, "back1_own", along)
-    keep, part, *out = on_core(
-        close,
-        [sides, three, sides] + [(r, columns) for r in cut(3 * rows, 2)],
-        both,
-        [terms, partials, halo3, a1, a2, base] + fields + [ctl],
-    )
-    parts = [swap(x, "adjoint") for x in out[1:]]
-    taken = swap(out[0], "gradient")
-    outer, add, cost = on_core(
+    outer, give, cost = on_core(
         last_edge,
         [plane, plane, (8, 128)],
         [],
-        [halo4_own, halo4_far, part, cost, from_pair(cost, max(1, len(steps) - 1))],
+        [halo4, part, cost, from_pair(cost, max(2, len(steps) - 1))],
+        after=[held(adjoint, pltpu.HBM)],
         cost=LONG,
     )
     if not whole:
         cost = lax.psum(cost, "space")
-    adjoint, gradient, objective = on_core(
-        functools.partial(assemble, sections * layers * rows * columns),
-        [(1, layers, rows, columns), (layers, rows, columns // 2), (1,)],
-        [core],
-        [part, outer, add, cost, keep, taken] + parts,
-        hbm_out=(0, 1),
-        smem_out=(2,),
-        name="assemble",
-    )
+    cells = sections * layers * rows * columns
+    (objective,) = on_core(functools.partial(finish, cells), [(1,)], [], [cost], smem_out=(0,), name="finish")
+    for far, value in ((False, outer), (True, swap(give, "outer"))):
+        adjoint = pl.pallas_call(
+            functools.partial(write_outer, far),
+            out_shape=jax.ShapeDtypeStruct(adjoint.shape, jnp.float32),
+            in_specs=[
+                pl.BlockSpec(memory_space=pltpu.SMEM),
+                pl.BlockSpec(memory_space=pltpu.VMEM),
+                pl.BlockSpec(memory_space=pl.ANY),
+            ],
+            out_specs=pl.BlockSpec(memory_space=pl.ANY),
+            scratch_shapes=[pltpu.SemaphoreType.DMA],
+            input_output_aliases={2: 0},
+            compiler_params=pltpu.CompilerParams(vmem_limit_bytes=VMEM_LIMIT),
+            name="write_outer",
+        )(held(core, pltpu.SMEM), held(value, pltpu.VMEM), held(adjoint, pltpu.HBM))
     return (adjoint, gradient, objective)
 
 

time: 60.2 us -> 57.2 us (0.950)
  starting transfers between devices: 38.8 us -> 33.6 us
  between operations: 0.89 us -> 2.15 us
  local copies, waits for them, and re-layouts: 0.02 us -> 0.97 us
  waiting for transfers between devices: 7.72 us -> 8.53 us
  Pallas kernels: 12.2 us -> 11.5 us
    ppermute x6 -> x4, starting transfers between devices: 4.83 us -> 2.75 us  [pass_on(): return lax.ppermute(x, AXES, across)]
    ppermute x15 -> x13, starting transfers between devices: 27.1 us -> 25.4 us  [swap(): return lax.ppermute(x, AXES, within)]
    ppermute x3, starting transfers between devices: 6.93 us -> 5.49 us  [from_pair(): lax.ppermute(x, 'space', [(i, i ^ steps[k]) for i in range(sections)])]
    pallas_call x1, Pallas kernels: 1.71 us -> 0.51 us  [shards(): pl.pallas_call(prepare, out_shape=[pltpu.SMEM((2, 8), jnp.float32)] + [pl...]
    unnamed x10 -> x12, local copies, waits for them, and re-layouts: 0.02 us -> 0.97 us
    pallas_call x11 -> x14, Pallas kernels: 6.58 us -> 7.23 us  [on_core(): pl.pallas_call(run, out_shape=out_shape, in_specs=[pl.BlockSpec(memory_sp...]
    ppermute x15 -> x13, waiting for transfers between devices: 3.75 us -> 4.22 us  [swap(): return lax.ppermute(x, AXES, within)]
    pallas_call x2 -> x4, Pallas kernels: 3.34 us -> 3.17 us  [the longest x2 1.34 us: shards(): pl.pallas_call(functools.partial(write_outer, far), out_shape=jax.ShapeDt...]
  transfers between devices with their start and end apart: 24 -> 20, of which waited for: 9 -> 10; matrix products, arithmetic and copies ran while one was open for 0% -> 0% of each run, Pallas kernels for 17% -> 17%
where the time goes in v5:
time: 57.2 us; the launch traced here: 56.7 us
  starting transfers between devices  33.6 us (59%)
  Pallas kernels  11.5 us (20%)
  waiting for transfers between devices  8.53 us (15%)
  between operations  2.15 us (4%)
  local copies, waits for them, and re-layouts  0.97 us (2%)
    ppermute x13, starting transfers between devices, swap(): return lax.ppermute(x, AXES, within)  25.4 us
    pallas_call x14, Pallas kernels, on_core(): pl.pallas_call(run, out_shape=out_shape, in_specs=[pl.BlockSpec(memory_sp...  7.23 us
    ppermute x3, starting transfers between devices, from_pair(): lax.ppermute(x, 'space', [(i, i ^ steps[k]) for i in range(sections)])  5.49 us
    ppermute x3, waiting for transfers between devices, from_pair(): lax.ppermute(x, 'space', [(i, i ^ steps[k]) for i in range(sections)])  4.3 us
    ppermute x13, waiting for transfers between devices, swap(): return lax.ppermute(x, AXES, within)  4.22 us
    ppermute x4, starting transfers between devices, pass_on(): return lax.ppermute(x, AXES, across)  2.75 us
    pallas_call x2, Pallas kernels, shards(): pl.pallas_call(functools.partial(write_outer, far), out_shape=jax.ShapeDt...  1.34 us
    pallas_call x1, Pallas kernels, shards(): pl.pallas_call(prepare_back, out_shape=[pltpu.SMEM((2,), jnp.float32)] +...  1.16 us
  transfers between devices with their start and end apart: 20, of which 10 were waited for; matrix products, arithmetic and copies ran while one was open for 0% of the time, Pallas kernels for 17%

profile of v5, /device:TPU:0, one launch (start us, length us, event | category | flops | bytes accessed | tf_op | source)
XLA Modules:
  0.0 56.7 jit_solution(2902468029458341992)
XLA Ops:
  1.2 1.7 %collective-permute-done.refs_2_.refs_3_.far = f32[1,4,64,512]{3,2,1,0:T(8,128)S(1)} collective-permute-done((f32[1,4,64,512]{3,2,1,0:T(8,128)}, f32[1,4,64,512]{3,2,1,0:T(8,128)S(1)}, u32[]{:S(2)}, u32[]{:S(2)}) %collective-permute-start) | collective-permute-done | bytes 524320 | tf_op jit(solution)/shard_map/swap_state/ppermute | solution.py:407
  3.1 0.7 %collective-permute-start.2 = (f32[3,64,512]{2,1,0:T(8,128)S(1)}, f32[3,64,512]{2,1,0:T(8,128)S(1)}, u32[]{:S(2)}, u32[]{:S(2)}) collective-permute-start(f32[3,64,512]{2,1,0:T(8,128)S(1)} %pack.1._), channel_id=1, source_target_pairs={{1,2},{2,1},{3,4},{4,3},{5,6},{6,5},{7,8},{8,7},{9,10},{10,9},{11,... | collective-permute-start | bytes 1179656 | tf_op jit(solution)/shard_map/pass_state/ppermute | solution.py:411
  5.1 0.7 %gather_numbers.1.own_numbers = f32[8,128]{1,0:T(8,128)S(1)} custom-call(s32[1,8]{1,0:T(1,128)} %index.1, s32[1]{0:T(128)S(6)} %copy.17.weight, s32[1]{0:T(128)S(6)} %copy.18.step, f32[3,64,512]{2,1,0:T(8,128)} %copy-done.4), custom_call_target="tpu_custom_call" | custom-call | tf_op jit(solution)/shard_map/gather_numbers/pallas_call | solution.py:427
  5.8 4.3 %collective-permute-start.1 = (f32[8,128]{1,0:T(8,128)S(1)}, f32[8,128]{1,0:T(8,128)S(1)}, u32[]{:S(2)}, u32[]{:S(2)}) collective-permute-start(f32[8,128]{1,0:T(8,128)S(1)} %gather_numbers.1.own_numbers), channel_id=1, source_target_pairs={{0,1},{1,0},{2,3},{3,2},{4,5},{5,4},{6,7},{7,6},{8,9},{9,8},{10,11... | collective-permute-start | bytes 12296 | tf_op jit(solution)/shard_map/swap_numbers/ppermute | solution.py:407
  10.1 0.8 %collective-permute-done.1.far_numbers = f32[8,128]{1,0:T(8,128)S(1)} collective-permute-done((f32[8,128]{1,0:T(8,128)S(1)}, f32[8,128]{1,0:T(8,128)S(1)}, u32[]{:S(2)}, u32[]{:S(2)}) %collective-permute-start.1) | collective-permute-done | bytes 4128 | tf_op jit(solution)/shard_map/swap_numbers/ppermute | solution.py:407
  10.9 0.9 %copy-done.5 = bf16[4,64,512]{2,1,0:T(8,128)(2,1)S(1)} copy-done((bf16[4,64,512]{2,1,0:T(8,128)(2,1)S(1)}, bf16[4,64,512]{2,1,0:T(8,128)(2,1)}, u32[]{:S(2)}) %copy-start.5) | copy-done | bytes 262168
  12.4 0.7 %first_stage.1 = (f32[2,64,512]{2,1,0:T(8,128)S(1)}, f32[2,64,512]{2,1,0:T(8,128)S(1)}, f32[2,64,512]{2,1,0:T(8,128)S(1)}) custom-call(s32[1]{0:T(128)} %bitcast.refs_0_.core, f32[2,8]{1,0:T(2,128)S(4)} %get-tuple-element.47.refs_1_.refs_0_.scal, f32[1,4,64,512]{3,2,1,0:T(8,128)S(1)} %copy-done, ...), custom_call_target="tpu_custom_call" | custom-call | tf_op jit(solution)/shard_map/first_stage/pallas_call | solution.py:373
  13.4 0.7 %collective-permute-start.3 = (f32[2,2,64,512]{3,2,1,0:T(8,128)S(1)}, f32[2,2,64,512]{3,2,1,0:T(8,128)S(1)}, u32[]{:S(2)}, u32[]{:S(2)}) collective-permute-start(f32[2,2,64,512]{3,2,1,0:T(8,128)S(1)} %first_edge.1._.refs_4_), channel_id=1, source_target_pairs={{1,2},{2,1},{3,4},{4,3},{5,6},{6,5},{7,8},{8,7},{9,10},{10,9},{11,... | collective-permute-start | bytes 1572872 | tf_op jit(solution)/shard_map/pass_stage2/ppermute | solution.py:411
  14.1 0.5 prepare_next.1
  15.0 7.6 %collective-permute-start.5 = (f32[64,512]{1,0:T(8,128)S(1)}, f32[64,512]{1,0:T(8,128)S(1)}, u32[]{:S(2)}, u32[]{:S(2)}) collective-permute-start(f32[64,512]{1,0:T(8,128)S(1)} %get-tuple-element.58.refs_5_), channel_id=1, source_target_pairs={{0,1},{1,0},{2,3},{3,2},{4,5},{5,4},{6,7},{7,6},{8,9},{9,8},{10,11... | collective-permute-start | bytes 393224 | tf_op jit(solution)/shard_map/swap_s2_own/ppermute | solution.py:407
  22.7 1.2 %prepare_back.1 = (f32[2]{0:T(128)S(4)}, f32[2,64,512]{2,1,0:T(8,128)S(1)}, f32[2,64,512]{2,1,0:T(8,128)S(1)}, f32[64,512]{1,0:T(8,128)S(1)}, f32[64,512]{1,0:T(8,128)S(1)}) custom-call(s32[1]{0:T(128)} %bitcast.refs_0_.core, bf16[4,64,512]{2,1,0:T(8,128)(2,1)} %goal.1, f32[8,128]{1,0:T(8,128)S(1)} %gather_numbers.1.own_numbers, ...), custom_call_target="tpu_custom_call" | custom-call | tf_op jit(solution)/shard_map/prepare_back/pallas_call | solution.py:457
  24.5 0.8 %third_stage.1.refs_3_ = f32[2,2,64,512]{3,2,1,0:T(8,128)S(1)} custom-call(s32[1]{0:T(128)} %bitcast.refs_0_.core, f32[2,8]{1,0:T(2,128)S(4)} %get-tuple-element.47.refs_1_.refs_0_.scal, f32[1,4,64,512]{3,2,1,0:T(8,128)S(1)} %copy-done, f32[1,4,64,512]{3,2,1,0:T(8,128)S(1)} %collective-permute-done.refs_2_.refs_3_.far, ...), custom_call_target="tpu_custom_call" | custom-call | tf_op jit(solution)/shard_map/third_stage/pallas_call | solution.py:373
  25.8 0.8 %turn.1 = (f32[2,64,512]{2,1,0:T(8,128)S(1)}, f32[2,64,512]{2,1,0:T(8,128)S(1)}, f32[2,2,64,512]{3,2,1,0:T(8,128)S(1)}, f32[2,2,64,512]{3,2,1,0:T(8,128)S(1)}, f32[2,64,512]{2,1,0:T(8,128)S(1)}) custom-call(f32[2,8]{1,0:T(2,128)S(4)} %get-tuple-element.47.refs_1_.refs_0_.scal, f32[2]{0:T(128)S(4)} %get-tuple-element.55.refs_1_, ...), custom_call_target="tpu_custom_call" | custom-call | tf_op jit(solution)/shard_map/turn/pallas_call | solution.py:373
  26.6 0.7 %collective-permute-start.8 = (f32[2,2,64,512]{3,2,1,0:T(8,128)S(1)}, f32[2,2,64,512]{3,2,1,0:T(8,128)S(1)}, u32[]{:S(2)}, u32[]{:S(2)}) collective-permute-start(f32[2,2,64,512]{3,2,1,0:T(8,128)S(1)} %get-tuple-element.64.refs_1_), channel_id=1, source_target_pairs={{1,2},{2,1},{3,4},{4,3},{5,6},{6,5},{7,8},{8,7},{9,10},{10,9},{11,... | collective-permute-start | bytes 1572872 | tf_op jit(solution)/shard_map/pass_back2/ppermute | solution.py:411
  27.3 0.5 turn_inner.1
  27.8 9.3 %collective-permute-start.9 = (f32[88,512]{1,0:T(8,128)S(1)}, f32[88,512]{1,0:T(8,128)S(1)}, u32[]{:S(2)}, u32[]{:S(2)}) collective-permute-start(f32[88,512]{1,0:T(8,128)S(1)} %get-tuple-element.72.refs_11_), channel_id=1, source_target_pairs={{0,1},{1,0},{2,3},{3,2},{4,5},{5,4},{6,7},{7,6},{8,9},{9,8},{10,11... | collective-permute-start | bytes 540680 | tf_op jit(solution)/shard_map/swap_pin/ppermute | solution.py:407
  37.7 0.5 collective-permute-done.9.refs_14_
  38.8 0.7 %back_second.1 = (f32[2,2,64,512]{3,2,1,0:T(8,128)S(1)}, f32[2,64,512]{2,1,0:T(8,128)S(1)}, f32[8,128]{1,0:T(8,128)S(1)}) custom-call(f32[2,8]{1,0:T(2,128)S(4)} %get-tuple-element.47.refs_1_.refs_0_.scal, f32[2,2,64,512]{3,2,1,0:T(8,128)S(1)} %get-tuple-element.64.refs_1_, f32[2,64,512]{2,1,0:T(8,128)S(1)} %get-tuple-element.65.refs_2_.refs_3_, ...), custom_call_target="tpu_custom_call" | custom-call | tf_op jit(solution)/shard_map/back_second/pallas_call | solution.py:373
  39.6 1.6 %collective-permute-start.12 = (f32[8,128]{1,0:T(8,128)S(1)}, f32[8,128]{1,0:T(8,128)S(1)}, u32[]{:S(2)}, u32[]{:S(2)}) collective-permute-start(f32[8,128]{1,0:T(8,128)S(1)} %get-tuple-element.76), channel_id=1, source_target_pairs={{0,4},{2,6},{4,0},{6,2},{8,12},{10,14},{12,8},{14,10},{1,5},{3,7},... | collective-permute-start | bytes 12296 | tf_op jit(solution)/shard_map/goal_sum/ppermute | solution.py:525
  41.2 2.0 %collective-permute-done.12 = f32[8,128]{1,0:T(8,128)S(1)} collective-permute-done((f32[8,128]{1,0:T(8,128)S(1)}, f32[8,128]{1,0:T(8,128)S(1)}, u32[]{:S(2)}, u32[]{:S(2)}) %collective-permute-start.12) | collective-permute-done | bytes 4128 | tf_op jit(solution)/shard_map/goal_sum/ppermute | solution.py:525
  43.2 2.6 %collective-permute-start.14 = (f32[8,128]{1,0:T(8,128)S(1)}, f32[8,128]{1,0:T(8,128)S(1)}, u32[]{:S(2)}, u32[]{:S(2)}) collective-permute-start(f32[8,128]{1,0:T(8,128)S(1)} %add.3.refs_7_.refs_13_), channel_id=1, source_target_pairs={{0,8},{2,10},{4,12},{6,14},{8,0},{10,2},{12,4},{14,6},{1,9},{3,11}... | collective-permute-start | bytes 12296 | tf_op jit(solution)/shard_map/goal_sum/ppermute | solution.py:525
  46.2 0.7 %collective-permute-start.13 = (f32[2,64,512]{2,1,0:T(8,128)S(1)}, f32[2,64,512]{2,1,0:T(8,128)S(1)}, u32[]{:S(2)}, u32[]{:S(2)}) collective-permute-start(f32[2,64,512]{2,1,0:T(8,128)S(1)} %get-tuple-element.77), channel_id=1, source_target_pairs={{1,2},{2,1},{3,4},{4,3},{5,6},{6,5},{7,8},{8,7},{9,10},{10,9},{11,... | collective-permute-start | bytes 786440 | tf_op jit(solution)/shard_map/pass_back1/ppermute | solution.py:411
  46.9 0.9 %collective-permute-done.14.refs_14_ = f32[8,128]{1,0:T(8,128)S(1)} collective-permute-done((f32[8,128]{1,0:T(8,128)S(1)}, f32[8,128]{1,0:T(8,128)S(1)}, u32[]{:S(2)}, u32[]{:S(2)}) %collective-permute-start.14) | collective-permute-done | bytes 4128 | tf_op jit(solution)/shard_map/goal_sum/ppermute | solution.py:525
  47.7 0.8 %close.1 = (f32[2,64,256]{2,1,0:T(8,128)S(1)}, f32[4,64,512]{2,1,0:T(8,128)S(1)}, f32[2,64,256]{2,1,0:T(8,128)S(1)}, f32[8,128]{1,0:T(8,128)S(1)}, f32[64,512]{1,0:T(8,128)S(1)}, /*index=5*/f32[64,512]{1,0:T(8,128)S(1)}) custom-call(s32[1]{0:T(128)} %bitcast.refs_0_.core, f32[2,8]{1,0:T(2,128)S(4)} %get-tuple-element.47.refs_1_.refs_0_.scal, ...), custom_call_target="tpu_custom_call" | custom-call | flops 80000000000 | bytes 240000000 | tf_op jit(solution)/shard_map/close/pallas_call | solution.py:373
  48.6 0.8 %collective-permute-start.16 = (f32[2,64,256]{2,1,0:T(8,128)S(1)}, f32[2,64,256]{2,1,0:T(8,128)S(1)}, u32[]{:S(2)}, u32[]{:S(2)}) collective-permute-start(f32[2,64,256]{2,1,0:T(8,128)S(1)} %get-tuple-element.83), channel_id=1, source_target_pairs={{0,1},{1,0},{2,3},{3,2},{4,5},{5,4},{6,7},{7,6},{8,9},{9,8},{10,11... | collective-permute-start | bytes 393224 | tf_op jit(solution)/shard_map/swap_gradient/ppermute | solution.py:407
  49.9 1.3 %collective-permute-start.15 = (f32[8,128]{1,0:T(8,128)S(1)}, f32[8,128]{1,0:T(8,128)S(1)}, u32[]{:S(2)}, u32[]{:S(2)}) collective-permute-start(f32[8,128]{1,0:T(8,128)S(1)} %get-tuple-element.81.refs_2_), channel_id=1, source_target_pairs={{0,2},{2,0},{4,6},{6,4},{8,10},{10,8},{12,14},{14,12},{1,3},{3,1},... | collective-permute-start | bytes 12296 | tf_op jit(solution)/shard_map/goal_sum/ppermute | solution.py:525
  51.1 0.9 %write_inner.1 = (f32[1,4,64,512]{3,2,1,0:T(8,128)}, f32[4,64,256]{2,1,0:T(8,128)}) custom-call(s32[1]{0:T(128)} %bitcast.refs_0_.core, f32[4,64,512]{2,1,0:T(8,128)S(1)} %get-tuple-element.80.refs_1_, f32[2,64,256]{2,1,0:T(8,128)S(1)} %get-tuple-element.82.refs_2_, f32[2,64,256]{2,1,0:T(8,128)S(1)} %collective-permute-done.16.refs_3_, ...), custom_call_target="tpu_custom_call" | custom-call | tf_op jit(solution)/shard_map/write_inner/pallas_call | solution.py:373
  52.1 1.4 %collective-permute-done.15.refs_3_ = f32[8,128]{1,0:T(8,128)S(1)} collective-permute-done((f32[8,128]{1,0:T(8,128)S(1)}, f32[8,128]{1,0:T(8,128)S(1)}, u32[]{:S(2)}, u32[]{:S(2)}) %collective-permute-start.15) | collective-permute-done | bytes 4128 | tf_op jit(solution)/shard_map/goal_sum/ppermute | solution.py:525
  53.5 1.2 %collective-permute-start.19 = (f32[64,512]{1,0:T(8,128)S(1)}, f32[64,512]{1,0:T(8,128)S(1)}, u32[]{:S(2)}, u32[]{:S(2)}) collective-permute-start(f32[64,512]{1,0:T(8,128)S(1)} %get-tuple-element.87), channel_id=1, source_target_pairs={{0,1},{1,0},{2,3},{3,2},{4,5},{5,4},{6,7},{7,6},{8,9},{9,8},{10,11... | collective-permute-start | bytes 393224 | tf_op jit(solution)/shard_map/swap_outer/ppermute | solution.py:407
  54.7 0.6 %finish.1 = f32[1]{0:T(128)} custom-call(f32[8,128]{1,0:T(8,128)S(1)} %get-tuple-element.90.refs_0_), custom_call_target="tpu_custom_call" | custom-call | tf_op jit(solution)/shard_map/finish/pallas_call | solution.py:373
  55.4 0.7 %write_outer.2._ = f32[1,4,64,512]{3,2,1,0:T(8,128)} custom-call(s32[1]{0:T(128)} %bitcast.refs_0_.core, f32[64,512]{1,0:T(8,128)S(1)} %get-tuple-element.88.value, f32[1,4,64,512]{3,2,1,0:T(8,128)} %get-tuple-element.86.refs_4_._), custom_call_target="tpu_custom_call", output_to_operand_aliasing={{}: (2, {})} | custom-call | tf_op jit(solution)/shard_map/write_outer/pallas_call | solution.py:561
  56.1 0.7 %write_outer.3 = f32[1,4,64,512]{3,2,1,0:T(8,128)} custom-call(s32[1]{0:T(128)} %bitcast.refs_0_.core, f32[64,512]{1,0:T(8,128)S(1)} %collective-permute-done.19.value, f32[1,4,64,512]{3,2,1,0:T(8,128)} %write_outer.2._), custom_call_target="tpu_custom_call", output_to_operand_aliasing={{}: (2, {})} | custom-call | tf_op jit(solution)/shard_map/write_outer/pallas_call | solution.py:561
  (41 shorter events, 5.1 us)
Async XLA Ops:
  0.6 2.3 %copy-start = (f32[1,4,64,512]{3,2,1,0:T(8,128)S(1)}, f32[1,4,64,512]{3,2,1,0:T(8,128)}, u32[]{:S(2)}) copy-start(f32[1,4,64,512]{3,2,1,0:T(8,128)} %refs_2_.5) | copy-start | bytes 1572868
  0.6 2.3 %copy-start.2 = (s32[3,4,64,64]{3,2,1,0:T(8,128)S(1)}, s32[3,4,64,64]{3,2,1,0:T(8,128)}, u32[]{:S(2)}) copy-start(s32[3,4,64,64]{3,2,1,0:T(8,128)} %mask.3) | copy-start | bytes 589828
  0.7 2.3 %copy-start.1 = (bf16[3,4,64,512]{3,2,1,0:T(8,128)(2,1)S(1)}, bf16[3,4,64,512]{3,2,1,0:T(8,128)(2,1)}, u32[]{:S(2)}) copy-start(bf16[3,4,64,512]{3,2,1,0:T(8,128)(2,1)} %speed.3) | copy-start | bytes 2359300
  0.7 2.3 %collective-permute-start = (f32[1,4,64,512]{3,2,1,0:T(8,128)}, f32[1,4,64,512]{3,2,1,0:T(8,128)S(1)}, u32[]{:S(2)}, u32[]{:S(2)}) collective-permute-start(f32[1,4,64,512]{3,2,1,0:T(8,128)} %refs_2_.5), channel_id=1, source_target_pairs={{0,1},{1,0},{2,3},{3,2},{4,5},{5,4},{6,7},{7,6},{8,9},{9,8},{10,11... | collective-permute-start | bytes 1572872 | tf_op jit(solution)/shard_map/swap_state/ppermute | solution.py:407
  2.9 8.0 %copy-start.3 = (f32[4,64,512]{2,1,0:T(8,128)S(1)}, f32[4,64,512]{2,1,0:T(8,128)}, u32[]{:S(2)}) copy-start(f32[4,64,512]{2,1,0:T(8,128)} %control.3) | copy-start | bytes 1572868
  3.1 2.0 %copy-start.4 = (f32[3,64,512]{2,1,0:T(8,128)}, f32[3,64,512]{2,1,0:T(8,128)S(1)}, u32[]{:S(2)}) copy-start(f32[3,64,512]{2,1,0:T(8,128)S(1)} %pack.1._) | copy-start | bytes 1179652
  3.1 9.9 %collective-permute-start.2 = (f32[3,64,512]{2,1,0:T(8,128)S(1)}, f32[3,64,512]{2,1,0:T(8,128)S(1)}, u32[]{:S(2)}, u32[]{:S(2)}) collective-permute-start(f32[3,64,512]{2,1,0:T(8,128)S(1)} %pack.1._), channel_id=1, source_target_pairs={{1,2},{2,1},{3,4},{4,3},{5,6},{6,5},{7,8},{8,7},{9,10},{10,9},{11,... | collective-permute-start | bytes 1179656 | tf_op jit(solution)/shard_map/pass_state/ppermute | solution.py:411
  5.8 5.1 %collective-permute-start.1 = (f32[8,128]{1,0:T(8,128)S(1)}, f32[8,128]{1,0:T(8,128)S(1)}, u32[]{:S(2)}, u32[]{:S(2)}) collective-permute-start(f32[8,128]{1,0:T(8,128)S(1)} %gather_numbers.1.own_numbers), channel_id=1, source_target_pairs={{0,1},{1,0},{2,3},{3,2},{4,5},{5,4},{6,7},{7,6},{8,9},{9,8},{10,11... | collective-permute-start | bytes 12296 | tf_op jit(solution)/shard_map/swap_numbers/ppermute | solution.py:407
  10.9 1.0 %copy-start.5 = (bf16[4,64,512]{2,1,0:T(8,128)(2,1)S(1)}, bf16[4,64,512]{2,1,0:T(8,128)(2,1)}, u32[]{:S(2)}) copy-start(bf16[4,64,512]{2,1,0:T(8,128)(2,1)} %decay.3) | copy-start | bytes 786436
  13.4 12.4 %collective-permute-start.3 = (f32[2,2,64,512]{3,2,1,0:T(8,128)S(1)}, f32[2,2,64,512]{3,2,1,0:T(8,128)S(1)}, u32[]{:S(2)}, u32[]{:S(2)}) collective-permute-start(f32[2,2,64,512]{3,2,1,0:T(8,128)S(1)} %first_edge.1._.refs_4_), channel_id=1, source_target_pairs={{1,2},{2,1},{3,4},{4,3},{5,6},{6,5},{7,8},{8,7},{9,10},{10,9},{11,... | collective-permute-start | bytes 1572872 | tf_op jit(solution)/shard_map/pass_stage2/ppermute | solution.py:411
  15.0 9.4 %collective-permute-start.5 = (f32[64,512]{1,0:T(8,128)S(1)}, f32[64,512]{1,0:T(8,128)S(1)}, u32[]{:S(2)}, u32[]{:S(2)}) collective-permute-start(f32[64,512]{1,0:T(8,128)S(1)} %get-tuple-element.58.refs_5_), channel_id=1, source_target_pairs={{0,1},{1,0},{2,3},{3,2},{4,5},{5,4},{6,7},{7,6},{8,9},{9,8},{10,11... | collective-permute-start | bytes 393224 | tf_op jit(solution)/shard_map/swap_s2_own/ppermute | solution.py:407
  22.7 1.8 %collective-permute-start.4 = (f32[64,512]{1,0:T(8,128)S(1)}, f32[64,512]{1,0:T(8,128)S(1)}, u32[]{:S(2)}, u32[]{:S(2)}) collective-permute-start(f32[64,512]{1,0:T(8,128)S(1)} %get-tuple-element.59.refs_6_), channel_id=1, source_target_pairs={{0,1},{1,0},{2,3},{3,2},{4,5},{5,4},{6,7},{7,6},{8,9},{9,8},{10,11... | collective-permute-start | bytes 393224 | tf_op jit(solution)/shard_map/swap_s2_far/ppermute | solution.py:407
  23.9 1.5 %collective-permute-start.6 = (f32[64,512]{1,0:T(8,128)S(1)}, f32[64,512]{1,0:T(8,128)S(1)}, u32[]{:S(2)}, u32[]{:S(2)}) collective-permute-start(f32[64,512]{1,0:T(8,128)S(1)} %get-tuple-element.62), channel_id=1, source_target_pairs={{0,1},{1,0},{2,3},{3,2},{4,5},{5,4},{6,7},{7,6},{8,9},{9,8},{10,11... | collective-permute-start | bytes 393224 | tf_op jit(solution)/shard_map/swap_after_o/ppermute | solution.py:407
  24.4 1.3 %collective-permute-start.7 = (f32[64,512]{1,0:T(8,128)S(1)}, f32[64,512]{1,0:T(8,128)S(1)}, u32[]{:S(2)}, u32[]{:S(2)}) collective-permute-start(f32[64,512]{1,0:T(8,128)S(1)} %get-tuple-element.63), channel_id=1, source_target_pairs={{0,1},{1,0},{2,3},{3,2},{4,5},{5,4},{6,7},{7,6},{8,9},{9,8},{10,11... | collective-permute-start | bytes 393224 | tf_op jit(solution)/shard_map/swap_after_i/ppermute | solution.py:407
  26.6 19.2 %collective-permute-start.8 = (f32[2,2,64,512]{3,2,1,0:T(8,128)S(1)}, f32[2,2,64,512]{3,2,1,0:T(8,128)S(1)}, u32[]{:S(2)}, u32[]{:S(2)}) collective-permute-start(f32[2,2,64,512]{3,2,1,0:T(8,128)S(1)} %get-tuple-element.64.refs_1_), channel_id=1, source_target_pairs={{1,2},{2,1},{3,4},{4,3},{5,6},{6,5},{7,8},{8,7},{9,10},{10,9},{11,... | collective-permute-start | bytes 1572872 | tf_op jit(solution)/shard_map/pass_back2/ppermute | solution.py:411
  27.8 10.4 %collective-permute-start.9 = (f32[88,512]{1,0:T(8,128)S(1)}, f32[88,512]{1,0:T(8,128)S(1)}, u32[]{:S(2)}, u32[]{:S(2)}) collective-permute-start(f32[88,512]{1,0:T(8,128)S(1)} %get-tuple-element.72.refs_11_), channel_id=1, source_target_pairs={{0,1},{1,0},{2,3},{3,2},{4,5},{5,4},{6,7},{7,6},{8,9},{9,8},{10,11... | collective-permute-start | bytes 540680 | tf_op jit(solution)/shard_map/swap_pin/ppermute | solution.py:407
  37.2 1.4 %collective-permute-start.10 = (f32[88,512]{1,0:T(8,128)S(1)}, f32[88,512]{1,0:T(8,128)S(1)}, u32[]{:S(2)}, u32[]{:S(2)}) collective-permute-start(f32[88,512]{1,0:T(8,128)S(1)} %get-tuple-element.73.refs_12_), channel_id=1, source_target_pairs={{0,1},{1,0},{2,3},{3,2},{4,5},{5,4},{6,7},{7,6},{8,9},{9,8},{10,11... | collective-permute-start | bytes 540680 | tf_op jit(solution)/shard_map/swap_pin/ppermute | solution.py:407
  37.2 1.6 %collective-permute-start.11 = (f32[88,512]{1,0:T(8,128)S(1)}, f32[88,512]{1,0:T(8,128)S(1)}, u32[]{:S(2)}, u32[]{:S(2)}) collective-permute-start(f32[88,512]{1,0:T(8,128)S(1)} %get-tuple-element.74.refs_13_), channel_id=1, source_target_pairs={{0,1},{1,0},{2,3},{3,2},{4,5},{5,4},{6,7},{7,6},{8,9},{9,8},{10,11... | collective-permute-start | bytes 540680 | tf_op jit(solution)/shard_map/swap_pin/ppermute | solution.py:407
  39.6 3.7 %collective-permute-start.12 = (f32[8,128]{1,0:T(8,128)S(1)}, f32[8,128]{1,0:T(8,128)S(1)}, u32[]{:S(2)}, u32[]{:S(2)}) collective-permute-start(f32[8,128]{1,0:T(8,128)S(1)} %get-tuple-element.76), channel_id=1, source_target_pairs={{0,4},{2,6},{4,0},{6,2},{8,12},{10,14},{12,8},{14,10},{1,5},{3,7},... | collective-permute-start | bytes 12296 | tf_op jit(solution)/shard_map/goal_sum/ppermute | solution.py:525
  43.2 4.5 %collective-permute-start.14 = (f32[8,128]{1,0:T(8,128)S(1)}, f32[8,128]{1,0:T(8,128)S(1)}, u32[]{:S(2)}, u32[]{:S(2)}) collective-permute-start(f32[8,128]{1,0:T(8,128)S(1)} %add.3.refs_7_.refs_13_), channel_id=1, source_target_pairs={{0,8},{2,10},{4,12},{6,14},{8,0},{10,2},{12,4},{14,6},{1,9},{3,11}... | collective-permute-start | bytes 12296 | tf_op jit(solution)/shard_map/goal_sum/ppermute | solution.py:525
  46.2 7.3 %collective-permute-start.13 = (f32[2,64,512]{2,1,0:T(8,128)S(1)}, f32[2,64,512]{2,1,0:T(8,128)S(1)}, u32[]{:S(2)}, u32[]{:S(2)}) collective-permute-start(f32[2,64,512]{2,1,0:T(8,128)S(1)} %get-tuple-element.77), channel_id=1, source_target_pairs={{1,2},{2,1},{3,4},{4,3},{5,6},{6,5},{7,8},{8,7},{9,10},{10,9},{11,... | collective-permute-start | bytes 786440 | tf_op jit(solution)/shard_map/pass_back1/ppermute | solution.py:411
  48.6 2.5 %collective-permute-start.16 = (f32[2,64,256]{2,1,0:T(8,128)S(1)}, f32[2,64,256]{2,1,0:T(8,128)S(1)}, u32[]{:S(2)}, u32[]{:S(2)}) collective-permute-start(f32[2,64,256]{2,1,0:T(8,128)S(1)} %get-tuple-element.83), channel_id=1, source_target_pairs={{0,1},{1,0},{2,3},{3,2},{4,5},{5,4},{6,7},{7,6},{8,9},{9,8},{10,11... | collective-permute-start | bytes 393224 | tf_op jit(solution)/shard_map/swap_gradient/ppermute | solution.py:407
  49.4 1.8 %collective-permute-start.17 = (f32[64,512]{1,0:T(8,128)S(1)}, f32[64,512]{1,0:T(8,128)S(1)}, u32[]{:S(2)}, u32[]{:S(2)}) collective-permute-start(f32[64,512]{1,0:T(8,128)S(1)} %get-tuple-element.84), channel_id=1, source_target_pairs={{0,1},{1,0},{2,3},{3,2},{4,5},{5,4},{6,7},{7,6},{8,9},{9,8},{10,11... | collective-permute-start | bytes 393224 | tf_op jit(solution)/shard_map/swap_adjoint/ppermute | solution.py:407
  49.4 1.7 %collective-permute-start.18 = (f32[64,512]{1,0:T(8,128)S(1)}, f32[64,512]{1,0:T(8,128)S(1)}, u32[]{:S(2)}, u32[]{:S(2)}) collective-permute-start(f32[64,512]{1,0:T(8,128)S(1)} %get-tuple-element.85), channel_id=1, source_target_pairs={{0,1},{1,0},{2,3},{3,2},{4,5},{5,4},{6,7},{7,6},{8,9},{9,8},{10,11... | collective-permute-start | bytes 393224 | tf_op jit(solution)/shard_map/swap_adjoint/ppermute | solution.py:407
  49.9 3.6 %collective-permute-start.15 = (f32[8,128]{1,0:T(8,128)S(1)}, f32[8,128]{1,0:T(8,128)S(1)}, u32[]{:S(2)}, u32[]{:S(2)}) collective-permute-start(f32[8,128]{1,0:T(8,128)S(1)} %get-tuple-element.81.refs_2_), channel_id=1, source_target_pairs={{0,2},{2,0},{4,6},{6,4},{8,10},{10,8},{12,14},{14,12},{1,3},{3,1},... | collective-permute-start | bytes 12296 | tf_op jit(solution)/shard_map/goal_sum/ppermute | solution.py:525
  53.5 2.5 %collective-permute-start.19 = (f32[64,512]{1,0:T(8,128)S(1)}, f32[64,512]{1,0:T(8,128)S(1)}, u32[]{:S(2)}, u32[]{:S(2)}) collective-permute-start(f32[64,512]{1,0:T(8,128)S(1)} %get-tuple-element.87), channel_id=1, source_target_pairs={{0,1},{1,0},{2,3},{3,2},{4,5},{5,4},{6,7},{7,6},{8,9},{9,8},{10,11... | collective-permute-start | bytes 393224 | tf_op jit(solution)/shard_map/swap_outer/ppermute | solution.py:407

commit v6 on v5

--- a/solution.py
+++ b/solution.py
@@ -15,7 +15,7 @@
 
 VMEM_LIMIT = 24 * 1024 * 1024
 AXES = ("space", "node")
-LONG = 40
+LONG = 8
 
 
 def cost_of(us):
@@ -145,15 +145,15 @@
         s1_next[j] = value + time_step * (l + a[4] * control[at])
 
 
-def prepare_back(core, goal, own_numbers, far_numbers, adjoint, _, weights, goals, adj, adj_out_o, adj_out_i):
+def prepare_back(core, goal, own_numbers, far_numbers, adjoint, _, weights, goals, adj, adj_out):
     me = core[0]
     weights[0] = own_numbers[...][0, 8] * (1.0 / weight_denominator)
     weights[1] = far_numbers[...][0, 8] * (1.0 / weight_denominator)
     for k, at in enumerate((3 * me, 1 + me)):
         goals[k] = goal[at].astype(jnp.float32)
         adj[k] = adjoint[0, at].astype(jnp.float32)
-    adj_out_o[...] = adjoint[0, 3 - 3 * me].astype(jnp.float32)
-    adj_out_i[...] = adjoint[0, 2 - me].astype(jnp.float32)
+    adj_out[0] = adjoint[0, 3 - 3 * me].astype(jnp.float32)
+    adj_out[1] = adjoint[0, 2 - me].astype(jnp.float32)
 
 
 def first_stage(core, scal, own, far, cx, cy, cz, dg, ctl, base, base_q, s1_in):
@@ -170,49 +170,51 @@
         base_q[j] = 0.75 * c_o + (0.25 * time_step) * (a[0] * (cx[1, 0] * s1_i) + push[0])
 
 
-def first_edge(scal, halo, base, base_q, cx, cy, cz, dg, msg):
+def first_edge(scal, halo, base, base_q, cx, cy, cz, dg, msg, s1_out):
     for j in range(2):
         a = rows_of(scal, j)
         s1_o = base[j] + (time_step * a[0]) * (cx[0, 0] * halo[1 - j])
-        msg[j, 0] = s1_o
-        msg[j, 1] = base_q[j] + 0.25 * (s1_o + time_step * (in_plane(s1_o, a, cy, cz, 0) - dg[j, 0] * s1_o))
-
-
-def second_inner(core, scal, own, far, msg, s1_in, s1_next, cx, cy, cz, dg, ctl, s2_own, s2_far):
+        s1_out[j] = s1_o
+        msg[j] = base_q[j] + 0.25 * (s1_o + time_step * (in_plane(s1_o, a, cy, cz, 0) - dg[j, 0] * s1_o))
+
+
+def second_inner(core, scal, own, far, s1_out, s1_in, s1_next, cx, cy, cz, dg, ctl, s2_own, s2_far):
     for j, (c, out) in enumerate(((own, s2_own), (far, s2_far))):
         a = rows_of(scal, j)
         s1_i = s1_in[j]
-        l_i = a[0] * (cx[0, 1] * msg[j, 0] + cx[1, 1] * s1_next[j]) + in_plane(s1_i, a, cy, cz, 1) - dg[j, 1] * s1_i
+        l_i = a[0] * (cx[0, 1] * s1_out[j] + cx[1, 1] * s1_next[j]) + in_plane(s1_i, a, cy, cz, 1) - dg[j, 1] * s1_i
         out[...] = 0.75 * c[0, 1 + core[0]] + 0.25 * (s1_i + time_step * (l_i + a[4] * ctl[1]))
 
 
-def third_stage(core, scal, own, far, msg, s2_own, s2_far, next_own, next_far, halo, cx, cy, cz, dg, ctl, base):
+def far_part(core, scal, own, far, halo, far_base, cx, step):
+    for j, c in enumerate((own, far)):
+        s1_h = far_base[1 - j] + (time_step * scal[j, 0]) * (halo[2] * c[0, 3 * core[0]])
+        step[j] = (0.25 * time_step * scal[j, 0]) * (cx[0, 0] * s1_h)
+
+
+def third_stage(core, scal, own, far, msg, s1_out, s2_own, s2_far, next_own, next_far, halo, step, cx, cy, cz, dg, ctl, base):
     me = core[0]
     parts = ((own, s2_own, next_own), (far, s2_far, next_far))
     for j, (c, s2, s2_next) in enumerate(parts):
         a = rows_of(scal, j)
-        q, s2_i = msg[j, 1], s2[...]
-        back = (0.25 * time_step * a[0]) * (halo[2] * msg[j, 0])
-        l_o = a[0] * (cx[0, 0] * back + cx[1, 0] * s2_i) + in_plane(q, a, cy, cz, 0) - dg[j, 0] * q
-        l_i = a[0] * (cx[0, 1] * q + cx[1, 1] * s2_next[...]) + in_plane(s2_i, a, cy, cz, 1) - dg[j, 1] * s2_i
-        base[j, 0] = c[0, 3 * me] / 3.0 + 2.0 / 3.0 * (q + time_step * (l_o + a[4] * ctl[0]))
+        c_o, s2_i = c[0, 3 * me], s2[...]
+        s2_o = msg[j] + step[j]
+        back = (0.25 * time_step * a[0]) * (halo[2] * s1_out[j])
+        l_o = a[0] * (cx[0, 0] * back + cx[1, 0] * s2_i) + in_plane(s2_o, a, cy, cz, 0) - dg[j, 0] * s2_o
+        l_i = a[0] * (cx[0, 1] * s2_o + cx[1, 1] * s2_next[...]) + in_plane(s2_i, a, cy, cz, 1) - dg[j, 1] * s2_i
+        base[j, 0] = c_o / 3.0 + 2.0 / 3.0 * (s2_o + time_step * (l_o + a[4] * ctl[0]))
         base[j, 1] = c[0, 1 + me] / 3.0 + 2.0 / 3.0 * (s2_i + time_step * (l_i + a[4] * ctl[1]))
 
 
-def finals(j, scal, halo, base, cx, cy, cz, dg):
-    a = rows_of(scal, j)
-    step = (0.25 * time_step * a[0]) * (cx[0, 0] * halo[1 - j, 0])
-    change = in_plane(step, a, cy, cz, 0) - dg[j, 0] * step + a[0] * (cx[0, 0] * halo[1 - j, 1])
-    outer = base[j, 0] + 2.0 / 3.0 * (step + time_step * change)
-    inner = base[j, 1] + (2.0 / 3.0 * time_step * a[0]) * (cx[0, 1] * step)
-    return outer, inner
-
-
-def turn(scal, weights, halo, base, cx, cy, cz, dg, goals, adj, after_o, after_i, final_own, final_far, term, msg, partial):
-    final_own[0], final_own[1] = finals(0, scal, halo, base, cx, cy, cz, dg)
-    final_far[0], final_far[1] = finals(1, scal, halo, base, cx, cy, cz, dg)
+def finals(j, scal, halo, base, cx):
+    return base[j, 0] + (2.0 / 3.0 * time_step * scal[j, 0]) * (cx[0, 0] * halo[1 - j]), base[j, 1]
+
+
+def turn(scal, weights, halo, base, cx, cy, cz, dg, goals, adj, after_far, final_own, final_far, term, msg, partial):
+    final_own[0], final_own[1] = finals(0, scal, halo, base, cx)
+    final_far[0], final_far[1] = finals(1, scal, halo, base, cx)
     first = [weights[0] * final_own[k] + weights[1] * final_far[k] for k in range(2)]
-    for j, (final, after) in enumerate(((final_own, (adj[0], adj[1])), (final_far, (after_o[...], after_i[...])))):
+    for j, (final, after) in enumerate(((final_own, (adj[0], adj[1])), (final_far, (after_far[0], after_far[1])))):
         a = rows_of(scal, j)
         u = []
         for k in range(2):
@@ -450,18 +452,19 @@
     both = [core, scal]
     states = [concentration, far]
     base, base_q, s1_in = on_core(first_stage, [pair] * 3, both, states + fields + [ctl])
-    (msg,) = on_core(
-        first_edge, [four], [scal], [halo, base, base_q] + fields, cost=LONG
+    far_base = pass_on(base, "stage1")
+    msg, s1_out = on_core(
+        first_edge, [pair, pair], [scal], [halo, base, base_q] + fields, cost=LONG
     )
     halo2 = pass_on(msg, "stage2")
-    weights, goals, adj, adj_out_o, adj_out_i = pl.pallas_call(
+    weights, goals, adj, adj_out = pl.pallas_call(
         prepare_back,
         out_shape=[pltpu.SMEM((2,), jnp.float32)]
-        + [pltpu.VMEM(s, jnp.float32) for s in (pair, pair, plane, plane)],
+        + [pltpu.VMEM(s, jnp.float32) for s in (pair, pair, pair)],
         in_specs=[pl.BlockSpec(memory_space=pltpu.SMEM)]
         + [pl.BlockSpec(memory_space=pltpu.VMEM)] * 4
         + [pl.BlockSpec(memory_space=pl.ANY)],
-        out_specs=[pl.BlockSpec(memory_space=pltpu.SMEM)] + [pl.BlockSpec(memory_space=pltpu.VMEM)] * 4,
+        out_specs=[pl.BlockSpec(memory_space=pltpu.SMEM)] + [pl.BlockSpec(memory_space=pltpu.VMEM)] * 3,
         compiler_params=pltpu.CompilerParams(vmem_limit_bytes=VMEM_LIMIT),
         name="prepare_back",
     )(
@@ -489,16 +492,17 @@
         msg,
     )
 
-    after_o, after_i = swap(adj_out_o, "after_o"), swap(adj_out_i, "after_i")
-
-    s2 = list(on_core(second_inner, [plane] * 2, both, states + [msg, s1_in, s1_next] + fields + [ctl]))
+    after = swap(adj_out, "after")
+
+    (far_step,) = on_core(far_part, [pair], both, states + [halo, far_base, cx], cost=LONG)
+    s2 = list(on_core(second_inner, [plane] * 2, both, states + [s1_out, s1_in, s1_next] + fields + [ctl]))
     s2_next = [swap(s2[1], "s2_far"), swap(s2[0], "s2_own")]
-    (base,) = on_core(third_stage, [four], both, states + [msg] + s2 + s2_next + [halo] + fields + [ctl])
+    (base,) = on_core(third_stage, [four], both, states + [msg, s1_out] + s2 + s2_next + [halo, far_step] + fields + [ctl])
     final_own, final_far, terms, msg3, partials = on_core(
         turn,
         [pair, pair, four, four, pair],
         [scal, weights],
-        [halo2, base] + fields + [goals, adj, after_o, after_i],
+        [halo2, base] + fields + [goals, adj, after],
     )
     halo3 = pass_on(msg3, "back2")
     part, cost, *pins = on_core(

time: 57.2 us -> 54.8 us (0.958)
  starting transfers between devices: 33.6 us -> 30.5 us
  waiting for transfers between devices: 8.53 us -> 9.6 us
    ppermute x13 -> x12, starting transfers between devices: 25.4 us -> 22.8 us  [swap(): return lax.ppermute(x, AXES, within)]
    ppermute x3, starting transfers between devices: 5.49 us -> 4.24 us  [from_pair(): lax.ppermute(x, 'space', [(i, i ^ steps[k]) for i in range(sections)])]
    ppermute x13 -> x12, waiting for transfers between devices: 4.22 us -> 5.04 us  [swap(): return lax.ppermute(x, AXES, within)]
    ppermute x4 -> x5, starting transfers between devices: 2.75 us -> 3.41 us  [pass_on(): return lax.ppermute(x, AXES, across)]
    pallas_call x14 -> x15, Pallas kernels: 7.23 us -> 7.03 us  [on_core(): pl.pallas_call(run, out_shape=out_shape, in_specs=[pl.BlockSpec(memory_sp...]
  transfers between devices with their start and end apart: 20 -> 20, of which waited for: 10 -> 12; matrix products, arithmetic and copies ran while one was open for 0% -> 0% of each run, Pallas kernels for 17% -> 18%
where the time goes in v6:
time: 54.8 us; the launch traced here: 54.4 us
  starting transfers between devices  30.5 us (56%)
  Pallas kernels  11.3 us (21%)
  waiting for transfers between devices  9.6 us (18%)
  between operations  2.15 us (4%)
  local copies, waits for them, and re-layouts  0.97 us (2%)
    ppermute x12, starting transfers between devices, swap(): return lax.ppermute(x, AXES, within)  22.8 us
    pallas_call x15, Pallas kernels, on_core(): pl.pallas_call(run, out_shape=out_shape, in_specs=[pl.BlockSpec(memory_sp...  7.03 us
    ppermute x12, waiting for transfers between devices, swap(): return lax.ppermute(x, AXES, within)  5.04 us
    ppermute x3, waiting for transfers between devices, from_pair(): lax.ppermute(x, 'space', [(i, i ^ steps[k]) for i in range(sections)])  4.55 us
    ppermute x3, starting transfers between devices, from_pair(): lax.ppermute(x, 'space', [(i, i ^ steps[k]) for i in range(sections)])  4.24 us
    ppermute x5, starting transfers between devices, pass_on(): return lax.ppermute(x, AXES, across)  3.41 us
    pallas_call x2, Pallas kernels, shards(): pl.pallas_call(functools.partial(write_outer, far), out_shape=jax.ShapeDt...  1.33 us
    pallas_call x1, Pallas kernels, shards(): pl.pallas_call(prepare_back, out_shape=[pltpu.SMEM((2,), jnp.float32)] +...  1.16 us
  transfers between devices with their start and end apart: 20, of which 12 were waited for; matrix products, arithmetic and copies ran while one was open for 0% of the time, Pallas kernels for 18%

profile of v6, /device:TPU:0, one launch (start us, length us, event | category | flops | bytes accessed | tf_op | source)
XLA Modules:
  0.0 54.4 jit_solution(14092674441129316153)
XLA Ops:
  0.6 0.5 collective-permute-start
  1.2 1.7 %collective-permute-done.refs_2_.refs_3_.far = f32[1,4,64,512]{3,2,1,0:T(8,128)S(1)} collective-permute-done((f32[1,4,64,512]{3,2,1,0:T(8,128)}, f32[1,4,64,512]{3,2,1,0:T(8,128)S(1)}, u32[]{:S(2)}, u32[]{:S(2)}) %collective-permute-start) | collective-permute-done | bytes 524320 | tf_op jit(solution)/shard_map/swap_state/ppermute | solution.py:409
  3.1 0.7 %collective-permute-start.2 = (f32[3,64,512]{2,1,0:T(8,128)S(1)}, f32[3,64,512]{2,1,0:T(8,128)S(1)}, u32[]{:S(2)}, u32[]{:S(2)}) collective-permute-start(f32[3,64,512]{2,1,0:T(8,128)S(1)} %pack.1._), channel_id=1, source_target_pairs={{1,2},{2,1},{3,4},{4,3},{5,6},{6,5},{7,8},{8,7},{9,10},{10,9},{11,... | collective-permute-start | bytes 1179656 | tf_op jit(solution)/shard_map/pass_state/ppermute | solution.py:413
  5.1 0.7 %gather_numbers.1.own_numbers = f32[8,128]{1,0:T(8,128)S(1)} custom-call(s32[1,8]{1,0:T(1,128)} %index.1, s32[1]{0:T(128)S(6)} %copy.17.weight, s32[1]{0:T(128)S(6)} %copy.18.step, f32[3,64,512]{2,1,0:T(8,128)} %copy-done.4), custom_call_target="tpu_custom_call" | custom-call | tf_op jit(solution)/shard_map/gather_numbers/pallas_call | solution.py:429
  5.8 4.3 %collective-permute-start.1 = (f32[8,128]{1,0:T(8,128)S(1)}, f32[8,128]{1,0:T(8,128)S(1)}, u32[]{:S(2)}, u32[]{:S(2)}) collective-permute-start(f32[8,128]{1,0:T(8,128)S(1)} %gather_numbers.1.own_numbers), channel_id=1, source_target_pairs={{0,1},{1,0},{2,3},{3,2},{4,5},{5,4},{6,7},{7,6},{8,9},{9,8},{10,11... | collective-permute-start | bytes 12296 | tf_op jit(solution)/shard_map/swap_numbers/ppermute | solution.py:409
  10.0 0.8 %collective-permute-done.1.far_numbers = f32[8,128]{1,0:T(8,128)S(1)} collective-permute-done((f32[8,128]{1,0:T(8,128)S(1)}, f32[8,128]{1,0:T(8,128)S(1)}, u32[]{:S(2)}, u32[]{:S(2)}) %collective-permute-start.1) | collective-permute-done | bytes 4128 | tf_op jit(solution)/shard_map/swap_numbers/ppermute | solution.py:409
  10.9 0.9 %copy-done.5 = bf16[4,64,512]{2,1,0:T(8,128)(2,1)S(1)} copy-done((bf16[4,64,512]{2,1,0:T(8,128)(2,1)S(1)}, bf16[4,64,512]{2,1,0:T(8,128)(2,1)}, u32[]{:S(2)}) %copy-start.5) | copy-done | bytes 262168
  12.3 0.7 %first_stage.1 = (f32[2,64,512]{2,1,0:T(8,128)S(1)}, f32[2,64,512]{2,1,0:T(8,128)S(1)}, f32[2,64,512]{2,1,0:T(8,128)S(1)}) custom-call(s32[1]{0:T(128)} %bitcast.refs_0_.core, f32[2,8]{1,0:T(2,128)S(4)} %get-tuple-element.48.refs_1_.refs_0_.scal, f32[1,4,64,512]{3,2,1,0:T(8,128)S(1)} %copy-done, ...), custom_call_target="tpu_custom_call" | custom-call | tf_op jit(solution)/shard_map/first_stage/pallas_call | solution.py:375
  13.0 0.7 %collective-permute-start.6 = (f32[2,64,512]{2,1,0:T(8,128)S(1)}, f32[2,64,512]{2,1,0:T(8,128)S(1)}, u32[]{:S(2)}, u32[]{:S(2)}) collective-permute-start(f32[2,64,512]{2,1,0:T(8,128)S(1)} %get-tuple-element.54.refs_2_), channel_id=1, source_target_pairs={{1,2},{2,1},{3,4},{4,3},{5,6},{6,5},{7,8},{8,7},{9,10},{10,9},{11,... | collective-permute-start | bytes 786440 | tf_op jit(solution)/shard_map/pass_stage1/ppermute | solution.py:413
  14.0 0.7 %collective-permute-start.3 = (f32[2,64,512]{2,1,0:T(8,128)S(1)}, f32[2,64,512]{2,1,0:T(8,128)S(1)}, u32[]{:S(2)}, u32[]{:S(2)}) collective-permute-start(f32[2,64,512]{2,1,0:T(8,128)S(1)} %get-tuple-element.56._.refs_4_), channel_id=1, source_target_pairs={{1,2},{2,1},{3,4},{4,3},{5,6},{6,5},{7,8},{8,7},{9,10},{10,9},{11,... | collective-permute-start | bytes 786440 | tf_op jit(solution)/shard_map/pass_stage2/ppermute | solution.py:413
  14.7 0.5 %prepare_next.1 = (f32[2,64,512]{2,1,0:T(8,128)S(1)}, f32[64,512]{1,0:T(8,128)S(1)}) custom-call(s32[1]{0:T(128)} %bitcast.refs_0_.core, f32[2,8]{1,0:T(2,128)S(4)} %get-tuple-element.48.refs_1_.refs_0_.scal, bf16[3,4,64,512]{3,2,1,0:T(8,128)(2,1)S(1)} %copy-done.1, s32[3,4,64,64]{3,2,1,0:T(8,128)S(1)} %copy-done.2, bf16[4,64,512]{2,1,0:T(8,128)(2,1)S(1)} %copy-done.5, ...), custom_call_target="tpu_custom_call" | custom-call | tf_op jit(solution)/shard_map/prepare_next/pallas_call | solution.py:477
  15.7 6.9 %collective-permute-start.5 = (f32[64,512]{1,0:T(8,128)S(1)}, f32[64,512]{1,0:T(8,128)S(1)}, u32[]{:S(2)}, u32[]{:S(2)}) collective-permute-start(f32[64,512]{1,0:T(8,128)S(1)} %get-tuple-element.61.refs_6_), channel_id=1, source_target_pairs={{0,1},{1,0},{2,3},{3,2},{4,5},{5,4},{6,7},{7,6},{8,9},{9,8},{10,11... | collective-permute-start | bytes 393224 | tf_op jit(solution)/shard_map/swap_s2_own/ppermute | solution.py:409
  22.7 1.2 %prepare_back.1 = (f32[2]{0:T(128)S(4)}, f32[2,64,512]{2,1,0:T(8,128)S(1)}, f32[2,64,512]{2,1,0:T(8,128)S(1)}, f32[2,64,512]{2,1,0:T(8,128)S(1)}) custom-call(s32[1]{0:T(128)} %bitcast.refs_0_.core, bf16[4,64,512]{2,1,0:T(8,128)(2,1)} %goal.1, f32[8,128]{1,0:T(8,128)S(1)} %gather_numbers.1.own_numbers, f32[8,128]{1,0:T(8,128)S(1)} %collective-permute-done.1.far_numbers, ...), custom_call_target="tpu_custom_call" | custom-call | tf_op jit(solution)/shard_map/prepare_back/pallas_call | solution.py:460
  24.5 0.8 %third_stage.1.refs_3_ = f32[2,2,64,512]{3,2,1,0:T(8,128)S(1)} custom-call(s32[1]{0:T(128)} %bitcast.refs_0_.core, f32[2,8]{1,0:T(2,128)S(4)} %get-tuple-element.48.refs_1_.refs_0_.scal, f32[1,4,64,512]{3,2,1,0:T(8,128)S(1)} %copy-done, f32[1,4,64,512]{3,2,1,0:T(8,128)S(1)} %collective-permute-done.refs_2_.refs_3_.far, ...), custom_call_target="tpu_custom_call" | custom-call | tf_op jit(solution)/shard_map/third_stage/pallas_call | solution.py:375
  25.6 0.5 %turn.1 = (f32[2,64,512]{2,1,0:T(8,128)S(1)}, f32[2,64,512]{2,1,0:T(8,128)S(1)}, f32[2,2,64,512]{3,2,1,0:T(8,128)S(1)}, f32[2,2,64,512]{3,2,1,0:T(8,128)S(1)}, f32[2,64,512]{2,1,0:T(8,128)S(1)}) custom-call(f32[2,8]{1,0:T(2,128)S(4)} %get-tuple-element.48.refs_1_.refs_0_.scal, f32[2]{0:T(128)S(4)} %get-tuple-element.57.refs_1_, ...), custom_call_target="tpu_custom_call" | custom-call | tf_op jit(solution)/shard_map/turn/pallas_call | solution.py:375
  26.1 0.7 %collective-permute-start.8 = (f32[2,2,64,512]{3,2,1,0:T(8,128)S(1)}, f32[2,2,64,512]{3,2,1,0:T(8,128)S(1)}, u32[]{:S(2)}, u32[]{:S(2)}) collective-permute-start(f32[2,2,64,512]{3,2,1,0:T(8,128)S(1)} %get-tuple-element.66.refs_1_), channel_id=1, source_target_pairs={{1,2},{2,1},{3,4},{4,3},{5,6},{6,5},{7,8},{8,7},{9,10},{10,9},{11,... | collective-permute-start | bytes 1572872 | tf_op jit(solution)/shard_map/pass_back2/ppermute | solution.py:413
  26.8 0.5 turn_inner.1
  27.3 6.5 %collective-permute-start.9 = (f32[88,512]{1,0:T(8,128)S(1)}, f32[88,512]{1,0:T(8,128)S(1)}, u32[]{:S(2)}, u32[]{:S(2)}) collective-permute-start(f32[88,512]{1,0:T(8,128)S(1)} %get-tuple-element.74.refs_11_), channel_id=1, source_target_pairs={{0,1},{1,0},{2,3},{3,2},{4,5},{5,4},{6,7},{7,6},{8,9},{9,8},{10,11... | collective-permute-start | bytes 540680 | tf_op jit(solution)/shard_map/swap_pin/ppermute | solution.py:409
  34.4 0.5 collective-permute-done.9.refs_14_
  35.5 0.7 %back_second.1 = (f32[2,2,64,512]{3,2,1,0:T(8,128)S(1)}, f32[2,64,512]{2,1,0:T(8,128)S(1)}, f32[8,128]{1,0:T(8,128)S(1)}) custom-call(f32[2,8]{1,0:T(2,128)S(4)} %get-tuple-element.48.refs_1_.refs_0_.scal, f32[2,2,64,512]{3,2,1,0:T(8,128)S(1)} %get-tuple-element.66.refs_1_, f32[2,64,512]{2,1,0:T(8,128)S(1)} %get-tuple-element.67.refs_2_.refs_3_, ...), custom_call_target="tpu_custom_call" | custom-call | tf_op jit(solution)/shard_map/back_second/pallas_call | solution.py:375
  36.3 1.6 %collective-permute-start.12 = (f32[8,128]{1,0:T(8,128)S(1)}, f32[8,128]{1,0:T(8,128)S(1)}, u32[]{:S(2)}, u32[]{:S(2)}) collective-permute-start(f32[8,128]{1,0:T(8,128)S(1)} %get-tuple-element.78), channel_id=1, source_target_pairs={{0,4},{2,6},{4,0},{6,2},{8,12},{10,14},{12,8},{14,10},{1,5},{3,7},... | collective-permute-start | bytes 12296 | tf_op jit(solution)/shard_map/goal_sum/ppermute | solution.py:529
  37.9 2.0 %collective-permute-done.12 = f32[8,128]{1,0:T(8,128)S(1)} collective-permute-done((f32[8,128]{1,0:T(8,128)S(1)}, f32[8,128]{1,0:T(8,128)S(1)}, u32[]{:S(2)}, u32[]{:S(2)}) %collective-permute-start.12) | collective-permute-done | bytes 4128 | tf_op jit(solution)/shard_map/goal_sum/ppermute | solution.py:529
  39.9 2.6 %collective-permute-start.14 = (f32[8,128]{1,0:T(8,128)S(1)}, f32[8,128]{1,0:T(8,128)S(1)}, u32[]{:S(2)}, u32[]{:S(2)}) collective-permute-start(f32[8,128]{1,0:T(8,128)S(1)} %add.3.refs_7_.refs_13_), channel_id=1, source_target_pairs={{0,8},{2,10},{4,12},{6,14},{8,0},{10,2},{12,4},{14,6},{1,9},{3,11}... | collective-permute-start | bytes 12296 | tf_op jit(solution)/shard_map/goal_sum/ppermute | solution.py:529
  42.9 0.7 %collective-permute-start.13 = (f32[2,64,512]{2,1,0:T(8,128)S(1)}, f32[2,64,512]{2,1,0:T(8,128)S(1)}, u32[]{:S(2)}, u32[]{:S(2)}) collective-permute-start(f32[2,64,512]{2,1,0:T(8,128)S(1)} %get-tuple-element.79), channel_id=1, source_target_pairs={{1,2},{2,1},{3,4},{4,3},{5,6},{6,5},{7,8},{8,7},{9,10},{10,9},{11,... | collective-permute-start | bytes 786440 | tf_op jit(solution)/shard_map/pass_back1/ppermute | solution.py:413
  43.6 0.9 %collective-permute-done.14.refs_14_ = f32[8,128]{1,0:T(8,128)S(1)} collective-permute-done((f32[8,128]{1,0:T(8,128)S(1)}, f32[8,128]{1,0:T(8,128)S(1)}, u32[]{:S(2)}, u32[]{:S(2)}) %collective-permute-start.14) | collective-permute-done | bytes 4128 | tf_op jit(solution)/shard_map/goal_sum/ppermute | solution.py:529
  44.5 0.8 %close.1 = (f32[2,64,256]{2,1,0:T(8,128)S(1)}, f32[4,64,512]{2,1,0:T(8,128)S(1)}, f32[2,64,256]{2,1,0:T(8,128)S(1)}, f32[8,128]{1,0:T(8,128)S(1)}, f32[64,512]{1,0:T(8,128)S(1)}, /*index=5*/f32[64,512]{1,0:T(8,128)S(1)}) custom-call(s32[1]{0:T(128)} %bitcast.refs_0_.core, f32[2,8]{1,0:T(2,128)S(4)} %get-tuple-element.48.refs_1_.refs_0_.scal, ...), custom_call_target="tpu_custom_call" | custom-call | flops 16000000000 | bytes 48000000 | tf_op jit(solution)/shard_map/close/pallas_call | solution.py:375
  45.3 2.9 %collective-permute-start.16 = (f32[2,64,256]{2,1,0:T(8,128)S(1)}, f32[2,64,256]{2,1,0:T(8,128)S(1)}, u32[]{:S(2)}, u32[]{:S(2)}) collective-permute-start(f32[2,64,256]{2,1,0:T(8,128)S(1)} %get-tuple-element.85), channel_id=1, source_target_pairs={{0,1},{1,0},{2,3},{3,2},{4,5},{5,4},{6,7},{7,6},{8,9},{9,8},{10,11... | collective-permute-start | bytes 393224 | tf_op jit(solution)/shard_map/swap_gradient/ppermute | solution.py:409
  49.7 0.9 %write_inner.1 = (f32[1,4,64,512]{3,2,1,0:T(8,128)}, f32[4,64,256]{2,1,0:T(8,128)}) custom-call(s32[1]{0:T(128)} %bitcast.refs_0_.core, f32[4,64,512]{2,1,0:T(8,128)S(1)} %get-tuple-element.82.refs_1_, f32[2,64,256]{2,1,0:T(8,128)S(1)} %get-tuple-element.84.refs_2_, f32[2,64,256]{2,1,0:T(8,128)S(1)} %collective-permute-done.16.refs_3_, ...), custom_call_target="tpu_custom_call" | custom-call | tf_op jit(solution)/shard_map/write_inner/pallas_call | solution.py:375
  50.7 1.6 %collective-permute-done.15.refs_3_ = f32[8,128]{1,0:T(8,128)S(1)} collective-permute-done((f32[8,128]{1,0:T(8,128)S(1)}, f32[8,128]{1,0:T(8,128)S(1)}, u32[]{:S(2)}, u32[]{:S(2)}) %collective-permute-start.15) | collective-permute-done | bytes 4128 | tf_op jit(solution)/shard_map/goal_sum/ppermute | solution.py:529
  52.4 0.6 %finish.1 = f32[1]{0:T(128)} custom-call(f32[8,128]{1,0:T(8,128)S(1)} %get-tuple-element.92.refs_0_), custom_call_target="tpu_custom_call" | custom-call | tf_op jit(solution)/shard_map/finish/pallas_call | solution.py:375
  53.1 0.7 %write_outer.2._ = f32[1,4,64,512]{3,2,1,0:T(8,128)} custom-call(s32[1]{0:T(128)} %bitcast.refs_0_.core, f32[64,512]{1,0:T(8,128)S(1)} %get-tuple-element.90.value, f32[1,4,64,512]{3,2,1,0:T(8,128)} %get-tuple-element.88.refs_4_._), custom_call_target="tpu_custom_call", output_to_operand_aliasing={{}: (2, {})} | custom-call | tf_op jit(solution)/shard_map/write_outer/pallas_call | solution.py:565
  53.8 0.7 %write_outer.3 = f32[1,4,64,512]{3,2,1,0:T(8,128)} custom-call(s32[1]{0:T(128)} %bitcast.refs_0_.core, f32[64,512]{1,0:T(8,128)S(1)} %collective-permute-done.19.value, f32[1,4,64,512]{3,2,1,0:T(8,128)} %write_outer.2._), custom_call_target="tpu_custom_call", output_to_operand_aliasing={{}: (2, {})} | custom-call | tf_op jit(solution)/shard_map/write_outer/pallas_call | solution.py:565
  (42 shorter events, 5.5 us)
Async XLA Ops:
  0.6 2.3 %collective-permute-start = (f32[1,4,64,512]{3,2,1,0:T(8,128)}, f32[1,4,64,512]{3,2,1,0:T(8,128)S(1)}, u32[]{:S(2)}, u32[]{:S(2)}) collective-permute-start(f32[1,4,64,512]{3,2,1,0:T(8,128)} %refs_2_.7), channel_id=1, source_target_pairs={{0,1},{1,0},{2,3},{3,2},{4,5},{5,4},{6,7},{7,6},{8,9},{9,8},{10,11... | collective-permute-start | bytes 1572872 | tf_op jit(solution)/shard_map/swap_state/ppermute | solution.py:409
  1.1 1.8 %copy-start = (f32[1,4,64,512]{3,2,1,0:T(8,128)S(1)}, f32[1,4,64,512]{3,2,1,0:T(8,128)}, u32[]{:S(2)}) copy-start(f32[1,4,64,512]{3,2,1,0:T(8,128)} %refs_2_.7) | copy-start | bytes 1572868
  1.2 1.8 %copy-start.1 = (bf16[3,4,64,512]{3,2,1,0:T(8,128)(2,1)S(1)}, bf16[3,4,64,512]{3,2,1,0:T(8,128)(2,1)}, u32[]{:S(2)}) copy-start(bf16[3,4,64,512]{3,2,1,0:T(8,128)(2,1)} %speed.3) | copy-start | bytes 2359300
  1.2 1.8 %copy-start.2 = (s32[3,4,64,64]{3,2,1,0:T(8,128)S(1)}, s32[3,4,64,64]{3,2,1,0:T(8,128)}, u32[]{:S(2)}) copy-start(s32[3,4,64,64]{3,2,1,0:T(8,128)} %mask.3) | copy-start | bytes 589828
  2.9 8.0 %copy-start.3 = (f32[4,64,512]{2,1,0:T(8,128)S(1)}, f32[4,64,512]{2,1,0:T(8,128)}, u32[]{:S(2)}) copy-start(f32[4,64,512]{2,1,0:T(8,128)} %control.3) | copy-start | bytes 1572868
  3.1 2.0 %copy-start.4 = (f32[3,64,512]{2,1,0:T(8,128)}, f32[3,64,512]{2,1,0:T(8,128)S(1)}, u32[]{:S(2)}) copy-start(f32[3,64,512]{2,1,0:T(8,128)S(1)} %pack.1._) | copy-start | bytes 1179652
  3.1 10.6 %collective-permute-start.2 = (f32[3,64,512]{2,1,0:T(8,128)S(1)}, f32[3,64,512]{2,1,0:T(8,128)S(1)}, u32[]{:S(2)}, u32[]{:S(2)}) collective-permute-start(f32[3,64,512]{2,1,0:T(8,128)S(1)} %pack.1._), channel_id=1, source_target_pairs={{1,2},{2,1},{3,4},{4,3},{5,6},{6,5},{7,8},{8,7},{9,10},{10,9},{11,... | collective-permute-start | bytes 1179656 | tf_op jit(solution)/shard_map/pass_state/ppermute | solution.py:413
  5.8 5.1 %collective-permute-start.1 = (f32[8,128]{1,0:T(8,128)S(1)}, f32[8,128]{1,0:T(8,128)S(1)}, u32[]{:S(2)}, u32[]{:S(2)}) collective-permute-start(f32[8,128]{1,0:T(8,128)S(1)} %gather_numbers.1.own_numbers), channel_id=1, source_target_pairs={{0,1},{1,0},{2,3},{3,2},{4,5},{5,4},{6,7},{7,6},{8,9},{9,8},{10,11... | collective-permute-start | bytes 12296 | tf_op jit(solution)/shard_map/swap_numbers/ppermute | solution.py:409
  10.9 1.0 %copy-start.5 = (bf16[4,64,512]{2,1,0:T(8,128)(2,1)S(1)}, bf16[4,64,512]{2,1,0:T(8,128)(2,1)}, u32[]{:S(2)}) copy-start(bf16[4,64,512]{2,1,0:T(8,128)(2,1)} %decay.3) | copy-start | bytes 786436
  13.0 11.4 %collective-permute-start.6 = (f32[2,64,512]{2,1,0:T(8,128)S(1)}, f32[2,64,512]{2,1,0:T(8,128)S(1)}, u32[]{:S(2)}, u32[]{:S(2)}) collective-permute-start(f32[2,64,512]{2,1,0:T(8,128)S(1)} %get-tuple-element.54.refs_2_), channel_id=1, source_target_pairs={{1,2},{2,1},{3,4},{4,3},{5,6},{6,5},{7,8},{8,7},{9,10},{10,9},{11,... | collective-permute-start | bytes 786440 | tf_op jit(solution)/shard_map/pass_stage1/ppermute | solution.py:413
  14.0 11.2 %collective-permute-start.3 = (f32[2,64,512]{2,1,0:T(8,128)S(1)}, f32[2,64,512]{2,1,0:T(8,128)S(1)}, u32[]{:S(2)}, u32[]{:S(2)}) collective-permute-start(f32[2,64,512]{2,1,0:T(8,128)S(1)} %get-tuple-element.56._.refs_4_), channel_id=1, source_target_pairs={{1,2},{2,1},{3,4},{4,3},{5,6},{6,5},{7,8},{8,7},{9,10},{10,9},{11,... | collective-permute-start | bytes 786440 | tf_op jit(solution)/shard_map/pass_stage2/ppermute | solution.py:413
  15.7 8.8 %collective-permute-start.5 = (f32[64,512]{1,0:T(8,128)S(1)}, f32[64,512]{1,0:T(8,128)S(1)}, u32[]{:S(2)}, u32[]{:S(2)}) collective-permute-start(f32[64,512]{1,0:T(8,128)S(1)} %get-tuple-element.61.refs_6_), channel_id=1, source_target_pairs={{0,1},{1,0},{2,3},{3,2},{4,5},{5,4},{6,7},{7,6},{8,9},{9,8},{10,11... | collective-permute-start | bytes 393224 | tf_op jit(solution)/shard_map/swap_s2_own/ppermute | solution.py:409
  22.7 1.8 %collective-permute-start.4 = (f32[64,512]{1,0:T(8,128)S(1)}, f32[64,512]{1,0:T(8,128)S(1)}, u32[]{:S(2)}, u32[]{:S(2)}) collective-permute-start(f32[64,512]{1,0:T(8,128)S(1)} %get-tuple-element.62.refs_7_), channel_id=1, source_target_pairs={{0,1},{1,0},{2,3},{3,2},{4,5},{5,4},{6,7},{7,6},{8,9},{9,8},{10,11... | collective-permute-start | bytes 393224 | tf_op jit(solution)/shard_map/swap_s2_far/ppermute | solution.py:409
  23.9 1.7 %collective-permute-start.7 = (f32[2,64,512]{2,1,0:T(8,128)S(1)}, f32[2,64,512]{2,1,0:T(8,128)S(1)}, u32[]{:S(2)}, u32[]{:S(2)}) collective-permute-start(f32[2,64,512]{2,1,0:T(8,128)S(1)} %get-tuple-element.65), channel_id=1, source_target_pairs={{0,1},{1,0},{2,3},{3,2},{4,5},{5,4},{6,7},{7,6},{8,9},{9,8},{10,11... | collective-permute-start | bytes 786440 | tf_op jit(solution)/shard_map/swap_after/ppermute | solution.py:409
  26.1 16.4 %collective-permute-start.8 = (f32[2,2,64,512]{3,2,1,0:T(8,128)S(1)}, f32[2,2,64,512]{3,2,1,0:T(8,128)S(1)}, u32[]{:S(2)}, u32[]{:S(2)}) collective-permute-start(f32[2,2,64,512]{3,2,1,0:T(8,128)S(1)} %get-tuple-element.66.refs_1_), channel_id=1, source_target_pairs={{1,2},{2,1},{3,4},{4,3},{5,6},{6,5},{7,8},{8,7},{9,10},{10,9},{11,... | collective-permute-start | bytes 1572872 | tf_op jit(solution)/shard_map/pass_back2/ppermute | solution.py:413
  27.3 7.6 %collective-permute-start.9 = (f32[88,512]{1,0:T(8,128)S(1)}, f32[88,512]{1,0:T(8,128)S(1)}, u32[]{:S(2)}, u32[]{:S(2)}) collective-permute-start(f32[88,512]{1,0:T(8,128)S(1)} %get-tuple-element.74.refs_11_), channel_id=1, source_target_pairs={{0,1},{1,0},{2,3},{3,2},{4,5},{5,4},{6,7},{7,6},{8,9},{9,8},{10,11... | collective-permute-start | bytes 540680 | tf_op jit(solution)/shard_map/swap_pin/ppermute | solution.py:409
  33.9 1.4 %collective-permute-start.10 = (f32[88,512]{1,0:T(8,128)S(1)}, f32[88,512]{1,0:T(8,128)S(1)}, u32[]{:S(2)}, u32[]{:S(2)}) collective-permute-start(f32[88,512]{1,0:T(8,128)S(1)} %get-tuple-element.75.refs_12_), channel_id=1, source_target_pairs={{0,1},{1,0},{2,3},{3,2},{4,5},{5,4},{6,7},{7,6},{8,9},{9,8},{10,11... | collective-permute-start | bytes 540680 | tf_op jit(solution)/shard_map/swap_pin/ppermute | solution.py:409
  33.9 1.6 %collective-permute-start.11 = (f32[88,512]{1,0:T(8,128)S(1)}, f32[88,512]{1,0:T(8,128)S(1)}, u32[]{:S(2)}, u32[]{:S(2)}) collective-permute-start(f32[88,512]{1,0:T(8,128)S(1)} %get-tuple-element.76.refs_13_), channel_id=1, source_target_pairs={{0,1},{1,0},{2,3},{3,2},{4,5},{5,4},{6,7},{7,6},{8,9},{9,8},{10,11... | collective-permute-start | bytes 540680 | tf_op jit(solution)/shard_map/swap_pin/ppermute | solution.py:409
  36.3 3.7 %collective-permute-start.12 = (f32[8,128]{1,0:T(8,128)S(1)}, f32[8,128]{1,0:T(8,128)S(1)}, u32[]{:S(2)}, u32[]{:S(2)}) collective-permute-start(f32[8,128]{1,0:T(8,128)S(1)} %get-tuple-element.78), channel_id=1, source_target_pairs={{0,4},{2,6},{4,0},{6,2},{8,12},{10,14},{12,8},{14,10},{1,5},{3,7},... | collective-permute-start | bytes 12296 | tf_op jit(solution)/shard_map/goal_sum/ppermute | solution.py:529
  39.9 4.5 %collective-permute-start.14 = (f32[8,128]{1,0:T(8,128)S(1)}, f32[8,128]{1,0:T(8,128)S(1)}, u32[]{:S(2)}, u32[]{:S(2)}) collective-permute-start(f32[8,128]{1,0:T(8,128)S(1)} %add.3.refs_7_.refs_13_), channel_id=1, source_target_pairs={{0,8},{2,10},{4,12},{6,14},{8,0},{10,2},{12,4},{14,6},{1,9},{3,11}... | collective-permute-start | bytes 12296 | tf_op jit(solution)/shard_map/goal_sum/ppermute | solution.py:529
  42.9 9.4 %collective-permute-start.13 = (f32[2,64,512]{2,1,0:T(8,128)S(1)}, f32[2,64,512]{2,1,0:T(8,128)S(1)}, u32[]{:S(2)}, u32[]{:S(2)}) collective-permute-start(f32[2,64,512]{2,1,0:T(8,128)S(1)} %get-tuple-element.79), channel_id=1, source_target_pairs={{1,2},{2,1},{3,4},{4,3},{5,6},{6,5},{7,8},{8,7},{9,10},{10,9},{11,... | collective-permute-start | bytes 786440 | tf_op jit(solution)/shard_map/pass_back1/ppermute | solution.py:413
  45.3 3.9 %collective-permute-start.16 = (f32[2,64,256]{2,1,0:T(8,128)S(1)}, f32[2,64,256]{2,1,0:T(8,128)S(1)}, u32[]{:S(2)}, u32[]{:S(2)}) collective-permute-start(f32[2,64,256]{2,1,0:T(8,128)S(1)} %get-tuple-element.85), channel_id=1, source_target_pairs={{0,1},{1,0},{2,3},{3,2},{4,5},{5,4},{6,7},{7,6},{8,9},{9,8},{10,11... | collective-permute-start | bytes 393224 | tf_op jit(solution)/shard_map/swap_gradient/ppermute | solution.py:409
  48.2 1.3 %collective-permute-start.17 = (f32[64,512]{1,0:T(8,128)S(1)}, f32[64,512]{1,0:T(8,128)S(1)}, u32[]{:S(2)}, u32[]{:S(2)}) collective-permute-start(f32[64,512]{1,0:T(8,128)S(1)} %get-tuple-element.86), channel_id=1, source_target_pairs={{0,1},{1,0},{2,3},{3,2},{4,5},{5,4},{6,7},{7,6},{8,9},{9,8},{10,11... | collective-permute-start | bytes 393224 | tf_op jit(solution)/shard_map/swap_adjoint/ppermute | solution.py:409
  48.3 1.5 %collective-permute-start.18 = (f32[64,512]{1,0:T(8,128)S(1)}, f32[64,512]{1,0:T(8,128)S(1)}, u32[]{:S(2)}, u32[]{:S(2)}) collective-permute-start(f32[64,512]{1,0:T(8,128)S(1)} %get-tuple-element.87), channel_id=1, source_target_pairs={{0,1},{1,0},{2,3},{3,2},{4,5},{5,4},{6,7},{7,6},{8,9},{9,8},{10,11... | collective-permute-start | bytes 393224 | tf_op jit(solution)/shard_map/swap_adjoint/ppermute | solution.py:409
  48.7 3.6 %collective-permute-start.15 = (f32[8,128]{1,0:T(8,128)S(1)}, f32[8,128]{1,0:T(8,128)S(1)}, u32[]{:S(2)}, u32[]{:S(2)}) collective-permute-start(f32[8,128]{1,0:T(8,128)S(1)} %get-tuple-element.83.refs_2_), channel_id=1, source_target_pairs={{0,2},{2,0},{4,6},{6,4},{8,10},{10,8},{12,14},{14,12},{1,3},{3,1},... | collective-permute-start | bytes 12296 | tf_op jit(solution)/shard_map/goal_sum/ppermute | solution.py:529
  52.4 1.4 %collective-permute-start.19 = (f32[64,512]{1,0:T(8,128)S(1)}, f32[64,512]{1,0:T(8,128)S(1)}, u32[]{:S(2)}, u32[]{:S(2)}) collective-permute-start(f32[64,512]{1,0:T(8,128)S(1)} %get-tuple-element.89), channel_id=1, source_target_pairs={{0,1},{1,0},{2,3},{3,2},{4,5},{5,4},{6,7},{7,6},{8,9},{9,8},{10,11... | collective-permute-start | bytes 393224 | tf_op jit(solution)/shard_map/swap_outer/ppermute | solution.py:409

commit v7 on v6

--- a/solution.py
+++ b/solution.py
@@ -13,7 +13,7 @@
 penalty = 0.1
 weight_denominator = 16.0
 
-VMEM_LIMIT = 24 * 1024 * 1024
+VMEM_LIMIT = 8 * 1024 * 1024
 AXES = ("space", "node")
 LONG = 8
 

time: 54.8 us -> 54.7 us (level)
  no operation moved by 1% of the time
where the time goes in v7:
time: 54.7 us; the launch traced here: 54.3 us
  starting transfers between devices  30.5 us (56%)
  Pallas kernels  11.1 us (20%)
  waiting for transfers between devices  9.62 us (18%)
  between operations  2.15 us (4%)
  local copies, waits for them, and re-layouts  0.97 us (2%)
    ppermute x12, starting transfers between devices, swap(): return lax.ppermute(x, AXES, within)  22.8 us
    pallas_call x15, Pallas kernels, on_core(): pl.pallas_call(run, out_shape=out_shape, in_specs=[pl.BlockSpec(memory_sp...  6.87 us
    ppermute x12, waiting for transfers between devices, swap(): return lax.ppermute(x, AXES, within)  5.04 us
    ppermute x3, waiting for transfers between devices, from_pair(): lax.ppermute(x, 'space', [(i, i ^ steps[k]) for i in range(sections)])  4.57 us
    ppermute x3, starting transfers between devices, from_pair(): lax.ppermute(x, 'space', [(i, i ^ steps[k]) for i in range(sections)])  4.24 us
    ppermute x5, starting transfers between devices, pass_on(): return lax.ppermute(x, AXES, across)  3.41 us
    pallas_call x2, Pallas kernels, shards(): pl.pallas_call(functools.partial(write_outer, far), out_shape=jax.ShapeDt...  1.33 us
    pallas_call x1, Pallas kernels, shards(): pl.pallas_call(prepare_back, out_shape=[pltpu.SMEM((2,), jnp.float32)] +...  1.16 us
  transfers between devices with their start and end apart: 20, of which 12 were waited for; matrix products, arithmetic and copies ran while one was open for 0% of the time, Pallas kernels for 18%

profile of v7, /device:TPU:0, one launch (start us, length us, event | category | flops | bytes accessed | tf_op | source)
XLA Modules:
  0.0 54.3 jit_solution(13280685682319919570)
XLA Ops:
  0.6 0.5 collective-permute-start
  1.2 1.7 %collective-permute-done.refs_2_.refs_3_.far = f32[1,4,64,512]{3,2,1,0:T(8,128)S(1)} collective-permute-done((f32[1,4,64,512]{3,2,1,0:T(8,128)}, f32[1,4,64,512]{3,2,1,0:T(8,128)S(1)}, u32[]{:S(2)}, u32[]{:S(2)}) %collective-permute-start) | collective-permute-done | bytes 524320 | tf_op jit(solution)/shard_map/swap_state/ppermute | solution.py:409
  3.1 0.7 %collective-permute-start.2 = (f32[3,64,512]{2,1,0:T(8,128)S(1)}, f32[3,64,512]{2,1,0:T(8,128)S(1)}, u32[]{:S(2)}, u32[]{:S(2)}) collective-permute-start(f32[3,64,512]{2,1,0:T(8,128)S(1)} %pack.1._), channel_id=1, source_target_pairs={{1,2},{2,1},{3,4},{4,3},{5,6},{6,5},{7,8},{8,7},{9,10},{10,9},{11,... | collective-permute-start | bytes 1179656 | tf_op jit(solution)/shard_map/pass_state/ppermute | solution.py:413
  5.1 0.7 %gather_numbers.1.own_numbers = f32[8,128]{1,0:T(8,128)S(1)} custom-call(s32[1,8]{1,0:T(1,128)} %index.1, s32[1]{0:T(128)S(6)} %copy.17.weight, s32[1]{0:T(128)S(6)} %copy.18.step, f32[3,64,512]{2,1,0:T(8,128)} %copy-done.4), custom_call_target="tpu_custom_call" | custom-call | tf_op jit(solution)/shard_map/gather_numbers/pallas_call | solution.py:429
  5.8 4.3 %collective-permute-start.1 = (f32[8,128]{1,0:T(8,128)S(1)}, f32[8,128]{1,0:T(8,128)S(1)}, u32[]{:S(2)}, u32[]{:S(2)}) collective-permute-start(f32[8,128]{1,0:T(8,128)S(1)} %gather_numbers.1.own_numbers), channel_id=1, source_target_pairs={{0,1},{1,0},{2,3},{3,2},{4,5},{5,4},{6,7},{7,6},{8,9},{9,8},{10,11... | collective-permute-start | bytes 12296 | tf_op jit(solution)/shard_map/swap_numbers/ppermute | solution.py:409
  10.0 0.8 %collective-permute-done.1.far_numbers = f32[8,128]{1,0:T(8,128)S(1)} collective-permute-done((f32[8,128]{1,0:T(8,128)S(1)}, f32[8,128]{1,0:T(8,128)S(1)}, u32[]{:S(2)}, u32[]{:S(2)}) %collective-permute-start.1) | collective-permute-done | bytes 4128 | tf_op jit(solution)/shard_map/swap_numbers/ppermute | solution.py:409
  10.9 0.9 %copy-done.5 = bf16[4,64,512]{2,1,0:T(8,128)(2,1)S(1)} copy-done((bf16[4,64,512]{2,1,0:T(8,128)(2,1)S(1)}, bf16[4,64,512]{2,1,0:T(8,128)(2,1)}, u32[]{:S(2)}) %copy-start.5) | copy-done | bytes 262168
  11.8 0.5 prepare.1
  12.3 0.7 %first_stage.1 = (f32[2,64,512]{2,1,0:T(8,128)S(1)}, f32[2,64,512]{2,1,0:T(8,128)S(1)}, f32[2,64,512]{2,1,0:T(8,128)S(1)}) custom-call(s32[1]{0:T(128)} %bitcast.refs_0_.core, f32[2,8]{1,0:T(2,128)S(4)} %get-tuple-element.48.refs_1_.refs_0_.scal, f32[1,4,64,512]{3,2,1,0:T(8,128)S(1)} %copy-done, ...), custom_call_target="tpu_custom_call" | custom-call | tf_op jit(solution)/shard_map/first_stage/pallas_call | solution.py:375
  13.0 0.7 %collective-permute-start.6 = (f32[2,64,512]{2,1,0:T(8,128)S(1)}, f32[2,64,512]{2,1,0:T(8,128)S(1)}, u32[]{:S(2)}, u32[]{:S(2)}) collective-permute-start(f32[2,64,512]{2,1,0:T(8,128)S(1)} %get-tuple-element.54.refs_2_), channel_id=1, source_target_pairs={{1,2},{2,1},{3,4},{4,3},{5,6},{6,5},{7,8},{8,7},{9,10},{10,9},{11,... | collective-permute-start | bytes 786440 | tf_op jit(solution)/shard_map/pass_stage1/ppermute | solution.py:413
  14.0 0.7 %collective-permute-start.3 = (f32[2,64,512]{2,1,0:T(8,128)S(1)}, f32[2,64,512]{2,1,0:T(8,128)S(1)}, u32[]{:S(2)}, u32[]{:S(2)}) collective-permute-start(f32[2,64,512]{2,1,0:T(8,128)S(1)} %get-tuple-element.56._.refs_4_), channel_id=1, source_target_pairs={{1,2},{2,1},{3,4},{4,3},{5,6},{6,5},{7,8},{8,7},{9,10},{10,9},{11,... | collective-permute-start | bytes 786440 | tf_op jit(solution)/shard_map/pass_stage2/ppermute | solution.py:413
  14.7 0.5 %prepare_next.1 = (f32[2,64,512]{2,1,0:T(8,128)S(1)}, f32[64,512]{1,0:T(8,128)S(1)}) custom-call(s32[1]{0:T(128)} %bitcast.refs_0_.core, f32[2,8]{1,0:T(2,128)S(4)} %get-tuple-element.48.refs_1_.refs_0_.scal, bf16[3,4,64,512]{3,2,1,0:T(8,128)(2,1)S(1)} %copy-done.1, s32[3,4,64,64]{3,2,1,0:T(8,128)S(1)} %copy-done.2, bf16[4,64,512]{2,1,0:T(8,128)(2,1)S(1)} %copy-done.5, ...), custom_call_target="tpu_custom_call" | custom-call | tf_op jit(solution)/shard_map/prepare_next/pallas_call | solution.py:477
  15.7 7.0 %collective-permute-start.5 = (f32[64,512]{1,0:T(8,128)S(1)}, f32[64,512]{1,0:T(8,128)S(1)}, u32[]{:S(2)}, u32[]{:S(2)}) collective-permute-start(f32[64,512]{1,0:T(8,128)S(1)} %get-tuple-element.61.refs_6_), channel_id=1, source_target_pairs={{0,1},{1,0},{2,3},{3,2},{4,5},{5,4},{6,7},{7,6},{8,9},{9,8},{10,11... | collective-permute-start | bytes 393224 | tf_op jit(solution)/shard_map/swap_s2_own/ppermute | solution.py:409
  22.7 1.2 %prepare_back.1 = (f32[2]{0:T(128)S(4)}, f32[2,64,512]{2,1,0:T(8,128)S(1)}, f32[2,64,512]{2,1,0:T(8,128)S(1)}, f32[2,64,512]{2,1,0:T(8,128)S(1)}) custom-call(s32[1]{0:T(128)} %bitcast.refs_0_.core, bf16[4,64,512]{2,1,0:T(8,128)(2,1)} %goal.1, f32[8,128]{1,0:T(8,128)S(1)} %gather_numbers.1.own_numbers, f32[8,128]{1,0:T(8,128)S(1)} %collective-permute-done.1.far_numbers, ...), custom_call_target="tpu_custom_call" | custom-call | tf_op jit(solution)/shard_map/prepare_back/pallas_call | solution.py:460
  24.5 0.8 %third_stage.1.refs_3_ = f32[2,2,64,512]{3,2,1,0:T(8,128)S(1)} custom-call(s32[1]{0:T(128)} %bitcast.refs_0_.core, f32[2,8]{1,0:T(2,128)S(4)} %get-tuple-element.48.refs_1_.refs_0_.scal, f32[1,4,64,512]{3,2,1,0:T(8,128)S(1)} %copy-done, f32[1,4,64,512]{3,2,1,0:T(8,128)S(1)} %collective-permute-done.refs_2_.refs_3_.far, ...), custom_call_target="tpu_custom_call" | custom-call | tf_op jit(solution)/shard_map/third_stage/pallas_call | solution.py:375
  25.6 0.5 turn.1
  26.1 0.7 %collective-permute-start.8 = (f32[2,2,64,512]{3,2,1,0:T(8,128)S(1)}, f32[2,2,64,512]{3,2,1,0:T(8,128)S(1)}, u32[]{:S(2)}, u32[]{:S(2)}) collective-permute-start(f32[2,2,64,512]{3,2,1,0:T(8,128)S(1)} %get-tuple-element.66.refs_1_), channel_id=1, source_target_pairs={{1,2},{2,1},{3,4},{4,3},{5,6},{6,5},{7,8},{8,7},{9,10},{10,9},{11,... | collective-permute-start | bytes 1572872 | tf_op jit(solution)/shard_map/pass_back2/ppermute | solution.py:413
  27.3 6.5 %collective-permute-start.9 = (f32[88,512]{1,0:T(8,128)S(1)}, f32[88,512]{1,0:T(8,128)S(1)}, u32[]{:S(2)}, u32[]{:S(2)}) collective-permute-start(f32[88,512]{1,0:T(8,128)S(1)} %get-tuple-element.74.refs_11_), channel_id=1, source_target_pairs={{0,1},{1,0},{2,3},{3,2},{4,5},{5,4},{6,7},{7,6},{8,9},{9,8},{10,11... | collective-permute-start | bytes 540680 | tf_op jit(solution)/shard_map/swap_pin/ppermute | solution.py:409
  34.3 0.5 collective-permute-done.9.refs_14_
  35.5 0.7 %back_second.1 = (f32[2,2,64,512]{3,2,1,0:T(8,128)S(1)}, f32[2,64,512]{2,1,0:T(8,128)S(1)}, f32[8,128]{1,0:T(8,128)S(1)}) custom-call(f32[2,8]{1,0:T(2,128)S(4)} %get-tuple-element.48.refs_1_.refs_0_.scal, f32[2,2,64,512]{3,2,1,0:T(8,128)S(1)} %get-tuple-element.66.refs_1_, f32[2,64,512]{2,1,0:T(8,128)S(1)} %get-tuple-element.67.refs_2_.refs_3_, ...), custom_call_target="tpu_custom_call" | custom-call | tf_op jit(solution)/shard_map/back_second/pallas_call | solution.py:375
  36.2 1.6 %collective-permute-start.12 = (f32[8,128]{1,0:T(8,128)S(1)}, f32[8,128]{1,0:T(8,128)S(1)}, u32[]{:S(2)}, u32[]{:S(2)}) collective-permute-start(f32[8,128]{1,0:T(8,128)S(1)} %get-tuple-element.78), channel_id=1, source_target_pairs={{0,4},{2,6},{4,0},{6,2},{8,12},{10,14},{12,8},{14,10},{1,5},{3,7},... | collective-permute-start | bytes 12296 | tf_op jit(solution)/shard_map/goal_sum/ppermute | solution.py:529
  37.8 2.0 %collective-permute-done.12 = f32[8,128]{1,0:T(8,128)S(1)} collective-permute-done((f32[8,128]{1,0:T(8,128)S(1)}, f32[8,128]{1,0:T(8,128)S(1)}, u32[]{:S(2)}, u32[]{:S(2)}) %collective-permute-start.12) | collective-permute-done | bytes 4128 | tf_op jit(solution)/shard_map/goal_sum/ppermute | solution.py:529
  39.9 2.6 %collective-permute-start.14 = (f32[8,128]{1,0:T(8,128)S(1)}, f32[8,128]{1,0:T(8,128)S(1)}, u32[]{:S(2)}, u32[]{:S(2)}) collective-permute-start(f32[8,128]{1,0:T(8,128)S(1)} %add.3.refs_7_.refs_13_), channel_id=1, source_target_pairs={{0,8},{2,10},{4,12},{6,14},{8,0},{10,2},{12,4},{14,6},{1,9},{3,11}... | collective-permute-start | bytes 12296 | tf_op jit(solution)/shard_map/goal_sum/ppermute | solution.py:529
  42.8 0.7 %collective-permute-start.13 = (f32[2,64,512]{2,1,0:T(8,128)S(1)}, f32[2,64,512]{2,1,0:T(8,128)S(1)}, u32[]{:S(2)}, u32[]{:S(2)}) collective-permute-start(f32[2,64,512]{2,1,0:T(8,128)S(1)} %get-tuple-element.79), channel_id=1, source_target_pairs={{1,2},{2,1},{3,4},{4,3},{5,6},{6,5},{7,8},{8,7},{9,10},{10,9},{11,... | collective-permute-start | bytes 786440 | tf_op jit(solution)/shard_map/pass_back1/ppermute | solution.py:413
  43.5 0.9 %collective-permute-done.14.refs_14_ = f32[8,128]{1,0:T(8,128)S(1)} collective-permute-done((f32[8,128]{1,0:T(8,128)S(1)}, f32[8,128]{1,0:T(8,128)S(1)}, u32[]{:S(2)}, u32[]{:S(2)}) %collective-permute-start.14) | collective-permute-done | bytes 4128 | tf_op jit(solution)/shard_map/goal_sum/ppermute | solution.py:529
  44.4 0.8 %close.1 = (f32[2,64,256]{2,1,0:T(8,128)S(1)}, f32[4,64,512]{2,1,0:T(8,128)S(1)}, f32[2,64,256]{2,1,0:T(8,128)S(1)}, f32[8,128]{1,0:T(8,128)S(1)}, f32[64,512]{1,0:T(8,128)S(1)}, /*index=5*/f32[64,512]{1,0:T(8,128)S(1)}) custom-call(s32[1]{0:T(128)} %bitcast.refs_0_.core, f32[2,8]{1,0:T(2,128)S(4)} %get-tuple-element.48.refs_1_.refs_0_.scal, ...), custom_call_target="tpu_custom_call" | custom-call | flops 16000000000 | bytes 48000000 | tf_op jit(solution)/shard_map/close/pallas_call | solution.py:375
  45.2 2.9 %collective-permute-start.16 = (f32[2,64,256]{2,1,0:T(8,128)S(1)}, f32[2,64,256]{2,1,0:T(8,128)S(1)}, u32[]{:S(2)}, u32[]{:S(2)}) collective-permute-start(f32[2,64,256]{2,1,0:T(8,128)S(1)} %get-tuple-element.85), channel_id=1, source_target_pairs={{0,1},{1,0},{2,3},{3,2},{4,5},{5,4},{6,7},{7,6},{8,9},{9,8},{10,11... | collective-permute-start | bytes 393224 | tf_op jit(solution)/shard_map/swap_gradient/ppermute | solution.py:409
  49.6 0.9 %write_inner.1 = (f32[1,4,64,512]{3,2,1,0:T(8,128)}, f32[4,64,256]{2,1,0:T(8,128)}) custom-call(s32[1]{0:T(128)} %bitcast.refs_0_.core, f32[4,64,512]{2,1,0:T(8,128)S(1)} %get-tuple-element.82.refs_1_, f32[2,64,256]{2,1,0:T(8,128)S(1)} %get-tuple-element.84.refs_2_, f32[2,64,256]{2,1,0:T(8,128)S(1)} %collective-permute-done.16.refs_3_, ...), custom_call_target="tpu_custom_call" | custom-call | tf_op jit(solution)/shard_map/write_inner/pallas_call | solution.py:375
  50.5 1.6 %collective-permute-done.15.refs_3_ = f32[8,128]{1,0:T(8,128)S(1)} collective-permute-done((f32[8,128]{1,0:T(8,128)S(1)}, f32[8,128]{1,0:T(8,128)S(1)}, u32[]{:S(2)}, u32[]{:S(2)}) %collective-permute-start.15) | collective-permute-done | bytes 4128 | tf_op jit(solution)/shard_map/goal_sum/ppermute | solution.py:529
  52.3 0.6 %finish.1 = f32[1]{0:T(128)} custom-call(f32[8,128]{1,0:T(8,128)S(1)} %get-tuple-element.92.refs_0_), custom_call_target="tpu_custom_call" | custom-call | tf_op jit(solution)/shard_map/finish/pallas_call | solution.py:375
  53.0 0.7 %write_outer.2._ = f32[1,4,64,512]{3,2,1,0:T(8,128)} custom-call(s32[1]{0:T(128)} %bitcast.refs_0_.core, f32[64,512]{1,0:T(8,128)S(1)} %get-tuple-element.90.value, f32[1,4,64,512]{3,2,1,0:T(8,128)} %get-tuple-element.88.refs_4_._), custom_call_target="tpu_custom_call", output_to_operand_aliasing={{}: (2, {})} | custom-call | tf_op jit(solution)/shard_map/write_outer/pallas_call | solution.py:565
  53.7 0.7 %write_outer.3 = f32[1,4,64,512]{3,2,1,0:T(8,128)} custom-call(s32[1]{0:T(128)} %bitcast.refs_0_.core, f32[64,512]{1,0:T(8,128)S(1)} %collective-permute-done.19.value, f32[1,4,64,512]{3,2,1,0:T(8,128)} %write_outer.2._), custom_call_target="tpu_custom_call", output_to_operand_aliasing={{}: (2, {})} | custom-call | tf_op jit(solution)/shard_map/write_outer/pallas_call | solution.py:565
  (42 shorter events, 5.5 us)
Async XLA Ops:
  0.6 2.3 %collective-permute-start = (f32[1,4,64,512]{3,2,1,0:T(8,128)}, f32[1,4,64,512]{3,2,1,0:T(8,128)S(1)}, u32[]{:S(2)}, u32[]{:S(2)}) collective-permute-start(f32[1,4,64,512]{3,2,1,0:T(8,128)} %refs_2_.7), channel_id=1, source_target_pairs={{0,1},{1,0},{2,3},{3,2},{4,5},{5,4},{6,7},{7,6},{8,9},{9,8},{10,11... | collective-permute-start | bytes 1572872 | tf_op jit(solution)/shard_map/swap_state/ppermute | solution.py:409
  1.1 1.8 %copy-start = (f32[1,4,64,512]{3,2,1,0:T(8,128)S(1)}, f32[1,4,64,512]{3,2,1,0:T(8,128)}, u32[]{:S(2)}) copy-start(f32[1,4,64,512]{3,2,1,0:T(8,128)} %refs_2_.7) | copy-start | bytes 1572868
  1.2 1.8 %copy-start.1 = (bf16[3,4,64,512]{3,2,1,0:T(8,128)(2,1)S(1)}, bf16[3,4,64,512]{3,2,1,0:T(8,128)(2,1)}, u32[]{:S(2)}) copy-start(bf16[3,4,64,512]{3,2,1,0:T(8,128)(2,1)} %speed.3) | copy-start | bytes 2359300
  1.2 1.8 %copy-start.2 = (s32[3,4,64,64]{3,2,1,0:T(8,128)S(1)}, s32[3,4,64,64]{3,2,1,0:T(8,128)}, u32[]{:S(2)}) copy-start(s32[3,4,64,64]{3,2,1,0:T(8,128)} %mask.3) | copy-start | bytes 589828
  2.9 8.0 %copy-start.3 = (f32[4,64,512]{2,1,0:T(8,128)S(1)}, f32[4,64,512]{2,1,0:T(8,128)}, u32[]{:S(2)}) copy-start(f32[4,64,512]{2,1,0:T(8,128)} %control.3) | copy-start | bytes 1572868
  3.1 2.0 %copy-start.4 = (f32[3,64,512]{2,1,0:T(8,128)}, f32[3,64,512]{2,1,0:T(8,128)S(1)}, u32[]{:S(2)}) copy-start(f32[3,64,512]{2,1,0:T(8,128)S(1)} %pack.1._) | copy-start | bytes 1179652
  3.1 10.6 %collective-permute-start.2 = (f32[3,64,512]{2,1,0:T(8,128)S(1)}, f32[3,64,512]{2,1,0:T(8,128)S(1)}, u32[]{:S(2)}, u32[]{:S(2)}) collective-permute-start(f32[3,64,512]{2,1,0:T(8,128)S(1)} %pack.1._), channel_id=1, source_target_pairs={{1,2},{2,1},{3,4},{4,3},{5,6},{6,5},{7,8},{8,7},{9,10},{10,9},{11,... | collective-permute-start | bytes 1179656 | tf_op jit(solution)/shard_map/pass_state/ppermute | solution.py:413
  5.8 5.1 %collective-permute-start.1 = (f32[8,128]{1,0:T(8,128)S(1)}, f32[8,128]{1,0:T(8,128)S(1)}, u32[]{:S(2)}, u32[]{:S(2)}) collective-permute-start(f32[8,128]{1,0:T(8,128)S(1)} %gather_numbers.1.own_numbers), channel_id=1, source_target_pairs={{0,1},{1,0},{2,3},{3,2},{4,5},{5,4},{6,7},{7,6},{8,9},{9,8},{10,11... | collective-permute-start | bytes 12296 | tf_op jit(solution)/shard_map/swap_numbers/ppermute | solution.py:409
  10.9 1.0 %copy-start.5 = (bf16[4,64,512]{2,1,0:T(8,128)(2,1)S(1)}, bf16[4,64,512]{2,1,0:T(8,128)(2,1)}, u32[]{:S(2)}) copy-start(bf16[4,64,512]{2,1,0:T(8,128)(2,1)} %decay.3) | copy-start | bytes 786436
  13.0 11.4 %collective-permute-start.6 = (f32[2,64,512]{2,1,0:T(8,128)S(1)}, f32[2,64,512]{2,1,0:T(8,128)S(1)}, u32[]{:S(2)}, u32[]{:S(2)}) collective-permute-start(f32[2,64,512]{2,1,0:T(8,128)S(1)} %get-tuple-element.54.refs_2_), channel_id=1, source_target_pairs={{1,2},{2,1},{3,4},{4,3},{5,6},{6,5},{7,8},{8,7},{9,10},{10,9},{11,... | collective-permute-start | bytes 786440 | tf_op jit(solution)/shard_map/pass_stage1/ppermute | solution.py:413
  14.0 11.2 %collective-permute-start.3 = (f32[2,64,512]{2,1,0:T(8,128)S(1)}, f32[2,64,512]{2,1,0:T(8,128)S(1)}, u32[]{:S(2)}, u32[]{:S(2)}) collective-permute-start(f32[2,64,512]{2,1,0:T(8,128)S(1)} %get-tuple-element.56._.refs_4_), channel_id=1, source_target_pairs={{1,2},{2,1},{3,4},{4,3},{5,6},{6,5},{7,8},{8,7},{9,10},{10,9},{11,... | collective-permute-start | bytes 786440 | tf_op jit(solution)/shard_map/pass_stage2/ppermute | solution.py:413
  15.7 8.8 %collective-permute-start.5 = (f32[64,512]{1,0:T(8,128)S(1)}, f32[64,512]{1,0:T(8,128)S(1)}, u32[]{:S(2)}, u32[]{:S(2)}) collective-permute-start(f32[64,512]{1,0:T(8,128)S(1)} %get-tuple-element.61.refs_6_), channel_id=1, source_target_pairs={{0,1},{1,0},{2,3},{3,2},{4,5},{5,4},{6,7},{7,6},{8,9},{9,8},{10,11... | collective-permute-start | bytes 393224 | tf_op jit(solution)/shard_map/swap_s2_own/ppermute | solution.py:409
  22.7 1.8 %collective-permute-start.4 = (f32[64,512]{1,0:T(8,128)S(1)}, f32[64,512]{1,0:T(8,128)S(1)}, u32[]{:S(2)}, u32[]{:S(2)}) collective-permute-start(f32[64,512]{1,0:T(8,128)S(1)} %get-tuple-element.62.refs_7_), channel_id=1, source_target_pairs={{0,1},{1,0},{2,3},{3,2},{4,5},{5,4},{6,7},{7,6},{8,9},{9,8},{10,11... | collective-permute-start | bytes 393224 | tf_op jit(solution)/shard_map/swap_s2_far/ppermute | solution.py:409
  23.9 1.7 %collective-permute-start.7 = (f32[2,64,512]{2,1,0:T(8,128)S(1)}, f32[2,64,512]{2,1,0:T(8,128)S(1)}, u32[]{:S(2)}, u32[]{:S(2)}) collective-permute-start(f32[2,64,512]{2,1,0:T(8,128)S(1)} %get-tuple-element.65), channel_id=1, source_target_pairs={{0,1},{1,0},{2,3},{3,2},{4,5},{5,4},{6,7},{7,6},{8,9},{9,8},{10,11... | collective-permute-start | bytes 786440 | tf_op jit(solution)/shard_map/swap_after/ppermute | solution.py:409
  26.1 16.4 %collective-permute-start.8 = (f32[2,2,64,512]{3,2,1,0:T(8,128)S(1)}, f32[2,2,64,512]{3,2,1,0:T(8,128)S(1)}, u32[]{:S(2)}, u32[]{:S(2)}) collective-permute-start(f32[2,2,64,512]{3,2,1,0:T(8,128)S(1)} %get-tuple-element.66.refs_1_), channel_id=1, source_target_pairs={{1,2},{2,1},{3,4},{4,3},{5,6},{6,5},{7,8},{8,7},{9,10},{10,9},{11,... | collective-permute-start | bytes 1572872 | tf_op jit(solution)/shard_map/pass_back2/ppermute | solution.py:413
  27.3 7.6 %collective-permute-start.9 = (f32[88,512]{1,0:T(8,128)S(1)}, f32[88,512]{1,0:T(8,128)S(1)}, u32[]{:S(2)}, u32[]{:S(2)}) collective-permute-start(f32[88,512]{1,0:T(8,128)S(1)} %get-tuple-element.74.refs_11_), channel_id=1, source_target_pairs={{0,1},{1,0},{2,3},{3,2},{4,5},{5,4},{6,7},{7,6},{8,9},{9,8},{10,11... | collective-permute-start | bytes 540680 | tf_op jit(solution)/shard_map/swap_pin/ppermute | solution.py:409
  33.8 1.4 %collective-permute-start.10 = (f32[88,512]{1,0:T(8,128)S(1)}, f32[88,512]{1,0:T(8,128)S(1)}, u32[]{:S(2)}, u32[]{:S(2)}) collective-permute-start(f32[88,512]{1,0:T(8,128)S(1)} %get-tuple-element.75.refs_12_), channel_id=1, source_target_pairs={{0,1},{1,0},{2,3},{3,2},{4,5},{5,4},{6,7},{7,6},{8,9},{9,8},{10,11... | collective-permute-start | bytes 540680 | tf_op jit(solution)/shard_map/swap_pin/ppermute | solution.py:409
  33.9 1.6 %collective-permute-start.11 = (f32[88,512]{1,0:T(8,128)S(1)}, f32[88,512]{1,0:T(8,128)S(1)}, u32[]{:S(2)}, u32[]{:S(2)}) collective-permute-start(f32[88,512]{1,0:T(8,128)S(1)} %get-tuple-element.76.refs_13_), channel_id=1, source_target_pairs={{0,1},{1,0},{2,3},{3,2},{4,5},{5,4},{6,7},{7,6},{8,9},{9,8},{10,11... | collective-permute-start | bytes 540680 | tf_op jit(solution)/shard_map/swap_pin/ppermute | solution.py:409
  36.2 3.7 %collective-permute-start.12 = (f32[8,128]{1,0:T(8,128)S(1)}, f32[8,128]{1,0:T(8,128)S(1)}, u32[]{:S(2)}, u32[]{:S(2)}) collective-permute-start(f32[8,128]{1,0:T(8,128)S(1)} %get-tuple-element.78), channel_id=1, source_target_pairs={{0,4},{2,6},{4,0},{6,2},{8,12},{10,14},{12,8},{14,10},{1,5},{3,7},... | collective-permute-start | bytes 12296 | tf_op jit(solution)/shard_map/goal_sum/ppermute | solution.py:529
  39.9 4.5 %collective-permute-start.14 = (f32[8,128]{1,0:T(8,128)S(1)}, f32[8,128]{1,0:T(8,128)S(1)}, u32[]{:S(2)}, u32[]{:S(2)}) collective-permute-start(f32[8,128]{1,0:T(8,128)S(1)} %add.3.refs_7_.refs_13_), channel_id=1, source_target_pairs={{0,8},{2,10},{4,12},{6,14},{8,0},{10,2},{12,4},{14,6},{1,9},{3,11}... | collective-permute-start | bytes 12296 | tf_op jit(solution)/shard_map/goal_sum/ppermute | solution.py:529
  42.8 9.4 %collective-permute-start.13 = (f32[2,64,512]{2,1,0:T(8,128)S(1)}, f32[2,64,512]{2,1,0:T(8,128)S(1)}, u32[]{:S(2)}, u32[]{:S(2)}) collective-permute-start(f32[2,64,512]{2,1,0:T(8,128)S(1)} %get-tuple-element.79), channel_id=1, source_target_pairs={{1,2},{2,1},{3,4},{4,3},{5,6},{6,5},{7,8},{8,7},{9,10},{10,9},{11,... | collective-permute-start | bytes 786440 | tf_op jit(solution)/shard_map/pass_back1/ppermute | solution.py:413
  45.2 3.9 %collective-permute-start.16 = (f32[2,64,256]{2,1,0:T(8,128)S(1)}, f32[2,64,256]{2,1,0:T(8,128)S(1)}, u32[]{:S(2)}, u32[]{:S(2)}) collective-permute-start(f32[2,64,256]{2,1,0:T(8,128)S(1)} %get-tuple-element.85), channel_id=1, source_target_pairs={{0,1},{1,0},{2,3},{3,2},{4,5},{5,4},{6,7},{7,6},{8,9},{9,8},{10,11... | collective-permute-start | bytes 393224 | tf_op jit(solution)/shard_map/swap_gradient/ppermute | solution.py:409
  48.1 1.3 %collective-permute-start.17 = (f32[64,512]{1,0:T(8,128)S(1)}, f32[64,512]{1,0:T(8,128)S(1)}, u32[]{:S(2)}, u32[]{:S(2)}) collective-permute-start(f32[64,512]{1,0:T(8,128)S(1)} %get-tuple-element.86), channel_id=1, source_target_pairs={{0,1},{1,0},{2,3},{3,2},{4,5},{5,4},{6,7},{7,6},{8,9},{9,8},{10,11... | collective-permute-start | bytes 393224 | tf_op jit(solution)/shard_map/swap_adjoint/ppermute | solution.py:409
  48.2 1.5 %collective-permute-start.18 = (f32[64,512]{1,0:T(8,128)S(1)}, f32[64,512]{1,0:T(8,128)S(1)}, u32[]{:S(2)}, u32[]{:S(2)}) collective-permute-start(f32[64,512]{1,0:T(8,128)S(1)} %get-tuple-element.87), channel_id=1, source_target_pairs={{0,1},{1,0},{2,3},{3,2},{4,5},{5,4},{6,7},{7,6},{8,9},{9,8},{10,11... | collective-permute-start | bytes 393224 | tf_op jit(solution)/shard_map/swap_adjoint/ppermute | solution.py:409
  48.6 3.6 %collective-permute-start.15 = (f32[8,128]{1,0:T(8,128)S(1)}, f32[8,128]{1,0:T(8,128)S(1)}, u32[]{:S(2)}, u32[]{:S(2)}) collective-permute-start(f32[8,128]{1,0:T(8,128)S(1)} %get-tuple-element.83.refs_2_), channel_id=1, source_target_pairs={{0,2},{2,0},{4,6},{6,4},{8,10},{10,8},{12,14},{14,12},{1,3},{3,1},... | collective-permute-start | bytes 12296 | tf_op jit(solution)/shard_map/goal_sum/ppermute | solution.py:529
  52.2 1.4 %collective-permute-start.19 = (f32[64,512]{1,0:T(8,128)S(1)}, f32[64,512]{1,0:T(8,128)S(1)}, u32[]{:S(2)}, u32[]{:S(2)}) collective-permute-start(f32[64,512]{1,0:T(8,128)S(1)} %get-tuple-element.89), channel_id=1, source_target_pairs={{0,1},{1,0},{2,3},{3,2},{4,5},{5,4},{6,7},{7,6},{8,9},{9,8},{10,11... | collective-permute-start | bytes 393224 | tf_op jit(solution)/shard_map/swap_outer/ppermute | solution.py:409

commit v8 on v7

--- a/solution.py
+++ b/solution.py
@@ -264,18 +264,16 @@
         first = own + far
         second = own * final_own[k] + far * final_far[k]
         total = total + goals[k] * (first + variance_gain * (second - first * first))
-    rows = total.shape[0]
+    rows, columns = total.shape
     total = sum(total[8 * r : 8 * r + 8] for r in range(rows // 8))
-    cost[...] = total
-    laid.put(total)
-
-
-def back_second(scal, msgs, partials, part, halo, near, cx, cy, cz, dg, cost_own, *rest):
+    cost[...] = sum(total[:, 128 * k : 128 * k + 128] for k in range(columns // 128))
+
+
+def back_second(scal, msgs, partials, part, halo, near, cx, cy, cz, dg, cost, cost_far, *rest):
     base, a2, total = rest[-3:]
     count, rows = (len(rest) - 3) // 2, msgs.shape[2]
     mine, theirs = get(rest[:count], 4, rows), get(rest[count:-3], 4, rows)
-    cost = cost_own[...] + theirs[4]
-    total[...] = sum(cost[:, 128 * k : 128 * k + 128] for k in range(cost.shape[1] // 128))
+    total[...] = cost[...] + cost_far[...]
     for j in range(2):
         a = rows_of(scal, j)
         pin, pin2 = theirs[2 - 2 * j], theirs[3 - 2 * j]
@@ -331,10 +329,12 @@
         give[k] = jnp.where(zero, high, low)
 
 
-def last_edge(halo, part, cost, cost_far, outer, give, total):
-    total[...] = cost[...] + cost_far[...]
-    give[...] = part[1] + time_step * halo[0]
+def last_edge(halo, part, cost, cost_far, outer, give):
+    rows = outer.shape[0]
     outer[...] = part[0] + time_step * halo[1]
+    give[:rows] = part[1] + time_step * halo[0]
+    give[rows:] = jnp.zeros((8, outer.shape[1]), jnp.float32)
+    give[rows:, :128] = cost[...] + cost_far[...]
 
 
 def write_inner(core, part, keep, taken, *rest):
@@ -348,15 +348,21 @@
     gradient[2 - me] = taken[1]
 
 
-def write_outer(far, core, value, _, out, sem):
-    at = 3 * core[0]
-    copy = pltpu.make_async_copy(value, out.at[0, 3 - at if far else at], sem)
+def write_outer(core, value, _, out, sem):
+    copy = pltpu.make_async_copy(value, out.at[0, 3 * core[0]], sem)
     copy.start()
     copy.wait()
 
 
-def finish(cells, cost, objective):
-    objective[0] = jnp.sum(cost[...]) / cells
+def finish(cells, core, mine, taken, _, out, objective, number, sems):
+    rows = mine.shape[0] - 8
+    copy = pltpu.make_async_copy(taken.at[:rows], out.at[0, 3 - 3 * core[0]], sems.at[0])
+    copy.start()
+    number[0] = jnp.sum(mine[rows:, :128] + taken[rows:, :128]) / cells
+    result = pltpu.make_async_copy(number, objective, sems.at[1])
+    result.start()
+    copy.wait()
+    result.wait()
 
 
 def on_core(body, outs, scalars, arrays, hbm_out=(), smem_out=(), after=(), cost=0, name=None):
@@ -507,28 +513,28 @@
     halo3 = pass_on(msg3, "back2")
     part, cost, *pins = on_core(
         turn_inner,
-        [pair, (8, columns)] + [(r, columns) for r in cut(4 * rows + 8, 3)],
+        [pair, (8, 128)] + [(r, columns) for r in cut(4 * rows, 3)],
         [scal, weights],
         [final_own, final_far, terms] + fields + [goals],
     )
+    whole = sections & (sections - 1) == 0
+    steps = [1 << k for k in range(sections.bit_length() - 1)] if whole else []
+    steps = steps[1:] + steps[:1]
+
+    def from_pair(x, k):
+        with jax.named_scope("goal_sum"):
+            if k >= len(steps):
+                return jnp.zeros_like(x)
+            flip = 3 if steps[k] == 1 else 2 * steps[k]
+            return lax.ppermute(x, AXES, [(i, i ^ flip) for i in range(ranks)])
+
     theirs = [swap(x, "pin") for x in pins]
     base, a2, cost = on_core(
         back_second,
         [four, pair, (8, 128)],
         [scal],
-        [msg3, partials, part, halo, near] + fields + [cost] + pins + theirs,
-    )
-    whole = sections & (sections - 1) == 0
-    steps = [1 << k for k in range(sections.bit_length() - 1)] if whole else []
-    steps = steps[1:] + steps[:1]
-
-    def from_pair(x, k):
-        with jax.named_scope("goal_sum"):
-            if k >= len(steps):
-                return jnp.zeros_like(x)
-            return lax.ppermute(x, "space", [(i, i ^ steps[k]) for i in range(sections)])
-
-    cost = cost + from_pair(cost, 0)
+        [msg3, partials, part, halo, near] + fields + [cost, from_pair(cost, 0)] + pins + theirs,
+    )
     a1, msg4 = on_core(second_back_edge, [pair, pair], [scal], [halo3, base] + fields, after=[cost])
     halo4 = pass_on(msg4, "back1")
     keep, part, give, cost, *out = on_core(
@@ -549,33 +555,42 @@
     )
     for k in range(2, len(steps) - 1):
         cost = cost + from_pair(cost, k)
-    outer, give, cost = on_core(
+    cost_far = from_pair(cost, max(2, len(steps) - 1))
+    if not whole:
+        cost = lax.psum(cost, "space")
+    outer, give = on_core(
         last_edge,
-        [plane, plane, (8, 128)],
+        [plane, (rows + 8, columns)],
         [],
-        [halo4, part, cost, from_pair(cost, max(2, len(steps) - 1))],
+        [halo4, part, cost, cost_far],
         after=[held(adjoint, pltpu.HBM)],
         cost=LONG,
     )
-    if not whole:
-        cost = lax.psum(cost, "space")
-    cells = sections * layers * rows * columns
-    (objective,) = on_core(functools.partial(finish, cells), [(1,)], [], [cost], smem_out=(0,), name="finish")
-    for far, value in ((False, outer), (True, swap(give, "outer"))):
-        adjoint = pl.pallas_call(
-            functools.partial(write_outer, far),
-            out_shape=jax.ShapeDtypeStruct(adjoint.shape, jnp.float32),
-            in_specs=[
-                pl.BlockSpec(memory_space=pltpu.SMEM),
-                pl.BlockSpec(memory_space=pltpu.VMEM),
-                pl.BlockSpec(memory_space=pl.ANY),
-            ],
-            out_specs=pl.BlockSpec(memory_space=pl.ANY),
-            scratch_shapes=[pltpu.SemaphoreType.DMA],
-            input_output_aliases={2: 0},
-            compiler_params=pltpu.CompilerParams(vmem_limit_bytes=VMEM_LIMIT),
-            name="write_outer",
-        )(held(core, pltpu.SMEM), held(value, pltpu.VMEM), held(adjoint, pltpu.HBM))
+    anywhere, in_smem = pl.BlockSpec(memory_space=pl.ANY), pl.BlockSpec(memory_space=pltpu.SMEM)
+    adjoint = pl.pallas_call(
+        write_outer,
+        out_shape=jax.ShapeDtypeStruct(adjoint.shape, jnp.float32),
+        in_specs=[in_smem, pl.BlockSpec(memory_space=pltpu.VMEM), anywhere],
+        out_specs=anywhere,
+        scratch_shapes=[pltpu.SemaphoreType.DMA],
+        input_output_aliases={2: 0},
+        compiler_params=pltpu.CompilerParams(vmem_limit_bytes=VMEM_LIMIT),
+        name="write_outer",
+    )(held(core, pltpu.SMEM), held(outer, pltpu.VMEM), held(adjoint, pltpu.HBM))
+    adjoint, objective = pl.pallas_call(
+        functools.partial(finish, sections * layers * rows * columns),
+        out_shape=[jax.ShapeDtypeStruct(adjoint.shape, jnp.float32), jax.ShapeDtypeStruct((1,), jnp.float32)],
+        in_specs=[in_smem] + [pl.BlockSpec(memory_space=pltpu.VMEM)] * 2 + [anywhere],
+        out_specs=[anywhere] * 2,
+        scratch_shapes=[pltpu.SMEM((1,), jnp.float32), pltpu.SemaphoreType.DMA((2,))],
+        input_output_aliases={3: 0},
+        compiler_params=pltpu.CompilerParams(vmem_limit_bytes=VMEM_LIMIT),
+        name="finish",
+    )(
+        held(core, pltpu.SMEM),
+        *[held(x, pltpu.VMEM) for x in (give, swap(give, "outer"))],
+        held(adjoint, pltpu.HBM),
+    )
     return (adjoint, gradient, objective)
 
 

time: 54.7 us -> 54.2 us (level)
  starting transfers between devices: 30.5 us -> 31.7 us
  waiting for transfers between devices: 9.62 us -> 8.42 us
    ppermute x12, starting transfers between devices: 22.8 us -> 24.1 us  [swap(): return lax.ppermute(x, AXES, within)]
    ppermute x12, waiting for transfers between devices: 5.04 us -> 4.43 us  [swap(): return lax.ppermute(x, AXES, within)]
    ppermute x3, waiting for transfers between devices: 4.57 us -> 3.97 us  [from_pair(): return lax.ppermute(x, AXES, [(i, i ^ flip) for i in range(ranks)])]
    pallas_call x15 -> x14, Pallas kernels: 6.87 us -> 6.45 us  [on_core(): pl.pallas_call(run, out_shape=out_shape, in_specs=[pl.BlockSpec(memory_sp...]
  transfers between devices with their start and end apart: 20 -> 20, of which waited for: 12 -> 10; matrix products, arithmetic and copies ran while one was open for 0% -> 0% of each run, Pallas kernels for 18% -> 17%
where the time goes in v8:
time: 54.2 us; the launch traced here: 53.9 us
  starting transfers between devices  31.7 us (58%)
  Pallas kernels  10.7 us (20%)
  waiting for transfers between devices  8.42 us (16%)
  between operations  2.13 us (4%)
  local copies, waits for them, and re-layouts  0.97 us (2%)
    ppermute x12, starting transfers between devices, swap(): return lax.ppermute(x, AXES, within)  24.1 us
    pallas_call x14, Pallas kernels, on_core(): pl.pallas_call(run, out_shape=out_shape, in_specs=[pl.BlockSpec(memory_sp...  6.45 us
    ppermute x12, waiting for transfers between devices, swap(): return lax.ppermute(x, AXES, within)  4.43 us
    ppermute x3, starting transfers between devices, from_pair(): return lax.ppermute(x, AXES, [(i, i ^ flip) for i in range(ranks)])  4.26 us
    ppermute x3, waiting for transfers between devices, from_pair(): return lax.ppermute(x, AXES, [(i, i ^ flip) for i in range(ranks)])  3.97 us
    ppermute x5, starting transfers between devices, pass_on(): return lax.ppermute(x, AXES, across)  3.41 us
    pallas_call x1, Pallas kernels, shards(): pl.pallas_call(prepare_back, out_shape=[pltpu.SMEM((2,), jnp.float32)] +...  1.16 us
  transfers between devices with their start and end apart: 20, of which 10 were waited for; matrix products, arithmetic and copies ran while one was open for 0% of the time, Pallas kernels for 17%

profile of v8, /device:TPU:0, one launch (start us, length us, event | category | flops | bytes accessed | tf_op | source)
XLA Modules:
  0.0 53.9 jit_solution(14005801247395793971)
XLA Ops:
  0.6 0.5 collective-permute-start
  1.2 1.7 %collective-permute-done.refs_2_.refs_3_.far = f32[1,4,64,512]{3,2,1,0:T(8,128)S(1)} collective-permute-done((f32[1,4,64,512]{3,2,1,0:T(8,128)}, f32[1,4,64,512]{3,2,1,0:T(8,128)S(1)}, u32[]{:S(2)}, u32[]{:S(2)}) %collective-permute-start) | collective-permute-done | bytes 524320 | tf_op jit(solution)/shard_map/swap_state/ppermute | solution.py:415
  3.1 0.7 %collective-permute-start.2 = (f32[3,64,512]{2,1,0:T(8,128)S(1)}, f32[3,64,512]{2,1,0:T(8,128)S(1)}, u32[]{:S(2)}, u32[]{:S(2)}) collective-permute-start(f32[3,64,512]{2,1,0:T(8,128)S(1)} %pack.1._), channel_id=1, source_target_pairs={{1,2},{2,1},{3,4},{4,3},{5,6},{6,5},{7,8},{8,7},{9,10},{10,9},{11,... | collective-permute-start | bytes 1179656 | tf_op jit(solution)/shard_map/pass_state/ppermute | solution.py:419
  5.1 0.7 %gather_numbers.1.own_numbers = f32[8,128]{1,0:T(8,128)S(1)} custom-call(s32[1,8]{1,0:T(1,128)} %index.1, s32[1]{0:T(128)S(6)} %copy.17.weight, s32[1]{0:T(128)S(6)} %copy.18.step, f32[3,64,512]{2,1,0:T(8,128)} %copy-done.4), custom_call_target="tpu_custom_call" | custom-call | tf_op jit(solution)/shard_map/gather_numbers/pallas_call | solution.py:435
  5.8 4.3 %collective-permute-start.1 = (f32[8,128]{1,0:T(8,128)S(1)}, f32[8,128]{1,0:T(8,128)S(1)}, u32[]{:S(2)}, u32[]{:S(2)}) collective-permute-start(f32[8,128]{1,0:T(8,128)S(1)} %gather_numbers.1.own_numbers), channel_id=1, source_target_pairs={{0,1},{1,0},{2,3},{3,2},{4,5},{5,4},{6,7},{7,6},{8,9},{9,8},{10,11... | collective-permute-start | bytes 12296 | tf_op jit(solution)/shard_map/swap_numbers/ppermute | solution.py:415
  10.0 0.8 %collective-permute-done.1.far_numbers = f32[8,128]{1,0:T(8,128)S(1)} collective-permute-done((f32[8,128]{1,0:T(8,128)S(1)}, f32[8,128]{1,0:T(8,128)S(1)}, u32[]{:S(2)}, u32[]{:S(2)}) %collective-permute-start.1) | collective-permute-done | bytes 4128 | tf_op jit(solution)/shard_map/swap_numbers/ppermute | solution.py:415
  10.9 0.9 %copy-done.5 = bf16[4,64,512]{2,1,0:T(8,128)(2,1)S(1)} copy-done((bf16[4,64,512]{2,1,0:T(8,128)(2,1)S(1)}, bf16[4,64,512]{2,1,0:T(8,128)(2,1)}, u32[]{:S(2)}) %copy-start.5) | copy-done | bytes 262168
  11.8 0.5 prepare.1
  12.3 0.7 %first_stage.1 = (f32[2,64,512]{2,1,0:T(8,128)S(1)}, f32[2,64,512]{2,1,0:T(8,128)S(1)}, f32[2,64,512]{2,1,0:T(8,128)S(1)}) custom-call(s32[1]{0:T(128)} %bitcast.refs_0_.core, f32[2,8]{1,0:T(2,128)S(4)} %get-tuple-element.49.refs_1_.refs_0_.scal, f32[1,4,64,512]{3,2,1,0:T(8,128)S(1)} %copy-done, ...), custom_call_target="tpu_custom_call" | custom-call | tf_op jit(solution)/shard_map/first_stage/pallas_call | solution.py:381
  13.0 0.7 %collective-permute-start.6 = (f32[2,64,512]{2,1,0:T(8,128)S(1)}, f32[2,64,512]{2,1,0:T(8,128)S(1)}, u32[]{:S(2)}, u32[]{:S(2)}) collective-permute-start(f32[2,64,512]{2,1,0:T(8,128)S(1)} %get-tuple-element.55.refs_2_), channel_id=1, source_target_pairs={{1,2},{2,1},{3,4},{4,3},{5,6},{6,5},{7,8},{8,7},{9,10},{10,9},{11,... | collective-permute-start | bytes 786440 | tf_op jit(solution)/shard_map/pass_stage1/ppermute | solution.py:419
  14.0 0.7 %collective-permute-start.3 = (f32[2,64,512]{2,1,0:T(8,128)S(1)}, f32[2,64,512]{2,1,0:T(8,128)S(1)}, u32[]{:S(2)}, u32[]{:S(2)}) collective-permute-start(f32[2,64,512]{2,1,0:T(8,128)S(1)} %get-tuple-element.57._.refs_4_), channel_id=1, source_target_pairs={{1,2},{2,1},{3,4},{4,3},{5,6},{6,5},{7,8},{8,7},{9,10},{10,9},{11,... | collective-permute-start | bytes 786440 | tf_op jit(solution)/shard_map/pass_stage2/ppermute | solution.py:419
  14.7 0.5 %prepare_next.1 = (f32[2,64,512]{2,1,0:T(8,128)S(1)}, f32[64,512]{1,0:T(8,128)S(1)}) custom-call(s32[1]{0:T(128)} %bitcast.refs_0_.core, f32[2,8]{1,0:T(2,128)S(4)} %get-tuple-element.49.refs_1_.refs_0_.scal, bf16[3,4,64,512]{3,2,1,0:T(8,128)(2,1)S(1)} %copy-done.1, s32[3,4,64,64]{3,2,1,0:T(8,128)S(1)} %copy-done.2, bf16[4,64,512]{2,1,0:T(8,128)(2,1)S(1)} %copy-done.5, ...), custom_call_target="tpu_custom_call" | custom-call | tf_op jit(solution)/shard_map/prepare_next/pallas_call | solution.py:483
  15.7 6.9 %collective-permute-start.5 = (f32[64,512]{1,0:T(8,128)S(1)}, f32[64,512]{1,0:T(8,128)S(1)}, u32[]{:S(2)}, u32[]{:S(2)}) collective-permute-start(f32[64,512]{1,0:T(8,128)S(1)} %get-tuple-element.62.refs_6_), channel_id=1, source_target_pairs={{0,1},{1,0},{2,3},{3,2},{4,5},{5,4},{6,7},{7,6},{8,9},{9,8},{10,11... | collective-permute-start | bytes 393224 | tf_op jit(solution)/shard_map/swap_s2_own/ppermute | solution.py:415
  22.7 1.2 %prepare_back.1 = (f32[2]{0:T(128)S(4)}, f32[2,64,512]{2,1,0:T(8,128)S(1)}, f32[2,64,512]{2,1,0:T(8,128)S(1)}, f32[2,64,512]{2,1,0:T(8,128)S(1)}) custom-call(s32[1]{0:T(128)} %bitcast.refs_0_.core, bf16[4,64,512]{2,1,0:T(8,128)(2,1)} %goal.1, f32[8,128]{1,0:T(8,128)S(1)} %gather_numbers.1.own_numbers, f32[8,128]{1,0:T(8,128)S(1)} %collective-permute-done.1.far_numbers, ...), custom_call_target="tpu_custom_call" | custom-call | tf_op jit(solution)/shard_map/prepare_back/pallas_call | solution.py:466
  24.5 0.8 %third_stage.1.refs_3_ = f32[2,2,64,512]{3,2,1,0:T(8,128)S(1)} custom-call(s32[1]{0:T(128)} %bitcast.refs_0_.core, f32[2,8]{1,0:T(2,128)S(4)} %get-tuple-element.49.refs_1_.refs_0_.scal, f32[1,4,64,512]{3,2,1,0:T(8,128)S(1)} %copy-done, f32[1,4,64,512]{3,2,1,0:T(8,128)S(1)} %collective-permute-done.refs_2_.refs_3_.far, ...), custom_call_target="tpu_custom_call" | custom-call | tf_op jit(solution)/shard_map/third_stage/pallas_call | solution.py:381
  25.6 0.6 %turn.1 = (f32[2,64,512]{2,1,0:T(8,128)S(1)}, f32[2,64,512]{2,1,0:T(8,128)S(1)}, f32[2,2,64,512]{3,2,1,0:T(8,128)S(1)}, f32[2,2,64,512]{3,2,1,0:T(8,128)S(1)}, f32[2,64,512]{2,1,0:T(8,128)S(1)}) custom-call(f32[2,8]{1,0:T(2,128)S(4)} %get-tuple-element.49.refs_1_.refs_0_.scal, f32[2]{0:T(128)S(4)} %get-tuple-element.58.refs_1_, ...), custom_call_target="tpu_custom_call" | custom-call | tf_op jit(solution)/shard_map/turn/pallas_call | solution.py:381
  26.1 0.7 %collective-permute-start.8 = (f32[2,2,64,512]{3,2,1,0:T(8,128)S(1)}, f32[2,2,64,512]{3,2,1,0:T(8,128)S(1)}, u32[]{:S(2)}, u32[]{:S(2)}) collective-permute-start(f32[2,2,64,512]{3,2,1,0:T(8,128)S(1)} %get-tuple-element.67.refs_1_), channel_id=1, source_target_pairs={{1,2},{2,1},{3,4},{4,3},{5,6},{6,5},{7,8},{8,7},{9,10},{10,9},{11,... | collective-permute-start | bytes 1572872 | tf_op jit(solution)/shard_map/pass_back2/ppermute | solution.py:419
  26.8 0.5 turn_inner.1
  27.4 6.5 %collective-permute-start.10 = (f32[88,512]{1,0:T(8,128)S(1)}, f32[88,512]{1,0:T(8,128)S(1)}, u32[]{:S(2)}, u32[]{:S(2)}) collective-permute-start(f32[88,512]{1,0:T(8,128)S(1)} %get-tuple-element.75.refs_12_), channel_id=1, source_target_pairs={{0,1},{1,0},{2,3},{3,2},{4,5},{5,4},{6,7},{7,6},{8,9},{9,8},{10,11... | collective-permute-start | bytes 540680 | tf_op jit(solution)/shard_map/swap_pin/ppermute | solution.py:415
  34.4 1.6 %collective-permute-start.9 = (f32[8,128]{1,0:T(8,128)S(1)}, f32[8,128]{1,0:T(8,128)S(1)}, u32[]{:S(2)}, u32[]{:S(2)}) collective-permute-start(f32[8,128]{1,0:T(8,128)S(1)} %get-tuple-element.74.refs_10_), channel_id=1, source_target_pairs={{0,4},{1,5},{2,6},{3,7},{4,0},{5,1},{6,2},{7,3},{8,12},{9,13},{10,... | collective-permute-start | bytes 12296 | tf_op jit(solution)/shard_map/goal_sum/ppermute | solution.py:529
  36.0 2.0 %collective-permute-done.9.refs_11_ = f32[8,128]{1,0:T(8,128)S(1)} collective-permute-done((f32[8,128]{1,0:T(8,128)S(1)}, f32[8,128]{1,0:T(8,128)S(1)}, u32[]{:S(2)}, u32[]{:S(2)}) %collective-permute-start.9) | collective-permute-done | bytes 4128 | tf_op jit(solution)/shard_map/goal_sum/ppermute | solution.py:529
  38.0 0.7 %back_second.1 = (f32[2,2,64,512]{3,2,1,0:T(8,128)S(1)}, f32[2,64,512]{2,1,0:T(8,128)S(1)}, f32[8,128]{1,0:T(8,128)S(1)}) custom-call(f32[2,8]{1,0:T(2,128)S(4)} %get-tuple-element.49.refs_1_.refs_0_.scal, f32[2,2,64,512]{3,2,1,0:T(8,128)S(1)} %get-tuple-element.67.refs_1_, f32[2,64,512]{2,1,0:T(8,128)S(1)} %get-tuple-element.68.refs_2_.refs_3_, ...), custom_call_target="tpu_custom_call" | custom-call | tf_op jit(solution)/shard_map/back_second/pallas_call | solution.py:381
  38.8 2.7 %collective-permute-start.14 = (f32[8,128]{1,0:T(8,128)S(1)}, f32[8,128]{1,0:T(8,128)S(1)}, u32[]{:S(2)}, u32[]{:S(2)}) collective-permute-start(f32[8,128]{1,0:T(8,128)S(1)} %get-tuple-element.79.refs_7_.refs_13_), channel_id=1, source_target_pairs={{0,8},{1,9},{2,10},{3,11},{4,12},{5,13},{6,14},{7,15},{8,0},{9,1},... | collective-permute-start | bytes 12296 | tf_op jit(solution)/shard_map/goal_sum/ppermute | solution.py:529
  41.8 0.7 %collective-permute-start.13 = (f32[2,64,512]{2,1,0:T(8,128)S(1)}, f32[2,64,512]{2,1,0:T(8,128)S(1)}, u32[]{:S(2)}, u32[]{:S(2)}) collective-permute-start(f32[2,64,512]{2,1,0:T(8,128)S(1)} %get-tuple-element.80), channel_id=1, source_target_pairs={{1,2},{2,1},{3,4},{4,3},{5,6},{6,5},{7,8},{8,7},{9,10},{10,9},{11,... | collective-permute-start | bytes 786440 | tf_op jit(solution)/shard_map/pass_back1/ppermute | solution.py:419
  42.5 0.9 %collective-permute-done.14.refs_14_ = f32[8,128]{1,0:T(8,128)S(1)} collective-permute-done((f32[8,128]{1,0:T(8,128)S(1)}, f32[8,128]{1,0:T(8,128)S(1)}, u32[]{:S(2)}, u32[]{:S(2)}) %collective-permute-start.14) | collective-permute-done | bytes 4128 | tf_op jit(solution)/shard_map/goal_sum/ppermute | solution.py:529
  43.3 0.8 %close.1 = (f32[2,64,256]{2,1,0:T(8,128)S(1)}, f32[4,64,512]{2,1,0:T(8,128)S(1)}, f32[2,64,256]{2,1,0:T(8,128)S(1)}, f32[8,128]{1,0:T(8,128)S(1)}, f32[64,512]{1,0:T(8,128)S(1)}, /*index=5*/f32[64,512]{1,0:T(8,128)S(1)}) custom-call(s32[1]{0:T(128)} %bitcast.refs_0_.core, f32[2,8]{1,0:T(2,128)S(4)} %get-tuple-element.49.refs_1_.refs_0_.scal, ...), custom_call_target="tpu_custom_call" | custom-call | flops 16000000000 | bytes 48000000 | tf_op jit(solution)/shard_map/close/pallas_call | solution.py:381
  44.2 4.0 %collective-permute-start.16 = (f32[2,64,256]{2,1,0:T(8,128)S(1)}, f32[2,64,256]{2,1,0:T(8,128)S(1)}, u32[]{:S(2)}, u32[]{:S(2)}) collective-permute-start(f32[2,64,256]{2,1,0:T(8,128)S(1)} %get-tuple-element.86), channel_id=1, source_target_pairs={{0,1},{1,0},{2,3},{3,2},{4,5},{5,4},{6,7},{7,6},{8,9},{9,8},{10,11... | collective-permute-start | bytes 393224 | tf_op jit(solution)/shard_map/swap_gradient/ppermute | solution.py:415
  49.7 0.9 %write_inner.1 = (f32[1,4,64,512]{3,2,1,0:T(8,128)}, f32[4,64,256]{2,1,0:T(8,128)}) custom-call(s32[1]{0:T(128)} %bitcast.refs_0_.core, f32[4,64,512]{2,1,0:T(8,128)S(1)} %get-tuple-element.83.refs_1_, f32[2,64,256]{2,1,0:T(8,128)S(1)} %get-tuple-element.85.refs_2_, f32[2,64,256]{2,1,0:T(8,128)S(1)} %collective-permute-done.16.refs_3_, ...), custom_call_target="tpu_custom_call" | custom-call | tf_op jit(solution)/shard_map/write_inner/pallas_call | solution.py:381
  50.7 1.1 %collective-permute-done.15.refs_3_ = f32[8,128]{1,0:T(8,128)S(1)} collective-permute-done((f32[8,128]{1,0:T(8,128)S(1)}, f32[8,128]{1,0:T(8,128)S(1)}, u32[]{:S(2)}, u32[]{:S(2)}) %collective-permute-start.15) | collective-permute-done | bytes 4128 | tf_op jit(solution)/shard_map/goal_sum/ppermute | solution.py:529
  52.0 0.7 %write_outer.1._ = f32[1,4,64,512]{3,2,1,0:T(8,128)} custom-call(s32[1]{0:T(128)} %bitcast.refs_0_.core, f32[64,512]{1,0:T(8,128)S(1)} %get-tuple-element.91.value, f32[1,4,64,512]{3,2,1,0:T(8,128)} %get-tuple-element.89.refs_4_._), custom_call_target="tpu_custom_call", output_to_operand_aliasing={{}: (2, {})} | custom-call | tf_op jit(solution)/shard_map/write_outer/pallas_call | solution.py:570
  52.7 0.6 %collective-permute-done.19.taken = f32[72,512]{1,0:T(8,128)S(1)} collective-permute-done((f32[72,512]{1,0:T(8,128)S(1)}, f32[72,512]{1,0:T(8,128)S(1)}, u32[]{:S(2)}, u32[]{:S(2)}) %collective-permute-start.19) | collective-permute-done | bytes 147488 | tf_op jit(solution)/shard_map/swap_outer/ppermute | solution.py:415
  53.2 0.7 %finish.1 = (f32[1,4,64,512]{3,2,1,0:T(8,128)}, f32[1]{0:T(128)}) custom-call(s32[1]{0:T(128)} %bitcast.refs_0_.core, f32[72,512]{1,0:T(8,128)S(1)} %get-tuple-element.90.mine, f32[72,512]{1,0:T(8,128)S(1)} %collective-permute-done.19.taken, f32[1,4,64,512]{3,2,1,0:T(8,128)} %write_outer.1._), custom_call_target="tpu_custom_call", output_to_operand_aliasing={{0}: (3, {})} | custom-call | tf_op jit(solution)/shard_map/finish/pallas_call | solution.py:580
  (40 shorter events, 4.5 us)
Async XLA Ops:
  0.6 2.3 %collective-permute-start = (f32[1,4,64,512]{3,2,1,0:T(8,128)}, f32[1,4,64,512]{3,2,1,0:T(8,128)S(1)}, u32[]{:S(2)}, u32[]{:S(2)}) collective-permute-start(f32[1,4,64,512]{3,2,1,0:T(8,128)} %refs_2_.7), channel_id=1, source_target_pairs={{0,1},{1,0},{2,3},{3,2},{4,5},{5,4},{6,7},{7,6},{8,9},{9,8},{10,11... | collective-permute-start | bytes 1572872 | tf_op jit(solution)/shard_map/swap_state/ppermute | solution.py:415
  1.1 1.8 %copy-start = (f32[1,4,64,512]{3,2,1,0:T(8,128)S(1)}, f32[1,4,64,512]{3,2,1,0:T(8,128)}, u32[]{:S(2)}) copy-start(f32[1,4,64,512]{3,2,1,0:T(8,128)} %refs_2_.7) | copy-start | bytes 1572868
  1.2 1.8 %copy-start.1 = (bf16[3,4,64,512]{3,2,1,0:T(8,128)(2,1)S(1)}, bf16[3,4,64,512]{3,2,1,0:T(8,128)(2,1)}, u32[]{:S(2)}) copy-start(bf16[3,4,64,512]{3,2,1,0:T(8,128)(2,1)} %speed.3) | copy-start | bytes 2359300
  1.2 1.8 %copy-start.2 = (s32[3,4,64,64]{3,2,1,0:T(8,128)S(1)}, s32[3,4,64,64]{3,2,1,0:T(8,128)}, u32[]{:S(2)}) copy-start(s32[3,4,64,64]{3,2,1,0:T(8,128)} %mask.3) | copy-start | bytes 589828
  2.9 8.0 %copy-start.3 = (f32[4,64,512]{2,1,0:T(8,128)S(1)}, f32[4,64,512]{2,1,0:T(8,128)}, u32[]{:S(2)}) copy-start(f32[4,64,512]{2,1,0:T(8,128)} %control.3) | copy-start | bytes 1572868
  3.1 2.0 %copy-start.4 = (f32[3,64,512]{2,1,0:T(8,128)}, f32[3,64,512]{2,1,0:T(8,128)S(1)}, u32[]{:S(2)}) copy-start(f32[3,64,512]{2,1,0:T(8,128)S(1)} %pack.1._) | copy-start | bytes 1179652
  3.1 10.6 %collective-permute-start.2 = (f32[3,64,512]{2,1,0:T(8,128)S(1)}, f32[3,64,512]{2,1,0:T(8,128)S(1)}, u32[]{:S(2)}, u32[]{:S(2)}) collective-permute-start(f32[3,64,512]{2,1,0:T(8,128)S(1)} %pack.1._), channel_id=1, source_target_pairs={{1,2},{2,1},{3,4},{4,3},{5,6},{6,5},{7,8},{8,7},{9,10},{10,9},{11,... | collective-permute-start | bytes 1179656 | tf_op jit(solution)/shard_map/pass_state/ppermute | solution.py:419
  5.8 5.1 %collective-permute-start.1 = (f32[8,128]{1,0:T(8,128)S(1)}, f32[8,128]{1,0:T(8,128)S(1)}, u32[]{:S(2)}, u32[]{:S(2)}) collective-permute-start(f32[8,128]{1,0:T(8,128)S(1)} %gather_numbers.1.own_numbers), channel_id=1, source_target_pairs={{0,1},{1,0},{2,3},{3,2},{4,5},{5,4},{6,7},{7,6},{8,9},{9,8},{10,11... | collective-permute-start | bytes 12296 | tf_op jit(solution)/shard_map/swap_numbers/ppermute | solution.py:415
  10.9 1.0 %copy-start.5 = (bf16[4,64,512]{2,1,0:T(8,128)(2,1)S(1)}, bf16[4,64,512]{2,1,0:T(8,128)(2,1)}, u32[]{:S(2)}) copy-start(bf16[4,64,512]{2,1,0:T(8,128)(2,1)} %decay.3) | copy-start | bytes 786436
  13.0 11.4 %collective-permute-start.6 = (f32[2,64,512]{2,1,0:T(8,128)S(1)}, f32[2,64,512]{2,1,0:T(8,128)S(1)}, u32[]{:S(2)}, u32[]{:S(2)}) collective-permute-start(f32[2,64,512]{2,1,0:T(8,128)S(1)} %get-tuple-element.55.refs_2_), channel_id=1, source_target_pairs={{1,2},{2,1},{3,4},{4,3},{5,6},{6,5},{7,8},{8,7},{9,10},{10,9},{11,... | collective-permute-start | bytes 786440 | tf_op jit(solution)/shard_map/pass_stage1/ppermute | solution.py:419
  14.0 11.2 %collective-permute-start.3 = (f32[2,64,512]{2,1,0:T(8,128)S(1)}, f32[2,64,512]{2,1,0:T(8,128)S(1)}, u32[]{:S(2)}, u32[]{:S(2)}) collective-permute-start(f32[2,64,512]{2,1,0:T(8,128)S(1)} %get-tuple-element.57._.refs_4_), channel_id=1, source_target_pairs={{1,2},{2,1},{3,4},{4,3},{5,6},{6,5},{7,8},{8,7},{9,10},{10,9},{11,... | collective-permute-start | bytes 786440 | tf_op jit(solution)/shard_map/pass_stage2/ppermute | solution.py:419
  15.7 8.8 %collective-permute-start.5 = (f32[64,512]{1,0:T(8,128)S(1)}, f32[64,512]{1,0:T(8,128)S(1)}, u32[]{:S(2)}, u32[]{:S(2)}) collective-permute-start(f32[64,512]{1,0:T(8,128)S(1)} %get-tuple-element.62.refs_6_), channel_id=1, source_target_pairs={{0,1},{1,0},{2,3},{3,2},{4,5},{5,4},{6,7},{7,6},{8,9},{9,8},{10,11... | collective-permute-start | bytes 393224 | tf_op jit(solution)/shard_map/swap_s2_own/ppermute | solution.py:415
  22.7 1.8 %collective-permute-start.4 = (f32[64,512]{1,0:T(8,128)S(1)}, f32[64,512]{1,0:T(8,128)S(1)}, u32[]{:S(2)}, u32[]{:S(2)}) collective-permute-start(f32[64,512]{1,0:T(8,128)S(1)} %get-tuple-element.63.refs_7_), channel_id=1, source_target_pairs={{0,1},{1,0},{2,3},{3,2},{4,5},{5,4},{6,7},{7,6},{8,9},{9,8},{10,11... | collective-permute-start | bytes 393224 | tf_op jit(solution)/shard_map/swap_s2_far/ppermute | solution.py:415
  23.9 1.7 %collective-permute-start.7 = (f32[2,64,512]{2,1,0:T(8,128)S(1)}, f32[2,64,512]{2,1,0:T(8,128)S(1)}, u32[]{:S(2)}, u32[]{:S(2)}) collective-permute-start(f32[2,64,512]{2,1,0:T(8,128)S(1)} %get-tuple-element.66), channel_id=1, source_target_pairs={{0,1},{1,0},{2,3},{3,2},{4,5},{5,4},{6,7},{7,6},{8,9},{9,8},{10,11... | collective-permute-start | bytes 786440 | tf_op jit(solution)/shard_map/swap_after/ppermute | solution.py:415
  26.1 15.3 %collective-permute-start.8 = (f32[2,2,64,512]{3,2,1,0:T(8,128)S(1)}, f32[2,2,64,512]{3,2,1,0:T(8,128)S(1)}, u32[]{:S(2)}, u32[]{:S(2)}) collective-permute-start(f32[2,2,64,512]{3,2,1,0:T(8,128)S(1)} %get-tuple-element.67.refs_1_), channel_id=1, source_target_pairs={{1,2},{2,1},{3,4},{4,3},{5,6},{6,5},{7,8},{8,7},{9,10},{10,9},{11,... | collective-permute-start | bytes 1572872 | tf_op jit(solution)/shard_map/pass_back2/ppermute | solution.py:419
  27.4 10.6 %collective-permute-start.10 = (f32[88,512]{1,0:T(8,128)S(1)}, f32[88,512]{1,0:T(8,128)S(1)}, u32[]{:S(2)}, u32[]{:S(2)}) collective-permute-start(f32[88,512]{1,0:T(8,128)S(1)} %get-tuple-element.75.refs_12_), channel_id=1, source_target_pairs={{0,1},{1,0},{2,3},{3,2},{4,5},{5,4},{6,7},{7,6},{8,9},{9,8},{10,11... | collective-permute-start | bytes 540680 | tf_op jit(solution)/shard_map/swap_pin/ppermute | solution.py:415
  33.9 4.1 %collective-permute-start.11 = (f32[88,512]{1,0:T(8,128)S(1)}, f32[88,512]{1,0:T(8,128)S(1)}, u32[]{:S(2)}, u32[]{:S(2)}) collective-permute-start(f32[88,512]{1,0:T(8,128)S(1)} %get-tuple-element.76.refs_13_), channel_id=1, source_target_pairs={{0,1},{1,0},{2,3},{3,2},{4,5},{5,4},{6,7},{7,6},{8,9},{9,8},{10,11... | collective-permute-start | bytes 540680 | tf_op jit(solution)/shard_map/swap_pin/ppermute | solution.py:415
  34.0 4.0 %collective-permute-start.12 = (f32[80,512]{1,0:T(8,128)S(1)}, f32[80,512]{1,0:T(8,128)S(1)}, u32[]{:S(2)}, u32[]{:S(2)}) collective-permute-start(f32[80,512]{1,0:T(8,128)S(1)} %get-tuple-element.77.refs_14_), channel_id=1, source_target_pairs={{0,1},{1,0},{2,3},{3,2},{4,5},{5,4},{6,7},{7,6},{8,9},{9,8},{10,11... | collective-permute-start | bytes 491528 | tf_op jit(solution)/shard_map/swap_pin/ppermute | solution.py:415
  34.4 3.6 %collective-permute-start.9 = (f32[8,128]{1,0:T(8,128)S(1)}, f32[8,128]{1,0:T(8,128)S(1)}, u32[]{:S(2)}, u32[]{:S(2)}) collective-permute-start(f32[8,128]{1,0:T(8,128)S(1)} %get-tuple-element.74.refs_10_), channel_id=1, source_target_pairs={{0,4},{1,5},{2,6},{3,7},{4,0},{5,1},{6,2},{7,3},{8,12},{9,13},{10,... | collective-permute-start | bytes 12296 | tf_op jit(solution)/shard_map/goal_sum/ppermute | solution.py:529
  38.8 4.6 %collective-permute-start.14 = (f32[8,128]{1,0:T(8,128)S(1)}, f32[8,128]{1,0:T(8,128)S(1)}, u32[]{:S(2)}, u32[]{:S(2)}) collective-permute-start(f32[8,128]{1,0:T(8,128)S(1)} %get-tuple-element.79.refs_7_.refs_13_), channel_id=1, source_target_pairs={{0,8},{1,9},{2,10},{3,11},{4,12},{5,13},{6,14},{7,15},{8,0},{9,1},... | collective-permute-start | bytes 12296 | tf_op jit(solution)/shard_map/goal_sum/ppermute | solution.py:529
  41.8 10.0 %collective-permute-start.13 = (f32[2,64,512]{2,1,0:T(8,128)S(1)}, f32[2,64,512]{2,1,0:T(8,128)S(1)}, u32[]{:S(2)}, u32[]{:S(2)}) collective-permute-start(f32[2,64,512]{2,1,0:T(8,128)S(1)} %get-tuple-element.80), channel_id=1, source_target_pairs={{1,2},{2,1},{3,4},{4,3},{5,6},{6,5},{7,8},{8,7},{9,10},{10,9},{11,... | collective-permute-start | bytes 786440 | tf_op jit(solution)/shard_map/pass_back1/ppermute | solution.py:419
  44.2 5.0 %collective-permute-start.16 = (f32[2,64,256]{2,1,0:T(8,128)S(1)}, f32[2,64,256]{2,1,0:T(8,128)S(1)}, u32[]{:S(2)}, u32[]{:S(2)}) collective-permute-start(f32[2,64,256]{2,1,0:T(8,128)S(1)} %get-tuple-element.86), channel_id=1, source_target_pairs={{0,1},{1,0},{2,3},{3,2},{4,5},{5,4},{6,7},{7,6},{8,9},{9,8},{10,11... | collective-permute-start | bytes 393224 | tf_op jit(solution)/shard_map/swap_gradient/ppermute | solution.py:415
  48.2 1.3 %collective-permute-start.17 = (f32[64,512]{1,0:T(8,128)S(1)}, f32[64,512]{1,0:T(8,128)S(1)}, u32[]{:S(2)}, u32[]{:S(2)}) collective-permute-start(f32[64,512]{1,0:T(8,128)S(1)} %get-tuple-element.87), channel_id=1, source_target_pairs={{0,1},{1,0},{2,3},{3,2},{4,5},{5,4},{6,7},{7,6},{8,9},{9,8},{10,11... | collective-permute-start | bytes 393224 | tf_op jit(solution)/shard_map/swap_adjoint/ppermute | solution.py:415
  48.3 1.5 %collective-permute-start.18 = (f32[64,512]{1,0:T(8,128)S(1)}, f32[64,512]{1,0:T(8,128)S(1)}, u32[]{:S(2)}, u32[]{:S(2)}) collective-permute-start(f32[64,512]{1,0:T(8,128)S(1)} %get-tuple-element.88), channel_id=1, source_target_pairs={{0,1},{1,0},{2,3},{3,2},{4,5},{5,4},{6,7},{7,6},{8,9},{9,8},{10,11... | collective-permute-start | bytes 393224 | tf_op jit(solution)/shard_map/swap_adjoint/ppermute | solution.py:415
  48.7 3.0 %collective-permute-start.15 = (f32[8,128]{1,0:T(8,128)S(1)}, f32[8,128]{1,0:T(8,128)S(1)}, u32[]{:S(2)}, u32[]{:S(2)}) collective-permute-start(f32[8,128]{1,0:T(8,128)S(1)} %get-tuple-element.84.refs_2_), channel_id=1, source_target_pairs={{0,3},{1,2},{2,1},{3,0},{4,7},{5,6},{6,5},{7,4},{8,11},{9,10},{10,... | collective-permute-start | bytes 12296 | tf_op jit(solution)/shard_map/goal_sum/ppermute | solution.py:529
  51.8 1.4 %collective-permute-start.19 = (f32[72,512]{1,0:T(8,128)S(1)}, f32[72,512]{1,0:T(8,128)S(1)}, u32[]{:S(2)}, u32[]{:S(2)}) collective-permute-start(f32[72,512]{1,0:T(8,128)S(1)} %get-tuple-element.90.mine), channel_id=1, source_target_pairs={{0,1},{1,0},{2,3},{3,2},{4,5},{5,4},{6,7},{7,6},{8,9},{9,8},{10,11... | collective-permute-start | bytes 442376 | tf_op jit(solution)/shard_map/swap_outer/ppermute | solution.py:415

commit v9 on v8

--- a/solution.py
+++ b/solution.py
@@ -248,7 +248,7 @@
     return [8 * (tiles // pieces + (k < tiles % pieces)) for k in range(pieces)]
 
 
-def turn_inner(scal, weights, final_own, final_far, terms, cx, cy, cz, dg, goals, part, cost, *pins):
+def turn_inner(scal, terms, cx, cy, cz, dg, part, *pins):
     laid = Laid(pins)
     for j in range(2):
         a = rows_of(scal, j)
@@ -258,6 +258,9 @@
         value = u[1] + time_step * spread
         part[j] = value
         laid.put(a[0] * (cx[1, 1] * value))
+
+
+def goal_sum(weights, final_own, final_far, goals, _, cost):
     total = 0.0
     for k in range(2):
         own, far = weights[0] * final_own[k], weights[1] * final_far[k]
@@ -269,11 +272,10 @@
     cost[...] = sum(total[:, 128 * k : 128 * k + 128] for k in range(columns // 128))
 
 
-def back_second(scal, msgs, partials, part, halo, near, cx, cy, cz, dg, cost, cost_far, *rest):
-    base, a2, total = rest[-3:]
-    count, rows = (len(rest) - 3) // 2, msgs.shape[2]
-    mine, theirs = get(rest[:count], 4, rows), get(rest[count:-3], 4, rows)
-    total[...] = cost[...] + cost_far[...]
+def back_second(scal, msgs, partials, part, halo, near, cx, cy, cz, dg, *rest):
+    base, a2 = rest[-2:]
+    count, rows = (len(rest) - 2) // 2, msgs.shape[2]
+    mine, theirs = get(rest[:count], 4, rows), get(rest[count:-2], 4, rows)
     for j in range(2):
         a = rows_of(scal, j)
         pin, pin2 = theirs[2 - 2 * j], theirs[3 - 2 * j]
@@ -329,6 +331,10 @@
         give[k] = jnp.where(zero, high, low)
 
 
+def combine(cost, cost_far, total):
+    total[...] = cost[...] + cost_far[...]
+
+
 def last_edge(halo, part, cost, cost_far, outer, give):
     rows = outer.shape[0]
     outer[...] = part[0] + time_step * halo[1]
@@ -511,12 +517,10 @@
         [halo2, base] + fields + [goals, adj, after],
     )
     halo3 = pass_on(msg3, "back2")
-    part, cost, *pins = on_core(
-        turn_inner,
-        [pair, (8, 128)] + [(r, columns) for r in cut(4 * rows, 3)],
-        [scal, weights],
-        [final_own, final_far, terms] + fields + [goals],
-    )
+    part, *pins = on_core(
+        turn_inner, [pair] + [(r, columns) for r in cut(4 * rows, 3)], [scal], [terms] + fields
+    )
+    (cost,) = on_core(goal_sum, [(8, 128)], [weights], [final_own, final_far, goals, part])
     whole = sections & (sections - 1) == 0
     steps = [1 << k for k in range(sections.bit_length() - 1)] if whole else []
     steps = steps[1:] + steps[:1]
@@ -529,12 +533,13 @@
             return lax.ppermute(x, AXES, [(i, i ^ flip) for i in range(ranks)])
 
     theirs = [swap(x, "pin") for x in pins]
-    base, a2, cost = on_core(
+    base, a2 = on_core(
         back_second,
-        [four, pair, (8, 128)],
+        [four, pair],
         [scal],
-        [msg3, partials, part, halo, near] + fields + [cost, from_pair(cost, 0)] + pins + theirs,
-    )
+        [msg3, partials, part, halo, near] + fields + pins + theirs,
+    )
+    (cost,) = on_core(combine, [(8, 128)], [], [cost, from_pair(cost, 0)], after=[a2])
     a1, msg4 = on_core(second_back_edge, [pair, pair], [scal], [halo3, base] + fields, after=[cost])
     halo4 = pass_on(msg4, "back1")
     keep, part, give, cost, *out = on_core(

time: 54.2 us -> 54.2 us (level)
  starting transfers between devices: 31.7 us -> 32.5 us
  waiting for transfers between devices: 8.42 us -> 7.71 us
    ppermute x12, starting transfers between devices: 24.1 us -> 24.8 us  [swap(): return lax.ppermute(x, AXES, within)]
    ppermute x3, waiting for transfers between devices: 3.97 us -> 3.25 us  [from_pair(): return lax.ppermute(x, AXES, [(i, i ^ flip) for i in range(ranks)])]
    pallas_call x14 -> x16, Pallas kernels: 6.45 us -> 6.33 us  [on_core(): pl.pallas_call(run, out_shape=out_shape, in_specs=[pl.BlockSpec(memory_sp...]
where the time goes in v9:
time: 54.2 us; the launch traced here: 53.9 us
  starting transfers between devices  32.5 us (60%)
  Pallas kernels  10.6 us (20%)
  waiting for transfers between devices  7.71 us (14%)
  between operations  2.14 us (4%)
  local copies, waits for them, and re-layouts  0.97 us (2%)
    ppermute x12, starting transfers between devices, swap(): return lax.ppermute(x, AXES, within)  24.8 us
    pallas_call x16, Pallas kernels, on_core(): pl.pallas_call(run, out_shape=out_shape, in_specs=[pl.BlockSpec(memory_sp...  6.33 us
    ppermute x12, waiting for transfers between devices, swap(): return lax.ppermute(x, AXES, within)  4.45 us
    ppermute x3, starting transfers between devices, from_pair(): return lax.ppermute(x, AXES, [(i, i ^ flip) for i in range(ranks)])  4.26 us
    ppermute x5, starting transfers between devices, pass_on(): return lax.ppermute(x, AXES, across)  3.41 us
    ppermute x3, waiting for transfers between devices, from_pair(): return lax.ppermute(x, AXES, [(i, i ^ flip) for i in range(ranks)])  3.25 us
    pallas_call x1, Pallas kernels, shards(): pl.pallas_call(prepare_back, out_shape=[pltpu.SMEM((2,), jnp.float32)] +...  1.16 us
  transfers between devices with their start and end apart: 20, of which 10 were waited for; matrix products, arithmetic and copies ran while one was open for 0% of the time, Pallas kernels for 17%

profile of v9, /device:TPU:0, one launch (start us, length us, event | category | flops | bytes accessed | tf_op | source)
XLA Modules:
  0.0 53.9 jit_solution(11994421621010545229)
XLA Ops:
  0.6 0.5 collective-permute-start
  1.2 1.7 %collective-permute-done.refs_2_.refs_3_.far = f32[1,4,64,512]{3,2,1,0:T(8,128)S(1)} collective-permute-done((f32[1,4,64,512]{3,2,1,0:T(8,128)}, f32[1,4,64,512]{3,2,1,0:T(8,128)S(1)}, u32[]{:S(2)}, u32[]{:S(2)}) %collective-permute-start) | collective-permute-done | bytes 524320 | tf_op jit(solution)/shard_map/swap_state/ppermute | solution.py:421
  3.1 0.7 %collective-permute-start.2 = (f32[3,64,512]{2,1,0:T(8,128)S(1)}, f32[3,64,512]{2,1,0:T(8,128)S(1)}, u32[]{:S(2)}, u32[]{:S(2)}) collective-permute-start(f32[3,64,512]{2,1,0:T(8,128)S(1)} %pack.1._), channel_id=1, source_target_pairs={{1,2},{2,1},{3,4},{4,3},{5,6},{6,5},{7,8},{8,7},{9,10},{10,9},{11,... | collective-permute-start | bytes 1179656 | tf_op jit(solution)/shard_map/pass_state/ppermute | solution.py:425
  5.1 0.7 %gather_numbers.1.own_numbers = f32[8,128]{1,0:T(8,128)S(1)} custom-call(s32[1,8]{1,0:T(1,128)} %index.1, s32[1]{0:T(128)S(6)} %copy.17.weight, s32[1]{0:T(128)S(6)} %copy.18.step, f32[3,64,512]{2,1,0:T(8,128)} %copy-done.4), custom_call_target="tpu_custom_call" | custom-call | tf_op jit(solution)/shard_map/gather_numbers/pallas_call | solution.py:441
  5.8 4.3 %collective-permute-start.1 = (f32[8,128]{1,0:T(8,128)S(1)}, f32[8,128]{1,0:T(8,128)S(1)}, u32[]{:S(2)}, u32[]{:S(2)}) collective-permute-start(f32[8,128]{1,0:T(8,128)S(1)} %gather_numbers.1.own_numbers), channel_id=1, source_target_pairs={{0,1},{1,0},{2,3},{3,2},{4,5},{5,4},{6,7},{7,6},{8,9},{9,8},{10,11... | collective-permute-start | bytes 12296 | tf_op jit(solution)/shard_map/swap_numbers/ppermute | solution.py:421
  10.0 0.8 %collective-permute-done.1.far_numbers = f32[8,128]{1,0:T(8,128)S(1)} collective-permute-done((f32[8,128]{1,0:T(8,128)S(1)}, f32[8,128]{1,0:T(8,128)S(1)}, u32[]{:S(2)}, u32[]{:S(2)}) %collective-permute-start.1) | collective-permute-done | bytes 4128 | tf_op jit(solution)/shard_map/swap_numbers/ppermute | solution.py:421
  10.9 0.9 %copy-done.5 = bf16[4,64,512]{2,1,0:T(8,128)(2,1)S(1)} copy-done((bf16[4,64,512]{2,1,0:T(8,128)(2,1)S(1)}, bf16[4,64,512]{2,1,0:T(8,128)(2,1)}, u32[]{:S(2)}) %copy-start.5) | copy-done | bytes 262168
  11.8 0.5 prepare.1
  12.3 0.7 %first_stage.1 = (f32[2,64,512]{2,1,0:T(8,128)S(1)}, f32[2,64,512]{2,1,0:T(8,128)S(1)}, f32[2,64,512]{2,1,0:T(8,128)S(1)}) custom-call(s32[1]{0:T(128)} %bitcast.refs_0_.core, f32[2,8]{1,0:T(2,128)S(4)} %get-tuple-element.47.refs_1_.refs_0_.scal, f32[1,4,64,512]{3,2,1,0:T(8,128)S(1)} %copy-done, ...), custom_call_target="tpu_custom_call" | custom-call | tf_op jit(solution)/shard_map/first_stage/pallas_call | solution.py:387
  13.0 0.7 %collective-permute-start.6 = (f32[2,64,512]{2,1,0:T(8,128)S(1)}, f32[2,64,512]{2,1,0:T(8,128)S(1)}, u32[]{:S(2)}, u32[]{:S(2)}) collective-permute-start(f32[2,64,512]{2,1,0:T(8,128)S(1)} %get-tuple-element.53.refs_2_), channel_id=1, source_target_pairs={{1,2},{2,1},{3,4},{4,3},{5,6},{6,5},{7,8},{8,7},{9,10},{10,9},{11,... | collective-permute-start | bytes 786440 | tf_op jit(solution)/shard_map/pass_stage1/ppermute | solution.py:425
  14.0 0.7 %collective-permute-start.3 = (f32[2,64,512]{2,1,0:T(8,128)S(1)}, f32[2,64,512]{2,1,0:T(8,128)S(1)}, u32[]{:S(2)}, u32[]{:S(2)}) collective-permute-start(f32[2,64,512]{2,1,0:T(8,128)S(1)} %get-tuple-element.55._.refs_4_), channel_id=1, source_target_pairs={{1,2},{2,1},{3,4},{4,3},{5,6},{6,5},{7,8},{8,7},{9,10},{10,9},{11,... | collective-permute-start | bytes 786440 | tf_op jit(solution)/shard_map/pass_stage2/ppermute | solution.py:425
  14.7 0.5 %prepare_next.1 = (f32[2,64,512]{2,1,0:T(8,128)S(1)}, f32[64,512]{1,0:T(8,128)S(1)}) custom-call(s32[1]{0:T(128)} %bitcast.refs_0_.core, f32[2,8]{1,0:T(2,128)S(4)} %get-tuple-element.47.refs_1_.refs_0_.scal, bf16[3,4,64,512]{3,2,1,0:T(8,128)(2,1)S(1)} %copy-done.1, s32[3,4,64,64]{3,2,1,0:T(8,128)S(1)} %copy-done.2, bf16[4,64,512]{2,1,0:T(8,128)(2,1)S(1)} %copy-done.5, ...), custom_call_target="tpu_custom_call" | custom-call | tf_op jit(solution)/shard_map/prepare_next/pallas_call | solution.py:489
  15.7 7.0 %collective-permute-start.4 = (f32[64,512]{1,0:T(8,128)S(1)}, f32[64,512]{1,0:T(8,128)S(1)}, u32[]{:S(2)}, u32[]{:S(2)}) collective-permute-start(f32[64,512]{1,0:T(8,128)S(1)} %get-tuple-element.61.refs_7_), channel_id=1, source_target_pairs={{0,1},{1,0},{2,3},{3,2},{4,5},{5,4},{6,7},{7,6},{8,9},{9,8},{10,11... | collective-permute-start | bytes 393224 | tf_op jit(solution)/shard_map/swap_s2_far/ppermute | solution.py:421
  22.7 1.2 %prepare_back.1 = (f32[2]{0:T(128)S(4)}, f32[2,64,512]{2,1,0:T(8,128)S(1)}, f32[2,64,512]{2,1,0:T(8,128)S(1)}, f32[2,64,512]{2,1,0:T(8,128)S(1)}) custom-call(s32[1]{0:T(128)} %bitcast.refs_0_.core, bf16[4,64,512]{2,1,0:T(8,128)(2,1)} %goal.1, f32[8,128]{1,0:T(8,128)S(1)} %gather_numbers.1.own_numbers, f32[8,128]{1,0:T(8,128)S(1)} %collective-permute-done.1.far_numbers, ...), custom_call_target="tpu_custom_call" | custom-call | tf_op jit(solution)/shard_map/prepare_back/pallas_call | solution.py:472
  23.9 0.5 collective-permute-start.7
  24.5 0.8 %third_stage.1.refs_3_ = f32[2,2,64,512]{3,2,1,0:T(8,128)S(1)} custom-call(s32[1]{0:T(128)} %bitcast.refs_0_.core, f32[2,8]{1,0:T(2,128)S(4)} %get-tuple-element.47.refs_1_.refs_0_.scal, f32[1,4,64,512]{3,2,1,0:T(8,128)S(1)} %copy-done, f32[1,4,64,512]{3,2,1,0:T(8,128)S(1)} %collective-permute-done.refs_2_.refs_3_.far, ...), custom_call_target="tpu_custom_call" | custom-call | tf_op jit(solution)/shard_map/third_stage/pallas_call | solution.py:387
  25.6 0.5 turn.1
  26.1 0.7 %collective-permute-start.8 = (f32[2,2,64,512]{3,2,1,0:T(8,128)S(1)}, f32[2,2,64,512]{3,2,1,0:T(8,128)S(1)}, u32[]{:S(2)}, u32[]{:S(2)}) collective-permute-start(f32[2,2,64,512]{3,2,1,0:T(8,128)S(1)} %get-tuple-element.65.refs_1_), channel_id=1, source_target_pairs={{1,2},{2,1},{3,4},{4,3},{5,6},{6,5},{7,8},{8,7},{9,10},{10,9},{11,... | collective-permute-start | bytes 1572872 | tf_op jit(solution)/shard_map/pass_back2/ppermute | solution.py:425
  27.2 6.5 %collective-permute-start.10 = (f32[88,512]{1,0:T(8,128)S(1)}, f32[88,512]{1,0:T(8,128)S(1)}, u32[]{:S(2)}, u32[]{:S(2)}) collective-permute-start(f32[88,512]{1,0:T(8,128)S(1)} %get-tuple-element.71.refs_11_), channel_id=1, source_target_pairs={{0,1},{1,0},{2,3},{3,2},{4,5},{5,4},{6,7},{7,6},{8,9},{9,8},{10,11... | collective-permute-start | bytes 540680 | tf_op jit(solution)/shard_map/swap_pin/ppermute | solution.py:421
  34.4 1.6 %collective-permute-start.12 = (f32[8,128]{1,0:T(8,128)S(1)}, f32[8,128]{1,0:T(8,128)S(1)}, u32[]{:S(2)}, u32[]{:S(2)}) collective-permute-start(f32[8,128]{1,0:T(8,128)S(1)} %goal_sum.1.refs_0_), channel_id=1, source_target_pairs={{0,4},{1,5},{2,6},{3,7},{4,0},{5,1},{6,2},{7,3},{8,12},{9,13},{10,... | collective-permute-start | bytes 12296 | tf_op jit(solution)/shard_map/goal_sum/ppermute | solution.py:533
  36.0 0.7 %back_second.1 = (f32[2,2,64,512]{3,2,1,0:T(8,128)S(1)}, f32[2,64,512]{2,1,0:T(8,128)S(1)}) custom-call(f32[2,8]{1,0:T(2,128)S(4)} %get-tuple-element.47.refs_1_.refs_0_.scal, f32[2,2,64,512]{3,2,1,0:T(8,128)S(1)} %get-tuple-element.65.refs_1_, f32[2,64,512]{2,1,0:T(8,128)S(1)} %get-tuple-element.66.refs_2_.refs_3_, ...), custom_call_target="tpu_custom_call" | custom-call | tf_op jit(solution)/shard_map/back_second/pallas_call | solution.py:387
  36.7 1.3 %collective-permute-done.12.refs_1_ = f32[8,128]{1,0:T(8,128)S(1)} collective-permute-done((f32[8,128]{1,0:T(8,128)S(1)}, f32[8,128]{1,0:T(8,128)S(1)}, u32[]{:S(2)}, u32[]{:S(2)}) %collective-permute-start.12) | collective-permute-done | bytes 4128 | tf_op jit(solution)/shard_map/goal_sum/ppermute | solution.py:533
  38.0 2.6 %collective-permute-start.14 = (f32[8,128]{1,0:T(8,128)S(1)}, f32[8,128]{1,0:T(8,128)S(1)}, u32[]{:S(2)}, u32[]{:S(2)}) collective-permute-start(f32[8,128]{1,0:T(8,128)S(1)} %combine.1.refs_7_.refs_13_), channel_id=1, source_target_pairs={{0,8},{1,9},{2,10},{3,11},{4,12},{5,13},{6,14},{7,15},{8,0},{9,1},... | collective-permute-start | bytes 12296 | tf_op jit(solution)/shard_map/goal_sum/ppermute | solution.py:533
  41.0 0.7 %collective-permute-start.13 = (f32[2,64,512]{2,1,0:T(8,128)S(1)}, f32[2,64,512]{2,1,0:T(8,128)S(1)}, u32[]{:S(2)}, u32[]{:S(2)}) collective-permute-start(f32[2,64,512]{2,1,0:T(8,128)S(1)} %get-tuple-element.77), channel_id=1, source_target_pairs={{1,2},{2,1},{3,4},{4,3},{5,6},{6,5},{7,8},{8,7},{9,10},{10,9},{11,... | collective-permute-start | bytes 786440 | tf_op jit(solution)/shard_map/pass_back1/ppermute | solution.py:425
  41.7 0.9 %collective-permute-done.14.refs_14_ = f32[8,128]{1,0:T(8,128)S(1)} collective-permute-done((f32[8,128]{1,0:T(8,128)S(1)}, f32[8,128]{1,0:T(8,128)S(1)}, u32[]{:S(2)}, u32[]{:S(2)}) %collective-permute-start.14) | collective-permute-done | bytes 4128 | tf_op jit(solution)/shard_map/goal_sum/ppermute | solution.py:533
  42.5 0.8 %close.1 = (f32[2,64,256]{2,1,0:T(8,128)S(1)}, f32[4,64,512]{2,1,0:T(8,128)S(1)}, f32[2,64,256]{2,1,0:T(8,128)S(1)}, f32[8,128]{1,0:T(8,128)S(1)}, f32[64,512]{1,0:T(8,128)S(1)}, /*index=5*/f32[64,512]{1,0:T(8,128)S(1)}) custom-call(s32[1]{0:T(128)} %bitcast.refs_0_.core, f32[2,8]{1,0:T(2,128)S(4)} %get-tuple-element.47.refs_1_.refs_0_.scal, ...), custom_call_target="tpu_custom_call" | custom-call | flops 16000000000 | bytes 48000000 | tf_op jit(solution)/shard_map/close/pallas_call | solution.py:387
  43.4 4.8 %collective-permute-start.16 = (f32[2,64,256]{2,1,0:T(8,128)S(1)}, f32[2,64,256]{2,1,0:T(8,128)S(1)}, u32[]{:S(2)}, u32[]{:S(2)}) collective-permute-start(f32[2,64,256]{2,1,0:T(8,128)S(1)} %get-tuple-element.82), channel_id=1, source_target_pairs={{0,1},{1,0},{2,3},{3,2},{4,5},{5,4},{6,7},{7,6},{8,9},{9,8},{10,11... | collective-permute-start | bytes 393224 | tf_op jit(solution)/shard_map/swap_gradient/ppermute | solution.py:421
  49.7 0.9 %write_inner.1 = (f32[1,4,64,512]{3,2,1,0:T(8,128)}, f32[4,64,256]{2,1,0:T(8,128)}) custom-call(s32[1]{0:T(128)} %bitcast.refs_0_.core, f32[4,64,512]{2,1,0:T(8,128)S(1)} %get-tuple-element.79.refs_1_, f32[2,64,256]{2,1,0:T(8,128)S(1)} %get-tuple-element.81.refs_2_, f32[2,64,256]{2,1,0:T(8,128)S(1)} %collective-permute-done.16.refs_3_, ...), custom_call_target="tpu_custom_call" | custom-call | tf_op jit(solution)/shard_map/write_inner/pallas_call | solution.py:387
  50.6 1.1 %collective-permute-done.15.refs_3_ = f32[8,128]{1,0:T(8,128)S(1)} collective-permute-done((f32[8,128]{1,0:T(8,128)S(1)}, f32[8,128]{1,0:T(8,128)S(1)}, u32[]{:S(2)}, u32[]{:S(2)}) %collective-permute-start.15) | collective-permute-done | bytes 4128 | tf_op jit(solution)/shard_map/goal_sum/ppermute | solution.py:533
  51.9 0.7 %write_outer.1._ = f32[1,4,64,512]{3,2,1,0:T(8,128)} custom-call(s32[1]{0:T(128)} %bitcast.refs_0_.core, f32[64,512]{1,0:T(8,128)S(1)} %get-tuple-element.87.value, f32[1,4,64,512]{3,2,1,0:T(8,128)} %get-tuple-element.85.refs_4_._), custom_call_target="tpu_custom_call", output_to_operand_aliasing={{}: (2, {})} | custom-call | tf_op jit(solution)/shard_map/write_outer/pallas_call | solution.py:575
  52.6 0.6 %collective-permute-done.19.taken = f32[72,512]{1,0:T(8,128)S(1)} collective-permute-done((f32[72,512]{1,0:T(8,128)S(1)}, f32[72,512]{1,0:T(8,128)S(1)}, u32[]{:S(2)}, u32[]{:S(2)}) %collective-permute-start.19) | collective-permute-done | bytes 147488 | tf_op jit(solution)/shard_map/swap_outer/ppermute | solution.py:421
  53.2 0.7 %finish.1 = (f32[1,4,64,512]{3,2,1,0:T(8,128)}, f32[1]{0:T(128)}) custom-call(s32[1]{0:T(128)} %bitcast.refs_0_.core, f32[72,512]{1,0:T(8,128)S(1)} %get-tuple-element.86.mine, f32[72,512]{1,0:T(8,128)S(1)} %collective-permute-done.19.taken, f32[1,4,64,512]{3,2,1,0:T(8,128)} %write_outer.1._), custom_call_target="tpu_custom_call", output_to_operand_aliasing={{0}: (3, {})} | custom-call | tf_op jit(solution)/shard_map/finish/pallas_call | solution.py:585
  (42 shorter events, 4.5 us)
Async XLA Ops:
  0.6 2.3 %collective-permute-start = (f32[1,4,64,512]{3,2,1,0:T(8,128)}, f32[1,4,64,512]{3,2,1,0:T(8,128)S(1)}, u32[]{:S(2)}, u32[]{:S(2)}) collective-permute-start(f32[1,4,64,512]{3,2,1,0:T(8,128)} %refs_2_.7), channel_id=1, source_target_pairs={{0,1},{1,0},{2,3},{3,2},{4,5},{5,4},{6,7},{7,6},{8,9},{9,8},{10,11... | collective-permute-start | bytes 1572872 | tf_op jit(solution)/shard_map/swap_state/ppermute | solution.py:421
  1.1 1.8 %copy-start = (f32[1,4,64,512]{3,2,1,0:T(8,128)S(1)}, f32[1,4,64,512]{3,2,1,0:T(8,128)}, u32[]{:S(2)}) copy-start(f32[1,4,64,512]{3,2,1,0:T(8,128)} %refs_2_.7) | copy-start | bytes 1572868
  1.2 1.8 %copy-start.1 = (bf16[3,4,64,512]{3,2,1,0:T(8,128)(2,1)S(1)}, bf16[3,4,64,512]{3,2,1,0:T(8,128)(2,1)}, u32[]{:S(2)}) copy-start(bf16[3,4,64,512]{3,2,1,0:T(8,128)(2,1)} %speed.3) | copy-start | bytes 2359300
  1.2 1.8 %copy-start.2 = (s32[3,4,64,64]{3,2,1,0:T(8,128)S(1)}, s32[3,4,64,64]{3,2,1,0:T(8,128)}, u32[]{:S(2)}) copy-start(s32[3,4,64,64]{3,2,1,0:T(8,128)} %mask.3) | copy-start | bytes 589828
  2.9 8.0 %copy-start.3 = (f32[4,64,512]{2,1,0:T(8,128)S(1)}, f32[4,64,512]{2,1,0:T(8,128)}, u32[]{:S(2)}) copy-start(f32[4,64,512]{2,1,0:T(8,128)} %control.3) | copy-start | bytes 1572868
  3.1 2.0 %copy-start.4 = (f32[3,64,512]{2,1,0:T(8,128)}, f32[3,64,512]{2,1,0:T(8,128)S(1)}, u32[]{:S(2)}) copy-start(f32[3,64,512]{2,1,0:T(8,128)S(1)} %pack.1._) | copy-start | bytes 1179652
  3.1 10.6 %collective-permute-start.2 = (f32[3,64,512]{2,1,0:T(8,128)S(1)}, f32[3,64,512]{2,1,0:T(8,128)S(1)}, u32[]{:S(2)}, u32[]{:S(2)}) collective-permute-start(f32[3,64,512]{2,1,0:T(8,128)S(1)} %pack.1._), channel_id=1, source_target_pairs={{1,2},{2,1},{3,4},{4,3},{5,6},{6,5},{7,8},{8,7},{9,10},{10,9},{11,... | collective-permute-start | bytes 1179656 | tf_op jit(solution)/shard_map/pass_state/ppermute | solution.py:425
  5.8 5.1 %collective-permute-start.1 = (f32[8,128]{1,0:T(8,128)S(1)}, f32[8,128]{1,0:T(8,128)S(1)}, u32[]{:S(2)}, u32[]{:S(2)}) collective-permute-start(f32[8,128]{1,0:T(8,128)S(1)} %gather_numbers.1.own_numbers), channel_id=1, source_target_pairs={{0,1},{1,0},{2,3},{3,2},{4,5},{5,4},{6,7},{7,6},{8,9},{9,8},{10,11... | collective-permute-start | bytes 12296 | tf_op jit(solution)/shard_map/swap_numbers/ppermute | solution.py:421
  10.9 1.0 %copy-start.5 = (bf16[4,64,512]{2,1,0:T(8,128)(2,1)S(1)}, bf16[4,64,512]{2,1,0:T(8,128)(2,1)}, u32[]{:S(2)}) copy-start(bf16[4,64,512]{2,1,0:T(8,128)(2,1)} %decay.3) | copy-start | bytes 786436
  13.0 11.4 %collective-permute-start.6 = (f32[2,64,512]{2,1,0:T(8,128)S(1)}, f32[2,64,512]{2,1,0:T(8,128)S(1)}, u32[]{:S(2)}, u32[]{:S(2)}) collective-permute-start(f32[2,64,512]{2,1,0:T(8,128)S(1)} %get-tuple-element.53.refs_2_), channel_id=1, source_target_pairs={{1,2},{2,1},{3,4},{4,3},{5,6},{6,5},{7,8},{8,7},{9,10},{10,9},{11,... | collective-permute-start | bytes 786440 | tf_op jit(solution)/shard_map/pass_stage1/ppermute | solution.py:425
  14.0 11.5 %collective-permute-start.3 = (f32[2,64,512]{2,1,0:T(8,128)S(1)}, f32[2,64,512]{2,1,0:T(8,128)S(1)}, u32[]{:S(2)}, u32[]{:S(2)}) collective-permute-start(f32[2,64,512]{2,1,0:T(8,128)S(1)} %get-tuple-element.55._.refs_4_), channel_id=1, source_target_pairs={{1,2},{2,1},{3,4},{4,3},{5,6},{6,5},{7,8},{8,7},{9,10},{10,9},{11,... | collective-permute-start | bytes 786440 | tf_op jit(solution)/shard_map/pass_stage2/ppermute | solution.py:425
  15.7 8.8 %collective-permute-start.4 = (f32[64,512]{1,0:T(8,128)S(1)}, f32[64,512]{1,0:T(8,128)S(1)}, u32[]{:S(2)}, u32[]{:S(2)}) collective-permute-start(f32[64,512]{1,0:T(8,128)S(1)} %get-tuple-element.61.refs_7_), channel_id=1, source_target_pairs={{0,1},{1,0},{2,3},{3,2},{4,5},{5,4},{6,7},{7,6},{8,9},{9,8},{10,11... | collective-permute-start | bytes 393224 | tf_op jit(solution)/shard_map/swap_s2_far/ppermute | solution.py:421
  22.7 1.8 %collective-permute-start.5 = (f32[64,512]{1,0:T(8,128)S(1)}, f32[64,512]{1,0:T(8,128)S(1)}, u32[]{:S(2)}, u32[]{:S(2)}) collective-permute-start(f32[64,512]{1,0:T(8,128)S(1)} %get-tuple-element.60.refs_6_), channel_id=1, source_target_pairs={{0,1},{1,0},{2,3},{3,2},{4,5},{5,4},{6,7},{7,6},{8,9},{9,8},{10,11... | collective-permute-start | bytes 393224 | tf_op jit(solution)/shard_map/swap_s2_own/ppermute | solution.py:421
  23.9 1.7 %collective-permute-start.7 = (f32[2,64,512]{2,1,0:T(8,128)S(1)}, f32[2,64,512]{2,1,0:T(8,128)S(1)}, u32[]{:S(2)}, u32[]{:S(2)}) collective-permute-start(f32[2,64,512]{2,1,0:T(8,128)S(1)} %get-tuple-element.64), channel_id=1, source_target_pairs={{0,1},{1,0},{2,3},{3,2},{4,5},{5,4},{6,7},{7,6},{8,9},{9,8},{10,11... | collective-permute-start | bytes 786440 | tf_op jit(solution)/shard_map/swap_after/ppermute | solution.py:421
  26.1 14.5 %collective-permute-start.8 = (f32[2,2,64,512]{3,2,1,0:T(8,128)S(1)}, f32[2,2,64,512]{3,2,1,0:T(8,128)S(1)}, u32[]{:S(2)}, u32[]{:S(2)}) collective-permute-start(f32[2,2,64,512]{3,2,1,0:T(8,128)S(1)} %get-tuple-element.65.refs_1_), channel_id=1, source_target_pairs={{1,2},{2,1},{3,4},{4,3},{5,6},{6,5},{7,8},{8,7},{9,10},{10,9},{11,... | collective-permute-start | bytes 1572872 | tf_op jit(solution)/shard_map/pass_back2/ppermute | solution.py:425
  27.2 8.8 %collective-permute-start.10 = (f32[88,512]{1,0:T(8,128)S(1)}, f32[88,512]{1,0:T(8,128)S(1)}, u32[]{:S(2)}, u32[]{:S(2)}) collective-permute-start(f32[88,512]{1,0:T(8,128)S(1)} %get-tuple-element.71.refs_11_), channel_id=1, source_target_pairs={{0,1},{1,0},{2,3},{3,2},{4,5},{5,4},{6,7},{7,6},{8,9},{9,8},{10,11... | collective-permute-start | bytes 540680 | tf_op jit(solution)/shard_map/swap_pin/ppermute | solution.py:421
  33.7 2.3 %collective-permute-start.9 = (f32[88,512]{1,0:T(8,128)S(1)}, f32[88,512]{1,0:T(8,128)S(1)}, u32[]{:S(2)}, u32[]{:S(2)}) collective-permute-start(f32[88,512]{1,0:T(8,128)S(1)} %get-tuple-element.70.refs_10_), channel_id=1, source_target_pairs={{0,1},{1,0},{2,3},{3,2},{4,5},{5,4},{6,7},{7,6},{8,9},{9,8},{10,11... | collective-permute-start | bytes 540680 | tf_op jit(solution)/shard_map/swap_pin/ppermute | solution.py:421
  33.8 2.2 %collective-permute-start.11 = (f32[80,512]{1,0:T(8,128)S(1)}, f32[80,512]{1,0:T(8,128)S(1)}, u32[]{:S(2)}, u32[]{:S(2)}) collective-permute-start(f32[80,512]{1,0:T(8,128)S(1)} %get-tuple-element.72.refs_12_), channel_id=1, source_target_pairs={{0,1},{1,0},{2,3},{3,2},{4,5},{5,4},{6,7},{7,6},{8,9},{9,8},{10,11... | collective-permute-start | bytes 491528 | tf_op jit(solution)/shard_map/swap_pin/ppermute | solution.py:421
  34.4 3.7 %collective-permute-start.12 = (f32[8,128]{1,0:T(8,128)S(1)}, f32[8,128]{1,0:T(8,128)S(1)}, u32[]{:S(2)}, u32[]{:S(2)}) collective-permute-start(f32[8,128]{1,0:T(8,128)S(1)} %goal_sum.1.refs_0_), channel_id=1, source_target_pairs={{0,4},{1,5},{2,6},{3,7},{4,0},{5,1},{6,2},{7,3},{8,12},{9,13},{10,... | collective-permute-start | bytes 12296 | tf_op jit(solution)/shard_map/goal_sum/ppermute | solution.py:533
  38.0 4.5 %collective-permute-start.14 = (f32[8,128]{1,0:T(8,128)S(1)}, f32[8,128]{1,0:T(8,128)S(1)}, u32[]{:S(2)}, u32[]{:S(2)}) collective-permute-start(f32[8,128]{1,0:T(8,128)S(1)} %combine.1.refs_7_.refs_13_), channel_id=1, source_target_pairs={{0,8},{1,9},{2,10},{3,11},{4,12},{5,13},{6,14},{7,15},{8,0},{9,1},... | collective-permute-start | bytes 12296 | tf_op jit(solution)/shard_map/goal_sum/ppermute | solution.py:533
  41.0 10.7 %collective-permute-start.13 = (f32[2,64,512]{2,1,0:T(8,128)S(1)}, f32[2,64,512]{2,1,0:T(8,128)S(1)}, u32[]{:S(2)}, u32[]{:S(2)}) collective-permute-start(f32[2,64,512]{2,1,0:T(8,128)S(1)} %get-tuple-element.77), channel_id=1, source_target_pairs={{1,2},{2,1},{3,4},{4,3},{5,6},{6,5},{7,8},{8,7},{9,10},{10,9},{11,... | collective-permute-start | bytes 786440 | tf_op jit(solution)/shard_map/pass_back1/ppermute | solution.py:425
  43.4 5.8 %collective-permute-start.16 = (f32[2,64,256]{2,1,0:T(8,128)S(1)}, f32[2,64,256]{2,1,0:T(8,128)S(1)}, u32[]{:S(2)}, u32[]{:S(2)}) collective-permute-start(f32[2,64,256]{2,1,0:T(8,128)S(1)} %get-tuple-element.82), channel_id=1, source_target_pairs={{0,1},{1,0},{2,3},{3,2},{4,5},{5,4},{6,7},{7,6},{8,9},{9,8},{10,11... | collective-permute-start | bytes 393224 | tf_op jit(solution)/shard_map/swap_gradient/ppermute | solution.py:421
  48.1 1.3 %collective-permute-start.17 = (f32[64,512]{1,0:T(8,128)S(1)}, f32[64,512]{1,0:T(8,128)S(1)}, u32[]{:S(2)}, u32[]{:S(2)}) collective-permute-start(f32[64,512]{1,0:T(8,128)S(1)} %get-tuple-element.83), channel_id=1, source_target_pairs={{0,1},{1,0},{2,3},{3,2},{4,5},{5,4},{6,7},{7,6},{8,9},{9,8},{10,11... | collective-permute-start | bytes 393224 | tf_op jit(solution)/shard_map/swap_adjoint/ppermute | solution.py:421
  48.2 1.5 %collective-permute-start.18 = (f32[64,512]{1,0:T(8,128)S(1)}, f32[64,512]{1,0:T(8,128)S(1)}, u32[]{:S(2)}, u32[]{:S(2)}) collective-permute-start(f32[64,512]{1,0:T(8,128)S(1)} %get-tuple-element.84), channel_id=1, source_target_pairs={{0,1},{1,0},{2,3},{3,2},{4,5},{5,4},{6,7},{7,6},{8,9},{9,8},{10,11... | collective-permute-start | bytes 393224 | tf_op jit(solution)/shard_map/swap_adjoint/ppermute | solution.py:421
  48.6 3.0 %collective-permute-start.15 = (f32[8,128]{1,0:T(8,128)S(1)}, f32[8,128]{1,0:T(8,128)S(1)}, u32[]{:S(2)}, u32[]{:S(2)}) collective-permute-start(f32[8,128]{1,0:T(8,128)S(1)} %get-tuple-element.80.refs_2_), channel_id=1, source_target_pairs={{0,3},{1,2},{2,1},{3,0},{4,7},{5,6},{6,5},{7,4},{8,11},{9,10},{10,... | collective-permute-start | bytes 12296 | tf_op jit(solution)/shard_map/goal_sum/ppermute | solution.py:533
  51.7 1.4 %collective-permute-start.19 = (f32[72,512]{1,0:T(8,128)S(1)}, f32[72,512]{1,0:T(8,128)S(1)}, u32[]{:S(2)}, u32[]{:S(2)}) collective-permute-start(f32[72,512]{1,0:T(8,128)S(1)} %get-tuple-element.86.mine), channel_id=1, source_target_pairs={{0,1},{1,0},{2,3},{3,2},{4,5},{5,4},{6,7},{7,6},{8,9},{9,8},{10,11... | collective-permute-start | bytes 442376 | tf_op jit(solution)/shard_map/swap_outer/ppermute | solution.py:421

commit v10 on v9

--- a/solution.py
+++ b/solution.py
@@ -51,7 +51,7 @@
 
 def node_scales(tiles, scal):
     levels = [-math.cos(math.pi * k / 8.0) for k in range(9)]
-    step = tiles[0][0, 9].astype(jnp.int32)
+    step = tiles[0][0, 8].astype(jnp.int32)
     half = step & 31
     wave = pick([math.sin(2.0 * math.pi * k / 64.0) for k in range(17)], jnp.minimum(half, 32 - half))
     phase = 1.0 + jnp.where(step < 32, 0.5, -0.5) * wave
@@ -84,10 +84,10 @@
     out[...] = jnp.zeros_like(out)
 
 
-def gather_numbers(index, weight, step, _, numbers):
+def gather_numbers(index, step, _, numbers):
     lane = lax.broadcasted_iota(jnp.int32, numbers.shape, 1)
     value = jnp.zeros(numbers.shape, jnp.int32)
-    for k, number in enumerate([index[0, k] for k in range(index.shape[1])] + [weight[0], step[0]]):
+    for k, number in enumerate([index[0, k] for k in range(index.shape[1])] + [step[0]]):
         value = jnp.where(lane == k, number, value)
     numbers[...] = value.astype(jnp.float32)
 
@@ -145,10 +145,10 @@
         s1_next[j] = value + time_step * (l + a[4] * control[at])
 
 
-def prepare_back(core, goal, own_numbers, far_numbers, adjoint, _, weights, goals, adj, adj_out):
+def prepare_back(core, own_weight, far_weight, goal, adjoint, _, weights, goals, adj, adj_out):
     me = core[0]
-    weights[0] = own_numbers[...][0, 8] * (1.0 / weight_denominator)
-    weights[1] = far_numbers[...][0, 8] * (1.0 / weight_denominator)
+    weights[0] = own_weight[0].astype(jnp.float32) * (1.0 / weight_denominator)
+    weights[1] = far_weight[0].astype(jnp.float32) * (1.0 / weight_denominator)
     for k, at in enumerate((3 * me, 1 + me)):
         goals[k] = goal[at].astype(jnp.float32)
         adj[k] = adjoint[0, at].astype(jnp.float32)
@@ -441,10 +441,10 @@
     numbers = pl.pallas_call(
         gather_numbers,
         out_shape=pltpu.VMEM((8, 128), jnp.float32),
-        in_specs=[pl.BlockSpec(memory_space=pltpu.SMEM)] * 3 + [pl.BlockSpec(memory_space=pl.ANY)],
+        in_specs=[pl.BlockSpec(memory_space=pltpu.SMEM)] * 2 + [pl.BlockSpec(memory_space=pl.ANY)],
         out_specs=pl.BlockSpec(memory_space=pltpu.VMEM),
         name="gather_numbers",
-    )(node_index, weight_num, step_index, packed)
+    )(node_index, step_index, packed)
     far_numbers = swap(numbers, "numbers")
 
     shapes = [four, four, four, four, pair]
@@ -473,16 +473,17 @@
         prepare_back,
         out_shape=[pltpu.SMEM((2,), jnp.float32)]
         + [pltpu.VMEM(s, jnp.float32) for s in (pair, pair, pair)],
-        in_specs=[pl.BlockSpec(memory_space=pltpu.SMEM)]
-        + [pl.BlockSpec(memory_space=pltpu.VMEM)] * 4
+        in_specs=[pl.BlockSpec(memory_space=pltpu.SMEM)] * 3
+        + [pl.BlockSpec(memory_space=pltpu.VMEM)] * 2
         + [pl.BlockSpec(memory_space=pl.ANY)],
         out_specs=[pl.BlockSpec(memory_space=pltpu.SMEM)] + [pl.BlockSpec(memory_space=pltpu.VMEM)] * 3,
         compiler_params=pltpu.CompilerParams(vmem_limit_bytes=VMEM_LIMIT),
         name="prepare_back",
     )(
         core,
+        weight_num,
+        swap(weight_num, "weight_num"),
         held(goal_weight, pltpu.HBM),
-        *[held(x, pltpu.VMEM) for x in (numbers, far_numbers)],
         held(adjoint_next, pltpu.HBM),
         msg,
     )

time: 54.2 us -> 53.7 us (level)
  waiting for transfers between devices: 7.71 us -> 7 us
    ppermute x12 -> x13, waiting for transfers between devices: 4.45 us -> 3.73 us  [swap(): return lax.ppermute(x, AXES, within)]
    pallas_call x1, Pallas kernels: 1.16 us -> 1.72 us  [shards(): pl.pallas_call(prepare_back, out_shape=[pltpu.SMEM((2,), jnp.float32)] +...]
    ppermute x12 -> x13, starting transfers between devices: 24.8 us -> 24.5 us  [swap(): return lax.ppermute(x, AXES, within)]
  transfers between devices with their start and end apart: 20 -> 21, of which waited for: 10 -> 10; matrix products, arithmetic and copies ran while one was open for 0% -> 0% of each run, Pallas kernels for 17% -> 18%
where the time goes in v10:
time: 53.7 us; the launch traced here: 53.4 us
  starting transfers between devices  32.2 us (60%)
  Pallas kernels  11.1 us (21%)
  waiting for transfers between devices  7 us (13%)
  between operations  2.14 us (4%)
  local copies, waits for them, and re-layouts  0.97 us (2%)
    ppermute x13, starting transfers between devices, swap(): return lax.ppermute(x, AXES, within)  24.5 us
    pallas_call x16, Pallas kernels, on_core(): pl.pallas_call(run, out_shape=out_shape, in_specs=[pl.BlockSpec(memory_sp...  6.31 us
    ppermute x3, starting transfers between devices, from_pair(): return lax.ppermute(x, AXES, [(i, i ^ flip) for i in range(ranks)])  4.26 us
    ppermute x13, waiting for transfers between devices, swap(): return lax.ppermute(x, AXES, within)  3.73 us
    ppermute x5, starting transfers between devices, pass_on(): return lax.ppermute(x, AXES, across)  3.41 us
    ppermute x3, waiting for transfers between devices, from_pair(): return lax.ppermute(x, AXES, [(i, i ^ flip) for i in range(ranks)])  3.25 us
    pallas_call x1, Pallas kernels, shards(): pl.pallas_call(prepare_back, out_shape=[pltpu.SMEM((2,), jnp.float32)] +...  1.72 us
  transfers between devices with their start and end apart: 21, of which 10 were waited for; matrix products, arithmetic and copies ran while one was open for 0% of the time, Pallas kernels for 18%

profile of v10, /device:TPU:0, one launch (start us, length us, event | category | flops | bytes accessed | tf_op | source)
XLA Modules:
  0.0 53.4 jit_solution(7470388824590607503)
XLA Ops:
  0.6 0.5 collective-permute-start
  1.2 1.7 %collective-permute-done.refs_2_.refs_3_.far = f32[1,4,64,512]{3,2,1,0:T(8,128)S(1)} collective-permute-done((f32[1,4,64,512]{3,2,1,0:T(8,128)}, f32[1,4,64,512]{3,2,1,0:T(8,128)S(1)}, u32[]{:S(2)}, u32[]{:S(2)}) %collective-permute-start) | collective-permute-done | bytes 524320 | tf_op jit(solution)/shard_map/swap_state/ppermute | solution.py:421
  3.1 0.7 %collective-permute-start.3 = (f32[3,64,512]{2,1,0:T(8,128)S(1)}, f32[3,64,512]{2,1,0:T(8,128)S(1)}, u32[]{:S(2)}, u32[]{:S(2)}) collective-permute-start(f32[3,64,512]{2,1,0:T(8,128)S(1)} %pack.1._), channel_id=1, source_target_pairs={{1,2},{2,1},{3,4},{4,3},{5,6},{6,5},{7,8},{8,7},{9,10},{10,9},{11,... | collective-permute-start | bytes 1179656 | tf_op jit(solution)/shard_map/pass_state/ppermute | solution.py:425
  4.4 0.7 %gather_numbers.1.own_numbers = f32[8,128]{1,0:T(8,128)S(1)} custom-call(s32[1,8]{1,0:T(1,128)} %index.1, s32[1]{0:T(128)S(6)} %copy.18.step, f32[3,64,512]{2,1,0:T(8,128)} %copy-done.4), custom_call_target="tpu_custom_call" | custom-call | tf_op jit(solution)/shard_map/gather_numbers/pallas_call | solution.py:441
  5.1 4.3 %collective-permute-start.1 = (f32[8,128]{1,0:T(8,128)S(1)}, f32[8,128]{1,0:T(8,128)S(1)}, u32[]{:S(2)}, u32[]{:S(2)}) collective-permute-start(f32[8,128]{1,0:T(8,128)S(1)} %gather_numbers.1.own_numbers), channel_id=1, source_target_pairs={{0,1},{1,0},{2,3},{3,2},{4,5},{5,4},{6,7},{7,6},{8,9},{9,8},{10,11... | collective-permute-start | bytes 12296 | tf_op jit(solution)/shard_map/swap_numbers/ppermute | solution.py:421
  10.2 0.9 %copy-done.5 = bf16[4,64,512]{2,1,0:T(8,128)(2,1)S(1)} copy-done((bf16[4,64,512]{2,1,0:T(8,128)(2,1)S(1)}, bf16[4,64,512]{2,1,0:T(8,128)(2,1)}, u32[]{:S(2)}) %copy-start.5) | copy-done | bytes 262168
  11.2 0.5 prepare.1
  11.7 0.7 %first_stage.1 = (f32[2,64,512]{2,1,0:T(8,128)S(1)}, f32[2,64,512]{2,1,0:T(8,128)S(1)}, f32[2,64,512]{2,1,0:T(8,128)S(1)}) custom-call(s32[1]{0:T(128)} %bitcast.refs_0_.core, f32[2,8]{1,0:T(2,128)S(4)} %get-tuple-element.47.refs_1_.refs_0_.scal, f32[1,4,64,512]{3,2,1,0:T(8,128)S(1)} %copy-done, ...), custom_call_target="tpu_custom_call" | custom-call | tf_op jit(solution)/shard_map/first_stage/pallas_call | solution.py:387
  12.4 0.7 %collective-permute-start.7 = (f32[2,64,512]{2,1,0:T(8,128)S(1)}, f32[2,64,512]{2,1,0:T(8,128)S(1)}, u32[]{:S(2)}, u32[]{:S(2)}) collective-permute-start(f32[2,64,512]{2,1,0:T(8,128)S(1)} %get-tuple-element.53.refs_2_), channel_id=1, source_target_pairs={{1,2},{2,1},{3,4},{4,3},{5,6},{6,5},{7,8},{8,7},{9,10},{10,9},{11,... | collective-permute-start | bytes 786440 | tf_op jit(solution)/shard_map/pass_stage1/ppermute | solution.py:425
  13.4 0.7 %collective-permute-start.4 = (f32[2,64,512]{2,1,0:T(8,128)S(1)}, f32[2,64,512]{2,1,0:T(8,128)S(1)}, u32[]{:S(2)}, u32[]{:S(2)}) collective-permute-start(f32[2,64,512]{2,1,0:T(8,128)S(1)} %get-tuple-element.55._.refs_4_), channel_id=1, source_target_pairs={{1,2},{2,1},{3,4},{4,3},{5,6},{6,5},{7,8},{8,7},{9,10},{10,9},{11,... | collective-permute-start | bytes 786440 | tf_op jit(solution)/shard_map/pass_stage2/ppermute | solution.py:425
  14.1 0.5 %prepare_next.1 = (f32[2,64,512]{2,1,0:T(8,128)S(1)}, f32[64,512]{1,0:T(8,128)S(1)}) custom-call(s32[1]{0:T(128)} %bitcast.refs_0_.core, f32[2,8]{1,0:T(2,128)S(4)} %get-tuple-element.47.refs_1_.refs_0_.scal, bf16[3,4,64,512]{3,2,1,0:T(8,128)(2,1)S(1)} %copy-done.1, s32[3,4,64,64]{3,2,1,0:T(8,128)S(1)} %copy-done.2, bf16[4,64,512]{2,1,0:T(8,128)(2,1)S(1)} %copy-done.5, ...), custom_call_target="tpu_custom_call" | custom-call | tf_op jit(solution)/shard_map/prepare_next/pallas_call | solution.py:490
  15.0 7.6 %collective-permute-start.5 = (f32[64,512]{1,0:T(8,128)S(1)}, f32[64,512]{1,0:T(8,128)S(1)}, u32[]{:S(2)}, u32[]{:S(2)}) collective-permute-start(f32[64,512]{1,0:T(8,128)S(1)} %get-tuple-element.61.refs_7_), channel_id=1, source_target_pairs={{0,1},{1,0},{2,3},{3,2},{4,5},{5,4},{6,7},{7,6},{8,9},{9,8},{10,11... | collective-permute-start | bytes 393224 | tf_op jit(solution)/shard_map/swap_s2_far/ppermute | solution.py:421
  22.7 1.7 %prepare_back.1 = (f32[2]{0:T(128)S(4)}, f32[2,64,512]{2,1,0:T(8,128)S(1)}, f32[2,64,512]{2,1,0:T(8,128)S(1)}, f32[2,64,512]{2,1,0:T(8,128)S(1)}) custom-call(s32[1]{0:T(128)} %bitcast.refs_0_.core, s32[1]{0:T(128)S(6)} %copy.17.own_weight, s32[1]{0:T(128)} %collective-permute-done.2.far_weight, bf16[4,64,512]{2,1,0:T(8,128)(2,1)} %goal.1, ...), custom_call_target="tpu_custom_call" | custom-call | tf_op jit(solution)/shard_map/prepare_back/pallas_call | solution.py:472
  24.5 0.5 collective-permute-start.8
  25.0 0.8 %third_stage.1.refs_3_ = f32[2,2,64,512]{3,2,1,0:T(8,128)S(1)} custom-call(s32[1]{0:T(128)} %bitcast.refs_0_.core, f32[2,8]{1,0:T(2,128)S(4)} %get-tuple-element.47.refs_1_.refs_0_.scal, f32[1,4,64,512]{3,2,1,0:T(8,128)S(1)} %copy-done, f32[1,4,64,512]{3,2,1,0:T(8,128)S(1)} %collective-permute-done.refs_2_.refs_3_.far, ...), custom_call_target="tpu_custom_call" | custom-call | tf_op jit(solution)/shard_map/third_stage/pallas_call | solution.py:387
  26.1 0.5 turn.1
  26.6 0.7 %collective-permute-start.9 = (f32[2,2,64,512]{3,2,1,0:T(8,128)S(1)}, f32[2,2,64,512]{3,2,1,0:T(8,128)S(1)}, u32[]{:S(2)}, u32[]{:S(2)}) collective-permute-start(f32[2,2,64,512]{3,2,1,0:T(8,128)S(1)} %get-tuple-element.65.refs_1_), channel_id=1, source_target_pairs={{1,2},{2,1},{3,4},{4,3},{5,6},{6,5},{7,8},{8,7},{9,10},{10,9},{11,... | collective-permute-start | bytes 1572872 | tf_op jit(solution)/shard_map/pass_back2/ppermute | solution.py:425
  27.7 5.8 %collective-permute-start.10 = (f32[88,512]{1,0:T(8,128)S(1)}, f32[88,512]{1,0:T(8,128)S(1)}, u32[]{:S(2)}, u32[]{:S(2)}) collective-permute-start(f32[88,512]{1,0:T(8,128)S(1)} %get-tuple-element.70.refs_10_), channel_id=1, source_target_pairs={{0,1},{1,0},{2,3},{3,2},{4,5},{5,4},{6,7},{7,6},{8,9},{9,8},{10,11... | collective-permute-start | bytes 540680 | tf_op jit(solution)/shard_map/swap_pin/ppermute | solution.py:421
  34.2 1.6 %collective-permute-start.13 = (f32[8,128]{1,0:T(8,128)S(1)}, f32[8,128]{1,0:T(8,128)S(1)}, u32[]{:S(2)}, u32[]{:S(2)}) collective-permute-start(f32[8,128]{1,0:T(8,128)S(1)} %goal_sum.1.refs_0_), channel_id=1, source_target_pairs={{0,4},{1,5},{2,6},{3,7},{4,0},{5,1},{6,2},{7,3},{8,12},{9,13},{10,... | collective-permute-start | bytes 12296 | tf_op jit(solution)/shard_map/goal_sum/ppermute | solution.py:534
  35.8 0.7 %back_second.1 = (f32[2,2,64,512]{3,2,1,0:T(8,128)S(1)}, f32[2,64,512]{2,1,0:T(8,128)S(1)}) custom-call(f32[2,8]{1,0:T(2,128)S(4)} %get-tuple-element.47.refs_1_.refs_0_.scal, f32[2,2,64,512]{3,2,1,0:T(8,128)S(1)} %get-tuple-element.65.refs_1_, f32[2,64,512]{2,1,0:T(8,128)S(1)} %get-tuple-element.66.refs_2_.refs_3_, ...), custom_call_target="tpu_custom_call" | custom-call | tf_op jit(solution)/shard_map/back_second/pallas_call | solution.py:387
  36.5 1.3 %collective-permute-done.13.refs_1_ = f32[8,128]{1,0:T(8,128)S(1)} collective-permute-done((f32[8,128]{1,0:T(8,128)S(1)}, f32[8,128]{1,0:T(8,128)S(1)}, u32[]{:S(2)}, u32[]{:S(2)}) %collective-permute-start.13) | collective-permute-done | bytes 4128 | tf_op jit(solution)/shard_map/goal_sum/ppermute | solution.py:534
  37.8 2.6 %collective-permute-start.15 = (f32[8,128]{1,0:T(8,128)S(1)}, f32[8,128]{1,0:T(8,128)S(1)}, u32[]{:S(2)}, u32[]{:S(2)}) collective-permute-start(f32[8,128]{1,0:T(8,128)S(1)} %combine.1.refs_7_.refs_13_), channel_id=1, source_target_pairs={{0,8},{1,9},{2,10},{3,11},{4,12},{5,13},{6,14},{7,15},{8,0},{9,1},... | collective-permute-start | bytes 12296 | tf_op jit(solution)/shard_map/goal_sum/ppermute | solution.py:534
  40.8 0.7 %collective-permute-start.14 = (f32[2,64,512]{2,1,0:T(8,128)S(1)}, f32[2,64,512]{2,1,0:T(8,128)S(1)}, u32[]{:S(2)}, u32[]{:S(2)}) collective-permute-start(f32[2,64,512]{2,1,0:T(8,128)S(1)} %get-tuple-element.77), channel_id=1, source_target_pairs={{1,2},{2,1},{3,4},{4,3},{5,6},{6,5},{7,8},{8,7},{9,10},{10,9},{11,... | collective-permute-start | bytes 786440 | tf_op jit(solution)/shard_map/pass_back1/ppermute | solution.py:425
  41.5 0.9 %collective-permute-done.15.refs_14_ = f32[8,128]{1,0:T(8,128)S(1)} collective-permute-done((f32[8,128]{1,0:T(8,128)S(1)}, f32[8,128]{1,0:T(8,128)S(1)}, u32[]{:S(2)}, u32[]{:S(2)}) %collective-permute-start.15) | collective-permute-done | bytes 4128 | tf_op jit(solution)/shard_map/goal_sum/ppermute | solution.py:534
  42.3 0.8 %close.1 = (f32[2,64,256]{2,1,0:T(8,128)S(1)}, f32[4,64,512]{2,1,0:T(8,128)S(1)}, f32[2,64,256]{2,1,0:T(8,128)S(1)}, f32[8,128]{1,0:T(8,128)S(1)}, f32[64,512]{1,0:T(8,128)S(1)}, /*index=5*/f32[64,512]{1,0:T(8,128)S(1)}) custom-call(s32[1]{0:T(128)} %bitcast.refs_0_.core, f32[2,8]{1,0:T(2,128)S(4)} %get-tuple-element.47.refs_1_.refs_0_.scal, ...), custom_call_target="tpu_custom_call" | custom-call | flops 16000000000 | bytes 48000000 | tf_op jit(solution)/shard_map/close/pallas_call | solution.py:387
  43.2 4.5 %collective-permute-start.17 = (f32[2,64,256]{2,1,0:T(8,128)S(1)}, f32[2,64,256]{2,1,0:T(8,128)S(1)}, u32[]{:S(2)}, u32[]{:S(2)}) collective-permute-start(f32[2,64,256]{2,1,0:T(8,128)S(1)} %get-tuple-element.82), channel_id=1, source_target_pairs={{0,1},{1,0},{2,3},{3,2},{4,5},{5,4},{6,7},{7,6},{8,9},{9,8},{10,11... | collective-permute-start | bytes 393224 | tf_op jit(solution)/shard_map/swap_gradient/ppermute | solution.py:421
  48.2 0.4 collective-permute-done.17.refs_3_
  49.2 0.9 %write_inner.1 = (f32[1,4,64,512]{3,2,1,0:T(8,128)}, f32[4,64,256]{2,1,0:T(8,128)}) custom-call(s32[1]{0:T(128)} %bitcast.refs_0_.core, f32[4,64,512]{2,1,0:T(8,128)S(1)} %get-tuple-element.79.refs_1_, f32[2,64,256]{2,1,0:T(8,128)S(1)} %get-tuple-element.81.refs_2_, f32[2,64,256]{2,1,0:T(8,128)S(1)} %collective-permute-done.17.refs_3_, ...), custom_call_target="tpu_custom_call" | custom-call | tf_op jit(solution)/shard_map/write_inner/pallas_call | solution.py:387
  50.1 1.1 %collective-permute-done.16.refs_3_ = f32[8,128]{1,0:T(8,128)S(1)} collective-permute-done((f32[8,128]{1,0:T(8,128)S(1)}, f32[8,128]{1,0:T(8,128)S(1)}, u32[]{:S(2)}, u32[]{:S(2)}) %collective-permute-start.16) | collective-permute-done | bytes 4128 | tf_op jit(solution)/shard_map/goal_sum/ppermute | solution.py:534
  51.4 0.7 %write_outer.1._ = f32[1,4,64,512]{3,2,1,0:T(8,128)} custom-call(s32[1]{0:T(128)} %bitcast.refs_0_.core, f32[64,512]{1,0:T(8,128)S(1)} %get-tuple-element.87.value, f32[1,4,64,512]{3,2,1,0:T(8,128)} %get-tuple-element.85.refs_4_._), custom_call_target="tpu_custom_call", output_to_operand_aliasing={{}: (2, {})} | custom-call | tf_op jit(solution)/shard_map/write_outer/pallas_call | solution.py:576
  52.1 0.6 %collective-permute-done.20.taken = f32[72,512]{1,0:T(8,128)S(1)} collective-permute-done((f32[72,512]{1,0:T(8,128)S(1)}, f32[72,512]{1,0:T(8,128)S(1)}, u32[]{:S(2)}, u32[]{:S(2)}) %collective-permute-start.20) | collective-permute-done | bytes 147488 | tf_op jit(solution)/shard_map/swap_outer/ppermute | solution.py:421
  52.7 0.7 %finish.1 = (f32[1,4,64,512]{3,2,1,0:T(8,128)}, f32[1]{0:T(128)}) custom-call(s32[1]{0:T(128)} %bitcast.refs_0_.core, f32[72,512]{1,0:T(8,128)S(1)} %get-tuple-element.86.mine, f32[72,512]{1,0:T(8,128)S(1)} %collective-permute-done.20.taken, f32[1,4,64,512]{3,2,1,0:T(8,128)} %write_outer.1._), custom_call_target="tpu_custom_call", output_to_operand_aliasing={{0}: (3, {})} | custom-call | tf_op jit(solution)/shard_map/finish/pallas_call | solution.py:586
  (44 shorter events, 4.2 us)
Async XLA Ops:
  0.6 2.3 %collective-permute-start = (f32[1,4,64,512]{3,2,1,0:T(8,128)}, f32[1,4,64,512]{3,2,1,0:T(8,128)S(1)}, u32[]{:S(2)}, u32[]{:S(2)}) collective-permute-start(f32[1,4,64,512]{3,2,1,0:T(8,128)} %refs_2_.7), channel_id=1, source_target_pairs={{0,1},{1,0},{2,3},{3,2},{4,5},{5,4},{6,7},{7,6},{8,9},{9,8},{10,11... | collective-permute-start | bytes 1572872 | tf_op jit(solution)/shard_map/swap_state/ppermute | solution.py:421
  1.1 1.8 %copy-start = (f32[1,4,64,512]{3,2,1,0:T(8,128)S(1)}, f32[1,4,64,512]{3,2,1,0:T(8,128)}, u32[]{:S(2)}) copy-start(f32[1,4,64,512]{3,2,1,0:T(8,128)} %refs_2_.7) | copy-start | bytes 1572868
  1.2 1.8 %copy-start.1 = (bf16[3,4,64,512]{3,2,1,0:T(8,128)(2,1)S(1)}, bf16[3,4,64,512]{3,2,1,0:T(8,128)(2,1)}, u32[]{:S(2)}) copy-start(bf16[3,4,64,512]{3,2,1,0:T(8,128)(2,1)} %speed.3) | copy-start | bytes 2359300
  1.2 1.8 %copy-start.2 = (s32[3,4,64,64]{3,2,1,0:T(8,128)S(1)}, s32[3,4,64,64]{3,2,1,0:T(8,128)}, u32[]{:S(2)}) copy-start(s32[3,4,64,64]{3,2,1,0:T(8,128)} %mask.3) | copy-start | bytes 589828
  2.9 7.3 %copy-start.3 = (f32[4,64,512]{2,1,0:T(8,128)S(1)}, f32[4,64,512]{2,1,0:T(8,128)}, u32[]{:S(2)}) copy-start(f32[4,64,512]{2,1,0:T(8,128)} %control.3) | copy-start | bytes 1572868
  3.1 1.4 %copy-start.4 = (f32[3,64,512]{2,1,0:T(8,128)}, f32[3,64,512]{2,1,0:T(8,128)S(1)}, u32[]{:S(2)}) copy-start(f32[3,64,512]{2,1,0:T(8,128)S(1)} %pack.1._) | copy-start | bytes 1179652
  3.1 10.0 %collective-permute-start.3 = (f32[3,64,512]{2,1,0:T(8,128)S(1)}, f32[3,64,512]{2,1,0:T(8,128)S(1)}, u32[]{:S(2)}, u32[]{:S(2)}) collective-permute-start(f32[3,64,512]{2,1,0:T(8,128)S(1)} %pack.1._), channel_id=1, source_target_pairs={{1,2},{2,1},{3,4},{4,3},{5,6},{6,5},{7,8},{8,7},{9,10},{10,9},{11,... | collective-permute-start | bytes 1179656 | tf_op jit(solution)/shard_map/pass_state/ppermute | solution.py:425
  5.1 5.1 %collective-permute-start.1 = (f32[8,128]{1,0:T(8,128)S(1)}, f32[8,128]{1,0:T(8,128)S(1)}, u32[]{:S(2)}, u32[]{:S(2)}) collective-permute-start(f32[8,128]{1,0:T(8,128)S(1)} %gather_numbers.1.own_numbers), channel_id=1, source_target_pairs={{0,1},{1,0},{2,3},{3,2},{4,5},{5,4},{6,7},{7,6},{8,9},{9,8},{10,11... | collective-permute-start | bytes 12296 | tf_op jit(solution)/shard_map/swap_numbers/ppermute | solution.py:421
  9.4 13.3 %collective-permute-start.2 = (s32[1]{0:T(128)}, s32[1]{0:T(128)}, u32[]{:S(2)}, u32[]{:S(2)}) collective-permute-start(s32[1]{0:T(128)} %param.18), channel_id=1, source_target_pairs={{0,1},{1,0},{2,3},{3,2},{4,5},{5,4},{6,7},{7,6},{8,9},{9,8},{10,11... | collective-permute-start | bytes 20 | tf_op jit(solution)/shard_map/swap_weight_num/ppermute | solution.py:421
  10.2 1.0 %copy-start.5 = (bf16[4,64,512]{2,1,0:T(8,128)(2,1)S(1)}, bf16[4,64,512]{2,1,0:T(8,128)(2,1)}, u32[]{:S(2)}) copy-start(bf16[4,64,512]{2,1,0:T(8,128)(2,1)} %decay.3) | copy-start | bytes 786436
  12.4 12.6 %collective-permute-start.7 = (f32[2,64,512]{2,1,0:T(8,128)S(1)}, f32[2,64,512]{2,1,0:T(8,128)S(1)}, u32[]{:S(2)}, u32[]{:S(2)}) collective-permute-start(f32[2,64,512]{2,1,0:T(8,128)S(1)} %get-tuple-element.53.refs_2_), channel_id=1, source_target_pairs={{1,2},{2,1},{3,4},{4,3},{5,6},{6,5},{7,8},{8,7},{9,10},{10,9},{11,... | collective-permute-start | bytes 786440 | tf_op jit(solution)/shard_map/pass_stage1/ppermute | solution.py:425
  13.4 12.7 %collective-permute-start.4 = (f32[2,64,512]{2,1,0:T(8,128)S(1)}, f32[2,64,512]{2,1,0:T(8,128)S(1)}, u32[]{:S(2)}, u32[]{:S(2)}) collective-permute-start(f32[2,64,512]{2,1,0:T(8,128)S(1)} %get-tuple-element.55._.refs_4_), channel_id=1, source_target_pairs={{1,2},{2,1},{3,4},{4,3},{5,6},{6,5},{7,8},{8,7},{9,10},{10,9},{11,... | collective-permute-start | bytes 786440 | tf_op jit(solution)/shard_map/pass_stage2/ppermute | solution.py:425
  15.0 10.0 %collective-permute-start.5 = (f32[64,512]{1,0:T(8,128)S(1)}, f32[64,512]{1,0:T(8,128)S(1)}, u32[]{:S(2)}, u32[]{:S(2)}) collective-permute-start(f32[64,512]{1,0:T(8,128)S(1)} %get-tuple-element.61.refs_7_), channel_id=1, source_target_pairs={{0,1},{1,0},{2,3},{3,2},{4,5},{5,4},{6,7},{7,6},{8,9},{9,8},{10,11... | collective-permute-start | bytes 393224 | tf_op jit(solution)/shard_map/swap_s2_far/ppermute | solution.py:421
  22.6 2.4 %collective-permute-start.6 = (f32[64,512]{1,0:T(8,128)S(1)}, f32[64,512]{1,0:T(8,128)S(1)}, u32[]{:S(2)}, u32[]{:S(2)}) collective-permute-start(f32[64,512]{1,0:T(8,128)S(1)} %get-tuple-element.60.refs_6_), channel_id=1, source_target_pairs={{0,1},{1,0},{2,3},{3,2},{4,5},{5,4},{6,7},{7,6},{8,9},{9,8},{10,11... | collective-permute-start | bytes 393224 | tf_op jit(solution)/shard_map/swap_s2_own/ppermute | solution.py:421
  24.5 1.7 %collective-permute-start.8 = (f32[2,64,512]{2,1,0:T(8,128)S(1)}, f32[2,64,512]{2,1,0:T(8,128)S(1)}, u32[]{:S(2)}, u32[]{:S(2)}) collective-permute-start(f32[2,64,512]{2,1,0:T(8,128)S(1)} %get-tuple-element.64), channel_id=1, source_target_pairs={{0,1},{1,0},{2,3},{3,2},{4,5},{5,4},{6,7},{7,6},{8,9},{9,8},{10,11... | collective-permute-start | bytes 786440 | tf_op jit(solution)/shard_map/swap_after/ppermute | solution.py:421
  26.6 13.8 %collective-permute-start.9 = (f32[2,2,64,512]{3,2,1,0:T(8,128)S(1)}, f32[2,2,64,512]{3,2,1,0:T(8,128)S(1)}, u32[]{:S(2)}, u32[]{:S(2)}) collective-permute-start(f32[2,2,64,512]{3,2,1,0:T(8,128)S(1)} %get-tuple-element.65.refs_1_), channel_id=1, source_target_pairs={{1,2},{2,1},{3,4},{4,3},{5,6},{6,5},{7,8},{8,7},{9,10},{10,9},{11,... | collective-permute-start | bytes 1572872 | tf_op jit(solution)/shard_map/pass_back2/ppermute | solution.py:425
  27.7 8.1 %collective-permute-start.10 = (f32[88,512]{1,0:T(8,128)S(1)}, f32[88,512]{1,0:T(8,128)S(1)}, u32[]{:S(2)}, u32[]{:S(2)}) collective-permute-start(f32[88,512]{1,0:T(8,128)S(1)} %get-tuple-element.70.refs_10_), channel_id=1, source_target_pairs={{0,1},{1,0},{2,3},{3,2},{4,5},{5,4},{6,7},{7,6},{8,9},{9,8},{10,11... | collective-permute-start | bytes 540680 | tf_op jit(solution)/shard_map/swap_pin/ppermute | solution.py:421
  33.5 2.3 %collective-permute-start.11 = (f32[88,512]{1,0:T(8,128)S(1)}, f32[88,512]{1,0:T(8,128)S(1)}, u32[]{:S(2)}, u32[]{:S(2)}) collective-permute-start(f32[88,512]{1,0:T(8,128)S(1)} %get-tuple-element.71.refs_11_), channel_id=1, source_target_pairs={{0,1},{1,0},{2,3},{3,2},{4,5},{5,4},{6,7},{7,6},{8,9},{9,8},{10,11... | collective-permute-start | bytes 540680 | tf_op jit(solution)/shard_map/swap_pin/ppermute | solution.py:421
  33.6 2.2 %collective-permute-start.12 = (f32[80,512]{1,0:T(8,128)S(1)}, f32[80,512]{1,0:T(8,128)S(1)}, u32[]{:S(2)}, u32[]{:S(2)}) collective-permute-start(f32[80,512]{1,0:T(8,128)S(1)} %get-tuple-element.72.refs_12_), channel_id=1, source_target_pairs={{0,1},{1,0},{2,3},{3,2},{4,5},{5,4},{6,7},{7,6},{8,9},{9,8},{10,11... | collective-permute-start | bytes 491528 | tf_op jit(solution)/shard_map/swap_pin/ppermute | solution.py:421
  34.2 3.7 %collective-permute-start.13 = (f32[8,128]{1,0:T(8,128)S(1)}, f32[8,128]{1,0:T(8,128)S(1)}, u32[]{:S(2)}, u32[]{:S(2)}) collective-permute-start(f32[8,128]{1,0:T(8,128)S(1)} %goal_sum.1.refs_0_), channel_id=1, source_target_pairs={{0,4},{1,5},{2,6},{3,7},{4,0},{5,1},{6,2},{7,3},{8,12},{9,13},{10,... | collective-permute-start | bytes 12296 | tf_op jit(solution)/shard_map/goal_sum/ppermute | solution.py:534
  37.8 4.5 %collective-permute-start.15 = (f32[8,128]{1,0:T(8,128)S(1)}, f32[8,128]{1,0:T(8,128)S(1)}, u32[]{:S(2)}, u32[]{:S(2)}) collective-permute-start(f32[8,128]{1,0:T(8,128)S(1)} %combine.1.refs_7_.refs_13_), channel_id=1, source_target_pairs={{0,8},{1,9},{2,10},{3,11},{4,12},{5,13},{6,14},{7,15},{8,0},{9,1},... | collective-permute-start | bytes 12296 | tf_op jit(solution)/shard_map/goal_sum/ppermute | solution.py:534
  40.8 10.4 %collective-permute-start.14 = (f32[2,64,512]{2,1,0:T(8,128)S(1)}, f32[2,64,512]{2,1,0:T(8,128)S(1)}, u32[]{:S(2)}, u32[]{:S(2)}) collective-permute-start(f32[2,64,512]{2,1,0:T(8,128)S(1)} %get-tuple-element.77), channel_id=1, source_target_pairs={{1,2},{2,1},{3,4},{4,3},{5,6},{6,5},{7,8},{8,7},{9,10},{10,9},{11,... | collective-permute-start | bytes 786440 | tf_op jit(solution)/shard_map/pass_back1/ppermute | solution.py:425
  43.2 5.5 %collective-permute-start.17 = (f32[2,64,256]{2,1,0:T(8,128)S(1)}, f32[2,64,256]{2,1,0:T(8,128)S(1)}, u32[]{:S(2)}, u32[]{:S(2)}) collective-permute-start(f32[2,64,256]{2,1,0:T(8,128)S(1)} %get-tuple-element.82), channel_id=1, source_target_pairs={{0,1},{1,0},{2,3},{3,2},{4,5},{5,4},{6,7},{7,6},{8,9},{9,8},{10,11... | collective-permute-start | bytes 393224 | tf_op jit(solution)/shard_map/swap_gradient/ppermute | solution.py:421
  47.7 1.3 %collective-permute-start.18 = (f32[64,512]{1,0:T(8,128)S(1)}, f32[64,512]{1,0:T(8,128)S(1)}, u32[]{:S(2)}, u32[]{:S(2)}) collective-permute-start(f32[64,512]{1,0:T(8,128)S(1)} %get-tuple-element.83), channel_id=1, source_target_pairs={{0,1},{1,0},{2,3},{3,2},{4,5},{5,4},{6,7},{7,6},{8,9},{9,8},{10,11... | collective-permute-start | bytes 393224 | tf_op jit(solution)/shard_map/swap_adjoint/ppermute | solution.py:421
  47.7 1.5 %collective-permute-start.19 = (f32[64,512]{1,0:T(8,128)S(1)}, f32[64,512]{1,0:T(8,128)S(1)}, u32[]{:S(2)}, u32[]{:S(2)}) collective-permute-start(f32[64,512]{1,0:T(8,128)S(1)} %get-tuple-element.84), channel_id=1, source_target_pairs={{0,1},{1,0},{2,3},{3,2},{4,5},{5,4},{6,7},{7,6},{8,9},{9,8},{10,11... | collective-permute-start | bytes 393224 | tf_op jit(solution)/shard_map/swap_adjoint/ppermute | solution.py:421
  48.2 3.0 %collective-permute-start.16 = (f32[8,128]{1,0:T(8,128)S(1)}, f32[8,128]{1,0:T(8,128)S(1)}, u32[]{:S(2)}, u32[]{:S(2)}) collective-permute-start(f32[8,128]{1,0:T(8,128)S(1)} %get-tuple-element.80.refs_2_), channel_id=1, source_target_pairs={{0,3},{1,2},{2,1},{3,0},{4,7},{5,6},{6,5},{7,4},{8,11},{9,10},{10,... | collective-permute-start | bytes 12296 | tf_op jit(solution)/shard_map/goal_sum/ppermute | solution.py:534
  51.2 1.4 %collective-permute-start.20 = (f32[72,512]{1,0:T(8,128)S(1)}, f32[72,512]{1,0:T(8,128)S(1)}, u32[]{:S(2)}, u32[]{:S(2)}) collective-permute-start(f32[72,512]{1,0:T(8,128)S(1)} %get-tuple-element.86.mine), channel_id=1, source_target_pairs={{0,1},{1,0},{2,3},{3,2},{4,5},{5,4},{6,7},{7,6},{8,9},{9,8},{10,11... | collective-permute-start | bytes 442376 | tf_op jit(solution)/shard_map/swap_outer/ppermute | solution.py:421
